TPU v7x, 128 devices: a whole 4x4x4 slice. The times are simulated.
128 devices in a mesh: pipe: 2 (over z_lo), tensor: 8 (over x, z_hi), dp: 8 (over y, core).
Axes of the slice: x: 4, y: 4, z: 4 (z_hi: 2, z_lo: 2; z = z_hi * 2 + z_lo), core: 2. Of those that a mesh axis runs over, the one named last changes fastest.
Arguments:
- inputs: bfloat16 [2, 768, 8, 1024], P(None, 'tensor', 'dp'), may hold values from -6 to 6
- segment_ids: int32 [2, 8, 768], P(None, 'dp'), may hold values from 0 to 3, never falling along the last dimension, each value on 1 to 384 neighbouring positions
- cotangent: bfloat16 [2, 768, 8, 1024], P(None, 'tensor', 'dp'), may hold values from -6 to 6
- ln1_gain: bfloat16 [2, 1024], P('pipe'), may hold values from 0.099609375 to 1.8984375
- ln1_bias: bfloat16 [2, 1024], P('pipe'), may hold values from -1.5 to 1.5
- w_qkv: bfloat16 [2, 1024, 3, 1024], P('pipe', None, None, 'tensor'), may hold values from -0.1875 to 0.1875
- qv_bias: bfloat16 [2, 2, 1024], P('pipe', None, 'tensor'), may hold values from -1.5 to 1.5
- w_out: bfloat16 [2, 1024, 1024], P('pipe', 'tensor'), may hold values from -1 to 1
- out_bias: bfloat16 [2, 1024], P('pipe'), may hold values from -1.5 to 1.5
- ln2_gain: bfloat16 [2, 1024], P('pipe'), may hold values from 0.099609375 to 1.8984375
- ln2_bias: bfloat16 [2, 1024], P('pipe'), may hold values from -1.5 to 1.5
- w_fc: bfloat16 [2, 1024, 4096], P('pipe', None, 'tensor'), may hold values from -0.1875 to 0.1875
- fc_bias: bfloat16 [2, 4096], P('pipe', 'tensor'), may hold values from -1.5 to 1.5
- w_proj: bfloat16 [2, 4096, 1024], P('pipe', 'tensor'), may hold values from -0.125 to 0.125
- proj_bias: bfloat16 [2, 1024], P('pipe'), may hold values from -1.5 to 1.5
Outputs:
- activations: bfloat16 [2, 2, 768, 8, 1024], P('pipe', None, 'tensor', 'dp')
- in_grads: bfloat16 [2, 2, 768, 8, 1024], P('pipe', None, 'tensor', 'dp')
- ln1_gain_grad: float32 [2, 1024], P('pipe')
- ln1_bias_grad: float32 [2, 1024], P('pipe')
- w_qkv_grad: float32 [2, 1024, 3, 1024], P('pipe', None, None, 'tensor')
- qv_bias_grad: float32 [2, 2, 1024], P('pipe', None, 'tensor')
- w_out_grad: float32 [2, 1024, 1024], P('pipe', 'tensor')
- out_bias_grad: float32 [2, 1024], P('pipe')
- ln2_gain_grad: float32 [2, 1024], P('pipe')
- ln2_bias_grad: float32 [2, 1024], P('pipe')
- w_fc_grad: float32 [2, 1024, 4096], P('pipe', None, 'tensor')
- fc_bias_grad: float32 [2, 4096], P('pipe', 'tensor')
- w_proj_grad: float32 [2, 4096, 1024], P('pipe', 'tensor')
- proj_bias_grad: float32 [2, 1024], P('pipe')
Inputs may be any that keep to these rules, and one draw needn't show every extreme that they name: `segment_ids`: along each sequence the document number never falls; each document has 1 to 384 tokens.
All inputs are finite; a program needn't handle non-finite values.
Results may differ from a plain program's by a relative error of at most 0.024.
Values may be sent and summed in bfloat16 or wider, within the bound.
No kernel may reach another device: no remote copies, remote signals or barrier semaphores. Data moves between devices by JAX's collectives and lax.ppermute only.
A program may use at most 128 MiB of HBM per device.

v0:
```python
import jax
import jax.numpy as jnp
from jax import lax
from jax.sharding import PartitionSpec as P

HEAD_DIM = 64
MICRO = 2


epsilon = 1e-05


def as_sent(shard):
    return jax.tree.map(lambda a: a.astype(jnp.bfloat16) if a.dtype == jnp.float32 else a, shard)


def shifted(shard, axis, by):
    peers = lax.axis_size(axis)
    pairs = [(i, i + by) for i in range(peers) if 0 <= i + by < peers]
    return lax.ppermute(shard, axis, pairs)


def norm_forward(stream, gain, shift):
    average = jnp.mean(stream, axis=-1, keepdims=True)
    centred = stream - average
    inverse_scale = lax.rsqrt(jnp.mean(centred * centred, axis=-1, keepdims=True) + epsilon)
    standard = centred * inverse_scale
    return (standard * gain + shift, standard, inverse_scale)


def norm_backward(incoming, standard, inverse_scale, gain):
    scaled = incoming * gain
    correction = (
        scaled
        - jnp.mean(scaled, axis=-1, keepdims=True)
        - standard * jnp.mean(scaled * standard, axis=-1, keepdims=True)
    )
    return (
        correction * inverse_scale,
        jnp.sum(incoming * standard, axis=(0, 1)),
        jnp.sum(incoming, axis=(0, 1)),
    )


def masked_scores(query, key_rows, segment):
    scores = jnp.einsum(
        "qhe,khe->hqk", query, key_rows, preferred_element_type=jnp.float32
    ) * HEAD_DIM ** (-0.5)
    positions = jnp.arange(segment.shape[0])
    allowed = (segment[:, None] == segment[None, :]) & (positions[None, :] <= positions[:, None])
    return jnp.where(allowed[None], scores, -1e30)


def attend_forward(element):
    stacked, segment = element
    query, key_rows, value_rows = (stacked[:, 0], stacked[:, 1], stacked[:, 2])
    scores = masked_scores(query, key_rows, segment)
    largest = jnp.max(scores, axis=-1, keepdims=True)
    exponent_terms = jnp.exp(scores - largest)
    summed = jnp.sum(exponent_terms, axis=-1, keepdims=True)
    soft_weights = (exponent_terms / summed).astype(jnp.bfloat16)
    context = jnp.einsum(
        "hqk,khe->qhe", soft_weights, value_rows, preferred_element_type=jnp.float32
    )
    return (context, largest + jnp.log(summed))


def attend_backward(element):
    stacked, segment, log_total, context_grad = element
    query, key_rows, value_rows = (stacked[:, 0], stacked[:, 1], stacked[:, 2])
    scores = masked_scores(query, key_rows, segment)
    soft_weights = jnp.exp(scores - log_total)
    rounded = soft_weights.astype(jnp.bfloat16)
    weight_grad = jnp.einsum(
        "qhe,khe->hqk", context_grad, value_rows, preferred_element_type=jnp.float32
    )
    value_grad = jnp.einsum(
        "hqk,qhe->khe", rounded, context_grad, preferred_element_type=jnp.float32
    )
    correction = jnp.sum(soft_weights * weight_grad, axis=-1, keepdims=True)
    score_grad = (soft_weights * (weight_grad - correction)).astype(jnp.bfloat16)
    query_grad = jnp.einsum(
        "hqk,khe->qhe", score_grad, key_rows, preferred_element_type=jnp.float32
    ) * HEAD_DIM ** (-0.5)
    key_grad = jnp.einsum(
        "hqk,qhe->khe", score_grad, query, preferred_element_type=jnp.float32
    ) * HEAD_DIM ** (-0.5)
    return (query_grad, key_grad, value_grad)


def rows_product(normed, weight):
    return (
        normed,
        jnp.einsum(
            "lbd,dw->lbw",
            lax.all_gather(normed, "tensor", axis=0, tiled=True),
            weight,
            preferred_element_type=jnp.float32,
        ),
    )


def rows_weight_grad(kept, grad_full):
    return jnp.einsum(
        "lbd,lbw->dw",
        lax.all_gather(kept, "tensor", axis=0, tiled=True),
        grad_full,
        preferred_element_type=jnp.float32,
    )


def branch_sum(values, weight):
    return lax.psum_scatter(
        jnp.einsum("lbw,wd->lbd", values, weight, preferred_element_type=jnp.float32).astype(
            jnp.bfloat16
        ),
        "tensor",
        scatter_dimension=0,
        tiled=True,
    ).astype(jnp.float32)


def input_sum(grad_full, weight):
    return lax.psum_scatter(
        jnp.einsum("lbw,dw->lbd", grad_full, weight, preferred_element_type=jnp.float32).astype(
            jnp.bfloat16
        ),
        "tensor",
        scatter_dimension=0,
        tiled=True,
    ).astype(jnp.float32)


def grad_rows(grad_local, weight, values):
    shard_rows = lax.all_gather(grad_local, "tensor", axis=0, tiled=True)
    product = jnp.einsum("lbd,wd->lbw", shard_rows, weight, preferred_element_type=jnp.float32)
    weight_grad = jnp.einsum("lbw,lbd->wd", values, shard_rows, preferred_element_type=jnp.float32)
    return (product, weight_grad)


def layer_forward(stream, segment_rows, weights):
    (
        gain_one,
        shift_one,
        w_qkv,
        qv_bias,
        w_out,
        out_bias,
        gain_two,
        shift_two,
        w_fc,
        fc_bias,
        w_proj,
        proj_bias,
    ) = weights
    model_width = stream.shape[-1]
    local_width = w_qkv.shape[2]
    normed_one, standard_one, inverse_one = norm_forward(stream, gain_one, shift_one)
    kept_one, projected = rows_product(
        normed_one.astype(jnp.bfloat16), w_qkv.reshape(model_width, 3 * local_width)
    )
    full_rows, batch_count = (projected.shape[0], projected.shape[1])
    biases = jnp.stack([qv_bias[0], jnp.zeros_like(qv_bias[0]), qv_bias[1]]).astype(jnp.float32)
    triple = (projected.reshape(full_rows, batch_count, 3, local_width) + biases).astype(
        jnp.bfloat16
    )
    head_view = jnp.moveaxis(
        triple.reshape(full_rows, batch_count, 3, local_width // HEAD_DIM, HEAD_DIM), 1, 0
    )
    context, log_total = lax.map(attend_forward, (head_view, segment_rows))
    context_low = (
        jnp.moveaxis(context, 0, 1)
        .reshape(full_rows, batch_count, local_width)
        .astype(jnp.bfloat16)
    )
    middle = stream + branch_sum(context_low, w_out) + out_bias
    normed_two, standard_two, inverse_two = norm_forward(middle, gain_two, shift_two)
    kept_two, gelu_input = rows_product(normed_two.astype(jnp.bfloat16), w_fc)
    gelu_input = gelu_input + fc_bias
    hidden = jax.nn.gelu(gelu_input, approximate=True).astype(jnp.bfloat16)
    result = middle + branch_sum(hidden, w_proj) + proj_bias
    saved = (
        standard_one,
        inverse_one,
        kept_one,
        triple,
        log_total,
        context_low,
        standard_two,
        inverse_two,
        kept_two,
        gelu_input,
        hidden,
    )
    return (result, saved)


def layer_backward(incoming, segment_rows, weights, saved):
    (
        gain_one,
        shift_one,
        w_qkv,
        qv_bias,
        w_out,
        out_bias,
        gain_two,
        shift_two,
        w_fc,
        fc_bias,
        w_proj,
        proj_bias,
    ) = weights
    (
        standard_one,
        inverse_one,
        kept_one,
        triple,
        log_total,
        context_low,
        standard_two,
        inverse_two,
        kept_two,
        gelu_input,
        hidden,
    ) = saved
    model_width = incoming.shape[-1]
    full_rows, batch_count, local_width = context_low.shape
    grad_feed = incoming.astype(jnp.bfloat16)
    proj_bias_grad = jnp.sum(grad_feed.astype(jnp.float32), axis=(0, 1))
    hidden_grad, w_proj_grad = grad_rows(grad_feed, w_proj, hidden)
    gelu_value, gelu_pull = jax.vjp(
        lambda values: jax.nn.gelu(values, approximate=True), gelu_input
    )
    gelu_grad = gelu_pull(hidden_grad)[0].astype(jnp.bfloat16)
    fc_bias_grad = jnp.sum(gelu_grad.astype(jnp.float32), axis=(0, 1))
    w_fc_grad = rows_weight_grad(kept_two, gelu_grad)
    normed_two_grad = input_sum(gelu_grad, w_fc)
    middle_norm, gain_two_grad, shift_two_grad = norm_backward(
        normed_two_grad, standard_two, inverse_two, gain_two
    )
    middle_grad = incoming + middle_norm
    grad_attention = middle_grad.astype(jnp.bfloat16)
    out_bias_grad = jnp.sum(grad_attention.astype(jnp.float32), axis=(0, 1))
    context_grad, w_out_grad = grad_rows(grad_attention, w_out, context_low)
    context_grad = context_grad.astype(jnp.bfloat16).reshape(
        full_rows, batch_count, local_width // HEAD_DIM, HEAD_DIM
    )
    head_view = jnp.moveaxis(
        triple.reshape(full_rows, batch_count, 3, local_width // HEAD_DIM, HEAD_DIM), 1, 0
    )
    query_grad, key_grad, value_grad = lax.map(
        attend_backward, (head_view, segment_rows, log_total, jnp.moveaxis(context_grad, 1, 0))
    )
    triple_grad = jnp.moveaxis(jnp.stack([query_grad, key_grad, value_grad], axis=2), 0, 1)
    triple_grad = triple_grad.reshape(full_rows, batch_count, 3 * local_width).astype(jnp.bfloat16)
    bias_sums = jnp.sum(triple_grad.astype(jnp.float32), axis=(0, 1)).reshape(3, local_width)
    qv_bias_grad = jnp.stack([bias_sums[0], bias_sums[2]])
    w_qkv_grad = rows_weight_grad(kept_one, triple_grad).reshape(model_width, 3, local_width)
    normed_one_grad = input_sum(triple_grad, w_qkv.reshape(model_width, 3 * local_width))
    stream_norm, gain_one_grad, shift_one_grad = norm_backward(
        normed_one_grad, standard_one, inverse_one, gain_one
    )
    stream_grad = middle_grad + stream_norm
    matrix_terms = (w_qkv_grad, qv_bias_grad, w_out_grad, w_fc_grad, fc_bias_grad, w_proj_grad)
    norm_terms = (
        gain_one_grad,
        shift_one_grad,
        out_bias_grad,
        gain_two_grad,
        shift_two_grad,
        proj_bias_grad,
    )
    return (stream_grad, matrix_terms, norm_terms)


def sum_weights(matrix_terms):
    return jax.tree.map(
        lambda part: part.astype(jnp.float32), lax.psum(as_sent(matrix_terms), "dp")
    )


def add_trees(left_tree, right_tree):
    return jax.tree.map(lambda left_item, right_item: left_item + right_item, left_tree, right_tree)


def on_device(
    inputs,
    segment_ids,
    cotangent,
    ln1_gain,
    ln1_bias,
    w_qkv,
    qv_bias,
    w_out,
    out_bias,
    ln2_gain,
    ln2_bias,
    w_fc,
    fc_bias,
    w_proj,
    proj_bias,
):
    weights = tuple(
        (
            item[0]
            for item in (
                ln1_gain,
                ln1_bias,
                w_qkv,
                qv_bias,
                w_out,
                out_bias,
                ln2_gain,
                ln2_bias,
                w_fc,
                fc_bias,
                w_proj,
                proj_bias,
            )
        )
    )
    first_section = lax.axis_index("pipe") == 0
    blank = jnp.zeros(inputs.shape[1:], jnp.bfloat16)
    received = blank
    outgoing_list = []
    saved_list = []
    for section_step in range(MICRO + 1):
        local_input = inputs[section_step] if section_step < MICRO else blank
        stream = jnp.where(first_section, local_input, received).astype(jnp.float32)
        segment_rows = jnp.where(
            first_section,
            segment_ids[min(section_step, MICRO - 1)],
            segment_ids[max(section_step - 1, 0)],
        )
        result, saved = layer_forward(stream, segment_rows, weights)
        outgoing = result.astype(jnp.bfloat16)
        outgoing_list.append(outgoing)
        saved_list.append(saved)
        if section_step < MICRO:
            received = shifted(outgoing, "pipe", 1)
    activations = jnp.stack(
        [
            jnp.where(first_section, outgoing_list[index_m], outgoing_list[index_m + 1])
            for index_m in range(MICRO)
        ]
    )
    returned = blank
    ingrad_list = []
    summed_grads = None
    norm_sums = None
    for section_step in range(MICRO + 1):
        early_step = max(section_step - 1, 0)
        later_step = min(section_step + 1, MICRO)
        saved = jax.tree.map(
            lambda early_item, later_item: jnp.where(first_section, early_item, later_item),
            saved_list[early_step],
            saved_list[later_step],
        )
        segment_rows = jnp.where(
            first_section, segment_ids[early_step], segment_ids[min(section_step, MICRO - 1)]
        )
        local_grad = cotangent[section_step] if section_step < MICRO else blank
        incoming = jnp.where(first_section, returned, local_grad).astype(jnp.float32)
        stream_grad, matrix_terms, norm_terms = layer_backward(
            incoming, segment_rows, weights, saved
        )
        outgoing = stream_grad.astype(jnp.bfloat16)
        ingrad_list.append(outgoing)
        if section_step < MICRO:
            returned = shifted(outgoing, "pipe", -1)
        summed_grads = (
            matrix_terms if summed_grads is None else add_trees(summed_grads, matrix_terms)
        )
        norm_sums = norm_terms if norm_sums is None else add_trees(norm_sums, norm_terms)
    matrix_total = sum_weights(summed_grads)
    norm_total = lax.psum(norm_sums, ("tensor", "dp"))
    in_grads = jnp.stack(
        [
            jnp.where(first_section, ingrad_list[index_m + 1], ingrad_list[index_m])
            for index_m in range(MICRO)
        ]
    )
    w_qkv_grad, qv_bias_grad, w_out_grad, w_fc_grad, fc_bias_grad, w_proj_grad = matrix_total
    gain_one_grad, shift_one_grad, out_bias_grad, gain_two_grad, shift_two_grad, proj_bias_grad = (
        norm_total
    )
    return (
        activations[None],
        in_grads[None],
        gain_one_grad[None],
        shift_one_grad[None],
        w_qkv_grad[None],
        qv_bias_grad[None],
        w_out_grad[None],
        out_bias_grad[None],
        gain_two_grad[None],
        shift_two_grad[None],
        w_fc_grad[None],
        fc_bias_grad[None],
        w_proj_grad[None],
        proj_bias_grad[None],
    )


def solution(mesh):
    return jax.shard_map(
        on_device,
        mesh=mesh,
        in_specs=(
            P(None, "tensor", "dp", None),
            P(None, "dp", None),
            P(None, "tensor", "dp", None),
            P("pipe", None),
            P("pipe", None),
            P("pipe", None, None, "tensor"),
            P("pipe", None, "tensor"),
            P("pipe", "tensor", None),
            P("pipe", None),
            P("pipe", None),
            P("pipe", None),
            P("pipe", None, "tensor"),
            P("pipe", "tensor"),
            P("pipe", "tensor", None),
            P("pipe", None),
        ),
        out_specs=(
            P("pipe", None, "tensor", "dp", None),
            P("pipe", None, "tensor", "dp", None),
            P("pipe", None),
            P("pipe", None),
            P("pipe", None, None, "tensor"),
            P("pipe", None, "tensor"),
            P("pipe", "tensor", None),
            P("pipe", None),
            P("pipe", None),
            P("pipe", None),
            P("pipe", None, "tensor"),
            P("pipe", "tensor"),
            P("pipe", "tensor", None),
            P("pipe", None),
        ),
        check_vma=False,
    )
```

profile of v0, /device:TPU:1, one launch (start us, length us, event | category | flops | bytes accessed | tf_op | source)
XLA Modules:
  0.0 2360.0 jit_solution(15740182052735173803)
XLA Ops:
  14.2 52.1 %all-gather.20.cloned.1.call-done = bf16[768,1,1024]{2,0,1:T(8,128)(2,1)} async-done(((bf16[96,1,1024]{2,0,1:T(8,128)(2,1)}), bf16[768,1,1024]{2,0,1:T(8,128)(2,1)}) %all-gather.20.cloned.1.call-update) | async-done | bytes 1572880 | tf_op jit(solution)/shard_map/all_gather | solution.py:96
  74.3 73.4 %reduce-scatter.13.cloned.1.call-done = bf16[96,1,1024]{2,0,1:T(8,128)(2,1)} async-done(((bf16[768,1,1024]{2,0,1:T(8,128)(2,1)}), bf16[96,1,1024]{2,0,1:T(8,128)(2,1)}) %reduce-scatter.13.cloned.1.call-update) | async-done | bytes 196624 | tf_op jit(solution)/shard_map/reduce_scatter | solution.py:113
  151.8 49.5 %all-gather.22.cloned.1.call-done = bf16[768,1,1024]{2,0,1:T(8,128)(2,1)} async-done(((bf16[96,1,1024]{2,0,1:T(8,128)(2,1)}), bf16[768,1,1024]{2,0,1:T(8,128)(2,1)}) %all-gather.22.cloned.1.call-update) | async-done | bytes 1572880 | tf_op jit(solution)/shard_map/all_gather | solution.py:96
  208.2 72.8 %reduce-scatter.15.cloned.1.call-done = bf16[96,1,1024]{2,0,1:T(8,128)(2,1)} async-done(((bf16[768,1,1024]{2,0,1:T(8,128)(2,1)}), bf16[96,1,1024]{2,0,1:T(8,128)(2,1)}) %reduce-scatter.15.cloned.1.call-update) | async-done | bytes 196624 | tf_op jit(solution)/shard_map/reduce_scatter | solution.py:113
  289.0 51.5 %all-gather.24.cloned.1.call-done = bf16[768,1,1024]{2,0,1:T(8,128)(2,1)} async-done(((bf16[96,1,1024]{2,0,1:T(8,128)(2,1)}), bf16[768,1,1024]{2,0,1:T(8,128)(2,1)}) %all-gather.24.cloned.1.call-update) | async-done | bytes 1572880 | tf_op jit(solution)/shard_map/all_gather | solution.py:96
  349.3 73.4 %reduce-scatter.17.cloned.1.call-done = bf16[96,1,1024]{2,0,1:T(8,128)(2,1)} async-done(((bf16[768,1,1024]{2,0,1:T(8,128)(2,1)}), bf16[96,1,1024]{2,0,1:T(8,128)(2,1)}) %reduce-scatter.17.cloned.1.call-update) | async-done | bytes 196624 | tf_op jit(solution)/shard_map/reduce_scatter | solution.py:113
  426.9 49.6 %all-gather.26.cloned.1.call-done = bf16[768,1,1024]{2,0,1:T(8,128)(2,1)} async-done(((bf16[96,1,1024]{2,0,1:T(8,128)(2,1)}), bf16[768,1,1024]{2,0,1:T(8,128)(2,1)}) %all-gather.26.cloned.1.call-update) | async-done | bytes 1572880 | tf_op jit(solution)/shard_map/all_gather | solution.py:96
  482.7 73.5 %reduce-scatter.19.cloned.1.call-done = bf16[96,1,1024]{2,0,1:T(8,128)(2,1)} async-done(((bf16[768,1,1024]{2,0,1:T(8,128)(2,1)}), bf16[96,1,1024]{2,0,1:T(8,128)(2,1)}) %reduce-scatter.19.cloned.1.call-update) | async-done | bytes 196624 | tf_op jit(solution)/shard_map/reduce_scatter | solution.py:113
  567.6 50.0 %all-gather.28.cloned.1.call-done = bf16[768,1,1024]{2,0,1:T(8,128)(2,1)} async-done(((bf16[96,1,1024]{2,0,1:T(8,128)(2,1)}), bf16[768,1,1024]{2,0,1:T(8,128)(2,1)}) %all-gather.28.cloned.1.call-update) | async-done | bytes 1572880 | tf_op jit(solution)/shard_map/all_gather | solution.py:96
  627.9 41.7 %all-gather.54.cloned.1.call-done = bf16[1,768,1,1024]{3,1,2,0:T(8,128)(2,1)} async-done(((bf16[1,96,1,1024]{3,1,2,0:T(8,128)(2,1)}), bf16[1,768,1,1024]{3,1,2,0:T(8,128)(2,1)}) %all-gather.54.cloned.1.call-update) | async-done | bytes 1572880 | tf_op jit(solution)/shard_map/all_gather | solution.py:135
  669.6 4.5 convert_reduce_fusion.2
  677.2 70.1 %reduce-scatter.21.cloned.1.call-done = bf16[96,1,1024]{2,0,1:T(8,128)(2,1)} async-done(((bf16[768,1,1024]{2,0,1:T(8,128)(2,1)}), bf16[96,1,1024]{2,0,1:T(8,128)(2,1)}) %reduce-scatter.21.cloned.1.call-update) | async-done | bytes 196624 | tf_op jit(solution)/shard_map/reduce_scatter | solution.py:113
  748.4 76.0 %reduce-scatter.25.cloned.1.call-done = bf16[96,1,1024]{2,0,1:T(8,128)(2,1)} async-done(((bf16[768,1,1024]{2,0,1:T(8,128)(2,1)}), bf16[96,1,1024]{2,0,1:T(8,128)(2,1)}) %reduce-scatter.25.cloned.1.call-update) | async-done | bytes 196624 | tf_op jit(solution)/shard_map/reduce_scatter | solution.py:124
  830.5 4.0 fusion.326
  834.5 44.6 %all-gather.32.cloned.1.call-done = bf16[768,1,1024]{2,0,1:T(8,128)(2,1)} async-done(((bf16[96,1,1024]{2,0,1:T(8,128)(2,1)}), bf16[768,1,1024]{2,0,1:T(8,128)(2,1)}) %all-gather.32.cloned.1.call-update) | async-done | bytes 1572880 | tf_op jit(solution)/shard_map/all_gather | solution.py:135
  881.2 4.3 multiply_reduce_fusion.2
  895.6 71.5 %reduce-scatter.27.cloned.1.call-done = bf16[96,1,1024]{2,0,1:T(8,128)(2,1)} async-done(((bf16[768,1,1024]{2,0,1:T(8,128)(2,1)}), bf16[96,1,1024]{2,0,1:T(8,128)(2,1)}) %reduce-scatter.27.cloned.1.call-update) | async-done | bytes 196624 | tf_op jit(solution)/shard_map/reduce_scatter | solution.py:124
  971.9 5.1 collective-permute-done.2
  977.8 40.9 %all-gather.30.cloned.1.call-done = bf16[768,1,1024]{2,0,1:T(8,128)(2,1)} async-done(((bf16[96,1,1024]{2,0,1:T(8,128)(2,1)}), bf16[768,1,1024]{2,0,1:T(8,128)(2,1)}) %all-gather.30.cloned.1.call-update) | async-done | bytes 1572880 | tf_op jit(solution)/shard_map/all_gather | solution.py:96
  1022.5 48.2 %all-gather.34.cloned.1.call-done = bf16[768,1,1024]{2,0,1:T(8,128)(2,1)} async-done(((bf16[96,1,1024]{2,0,1:T(8,128)(2,1)}), bf16[768,1,1024]{2,0,1:T(8,128)(2,1)}) %all-gather.34.cloned.1.call-update) | async-done | bytes 1572880 | tf_op jit(solution)/shard_map/all_gather | solution.py:135
  1070.8 4.5 convert_reduce_fusion.1
  1078.8 73.0 %reduce-scatter.29.cloned.1.call-done = bf16[96,1,1024]{2,0,1:T(8,128)(2,1)} async-done(((bf16[768,1,1024]{2,0,1:T(8,128)(2,1)}), bf16[96,1,1024]{2,0,1:T(8,128)(2,1)}) %reduce-scatter.29.cloned.1.call-update) | async-done | bytes 196624 | tf_op jit(solution)/shard_map/reduce_scatter | solution.py:124
  1161.5 44.4 %all-gather.36.cloned.1.call-done = bf16[768,1,1024]{2,0,1:T(8,128)(2,1)} async-done(((bf16[96,1,1024]{2,0,1:T(8,128)(2,1)}), bf16[768,1,1024]{2,0,1:T(8,128)(2,1)}) %all-gather.36.cloned.1.call-update) | async-done | bytes 1572880 | tf_op jit(solution)/shard_map/all_gather | solution.py:135
  1208.1 4.3 multiply_reduce_fusion.1
  1220.4 73.4 %reduce-scatter.31.cloned.1.call-done = bf16[96,1,1024]{2,0,1:T(8,128)(2,1)} async-done(((bf16[768,1,1024]{2,0,1:T(8,128)(2,1)}), bf16[96,1,1024]{2,0,1:T(8,128)(2,1)}) %reduce-scatter.31.cloned.1.call-update) | async-done | bytes 196624 | tf_op jit(solution)/shard_map/reduce_scatter | solution.py:124
  1299.8 5.1 collective-permute-done.3
  1305.7 50.7 %all-gather.38.cloned.1.call-done = bf16[768,1,1024]{2,0,1:T(8,128)(2,1)} async-done(((bf16[96,1,1024]{2,0,1:T(8,128)(2,1)}), bf16[768,1,1024]{2,0,1:T(8,128)(2,1)}) %all-gather.38.cloned.1.call-update) | async-done | bytes 1572880 | tf_op jit(solution)/shard_map/all_gather | solution.py:135
  1356.4 4.4 convert_reduce_fusion
  1366.9 70.6 %reduce-scatter.33.cloned.1.call-done = bf16[96,1,1024]{2,0,1:T(8,128)(2,1)} async-done(((bf16[768,1,1024]{2,0,1:T(8,128)(2,1)}), bf16[96,1,1024]{2,0,1:T(8,128)(2,1)}) %reduce-scatter.33.cloned.1.call-update) | async-done | bytes 196624 | tf_op jit(solution)/shard_map/reduce_scatter | solution.py:124
  1442.7 46.5 %all-gather.48.cloned.1.call-done = bf16[768,1,1024]{2,0,1:T(8,128)(2,1)} async-done(((bf16[96,1,1024]{2,0,1:T(8,128)(2,1)}), bf16[768,1,1024]{2,0,1:T(8,128)(2,1)}) %all-gather.48.cloned.1.call-update) | async-done | bytes 1572880 | tf_op jit(solution)/shard_map/all_gather | solution.py:106
  1489.3 4.1 fusion.79
  1502.0 5.6 fusion.92
  1507.6 34.5 %all-gather.50.cloned.1.call-done = bf16[768,1,1024]{2,0,1:T(8,128)(2,1)} async-done(((bf16[96,1,1024]{2,0,1:T(8,128)(2,1)}), bf16[768,1,1024]{2,0,1:T(8,128)(2,1)}) %all-gather.50.cloned.1.call-update) | async-done | bytes 1572880 | tf_op jit(solution)/shard_map/all_gather | solution.py:106
  1542.1 4.1 fusion.77
  1547.3 46.8 %all-gather.44.cloned.1.call-done = bf16[768,1,1024]{2,0,1:T(8,128)(2,1)} async-done(((bf16[96,1,1024]{2,0,1:T(8,128)(2,1)}), bf16[768,1,1024]{2,0,1:T(8,128)(2,1)}) %all-gather.44.cloned.1.call-update) | async-done | bytes 1572880 | tf_op jit(solution)/shard_map/all_gather | solution.py:106
  1598.0 5.4 fusion.157
  1603.4 42.9 %all-gather.52.cloned.1.call-done = bf16[768,1,1024]{2,0,1:T(8,128)(2,1)} async-done(((bf16[96,1,1024]{2,0,1:T(8,128)(2,1)}), bf16[768,1,1024]{2,0,1:T(8,128)(2,1)}) %all-gather.52.cloned.1.call-update) | async-done | bytes 1572880 | tf_op jit(solution)/shard_map/all_gather | solution.py:106
  1646.3 5.0 fusion.154
  1651.3 47.7 %all-gather.40.cloned.1.call-done = bf16[768,1,1024]{2,0,1:T(8,128)(2,1)} async-done(((bf16[96,1,1024]{2,0,1:T(8,128)(2,1)}), bf16[768,1,1024]{2,0,1:T(8,128)(2,1)}) %all-gather.40.cloned.1.call-update) | async-done | bytes 1572880 | tf_op jit(solution)/shard_map/all_gather | solution.py:135
  1701.1 4.3 multiply_reduce_fusion
  1712.6 38.4 %all-gather.46.cloned.1.call-done = bf16[768,1,1024]{2,0,1:T(8,128)(2,1)} async-done(((bf16[96,1,1024]{2,0,1:T(8,128)(2,1)}), bf16[768,1,1024]{2,0,1:T(8,128)(2,1)}) %all-gather.46.cloned.1.call-update) | async-done | bytes 1572880 | tf_op jit(solution)/shard_map/all_gather | solution.py:106
  1754.9 48.3 %all-gather.42.cloned.1.call-done = bf16[768,1,1024]{2,0,1:T(8,128)(2,1)} async-done(((bf16[96,1,1024]{2,0,1:T(8,128)(2,1)}), bf16[768,1,1024]{2,0,1:T(8,128)(2,1)}) %all-gather.42.cloned.1.call-update) | async-done | bytes 1572880 | tf_op jit(solution)/shard_map/all_gather | solution.py:106
  1803.2 4.3 fusion.169
  1812.2 68.1 %reduce-scatter.23.cloned.1.call-done = bf16[96,1,1024]{2,0,1:T(8,128)(2,1)} async-done(((bf16[768,1,1024]{2,0,1:T(8,128)(2,1)}), bf16[96,1,1024]{2,0,1:T(8,128)(2,1)}) %reduce-scatter.23.cloned.1.call-update) | async-done | bytes 196624 | tf_op jit(solution)/shard_map/reduce_scatter | solution.py:113
  1882.7 13.6 all-reduce.1
  1897.4 53.8 %all-reduce.5.cloned.1.call-done = (bf16[1,1024,3,128]{3,1,2,0:T(8,128)(2,1)}, bf16[1,128,1024]{2,1,0:T(8,128)(2,1)}, bf16[1,1024,512]{2,1,0:T(8,128)(2,1)}, bf16[1,512,1024]{2,1,0:T(8,128)(2,1)}) async-done(((bf16[1,1024,3,128]{3,1,2,0:T(8,128)(2,1)}, bf16[1,128,1024]{2,1,0:T(8,128)(2,1)}, bf16[1,1024,512]{2,1,0:T(8,128)(2,1)}, bf16[1,512,1024]{2,1,0:T(8,128)(2,1)}), (bf16[1,1024,3,128]{3,1,2,0:T(8,128)(2,1)}, ...) | async-done | bytes 3145744 | tf_op jit(solution)/shard_map/psum | solution.py:278
  1957.9 71.9 %reduce-scatter.35.cloned.1.call-done = bf16[96,1,1024]{2,0,1:T(8,128)(2,1)} async-done(((bf16[768,1,1024]{2,0,1:T(8,128)(2,1)}), bf16[96,1,1024]{2,0,1:T(8,128)(2,1)}) %reduce-scatter.35.cloned.1.call-update) | async-done | bytes 196624 | tf_op jit(solution)/shard_map/reduce_scatter | solution.py:124
  2033.3 319.6 %all-reduce = (f32[1,1024]{1,0:T(1,128)}, f32[1,1024]{1,0:T(1,128)}, f32[1,1024]{1,0:T(1,128)}, f32[1,1024]{1,0:T(1,128)}, f32[1,1024]{1,0:T(1,128)}, /*index=5*/f32[1,1024]{1,0:T(1,128)}) all-reduce(f32[1,1024]{1,0:T(1,128)S(1)} %bitcast.604, ...), channel_id=1, replica_groups=mesh['pipe'=2,'tensor'=8,'dp'=8] {'tensor','dp'}, use_global_device_ids=true, to_apply=%region_48.49 | all-reduce | flops 6144 | bytes 49152 | tf_op jit(solution)/shard_map/psum | solution.py:376
  (542 shorter events, 191.6 us)
Async XLA Ops:
  7.2 198.0 %copy-start = (bf16[1,512,1024]{2,1,0:T(8,128)(2,1)S(1)}, bf16[1,512,1024]{2,1,0:T(8,128)(2,1)}, u32[]{:S(2)}) copy-start(bf16[1,512,1024]{2,1,0:T(8,128)(2,1)} %param.28) | copy-start | bytes 3145732
  7.2 59.1 %all-gather.20.cloned.1.call-start = ((), (), s32[]{:S(2)}) async-start(), calls=%async_computation.12 | async-start | bytes 1769472 | tf_op jit(solution)/shard_map/all_gather | solution.py:96
  13.3 134.4 %reduce-scatter.13.cloned.1.call-start = ((), (), s32[]{:S(2)}) async-start(), calls=%async_computation.13 | async-start | bytes 1769472 | tf_op jit(solution)/shard_map/reduce_scatter | solution.py:113
  13.8 326.7 %copy-start.131 = (f32[3,128]{1,0:T(4,128)}, f32[3,128]{1,0:T(4,128)S(1)}, u32[]{:S(2)}) copy-start(f32[3,128]{1,0:T(4,128)S(1)} %maximum_convert_fusion.3) | copy-start | bytes 4612
  74.1 77.7 %copy-start.132 = (bf16[1,512]{1,0:T(2,128)(2,1)S(1)}, bf16[1,512]{1,0:T(2,128)(2,1)}, u32[]{:S(2)}) copy-start(bf16[1,512]{1,0:T(2,128)(2,1)} %param.27) | copy-start | bytes 3076
  74.2 127.2 %all-gather.22.cloned.1.call-start = ((), (), s32[]{:S(2)}) async-start(), calls=%async_computation.14 | async-start | bytes 1769472 | tf_op jit(solution)/shard_map/all_gather | solution.py:96
  151.8 129.2 %reduce-scatter.15.cloned.1.call-start = ((), (), s32[]{:S(2)}) async-start(), calls=%async_computation.15 | async-start | bytes 1769472 | tf_op jit(solution)/shard_map/reduce_scatter | solution.py:113
  207.5 133.0 %all-gather.24.cloned.1.call-start = ((), (), s32[]{:S(2)}) async-start(), calls=%async_computation.16 | async-start | bytes 1769472 | tf_op jit(solution)/shard_map/all_gather | solution.py:96
  282.1 4.9 collective-permute-start
  288.4 134.3 %reduce-scatter.17.cloned.1.call-start = ((), (), s32[]{:S(2)}) async-start(), calls=%async_computation.17 | async-start | bytes 1769472 | tf_op jit(solution)/shard_map/reduce_scatter | solution.py:113
  349.2 127.3 %copy-start.134 = (f32[1,512]{1,0:T(1,128)S(1)}, f32[1,512]{1,0:T(1,128)}, u32[]{:S(2)}) copy-start(f32[1,512]{1,0:T(1,128)} %copy-done.133) | copy-start | bytes 6148
  349.2 127.3 %all-gather.26.cloned.1.call-start = ((), (), s32[]{:S(2)}) async-start(), calls=%async_computation.18 | async-start | bytes 1769472 | tf_op jit(solution)/shard_map/all_gather | solution.py:96
  423.8 400.7 %copy-start.82 = (f32[96]{0:T(128)}, f32[96]{0:T(128)S(1)}, u32[]{:S(2)}) copy-start(f32[96]{0:T(128)S(1)} %broadcast_multiply_fusion.14) | copy-start | bytes 1156
  426.9 129.3 %reduce-scatter.19.cloned.1.call-start = ((), (), s32[]{:S(2)}) async-start(), calls=%async_computation.19 | async-start | bytes 1769472 | tf_op jit(solution)/shard_map/reduce_scatter | solution.py:113
  482.6 80.5 %copy-start.125 = (f32[96]{0:T(128)S(1)}, f32[96]{0:T(128)}, u32[]{:S(2)}) copy-start(f32[96]{0:T(128)} %copy-done.124) | copy-start | bytes 1156
  482.6 82.8 %copy-start.49 = (bf16[2,96,1,1024]{3,1,2,0:T(8,128)(2,1)S(1)}, bf16[2,96,1,1024]{3,1,2,0:T(8,128)(2,1)}, u32[]{:S(2)}) copy-start(bf16[2,96,1,1024]{3,1,2,0:T(8,128)(2,1)} %param.17) | copy-start | bytes 1179652
  482.7 134.9 %all-gather.28.cloned.1.call-start = ((), (), s32[]{:S(2)}) async-start(), calls=%async_computation.20 | async-start | bytes 1769472 | tf_op jit(solution)/shard_map/all_gather | solution.py:96
  557.9 4.8 collective-permute-start.1
  565.3 104.3 %all-gather.54.cloned.1.call-start = ((), (), s32[]{:S(2)}) async-start(), calls=%async_computation.41 | async-start | bytes 1769472 | tf_op jit(solution)/shard_map/all_gather | solution.py:135
  566.8 180.6 %reduce-scatter.21.cloned.1.call-start = ((), (), s32[]{:S(2)}) async-start(), calls=%async_computation.21 | async-start | bytes 1769472 | tf_op jit(solution)/shard_map/reduce_scatter | solution.py:113
  627.9 196.6 %reduce-scatter.25.cloned.1.call-start = ((), (), s32[]{:S(2)}) async-start(), calls=%async_computation.24 | async-start | bytes 1769472 | tf_op jit(solution)/shard_map/reduce_scatter | solution.py:124
  677.1 147.3 %copy-start.90 = (f32[96]{0:T(128)S(1)}, f32[96]{0:T(128)}, u32[]{:S(2)}) copy-start(f32[96]{0:T(128)} %copy-done.89) | copy-start | bytes 1156
  677.1 147.3 %copy-start.94 = (f32[96]{0:T(128)S(1)}, f32[96]{0:T(128)}, u32[]{:S(2)}) copy-start(f32[96]{0:T(128)} %copy-done.93) | copy-start | bytes 1156
  677.1 147.3 %copy-start.103 = (f32[96]{0:T(128)S(1)}, f32[96]{0:T(128)}, u32[]{:S(2)}) copy-start(f32[96]{0:T(128)} %copy-done.102) | copy-start | bytes 1156
  677.1 149.5 %copy-start.123 = (f32[96]{0:T(128)S(1)}, f32[96]{0:T(128)}, u32[]{:S(2)}) copy-start(f32[96]{0:T(128)} %copy-done.122) | copy-start | bytes 1156
  677.2 201.9 %all-gather.32.cloned.1.call-start = ((), (), s32[]{:S(2)}) async-start(), calls=%async_computation.25 | async-start | bytes 1769472 | tf_op jit(solution)/shard_map/all_gather | solution.py:135
  748.4 81.0 %copy-start.84 = (f32[96]{0:T(128)}, f32[96]{0:T(128)S(1)}, u32[]{:S(2)}) copy-start(f32[96]{0:T(128)S(1)} %broadcast_multiply_fusion.12) | copy-start | bytes 1156
  829.5 137.6 %reduce-scatter.27.cloned.1.call-start = ((), (), s32[]{:S(2)}) async-start(), calls=%async_computation.26 | async-start | bytes 1769472 | tf_op jit(solution)/shard_map/reduce_scatter | solution.py:124
  893.5 125.2 %all-gather.30.cloned.1.call-start = ((), (), s32[]{:S(2)}) async-start(), calls=%async_computation.22 | async-start | bytes 1769472 | tf_op jit(solution)/shard_map/all_gather | solution.py:96
  895.5 123.2 %copy-start.135 = (f32[1,512]{1,0:T(1,128)S(1)}, f32[1,512]{1,0:T(1,128)}, u32[]{:S(2)}) copy-start(f32[1,512]{1,0:T(1,128)} %copy-done.133) | copy-start | bytes 6148
  895.5 175.2 %all-gather.34.cloned.1.call-start = ((), (), s32[]{:S(2)}) async-start(), calls=%async_computation.27 | async-start | bytes 1769472 | tf_op jit(solution)/shard_map/all_gather | solution.py:135
  970.6 6.4 collective-permute-start.2
  977.8 174.1 %reduce-scatter.29.cloned.1.call-start = ((), (), s32[]{:S(2)}) async-start(), calls=%async_computation.28 | async-start | bytes 1769472 | tf_op jit(solution)/shard_map/reduce_scatter | solution.py:124
  1078.4 127.5 %all-gather.36.cloned.1.call-start = ((), (), s32[]{:S(2)}) async-start(), calls=%async_computation.29 | async-start | bytes 1769472 | tf_op jit(solution)/shard_map/all_gather | solution.py:135
  1156.2 137.6 %reduce-scatter.31.cloned.1.call-start = ((), (), s32[]{:S(2)}) async-start(), calls=%async_computation.30 | async-start | bytes 1769472 | tf_op jit(solution)/shard_map/reduce_scatter | solution.py:124
  1220.4 136.0 %all-gather.38.cloned.1.call-start = ((), (), s32[]{:S(2)}) async-start(), calls=%async_computation.31 | async-start | bytes 1769472 | tf_op jit(solution)/shard_map/all_gather | solution.py:135
  1298.5 6.4 collective-permute-start.3
  1305.7 131.8 %reduce-scatter.33.cloned.1.call-start = ((), (), s32[]{:S(2)}) async-start(), calls=%async_computation.32 | async-start | bytes 1769472 | tf_op jit(solution)/shard_map/reduce_scatter | solution.py:124
  1364.0 125.3 %all-gather.48.cloned.1.call-start = ((), (), s32[]{:S(2)}) async-start(), calls=%async_computation.38 | async-start | bytes 1769472 | tf_op jit(solution)/shard_map/all_gather | solution.py:106
  1364.7 177.3 %all-gather.50.cloned.1.call-start = ((), (), s32[]{:S(2)}) async-start(), calls=%async_computation.39 | async-start | bytes 1769472 | tf_op jit(solution)/shard_map/all_gather | solution.py:106
  1365.5 228.6 %all-gather.44.cloned.1.call-start = ((), (), s32[]{:S(2)}) async-start(), calls=%async_computation.36 | async-start | bytes 1769472 | tf_op jit(solution)/shard_map/all_gather | solution.py:106
  1366.1 280.3 %all-gather.52.cloned.1.call-start = ((), (), s32[]{:S(2)}) async-start(), calls=%async_computation.40 | async-start | bytes 1769472 | tf_op jit(solution)/shard_map/all_gather | solution.py:106
  1366.9 332.1 %all-gather.40.cloned.1.call-start = ((), (), s32[]{:S(2)}) async-start(), calls=%async_computation.33 | async-start | bytes 1769472 | tf_op jit(solution)/shard_map/all_gather | solution.py:135
  1441.1 309.9 %all-gather.46.cloned.1.call-start = ((), (), s32[]{:S(2)}) async-start(), calls=%async_computation.37 | async-start | bytes 1769472 | tf_op jit(solution)/shard_map/all_gather | solution.py:106
  1441.9 361.3 %all-gather.42.cloned.1.call-start = ((), (), s32[]{:S(2)}) async-start(), calls=%async_computation.35 | async-start | bytes 1769472 | tf_op jit(solution)/shard_map/all_gather | solution.py:106
  1442.7 437.6 %reduce-scatter.23.cloned.1.call-start = ((), (), s32[]{:S(2)}) async-start(), calls=%async_computation.23 | async-start | bytes 1769472 | tf_op jit(solution)/shard_map/reduce_scatter | solution.py:113
  1501.8 449.5 %all-reduce.5.cloned.1.call-start = ((), (), s32[]{:S(2)}) async-start(), calls=%async_computation.42 | async-start | bytes 6291456 | tf_op jit(solution)/shard_map/psum | solution.py:278
  1807.5 222.3 %reduce-scatter.35.cloned.1.call-start = ((), (), s32[]{:S(2)}) async-start(), calls=%async_computation.34 | async-start | bytes 1769472 | tf_op jit(solution)/shard_map/reduce_scatter | solution.py:124
  (145 other events, 4912.2 us)
Sparse Core Ops, SparseCore 0:
  13.4 52.8 all-gather.19
  74.3 73.3 reduce-scatter.12
  151.9 49.4 all-gather.21
  207.6 73.3 reduce-scatter.14
  288.5 52.0 all-gather.23
  349.3 73.3 reduce-scatter.16
  427.0 49.4 all-gather.25
  482.8 73.3 reduce-scatter.18
  565.5 52.0 all-gather.27
  619.7 49.8 all-gather.53
  673.9 73.3 reduce-scatter.20
  751.5 72.9 reduce-scatter.24
  829.6 49.4 all-gather.31
  893.7 73.3 reduce-scatter.26
  969.2 49.4 all-gather.29
  1020.9 49.8 all-gather.33
  1078.5 73.3 reduce-scatter.28
  1156.3 49.4 all-gather.35
  1220.5 73.3 reduce-scatter.30
  1305.8 50.5 all-gather.37
  1364.1 73.3 reduce-scatter.32
  1439.8 49.4 all-gather.47
  1492.2 49.8 all-gather.49
  1544.2 49.8 all-gather.43
  1596.4 49.8 all-gather.51
  1649.1 49.8 all-gather.39
  1701.1 49.8 all-gather.45
  1753.3 49.8 all-gather.41
  1807.0 73.3 reduce-scatter.22
  1883.9 67.2 all-reduce.4
  1955.0 74.7 reduce-scatter.34
where the time goes:
time: 2370 us; the launch traced here: 2360 us
  waiting for transfers between devices  1770 us (75%)
  blocking collectives  333 us (14%)
  matrix products  146 us (6%)
  other arithmetic  72.3 us (3%)
    reduce_scatter x6, waiting for transfers between devices, input_sum(): lax.psum_scatter(jnp.einsum('lbw,dw->lbd', grad_full, weight, preferred_e...  436 us
    reduce_scatter x6, waiting for transfers between devices, branch_sum(): lax.psum_scatter(jnp.einsum('lbw,wd->lbd', values, weight, preferred_elem...  431 us
    psum x1, blocking collectives, on_device(): norm_total = lax.psum(norm_sums, ('tensor', 'dp'))  320 us
    all_gather x6, waiting for transfers between devices, rows_product(): lax.all_gather(normed, 'tensor', axis=0, tiled=True)  294 us
    all_gather x6, waiting for transfers between devices, grad_rows(): shard_rows = lax.all_gather(grad_local, 'tensor', axis=0, tiled=True)  277 us
    all_gather x6, waiting for transfers between devices, rows_weight_grad(): lax.all_gather(kept, 'tensor', axis=0, tiled=True)  257 us
    psum x1, waiting for transfers between devices, sum_weights(): lax.psum(as_sent(matrix_terms), 'dp')  53.8 us
  transfers between devices with their start and end apart: 35, of which 35 were waited for; matrix products, arithmetic and copies ran while one was open for 5% of the time, Pallas kernels for 0%

commit v1 on v0

v1 whole, which is shorter than its diff:
```python
import jax
import jax.numpy as jnp
from jax import lax
from jax.sharding import PartitionSpec as P

HEAD_DIM = 64
BLOCK = 96
WIDTH = 1024
epsilon = 1e-05
AXES = ("pipe", "tensor", "dp")
bf16 = jnp.bfloat16
f32 = jnp.float32


def spot(axes, x, z, y, core):
    index = 0
    for axis in axes:
        if axis == "pipe":
            index = index * 2 + z % 2
        elif axis == "tensor":
            index = index * 8 + x * 2 + z // 2
        else:
            index = index * 8 + y * 2 + core
    return index


def move(array, axes, rule):
    pairs = {}
    for x in range(4):
        for z in range(4):
            for y in range(4):
                for core in range(2):
                    goal = rule(x, z, y, core)
                    if goal is not None:
                        pairs[spot(axes, x, z, y, core)] = spot(axes, *goal)
    return lax.ppermute(array, axes, sorted(pairs.items()))


def along_x(array, by):
    return move(array, ("tensor",), lambda x, z, y, core: ((x + by) % 4, z, y, core))


def along_y(array, by):
    return move(array, ("dp",), lambda x, z, y, core: (x, z, (y + by) % 4, core))


def along_z(array, by, only=None):
    def rule(x, z, y, core):
        return (x, (z + by) % 4, y, core) if only is None or z % 2 == only else None

    return move(array, ("pipe", "tensor"), rule)


def other_core(array):
    return move(array, ("dp",), lambda x, z, y, core: (x, z, y, 1 - core))


def turned(array):
    return move(
        array, ("tensor", "dp"), lambda x, z, y, core: (x, core * 2 + z % 2, y, z // 2)
    )


def pick(array, index, axis=0):
    return lax.dynamic_index_in_dim(array, index, axis, keepdims=False)


def place(buffer, piece, starts):
    return lax.dynamic_update_slice(buffer, piece, starts)


def gather_rows(rows):
    return jnp.concatenate([rows] + [along_x(rows, by) for by in (1, 2, 3)], axis=0)


def scatter_rows(partial):
    parts = partial.astype(bf16).reshape(4, BLOCK, WIDTH)
    total = parts[0].astype(f32)
    for by in (1, 2, 3):
        total = total + along_x(parts[by], -by).astype(f32)
    return total


def dot(left, right, left_dim, right_dim):
    return lax.dot_general(
        left, right, (((left_dim,), (right_dim,)), ((), ())), preferred_element_type=f32
    )


def norm_forward(stream, gain, shift):
    average = jnp.mean(stream, axis=-1, keepdims=True)
    centred = stream - average
    inverse_scale = lax.rsqrt(jnp.mean(centred * centred, axis=-1, keepdims=True) + epsilon)
    standard = centred * inverse_scale
    return (standard * gain + shift).astype(bf16), standard, inverse_scale


def norm_backward(incoming, standard, inverse_scale, gain):
    scaled = incoming * gain
    correction = (
        scaled
        - jnp.mean(scaled, axis=-1, keepdims=True)
        - standard * jnp.mean(scaled * standard, axis=-1, keepdims=True)
    )
    return (
        correction * inverse_scale,
        jnp.sum(incoming * standard, axis=0),
        jnp.sum(incoming, axis=0),
    )


def masked_scores(query, keys, allowed):
    scores = jnp.einsum("qhe,khe->hqk", query, keys, preferred_element_type=f32)
    return jnp.where(allowed[None], scores * HEAD_DIM ** (-0.5), -1e30)


def attend_forward(query, keys, values, allowed):
    scores = masked_scores(query, keys, allowed)
    largest = jnp.max(scores, axis=-1, keepdims=True)
    terms = jnp.exp(scores - largest)
    summed = jnp.sum(terms, axis=-1, keepdims=True)
    weights = (terms / summed).astype(bf16)
    context = jnp.einsum("hqk,khe->qhe", weights, values, preferred_element_type=f32)
    return context.astype(bf16), largest + jnp.log(summed)


def attend_backward(query, keys, values, allowed, log_total, context_grad):
    weights = jnp.exp(masked_scores(query, keys, allowed) - log_total)
    weight_grad = jnp.einsum("qhe,khe->hqk", context_grad, values, preferred_element_type=f32)
    value_grad = jnp.einsum(
        "hqk,qhe->khe", weights.astype(bf16), context_grad, preferred_element_type=f32
    )
    correction = jnp.sum(weights * weight_grad, axis=-1, keepdims=True)
    score_grad = (weights * (weight_grad - correction)).astype(bf16)
    query_grad = jnp.einsum("hqk,khe->qhe", score_grad, keys, preferred_element_type=f32)
    key_grad = jnp.einsum("hqk,qhe->khe", score_grad, query, preferred_element_type=f32)
    scale = HEAD_DIM ** (-0.5)
    return query_grad * scale, key_grad * scale, value_grad


def split_heads(projected):
    view = projected.reshape(4 * BLOCK, 2, 3, 2, HEAD_DIM)
    return tuple(view[:, :, part].reshape(4 * BLOCK, 4, HEAD_DIM) for part in range(3))


def layer_forward(stream, allowed, vectors, weights):
    gain_one, shift_one, out_bias, gain_two, shift_two, proj_bias, qkv_bias, fc_bias = vectors
    w_qkv, w_out, w_fc, w_proj = weights
    normed_one, standard_one, inverse_one = norm_forward(stream, gain_one, shift_one)
    rows_one = gather_rows(normed_one)
    projected = (dot(rows_one, w_qkv, 1, 0) + qkv_bias).astype(bf16)
    query, key, value = split_heads(projected)
    both = jnp.stack([key, value]).reshape(2, 4 * BLOCK, 256)
    keys, values = (
        part.reshape(8 * BLOCK, 4, HEAD_DIM)
        for part in jnp.concatenate([both, other_core(both)], axis=1)
    )
    context, log_total = attend_forward(query, keys, values, allowed)
    context = context.reshape(4 * BLOCK, 256)
    middle = stream + scatter_rows(dot(context, w_out, 1, 0)) + out_bias
    normed_two, standard_two, inverse_two = norm_forward(middle, gain_two, shift_two)
    rows_two = gather_rows(normed_two)
    gelu_input = dot(rows_two, w_fc, 1, 0) + fc_bias
    hidden = jax.nn.gelu(gelu_input, approximate=True).astype(bf16)
    result = middle + scatter_rows(dot(hidden, w_proj, 1, 0)) + proj_bias
    saved = (
        (standard_one, inverse_one, rows_one),
        (query, keys, values, log_total, context),
        (standard_two, inverse_two, rows_two, gelu_input, hidden),
    )
    return result.astype(bf16), saved


def halves(grad, rows):
    return grad.astype(bf16).reshape(2, 2, rows, WIDTH)


def layer_backward(incoming, allowed, vectors, weights, saved):
    gain_one, shift_one, out_bias, gain_two, shift_two, proj_bias, qkv_bias, fc_bias = vectors
    w_qkv, w_out, w_fc, w_proj = weights
    (
        (standard_one, inverse_one, rows_one),
        (query, keys, values, log_total, context),
        (standard_two, inverse_two, rows_two, gelu_input, hidden),
    ) = saved
    grad_feed = incoming.astype(bf16)
    proj_bias_grad = jnp.sum(grad_feed.astype(f32), axis=0)
    feed_rows = gather_rows(grad_feed)
    hidden_grad = dot(feed_rows, w_proj, 1, 1)
    gelu_pull = jax.vjp(lambda item: jax.nn.gelu(item, approximate=True), gelu_input)[1]
    gelu_grad = gelu_pull(hidden_grad)[0].astype(bf16)
    normed_two_grad = scatter_rows(dot(gelu_grad, w_fc, 1, 1))
    fc_bias_grad = jnp.sum(gelu_grad.astype(f32), axis=0)
    w_proj_grad = dot(hidden, feed_rows, 0, 0)
    w_fc_grad = dot(gelu_grad, rows_two, 0, 0)
    middle_norm, gain_two_grad, shift_two_grad = norm_backward(
        normed_two_grad, standard_two, inverse_two, gain_two
    )
    middle_grad = incoming + middle_norm
    grad_attention = middle_grad.astype(bf16)
    out_bias_grad = jnp.sum(grad_attention.astype(f32), axis=0)
    attention_rows = gather_rows(grad_attention)
    context_grad = dot(attention_rows, w_out, 1, 1).astype(bf16)
    w_out_grad = dot(context, attention_rows, 0, 0)
    query_grad, key_grad, value_grad = attend_backward(
        query,
        keys,
        values,
        allowed,
        log_total,
        context_grad.reshape(4 * BLOCK, 4, HEAD_DIM),
    )
    both = jnp.stack([key_grad, value_grad]).reshape(2, 8 * BLOCK, 256)
    arrived = other_core(both[:, 4 * BLOCK :].astype(bf16))
    summed = both[:, : 4 * BLOCK] + arrived.astype(f32)
    triple = jnp.stack([query_grad.reshape(4 * BLOCK, 256), summed[0], summed[1]], axis=1)
    triple = triple.astype(bf16).reshape(4 * BLOCK, 3, 2, 128)
    triple = jnp.moveaxis(triple, 2, 1).reshape(4 * BLOCK, 768)
    normed_one_grad = scatter_rows(dot(triple, w_qkv, 1, 1))
    qkv_bias_grad = jnp.sum(triple.astype(f32), axis=0)
    w_qkv_grad = dot(triple, rows_one, 0, 0)
    stream_norm, gain_one_grad, shift_one_grad = norm_backward(
        normed_one_grad, standard_one, inverse_one, gain_one
    )
    stream_grad = middle_grad + stream_norm
    feed_group = jnp.concatenate([halves(w_fc_grad, 256), halves(w_proj_grad, 256)], axis=2)
    attention_group = jnp.concatenate([halves(w_qkv_grad, 192), halves(w_out_grad, 64)], axis=2)
    early = (out_bias_grad, gain_two_grad, shift_two_grad, proj_bias_grad, fc_bias_grad)
    late = (gain_one_grad, shift_one_grad, qkv_bias_grad)
    return stream_grad, feed_group, attention_group, early, late


def to_owner(group, layer, here):
    pipe, high, core = here
    sent = other_core(pick(group, 1 - core, 1))
    mine = (pick(group, core, 1).astype(f32) + sent.astype(f32)).astype(bf16)
    near, far = pick(mine, high), pick(mine, 1 - high)
    step = 1 if layer == 1 else -1
    total = jnp.where(pipe == layer, near.astype(f32), 0.0)
    total = total + along_z(near, step, only=1 - layer).astype(f32)
    total = total + along_z(far, -step, only=1 - layer).astype(f32)
    total = total + along_z(far, 2, only=layer).astype(f32)
    return total.astype(bf16)


def over_y(total):
    rows = total.shape[0]
    y = lax.axis_index("dp") // 2
    chunks = total.reshape(4, rows // 4, WIDTH)
    own = pick(chunks, y).astype(f32)
    for by in (1, 2, 3):
        own = own + along_y(pick(chunks, (y + by) % 4), by).astype(f32)
    own = own.astype(bf16)
    whole = jnp.zeros((4, rows // 4, WIDTH), bf16)
    whole = place(whole, own[None], (y, 0, 0))
    for by in (1, 2, 3):
        whole = place(whole, along_y(own, by)[None], ((y - by) % 4, 0, 0))
    whole = whole.reshape(rows, WIDTH)
    core = lax.axis_index("dp") % 2
    both = jnp.zeros((2, rows, WIDTH), bf16)
    both = place(both, whole[None], (core, 0, 0))
    return place(both, other_core(whole)[None], (1 - core, 0, 0)).astype(f32)


def everywhere(array):
    array = array + other_core(array)
    for along in (along_x, along_y, along_z):
        array = array + along(array, 1) + along(array, 2) + along(array, 3)
    return array


def spread_weights(here, w_qkv, w_out, w_fc, w_proj, smalls):
    pipe, high, core = here
    z = high * 2 + pipe
    group_one = jnp.concatenate(
        [lax.dynamic_slice_in_dim(w_qkv, core * 512, 512, 0), smalls], axis=0
    )
    group_two = jnp.concatenate(
        [
            lax.dynamic_slice_in_dim(w_out, core * 64, 64, 0),
            lax.dynamic_slice_in_dim(w_proj, core * 256, 256, 0),
        ],
        axis=0,
    )
    group_three = lax.dynamic_slice_in_dim(w_fc, core * 512, 512, 0)
    all_qkv = jnp.zeros((2, 1024, 768), bf16)
    all_out = jnp.zeros((2, 256, 1024), bf16)
    all_fc = jnp.zeros((2, 1024, 1024), bf16)
    all_proj = jnp.zeros((2, 1024, 1024), bf16)
    all_small = jnp.zeros((2, 2, 32, 384), bf16)
    all_qkv = place(all_qkv, w_qkv[None], (pipe, 0, high * 384))
    all_out = place(all_out, w_out[None], (pipe, high * 128, 0))
    all_fc = place(all_fc, w_fc[None], (pipe, 0, high * 512))
    all_proj = place(all_proj, w_proj[None], (pipe, high * 512, 0))
    all_small = place(all_small, smalls[None, None], (pipe, high, 0, 0))
    order = (1, 3, 2)
    came = [along_z(group_one, by) for by in order]
    swapped = other_core(jnp.stack([item[:512] for item in came]))
    for i, by in enumerate(order):
        source = (z - by) % 4
        layer, slot = source % 2, source // 2
        all_small = place(all_small, came[i][None, None, 512:], (layer, slot, 0, 0))
        all_qkv = place(all_qkv, came[i][None, :512], (layer, core * 512, slot * 384))
        all_qkv = place(all_qkv, swapped[i][None], (layer, (1 - core) * 512, slot * 384))
    came = [along_z(group_two, by) for by in order]
    swapped = other_core(jnp.stack(came))
    for i, by in enumerate(order):
        source = (z - by) % 4
        layer, slot = source % 2, source // 2
        for half, item in ((core, came[i]), (1 - core, swapped[i])):
            all_out = place(all_out, item[None, :64], (layer, slot * 128 + half * 64, 0))
            all_proj = place(all_proj, item[None, 64:], (layer, slot * 512 + half * 256, 0))
    came = [along_z(group_three, by) for by in order]
    swapped = other_core(jnp.stack(came))
    for i, by in enumerate(order):
        source = (z - by) % 4
        layer, slot = source % 2, source // 2
        for half, item in ((core, came[i]), (1 - core, swapped[i])):
            all_fc = place(all_fc, item[None], (layer, half * 512, slot * 512))
    return all_qkv, all_out, all_fc, all_proj, all_small


def on_device(
    inputs,
    segment_ids,
    cotangent,
    ln1_gain,
    ln1_bias,
    w_qkv,
    qv_bias,
    w_out,
    out_bias,
    ln2_gain,
    ln2_bias,
    w_fc,
    fc_bias,
    w_proj,
    proj_bias,
):
    pipe = lax.axis_index("pipe")
    tensor = lax.axis_index("tensor")
    dp = lax.axis_index("dp")
    x, high, core = tensor // 2, tensor % 2, dp % 2
    here = (pipe, high, core)
    stream = turned(pick(inputs, pipe).reshape(BLOCK, WIDTH)).astype(f32)
    cotangent_rows = turned(pick(cotangent, pipe).reshape(BLOCK, WIDTH)).astype(f32)
    segments = pick(segment_ids, pipe).reshape(8, BLOCK)
    segments = jnp.where(high == core, segments, other_core(segments))
    slots = ((x - jnp.arange(4)) % 4) * 2
    blocks = jnp.concatenate([slots + core, slots + 1 - core])
    numbers = segments[blocks].reshape(-1)
    positions = (blocks[:, None] * BLOCK + jnp.arange(BLOCK)[None]).reshape(-1)
    allowed = (numbers[: 4 * BLOCK, None] == numbers[None]) & (
        positions[None] <= positions[: 4 * BLOCK, None]
    )

    smalls = jnp.concatenate(
        [
            ln1_gain[0],
            ln1_bias[0],
            out_bias[0],
            ln2_gain[0],
            ln2_bias[0],
            proj_bias[0],
            qv_bias[0].reshape(-1),
            fc_bias[0],
            jnp.zeros((32 * 384 - 6912,), bf16),
        ]
    ).reshape(32, 384)
    all_qkv, all_out, all_fc, all_proj, all_small = spread_weights(
        here, w_qkv[0].reshape(WIDTH, 384), w_out[0], w_fc[0], w_proj[0], smalls
    )
    weights, vectors = [], []
    for layer in range(2):
        weights.append((all_qkv[layer], all_out[layer], all_fc[layer], all_proj[layer]))
        flat = all_small[layer].reshape(2, -1).astype(f32)
        norms = tuple(flat[0, i * WIDTH : (i + 1) * WIDTH] for i in range(6))
        pairs = flat[:, 6144:6400].reshape(2, 2, 128)
        none = jnp.zeros((2, 128), f32)
        qkv_bias = jnp.stack([pairs[:, 0], none, pairs[:, 1]], axis=1).reshape(-1)
        vectors.append(norms + (qkv_bias, flat[:, 6400:6912].reshape(-1)))

    first, saved_first = layer_forward(stream, allowed, vectors[0], weights[0])
    second, saved_second = layer_forward(first.astype(f32), allowed, vectors[1], weights[1])
    middle_grad, feed_one, attention_one, early_one, late_one = layer_backward(
        cotangent_rows, allowed, vectors[1], weights[1], saved_second
    )
    middle_low = middle_grad.astype(bf16)
    feed_owned = to_owner(feed_one, 1, here)
    attention_owned = to_owner(attention_one, 1, here)
    last_grad, feed_zero, attention_zero, early_zero, late_zero = layer_backward(
        middle_low.astype(f32), allowed, vectors[0], weights[0], saved_first
    )
    last_low = last_grad.astype(bf16)
    feed_owned = jnp.where(pipe == 1, feed_owned, to_owner(feed_zero, 0, here))
    attention_owned = jnp.where(pipe == 1, attention_owned, to_owner(attention_zero, 0, here))
    feed_total = over_y(feed_owned)
    attention_total = over_y(attention_owned)

    def bias_rows(fc_bias_grad):
        return place(jnp.zeros((4, WIDTH), f32), fc_bias_grad[None], (x, 0))

    def late_rows(late):
        gain_grad, shift_grad, qkv_grad = late
        parts = qkv_grad.reshape(2, 3, 128)
        pairs = jnp.stack([parts[:, 0], parts[:, 2]]).reshape(2, 256)
        wide = place(jnp.zeros((2, WIDTH), f32), pairs, (0, x * 256))
        return jnp.concatenate([gain_grad[None], shift_grad[None], wide])

    early = jnp.stack(
        [
            jnp.concatenate([jnp.stack(item[:4]), bias_rows(item[4])])
            for item in (early_zero, early_one)
        ]
    )
    early = pick(lax.psum(early, AXES), pipe)
    late = pick(everywhere(jnp.stack([late_rows(late_zero), late_rows(late_one)])), pipe)

    w_fc_grad = feed_total[:, :256].reshape(512, WIDTH).T
    w_proj_grad = feed_total[:, 256:].reshape(512, WIDTH)
    w_qkv_grad = attention_total[:, :192].reshape(384, WIDTH).T.reshape(WIDTH, 3, 128)
    w_out_grad = attention_total[:, 192:].reshape(128, WIDTH)
    fc_bias_grad = lax.dynamic_slice(early[4:], (x, high * 512), (1, 512))[0]
    qv_bias_grad = lax.dynamic_slice(late[2:], (0, tensor * 128), (2, 128))

    def placed(own, other):
        def crossed(array):
            return move(
                array,
                AXES,
                lambda x, z, y, core: (x, core * 2 + 1 - z % 2, y, z // 2),
            )

        stays = turned(own)
        comes = crossed(other)
        return jnp.where(pipe == 0, jnp.stack([stays, comes]), jnp.stack([comes, stays]))

    activations = placed(
        jnp.where(pipe == 0, first, second), jnp.where(pipe == 0, second, first)
    )
    in_grads = placed(
        jnp.where(pipe == 0, last_low, middle_low), jnp.where(pipe == 0, middle_low, last_low)
    )
    return (
        activations[None, :, :, None],
        in_grads[None, :, :, None],
        late[0][None],
        late[1][None],
        w_qkv_grad[None],
        qv_bias_grad[None],
        w_out_grad[None],
        early[0][None],
        early[1][None],
        early[2][None],
        w_fc_grad[None],
        fc_bias_grad[None],
        w_proj_grad[None],
        early[3][None],
    )


def solution(mesh):
    return jax.shard_map(
        on_device,
        mesh=mesh,
        in_specs=(
            P(None, "tensor", "dp", None),
            P(None, "dp", None),
            P(None, "tensor", "dp", None),
            P("pipe", None),
            P("pipe", None),
            P("pipe", None, None, "tensor"),
            P("pipe", None, "tensor"),
            P("pipe", "tensor", None),
            P("pipe", None),
            P("pipe", None),
            P("pipe", None),
            P("pipe", None, "tensor"),
            P("pipe", "tensor"),
            P("pipe", "tensor", None),
            P("pipe", None),
        ),
        out_specs=(
            P("pipe", None, "tensor", "dp", None),
            P("pipe", None, "tensor", "dp", None),
            P("pipe", None),
            P("pipe", None),
            P("pipe", None, None, "tensor"),
            P("pipe", None, "tensor"),
            P("pipe", "tensor", None),
            P("pipe", None),
            P("pipe", None),
            P("pipe", None),
            P("pipe", None, "tensor"),
            P("pipe", "tensor"),
            P("pipe", "tensor", None),
            P("pipe", None),
        ),
        check_vma=False,
    )
```

time: 2370 us -> 746 us (0.31)
  waiting for transfers between devices: 1770 us -> 355 us
  blocking collectives: 333 us -> 0 us
  starting transfers between devices: 9.77 us -> 157 us
  matrix products: 146 us -> 63.3 us
  local copies, waits for them, and re-layouts: 13.5 us -> 87.8 us
    reduce_scatter x12 -> x0, waiting for transfers between devices: 868 us -> none  [the longest x6 436 us: input_sum(): lax.psum_scatter(jnp.einsum('lbw,dw->lbd', grad_full, weight, preferred_e...]
    all_gather x18 -> x0, waiting for transfers between devices: 828 us -> none  [the longest x6 294 us: rows_product(): lax.all_gather(normed, 'tensor', axis=0, tiled=True)]
    psum x2 -> x0, blocking collectives: 333 us -> none  [the longest x1 320 us: on_device(): norm_total = lax.psum(norm_sums, ('tensor', 'dp'))]
    ppermute x4 -> x111, waiting for transfers between devices: 15.4 us -> 223 us  [move(): return lax.ppermute(array, axes, sorted(pairs.items()))]
    ppermute x4 -> x111, starting transfers between devices: 7.13 us -> 157 us  [move(): return lax.ppermute(array, axes, sorted(pairs.items()))]
    dot_general x57 -> x36, matrix products: 146 us -> 63.3 us  [the longest x24 44.7 us: dot(): lax.dot_general(left, right, (((left_dim,), (right_dim,)), ((), ())), pre...]
    psum x1, waiting for transfers between devices: 53.8 us -> 132 us  [on_device(): early = pick(lax.psum(early, AXES), pipe)]
    dynamic_update_slice x0 -> x44, local copies, waits for them, and re-layouts: none -> 33.6 us  [place(): return lax.dynamic_update_slice(buffer, piece, starts)]
  transfers between devices with their start and end apart: 35 -> 112, of which waited for: 35 -> 41; matrix products, arithmetic and copies ran while one was open for 5% -> 23% of each run, Pallas kernels for 0% -> 0%
where the time goes in v1:
time: 746 us; the launch traced here: 734 us
  waiting for transfers between devices  355 us (48%)
  starting transfers between devices  157 us (21%)
  local copies, waits for them, and re-layouts  87.8 us (12%)
  matrix products  63.3 us (8%)
  other arithmetic  53.3 us (7%)
  between operations  17.7 us (2%)
    ppermute x111, waiting for transfers between devices, move(): return lax.ppermute(array, axes, sorted(pairs.items()))  223 us
    ppermute x111, starting transfers between devices, move(): return lax.ppermute(array, axes, sorted(pairs.items()))  157 us
    psum x1, waiting for transfers between devices, on_device(): early = pick(lax.psum(early, AXES), pipe)  132 us
    dot_general x24, matrix products, dot(): lax.dot_general(left, right, (((left_dim,), (right_dim,)), ((), ())), pre...  44.7 us
    dynamic_update_slice x44, local copies, waits for them, and re-layouts, place(): return lax.dynamic_update_slice(buffer, piece, starts)  33.6 us
    unnamed x221, local copies, waits for them, and re-layouts  19.3 us
  transfers between devices with their start and end apart: 112, of which 41 were waited for; matrix products, arithmetic and copies ran while one was open for 23% of the time, Pallas kernels for 0%

profile of v1, /device:TPU:1, one launch (start us, length us, event | category | flops | bytes accessed | tf_op | source)
XLA Modules:
  0.0 734.5 jit_solution(12253756819364765724)
XLA Ops:
  22.0 4.7 collective-permute-start
  40.6 8.9 %collective-permute-done = bf16[96,1024]{1,0:T(8,128)(2,1)S(1)} collective-permute-done((bf16[96,1024]{1,0:T(8,128)(2,1)S(1)}, bf16[96,1024]{1,0:T(8,128)(2,1)S(1)}, u32[]{:S(2)}, u32[]{:S(2)}) %collective-permute-start) | collective-permute-done | bytes 196640 | tf_op jit(solution)/shard_map/ppermute | solution.py:36
  51.0 3.0 collective-permute-start.42
  61.1 14.3 %collective-permute-done.42 = bf16[96,1024]{1,0:T(8,128)(2,1)} collective-permute-done((bf16[96,1024]{1,0:T(8,128)(2,1)}, bf16[96,1024]{1,0:T(8,128)(2,1)}, u32[]{:S(2)}, u32[]{:S(2)}) %collective-permute-start.42) | collective-permute-done | bytes 196640 | tf_op jit(solution)/shard_map/ppermute | solution.py:36
  85.7 19.9 %collective-permute-done.10 = bf16[320,1024]{1,0:T(8,128)(2,1)} collective-permute-done((bf16[320,1024]{1,0:T(8,128)(2,1)}, bf16[320,1024]{1,0:T(8,128)(2,1)}, u32[]{:S(2)}, u32[]{:S(2)}) %collective-permute-start.10) | collective-permute-done | bytes 655392 | tf_op jit(solution)/shard_map/ppermute | solution.py:36
  123.1 3.1 fusion.52
  155.5 4.3 collective-permute-done.15
  164.9 6.1 collective-permute-done.19
  171.0 4.2 collective-permute-done.17
  181.1 8.0 %collective-permute-done.26 = bf16[96,1024]{1,0:T(8,128)(2,1)S(1)} collective-permute-done((bf16[96,1024]{1,0:T(8,128)(2,1)S(1)}, bf16[96,1024]{1,0:T(8,128)(2,1)S(1)}, u32[]{:S(2)}, u32[]{:S(2)}) %collective-permute-start.26) | collective-permute-done | bytes 196640 | tf_op jit(solution)/shard_map/ppermute | solution.py:36
  189.8 3.1 collective-permute-start.29
  199.8 5.4 collective-permute-done.27
  205.2 3.1 fusion.53
  224.7 9.3 %collective-permute-done.33 = bf16[96,1024]{1,0:T(8,128)(2,1)S(1)} collective-permute-done((bf16[96,1024]{1,0:T(8,128)(2,1)S(1)}, bf16[96,1024]{1,0:T(8,128)(2,1)S(1)}, u32[]{:S(2)}, u32[]{:S(2)}) %collective-permute-start.33) | collective-permute-done | bytes 196640 | tf_op jit(solution)/shard_map/ppermute | solution.py:36
  238.3 3.8 collective-permute-done.36
  244.3 5.4 collective-permute-done.34
  253.1 3.3 convert_reduce_fusion
  262.1 2.8 collective-permute-start.48
  272.8 7.4 %collective-permute-done.48 = bf16[96,1024]{1,0:T(8,128)(2,1)} collective-permute-done((bf16[96,1024]{1,0:T(8,128)(2,1)}, bf16[96,1024]{1,0:T(8,128)(2,1)}, u32[]{:S(2)}, u32[]{:S(2)}) %collective-permute-start.48) | collective-permute-done | bytes 196640 | tf_op jit(solution)/shard_map/ppermute | solution.py:36
  286.0 3.4 collective-permute-start.50
  292.1 3.6 collective-permute-start.41
  296.5 2.9 collective-permute-start.40
  301.5 4.0 multiply_reduce_fusion.1
  316.2 5.2 collective-permute-start.55
  326.9 3.4 collective-permute-done.54
  338.7 3.1 collective-permute-done.57
  341.8 5.3 collective-permute-done.56
  356.9 4.4 convolution_convert_fusion
  368.9 3.1 fusion.15
  372.0 3.4 collective-permute-start.64
  376.0 132.0 %all-reduce.2.cloned.1.call-done = f32[2,8,1024]{2,1,0:T(8,128)} async-done(((f32[2,8,1024]{2,1,0:T(8,128)}), f32[2,8,1024]{2,1,0:T(8,128)}) %all-reduce.2.cloned.1.call-update) | async-done | bytes 65552 | tf_op jit(solution)/shard_map/psum | solution.py:416
  513.4 4.0 multiply_reduce_fusion
  551.3 4.2 collective-permute-start.83
  563.5 3.9 collective-permute-done.75
  567.4 3.5 collective-permute-start.82
  570.9 4.1 collective-permute-start.88
  575.0 21.9 %collective-permute-done.83 = bf16[256,1024]{1,0:T(8,128)(2,1)S(1)} collective-permute-done((bf16[256,1024]{1,0:T(8,128)(2,1)S(1)}, bf16[256,1024]{1,0:T(8,128)(2,1)S(1)}, u32[]{:S(2)}, u32[]{:S(2)}) %collective-permute-start.83) | collective-permute-done | bytes 524320 | tf_op jit(solution)/shard_map/ppermute | solution.py:36
  600.7 5.8 collective-permute-start.98
  607.9 3.2 collective-permute-start.103
  617.1 11.1 %collective-permute-done.98 = bf16[512,1024]{1,0:T(8,128)(2,1)S(1)} collective-permute-done((bf16[512,1024]{1,0:T(8,128)(2,1)S(1)}, bf16[512,1024]{1,0:T(8,128)(2,1)S(1)}, u32[]{:S(2)}, u32[]{:S(2)}) %collective-permute-start.98) | collective-permute-done | bytes 1048608 | tf_op jit(solution)/shard_map/ppermute | solution.py:36
  628.2 3.4 collective-permute-start.80
  631.8 22.5 %collective-permute-done.103 = bf16[512,1024]{1,0:T(8,128)(2,1)S(1)} collective-permute-done((bf16[512,1024]{1,0:T(8,128)(2,1)S(1)}, bf16[512,1024]{1,0:T(8,128)(2,1)S(1)}, u32[]{:S(2)}, u32[]{:S(2)}) %collective-permute-start.103) | collective-permute-done | bytes 1048608 | tf_op jit(solution)/shard_map/ppermute | solution.py:36
  655.8 7.1 collective-permute-done.102
  671.4 3.3 collective-permute-start.70
  674.7 9.6 %collective-permute-start.69 = (bf16[96,1024]{1,0:T(8,128)(2,1)S(1)}, bf16[96,1024]{1,0:T(8,128)(2,1)S(1)}, u32[]{:S(2)}, u32[]{:S(2)}) collective-permute-start(bf16[96,1024]{1,0:T(8,128)(2,1)S(1)} %get-tuple-element.88), channel_id=1, source_target_pairs={{0,0},{1,8},{2,2},{3,10},{4,4},{5,12},{6,6},{7,14},{8,1},{9,9},{10... | collective-permute-start | bytes 589832 | tf_op jit(solution)/shard_map/ppermute | solution.py:36
  687.9 5.3 collective-permute-done.92
  694.1 13.2 %collective-permute-done.107 = bf16[128,1024]{1,0:T(8,128)(2,1)S(1)} collective-permute-done((bf16[128,1024]{1,0:T(8,128)(2,1)S(1)}, bf16[128,1024]{1,0:T(8,128)(2,1)S(1)}, u32[]{:S(2)}, u32[]{:S(2)}) %collective-permute-start.107) | collective-permute-done | bytes 262176 | tf_op jit(solution)/shard_map/ppermute | solution.py:36
  707.4 7.9 %collective-permute-done.109 = bf16[128,1024]{1,0:T(8,128)(2,1)S(1)} collective-permute-done((bf16[128,1024]{1,0:T(8,128)(2,1)S(1)}, bf16[128,1024]{1,0:T(8,128)(2,1)S(1)}, u32[]{:S(2)}, u32[]{:S(2)}) %collective-permute-start.109) | collective-permute-done | bytes 262176 | tf_op jit(solution)/shard_map/ppermute | solution.py:36
  (669 shorter events, 288.7 us)
Async XLA Ops:
  7.2 500.8 %all-reduce.2.cloned.1.call-start = ((), (), s32[]{:S(2)}) async-start(), calls=%async_computation | async-start | bytes 131072 | tf_op jit(solution)/shard_map/psum | solution.py:416
  16.1 33.7 %collective-permute-start.1 = (bf16[544,384]{0,1:T(8,128)(2,1)}, bf16[544,384]{0,1:T(8,128)(2,1)}, u32[]{:S(2)}, u32[]{:S(2)}) collective-permute-start(bf16[544,384]{0,1:T(8,128)(2,1)} %pad_maximum_fusion.17), channel_id=1, source_target_pairs={{0,64},{8,72},{16,80},{24,88},{32,96},{40,104},{48,112},{56,120},{... | collective-permute-start | bytes 1253384 | tf_op jit(solution)/shard_map/ppermute | solution.py:36
  18.6 32.3 %collective-permute-start.2 = (bf16[544,384]{0,1:T(8,128)(2,1)}, bf16[544,384]{0,1:T(8,128)(2,1)}, u32[]{:S(2)}, u32[]{:S(2)}) collective-permute-start(bf16[544,384]{0,1:T(8,128)(2,1)} %pad_maximum_fusion.17), channel_id=1, source_target_pairs={{0,72},{8,64},{16,88},{24,80},{32,104},{40,96},{48,120},{56,112},{... | collective-permute-start | bytes 1253384 | tf_op jit(solution)/shard_map/ppermute | solution.py:36
  20.7 34.2 %collective-permute-start.3 = (bf16[544,384]{0,1:T(8,128)(2,1)}, bf16[544,384]{0,1:T(8,128)(2,1)}, u32[]{:S(2)}, u32[]{:S(2)}) collective-permute-start(bf16[544,384]{0,1:T(8,128)(2,1)} %pad_maximum_fusion.17), channel_id=1, source_target_pairs={{0,8},{8,0},{16,24},{24,16},{32,40},{40,32},{48,56},{56,48},{64,72... | collective-permute-start | bytes 1253384 | tf_op jit(solution)/shard_map/ppermute | solution.py:36
  22.0 27.4 %collective-permute-start = (bf16[96,1024]{1,0:T(8,128)(2,1)S(1)}, bf16[96,1024]{1,0:T(8,128)(2,1)S(1)}, u32[]{:S(2)}, u32[]{:S(2)}) collective-permute-start(bf16[96,1024]{1,0:T(8,128)(2,1)S(1)} %dynamic-slice_bitcast_fusion.14), channel_id=1, source_target_pairs={{0,0},{1,8},{2,2},{3,10},{4,4},{5,12},{6,6},{7,14},{8,1},{9,9},{10... | collective-permute-start | bytes 589832 | tf_op jit(solution)/shard_map/ppermute | solution.py:36
  39.5 35.9 %collective-permute-start.20 = (bf16[512,512]{1,0:T(8,128)(2,1)}, bf16[512,512]{1,0:T(8,128)(2,1)}, u32[]{:S(2)}, u32[]{:S(2)}) collective-permute-start(bf16[512,512]{1,0:T(8,128)(2,1)} %dynamic-slice_bitcast_fusion.8), channel_id=1, source_target_pairs={{0,64},{8,72},{16,80},{24,88},{32,96},{40,104},{48,112},{56,120},{... | collective-permute-start | bytes 1572872 | tf_op jit(solution)/shard_map/ppermute | solution.py:36
  49.5 25.9 %collective-permute-start.22 = (bf16[512,512]{1,0:T(8,128)(2,1)}, bf16[512,512]{1,0:T(8,128)(2,1)}, u32[]{:S(2)}, u32[]{:S(2)}) collective-permute-start(bf16[512,512]{1,0:T(8,128)(2,1)} %dynamic-slice_bitcast_fusion.8), channel_id=1, source_target_pairs={{0,8},{8,0},{16,24},{24,16},{32,40},{40,32},{48,56},{56,48},{64,72... | collective-permute-start | bytes 1572872 | tf_op jit(solution)/shard_map/ppermute | solution.py:36
  49.9 30.1 %collective-permute-start.21 = (bf16[512,512]{1,0:T(8,128)(2,1)}, bf16[512,512]{1,0:T(8,128)(2,1)}, u32[]{:S(2)}, u32[]{:S(2)}) collective-permute-start(bf16[512,512]{1,0:T(8,128)(2,1)} %dynamic-slice_bitcast_fusion.8), channel_id=1, source_target_pairs={{0,72},{8,64},{16,88},{24,80},{32,104},{40,96},{48,120},{56,112},{... | collective-permute-start | bytes 1572872 | tf_op jit(solution)/shard_map/ppermute | solution.py:36
  51.0 24.4 %collective-permute-start.42 = (bf16[96,1024]{1,0:T(8,128)(2,1)}, bf16[96,1024]{1,0:T(8,128)(2,1)}, u32[]{:S(2)}, u32[]{:S(2)}) collective-permute-start(bf16[96,1024]{1,0:T(8,128)(2,1)} %dynamic-slice_bitcast_fusion.13), channel_id=1, source_target_pairs={{0,0},{1,8},{2,2},{3,10},{4,4},{5,12},{6,6},{7,14},{8,1},{9,9},{10... | collective-permute-start | bytes 589832 | tf_op jit(solution)/shard_map/ppermute | solution.py:36
  60.4 52.8 %collective-permute-start.7 = (bf16[3,512,384]{1,2,0:T(8,128)(2,1)}, bf16[3,512,384]{1,2,0:T(8,128)(2,1)}, u32[]{:S(2)}, u32[]{:S(2)}) collective-permute-start(bf16[3,512,384]{1,2,0:T(8,128)(2,1)} %pad_maximum_fusion.2), channel_id=1, source_target_pairs={{0,1},{1,0},{2,3},{3,2},{4,5},{5,4},{6,7},{7,6},{8,9},{9,8},{10,11... | collective-permute-start | bytes 3538952 | tf_op jit(solution)/shard_map/ppermute | solution.py:36
  75.3 30.3 %collective-permute-start.10 = (bf16[320,1024]{1,0:T(8,128)(2,1)}, bf16[320,1024]{1,0:T(8,128)(2,1)}, u32[]{:S(2)}, u32[]{:S(2)}) collective-permute-start(bf16[320,1024]{1,0:T(8,128)(2,1)} %pad_maximum_fusion.14), channel_id=1, source_target_pairs={{0,64},{8,72},{16,80},{24,88},{32,96},{40,104},{48,112},{56,120},{... | collective-permute-start | bytes 1966088 | tf_op jit(solution)/shard_map/ppermute | solution.py:36
  75.3 33.0 %collective-permute-start.12 = (bf16[320,1024]{1,0:T(8,128)(2,1)}, bf16[320,1024]{1,0:T(8,128)(2,1)S(1)}, u32[]{:S(2)}, u32[]{:S(2)}) collective-permute-start(bf16[320,1024]{1,0:T(8,128)(2,1)} %pad_maximum_fusion.14), channel_id=1, source_target_pairs={{0,8},{8,0},{16,24},{24,16},{32,40},{40,32},{48,56},{56,48},{64,72... | collective-permute-start | bytes 1966088 | tf_op jit(solution)/shard_map/ppermute | solution.py:36
  75.4 33.9 %collective-permute-start.11 = (bf16[320,1024]{1,0:T(8,128)(2,1)}, bf16[320,1024]{1,0:T(8,128)(2,1)}, u32[]{:S(2)}, u32[]{:S(2)}) collective-permute-start(bf16[320,1024]{1,0:T(8,128)(2,1)} %pad_maximum_fusion.14), channel_id=1, source_target_pairs={{0,72},{8,64},{16,88},{24,80},{32,104},{40,96},{48,120},{56,112},{... | collective-permute-start | bytes 1966088 | tf_op jit(solution)/shard_map/ppermute | solution.py:36
  79.9 115.4 %collective-permute-start.43 = (bf16[96,1024]{1,0:T(8,128)(2,1)}, bf16[96,1024]{1,0:T(8,128)(2,1)}, u32[]{:S(2)}, u32[]{:S(2)}) collective-permute-start(bf16[96,1024]{1,0:T(8,128)(2,1)} %collective-permute-done.42), channel_id=1, source_target_pairs={{0,16},{8,24},{16,32},{24,40},{32,48},{40,56},{48,0},{56,8},{1,17}... | collective-permute-start | bytes 589832 | tf_op jit(solution)/shard_map/ppermute | solution.py:36
  105.6 106.9 %collective-permute-start.44 = (bf16[96,1024]{1,0:T(8,128)(2,1)}, bf16[96,1024]{1,0:T(8,128)(2,1)}, u32[]{:S(2)}, u32[]{:S(2)}) collective-permute-start(bf16[96,1024]{1,0:T(8,128)(2,1)} %collective-permute-done.42), channel_id=1, source_target_pairs={{0,32},{8,40},{16,48},{24,56},{32,0},{40,8},{48,16},{56,24},{1,33}... | collective-permute-start | bytes 589832 | tf_op jit(solution)/shard_map/ppermute | solution.py:36
  122.2 20.0 %collective-permute-start.13 = (bf16[3,320,1024]{2,1,0:T(8,128)(2,1)}, bf16[3,320,1024]{2,1,0:T(8,128)(2,1)}, u32[]{:S(2)}, u32[]{:S(2)}) collective-permute-start(bf16[3,320,1024]{2,1,0:T(8,128)(2,1)} %pad_maximum_fusion), channel_id=1, source_target_pairs={{0,1},{1,0},{2,3},{3,2},{4,5},{5,4},{6,7},{7,6},{8,9},{9,8},{10,11... | collective-permute-start | bytes 5898248 | tf_op jit(solution)/shard_map/ppermute | solution.py:36
  195.4 18.7 %collective-permute-start.45 = (bf16[96,1024]{1,0:T(8,128)(2,1)}, bf16[96,1024]{1,0:T(8,128)(2,1)}, u32[]{:S(2)}, u32[]{:S(2)}) collective-permute-start(bf16[96,1024]{1,0:T(8,128)(2,1)} %collective-permute-done.42), channel_id=1, source_target_pairs={{0,48},{8,56},{16,0},{24,8},{32,16},{40,24},{48,32},{56,40},{1,49}... | collective-permute-start | bytes 589832 | tf_op jit(solution)/shard_map/ppermute | solution.py:36
  259.8 26.2 %collective-permute-start.39 = (bf16[96,1024]{1,0:T(8,128)(2,1)}, bf16[96,1024]{1,0:T(8,128)(2,1)}, u32[]{:S(2)}, u32[]{:S(2)}) collective-permute-start(bf16[96,1024]{1,0:T(8,128)(2,1)} %get-tuple-element.128), channel_id=1, source_target_pairs={{0,16},{8,24},{16,32},{24,40},{32,48},{40,56},{48,0},{56,8},{1,17}... | collective-permute-start | bytes 589832 | tf_op jit(solution)/shard_map/ppermute | solution.py:36
  259.8 29.6 %collective-permute-start.38 = (bf16[96,1024]{1,0:T(8,128)(2,1)}, bf16[96,1024]{1,0:T(8,128)(2,1)}, u32[]{:S(2)}, u32[]{:S(2)}) collective-permute-start(bf16[96,1024]{1,0:T(8,128)(2,1)} %get-tuple-element.129), channel_id=1, source_target_pairs={{0,32},{8,40},{16,48},{24,56},{32,0},{40,8},{48,16},{56,24},{1,33}... | collective-permute-start | bytes 589832 | tf_op jit(solution)/shard_map/ppermute | solution.py:36
  262.1 18.1 %collective-permute-start.48 = (bf16[96,1024]{1,0:T(8,128)(2,1)}, bf16[96,1024]{1,0:T(8,128)(2,1)}, u32[]{:S(2)}, u32[]{:S(2)}) collective-permute-start(bf16[96,1024]{1,0:T(8,128)(2,1)} %get-tuple-element.125), channel_id=1, source_target_pairs={{0,16},{8,24},{16,32},{24,40},{32,48},{40,56},{48,0},{56,8},{1,17}... | collective-permute-start | bytes 589832 | tf_op jit(solution)/shard_map/ppermute | solution.py:36
  265.6 15.8 %collective-permute-start.46 = (bf16[96,1024]{1,0:T(8,128)(2,1)}, bf16[96,1024]{1,0:T(8,128)(2,1)}, u32[]{:S(2)}, u32[]{:S(2)}) collective-permute-start(bf16[96,1024]{1,0:T(8,128)(2,1)} %get-tuple-element.124), channel_id=1, source_target_pairs={{0,48},{8,56},{16,0},{24,8},{32,16},{40,24},{48,32},{56,40},{1,49}... | collective-permute-start | bytes 589832 | tf_op jit(solution)/shard_map/ppermute | solution.py:36
  280.2 261.7 %collective-permute-start.96 = (bf16[2,512,1024]{2,1,0:T(8,128)(2,1)}, bf16[2,512,1024]{2,1,0:T(8,128)(2,1)}, u32[]{:S(2)}, u32[]{:S(2)}) collective-permute-start(bf16[2,512,1024]{2,1,0:T(8,128)(2,1)} %fusion.19), channel_id=1, source_target_pairs={{0,1},{1,0},{2,3},{3,2},{4,5},{5,4},{6,7},{7,6},{8,9},{9,8},{10,11... | collective-permute-start | bytes 6291464 | tf_op jit(solution)/shard_map/ppermute | solution.py:36
  292.1 18.5 %collective-permute-start.41 = (bf16[96,1024]{1,0:T(8,128)(2,1)}, bf16[96,1024]{1,0:T(8,128)(2,1)}, u32[]{:S(2)}, u32[]{:S(2)}) collective-permute-start(bf16[96,1024]{1,0:T(8,128)(2,1)} %broadcast_select_fusion.2), channel_id=1, source_target_pairs={{0,64},{1,72},{2,66},{3,74},{4,68},{5,76},{6,70},{7,78},{8,65},{9,... | collective-permute-start | bytes 589832 | tf_op jit(solution)/shard_map/ppermute | solution.py:36
  326.0 197.0 %collective-permute-start.81 = (bf16[2,256,1024]{2,1,0:T(8,128)(2,1)}, bf16[2,256,1024]{2,1,0:T(8,128)(2,1)}, u32[]{:S(2)}, u32[]{:S(2)}) collective-permute-start(bf16[2,256,1024]{2,1,0:T(8,128)(2,1)} %fusion.64), channel_id=1, source_target_pairs={{0,1},{1,0},{2,3},{3,2},{4,5},{5,4},{6,7},{7,6},{8,9},{9,8},{10,11... | collective-permute-start | bytes 3145736 | tf_op jit(solution)/shard_map/ppermute | solution.py:36
  372.0 138.9 %collective-permute-start.64 = (bf16[96,1024]{1,0:T(8,128)(2,1)S(1)}, bf16[96,1024]{1,0:T(8,128)(2,1)S(1)}, u32[]{:S(2)}, u32[]{:S(2)}) collective-permute-start(bf16[96,1024]{1,0:T(8,128)(2,1)S(1)} %get-tuple-element.77), channel_id=1, source_target_pairs={{0,48},{8,56},{16,0},{24,8},{32,16},{40,24},{48,32},{56,40},{1,49}... | collective-permute-start | bytes 589832 | tf_op jit(solution)/shard_map/ppermute | solution.py:36
  375.4 135.6 %collective-permute-start.63 = (bf16[96,1024]{1,0:T(8,128)(2,1)S(1)}, bf16[96,1024]{1,0:T(8,128)(2,1)}, u32[]{:S(2)}, u32[]{:S(2)}) collective-permute-start(bf16[96,1024]{1,0:T(8,128)(2,1)S(1)} %get-tuple-element.77), channel_id=1, source_target_pairs={{0,32},{8,40},{16,48},{24,56},{32,0},{40,8},{48,16},{56,24},{1,33}... | collective-permute-start | bytes 589832 | tf_op jit(solution)/shard_map/ppermute | solution.py:36
  375.6 136.0 %collective-permute-start.62 = (bf16[96,1024]{1,0:T(8,128)(2,1)S(1)}, bf16[96,1024]{1,0:T(8,128)(2,1)}, u32[]{:S(2)}, u32[]{:S(2)}) collective-permute-start(bf16[96,1024]{1,0:T(8,128)(2,1)S(1)} %get-tuple-element.77), channel_id=1, source_target_pairs={{0,16},{8,24},{16,32},{24,40},{32,48},{40,56},{48,0},{56,8},{1,17}... | collective-permute-start | bytes 589832 | tf_op jit(solution)/shard_map/ppermute | solution.py:36
  510.9 87.2 %collective-permute-start.100 = (bf16[2,512,1024]{2,1,0:T(8,128)(2,1)}, bf16[2,512,1024]{2,1,0:T(8,128)(2,1)S(1)}, u32[]{:S(2)}, u32[]{:S(2)}) collective-permute-start(bf16[2,512,1024]{2,1,0:T(8,128)(2,1)} %fusion.15), channel_id=1, source_target_pairs={{0,1},{1,0},{2,3},{3,2},{4,5},{5,4},{6,7},{7,6},{8,9},{9,8},{10,11... | collective-permute-start | bytes 6291464 | tf_op jit(solution)/shard_map/ppermute | solution.py:36
  535.3 23.8 %collective-permute-start.85 = (bf16[2,256,1024]{2,1,0:T(8,128)(2,1)S(1)}, bf16[2,256,1024]{2,1,0:T(8,128)(2,1)S(1)}, u32[]{:S(2)}, u32[]{:S(2)}) collective-permute-start(bf16[2,256,1024]{2,1,0:T(8,128)(2,1)S(1)} %fusion.60), channel_id=1, source_target_pairs={{0,1},{1,0},{2,3},{3,2},{4,5},{5,4},{6,7},{7,6},{8,9},{9,8},{10,11... | collective-permute-start | bytes 3145736 | tf_op jit(solution)/shard_map/ppermute | solution.py:36
  548.1 22.8 %collective-permute-start.84 = (bf16[256,1024]{1,0:T(8,128)(2,1)S(1)}, bf16[256,1024]{1,0:T(8,128)(2,1)S(1)}, u32[]{:S(2)}, u32[]{:S(2)}) collective-permute-start(bf16[256,1024]{1,0:T(8,128)(2,1)S(1)} %get-tuple-element.114), channel_id=1, source_target_pairs={{64,72},{72,64},{80,88},{88,80},{96,104},{104,96},{112,120},{120,1... | collective-permute-start | bytes 1572872 | tf_op jit(solution)/shard_map/ppermute | solution.py:36
  551.3 45.6 %collective-permute-start.83 = (bf16[256,1024]{1,0:T(8,128)(2,1)S(1)}, bf16[256,1024]{1,0:T(8,128)(2,1)S(1)}, u32[]{:S(2)}, u32[]{:S(2)}) collective-permute-start(bf16[256,1024]{1,0:T(8,128)(2,1)S(1)} %get-tuple-element.114), channel_id=1, source_target_pairs={{0,72},{8,64},{16,88},{24,80},{32,104},{40,96},{48,120},{56,112},{... | collective-permute-start | bytes 1572872 | tf_op jit(solution)/shard_map/ppermute | solution.py:36
  558.3 48.2 %collective-permute-start.99 = (bf16[512,1024]{1,0:T(8,128)(2,1)S(1)}, bf16[512,1024]{1,0:T(8,128)(2,1)S(1)}, u32[]{:S(2)}, u32[]{:S(2)}) collective-permute-start(bf16[512,1024]{1,0:T(8,128)(2,1)S(1)} %get-tuple-element.107), channel_id=1, source_target_pairs={{64,72},{72,64},{80,88},{88,80},{96,104},{104,96},{112,120},{120,1... | collective-permute-start | bytes 3145736 | tf_op jit(solution)/shard_map/ppermute | solution.py:36
  567.4 33.3 %collective-permute-start.82 = (bf16[256,1024]{1,0:T(8,128)(2,1)S(1)}, bf16[256,1024]{1,0:T(8,128)(2,1)S(1)}, u32[]{:S(2)}, u32[]{:S(2)}) collective-permute-start(bf16[256,1024]{1,0:T(8,128)(2,1)S(1)} %get-tuple-element.113), channel_id=1, source_target_pairs={{0,64},{8,72},{16,80},{24,88},{32,96},{40,104},{48,112},{56,120},{... | collective-permute-start | bytes 1572872 | tf_op jit(solution)/shard_map/ppermute | solution.py:36
  570.9 37.0 %collective-permute-start.88 = (bf16[256,1024]{1,0:T(8,128)(2,1)S(1)}, bf16[256,1024]{1,0:T(8,128)(2,1)S(1)}, u32[]{:S(2)}, u32[]{:S(2)}) collective-permute-start(bf16[256,1024]{1,0:T(8,128)(2,1)S(1)} %get-tuple-element.112), channel_id=1, source_target_pairs={{0,8},{8,0},{16,24},{24,16},{32,40},{40,32},{48,56},{56,48},{1,9},... | collective-permute-start | bytes 1572872 | tf_op jit(solution)/shard_map/ppermute | solution.py:36
  596.8 16.4 %collective-permute-start.87 = (bf16[256,1024]{1,0:T(8,128)(2,1)S(1)}, bf16[256,1024]{1,0:T(8,128)(2,1)S(1)}, u32[]{:S(2)}, u32[]{:S(2)}) collective-permute-start(bf16[256,1024]{1,0:T(8,128)(2,1)S(1)} %get-tuple-element.112), channel_id=1, source_target_pairs={{64,8},{72,0},{80,24},{88,16},{96,40},{104,32},{112,56},{120,48},{... | collective-permute-start | bytes 1572872 | tf_op jit(solution)/shard_map/ppermute | solution.py:36
  598.1 16.3 %collective-permute-start.86 = (bf16[256,1024]{1,0:T(8,128)(2,1)S(1)}, bf16[256,1024]{1,0:T(8,128)(2,1)S(1)}, u32[]{:S(2)}, u32[]{:S(2)}) collective-permute-start(bf16[256,1024]{1,0:T(8,128)(2,1)S(1)} %get-tuple-element.111), channel_id=1, source_target_pairs={{64,0},{72,8},{80,16},{88,24},{96,32},{104,40},{112,48},{120,56},{... | collective-permute-start | bytes 1572872 | tf_op jit(solution)/shard_map/ppermute | solution.py:36
  600.7 27.5 %collective-permute-start.98 = (bf16[512,1024]{1,0:T(8,128)(2,1)S(1)}, bf16[512,1024]{1,0:T(8,128)(2,1)S(1)}, u32[]{:S(2)}, u32[]{:S(2)}) collective-permute-start(bf16[512,1024]{1,0:T(8,128)(2,1)S(1)} %get-tuple-element.107), channel_id=1, source_target_pairs={{0,72},{8,64},{16,88},{24,80},{32,104},{40,96},{48,120},{56,112},{... | collective-permute-start | bytes 3145736 | tf_op jit(solution)/shard_map/ppermute | solution.py:36
  606.6 25.0 %collective-permute-start.97 = (bf16[512,1024]{1,0:T(8,128)(2,1)S(1)}, bf16[512,1024]{1,0:T(8,128)(2,1)S(1)}, u32[]{:S(2)}, u32[]{:S(2)}) collective-permute-start(bf16[512,1024]{1,0:T(8,128)(2,1)S(1)} %get-tuple-element.106), channel_id=1, source_target_pairs={{0,64},{8,72},{16,80},{24,88},{32,96},{40,104},{48,112},{56,120},{... | collective-permute-start | bytes 3145736 | tf_op jit(solution)/shard_map/ppermute | solution.py:36
  607.9 46.4 %collective-permute-start.103 = (bf16[512,1024]{1,0:T(8,128)(2,1)S(1)}, bf16[512,1024]{1,0:T(8,128)(2,1)S(1)}, u32[]{:S(2)}, u32[]{:S(2)}) collective-permute-start(bf16[512,1024]{1,0:T(8,128)(2,1)S(1)} %get-tuple-element.105), channel_id=1, source_target_pairs={{0,8},{8,0},{16,24},{24,16},{32,40},{40,32},{48,56},{56,48},{1,9},... | collective-permute-start | bytes 3145736 | tf_op jit(solution)/shard_map/ppermute | solution.py:36
  613.2 49.7 %collective-permute-start.102 = (bf16[512,1024]{1,0:T(8,128)(2,1)S(1)}, bf16[512,1024]{1,0:T(8,128)(2,1)S(1)}, u32[]{:S(2)}, u32[]{:S(2)}) collective-permute-start(bf16[512,1024]{1,0:T(8,128)(2,1)S(1)} %get-tuple-element.105), channel_id=1, source_target_pairs={{64,8},{72,0},{80,24},{88,16},{96,40},{104,32},{112,56},{120,48},{... | collective-permute-start | bytes 3145736 | tf_op jit(solution)/shard_map/ppermute | solution.py:36
  614.5 49.7 %collective-permute-start.101 = (bf16[512,1024]{1,0:T(8,128)(2,1)S(1)}, bf16[512,1024]{1,0:T(8,128)(2,1)S(1)}, u32[]{:S(2)}, u32[]{:S(2)}) collective-permute-start(bf16[512,1024]{1,0:T(8,128)(2,1)S(1)} %get-tuple-element.104), channel_id=1, source_target_pairs={{64,0},{72,8},{80,16},{88,24},{96,32},{104,40},{112,48},{120,56},{... | collective-permute-start | bytes 3145736 | tf_op jit(solution)/shard_map/ppermute | solution.py:36
  628.2 39.6 %collective-permute-start.80 = (f32[2,4,1024]{2,1,0:T(4,128)S(1)}, f32[2,4,1024]{2,1,0:T(4,128)S(1)}, u32[]{:S(2)}, u32[]{:S(2)}) collective-permute-start(f32[2,4,1024]{2,1,0:T(4,128)S(1)} %bitcast.499), channel_id=1, source_target_pairs={{0,72},{8,64},{16,88},{24,80},{32,104},{40,96},{48,120},{56,112},{... | collective-permute-start | bytes 98312 | tf_op jit(solution)/shard_map/ppermute | solution.py:36
  631.6 36.3 %collective-permute-start.78 = (f32[2,4,1024]{2,1,0:T(4,128)S(1)}, f32[2,4,1024]{2,1,0:T(4,128)S(1)}, u32[]{:S(2)}, u32[]{:S(2)}) collective-permute-start(f32[2,4,1024]{2,1,0:T(4,128)S(1)} %bitcast.500), channel_id=1, source_target_pairs={{0,64},{8,72},{16,80},{24,88},{32,96},{40,104},{48,112},{56,120},{... | collective-permute-start | bytes 98312 | tf_op jit(solution)/shard_map/ppermute | solution.py:36
  654.3 16.4 %collective-permute-start.79 = (f32[2,4,1024]{2,1,0:T(4,128)S(1)}, f32[2,4,1024]{2,1,0:T(4,128)S(1)}, u32[]{:S(2)}, u32[]{:S(2)}) collective-permute-start(f32[2,4,1024]{2,1,0:T(4,128)S(1)} %bitcast.501), channel_id=1, source_target_pairs={{0,8},{8,0},{16,24},{24,16},{32,40},{40,32},{48,56},{56,48},{64,72... | collective-permute-start | bytes 98312 | tf_op jit(solution)/shard_map/ppermute | solution.py:36
  667.9 16.5 %collective-permute-start.106 = (bf16[128,1024]{1,0:T(8,128)(2,1)S(1)}, bf16[128,1024]{1,0:T(8,128)(2,1)S(1)}, u32[]{:S(2)}, u32[]{:S(2)}) collective-permute-start(bf16[128,1024]{1,0:T(8,128)(2,1)S(1)} %get-tuple-element.109), channel_id=1, source_target_pairs={{0,6},{1,7},{2,0},{3,1},{4,2},{5,3},{6,4},{7,5},{8,14},{9,15},{10,... | collective-permute-start | bytes 786440 | tf_op jit(solution)/shard_map/ppermute | solution.py:36
  671.4 46.1 %collective-permute-start.70 = (bf16[96,1024]{1,0:T(8,128)(2,1)S(1)}, bf16[96,1024]{1,0:T(8,128)(2,1)S(1)}, u32[]{:S(2)}, u32[]{:S(2)}) collective-permute-start(bf16[96,1024]{1,0:T(8,128)(2,1)S(1)} %broadcast_select_fusion), channel_id=1, source_target_pairs={{0,64},{1,72},{2,66},{3,74},{4,68},{5,76},{6,70},{7,78},{8,65},{9,... | collective-permute-start | bytes 589832 | tf_op jit(solution)/shard_map/ppermute | solution.py:36
  674.7 42.7 %collective-permute-start.69 = (bf16[96,1024]{1,0:T(8,128)(2,1)S(1)}, bf16[96,1024]{1,0:T(8,128)(2,1)S(1)}, u32[]{:S(2)}, u32[]{:S(2)}) collective-permute-start(bf16[96,1024]{1,0:T(8,128)(2,1)S(1)} %get-tuple-element.88), channel_id=1, source_target_pairs={{0,0},{1,8},{2,2},{3,10},{4,4},{5,12},{6,6},{7,14},{8,1},{9,9},{10... | collective-permute-start | bytes 589832 | tf_op jit(solution)/shard_map/ppermute | solution.py:36
  686.0 30.1 %collective-permute-start.94 = (bf16[64,1024]{1,0:T(8,128)(2,1)S(1)}, bf16[64,1024]{1,0:T(8,128)(2,1)S(1)}, u32[]{:S(2)}, u32[]{:S(2)}) collective-permute-start(bf16[64,1024]{1,0:T(8,128)(2,1)S(1)} %get-tuple-element.83), channel_id=1, source_target_pairs={{0,6},{1,7},{2,0},{3,1},{4,2},{5,3},{6,4},{7,5},{8,14},{9,15},{10,... | collective-permute-start | bytes 393224 | tf_op jit(solution)/shard_map/ppermute | solution.py:36
  (166 other events, 1685.0 us)
Sparse Core Ops, SparseCore 0:
  369.0 138.9 all-reduce.1

commit v2 on v1

--- a/solution.py
+++ b/solution.py
@@ -1,6 +1,8 @@
 import jax
 import jax.numpy as jnp
 from jax import lax
+from jax.experimental import pallas as pl
+from jax.experimental.pallas import tpu as pltpu
 from jax.sharding import PartitionSpec as P
 
 HEAD_DIM = 64
@@ -175,7 +177,7 @@
     return grad.astype(bf16).reshape(2, 2, rows, WIDTH)
 
 
-def layer_backward(incoming, allowed, vectors, weights, saved):
+def layer_backward(incoming, allowed, vectors, weights, saved, hook):
     gain_one, shift_one, out_bias, gain_two, shift_two, proj_bias, qkv_bias, fc_bias = vectors
     w_qkv, w_out, w_fc, w_proj = weights
     (
@@ -185,21 +187,24 @@
     ) = saved
     grad_feed = incoming.astype(bf16)
     proj_bias_grad = jnp.sum(grad_feed.astype(f32), axis=0)
-    feed_rows = gather_rows(grad_feed)
+    feed_rows = hook(0, gather_rows(grad_feed))
     hidden_grad = dot(feed_rows, w_proj, 1, 1)
     gelu_pull = jax.vjp(lambda item: jax.nn.gelu(item, approximate=True), gelu_input)[1]
     gelu_grad = gelu_pull(hidden_grad)[0].astype(bf16)
     normed_two_grad = scatter_rows(dot(gelu_grad, w_fc, 1, 1))
     fc_bias_grad = jnp.sum(gelu_grad.astype(f32), axis=0)
-    w_proj_grad = dot(hidden, feed_rows, 0, 0)
-    w_fc_grad = dot(gelu_grad, rows_two, 0, 0)
+    feed_group = jnp.concatenate(
+        [halves(dot(gelu_grad, rows_two, 0, 0), 256), halves(dot(hidden, feed_rows, 0, 0), 256)],
+        axis=2,
+    )
+    normed_two_grad = hook(1, normed_two_grad, feed_group)
     middle_norm, gain_two_grad, shift_two_grad = norm_backward(
         normed_two_grad, standard_two, inverse_two, gain_two
     )
     middle_grad = incoming + middle_norm
     grad_attention = middle_grad.astype(bf16)
     out_bias_grad = jnp.sum(grad_attention.astype(f32), axis=0)
-    attention_rows = gather_rows(grad_attention)
+    attention_rows = hook(2, gather_rows(grad_attention))
     context_grad = dot(attention_rows, w_out, 1, 1).astype(bf16)
     w_out_grad = dot(context, attention_rows, 0, 0)
     query_grad, key_grad, value_grad = attend_backward(
@@ -215,26 +220,37 @@
     summed = both[:, : 4 * BLOCK] + arrived.astype(f32)
     triple = jnp.stack([query_grad.reshape(4 * BLOCK, 256), summed[0], summed[1]], axis=1)
     triple = triple.astype(bf16).reshape(4 * BLOCK, 3, 2, 128)
-    triple = jnp.moveaxis(triple, 2, 1).reshape(4 * BLOCK, 768)
-    normed_one_grad = scatter_rows(dot(triple, w_qkv, 1, 1))
+    triple = hook(3, jnp.moveaxis(triple, 2, 1).reshape(4 * BLOCK, 768))
+    attention_group = jnp.concatenate(
+        [halves(dot(triple, rows_one, 0, 0), 192), halves(w_out_grad, 64)], axis=2
+    )
+    normed_one_grad = hook(4, scatter_rows(dot(triple, w_qkv, 1, 1)), attention_group)
     qkv_bias_grad = jnp.sum(triple.astype(f32), axis=0)
-    w_qkv_grad = dot(triple, rows_one, 0, 0)
     stream_norm, gain_one_grad, shift_one_grad = norm_backward(
         normed_one_grad, standard_one, inverse_one, gain_one
     )
     stream_grad = middle_grad + stream_norm
-    feed_group = jnp.concatenate([halves(w_fc_grad, 256), halves(w_proj_grad, 256)], axis=2)
-    attention_group = jnp.concatenate([halves(w_qkv_grad, 192), halves(w_out_grad, 64)], axis=2)
     early = (out_bias_grad, gain_two_grad, shift_two_grad, proj_bias_grad, fc_bias_grad)
     late = (gain_one_grad, shift_one_grad, qkv_bias_grad)
-    return stream_grad, feed_group, attention_group, early, late
-
-
-def to_owner(group, layer, here):
-    pipe, high, core = here
+    return stream_grad, early, late
+
+
+def over_cores(group, core):
     sent = other_core(pick(group, 1 - core, 1))
     mine = (pick(group, core, 1).astype(f32) + sent.astype(f32)).astype(bf16)
-    near, far = pick(mine, high), pick(mine, 1 - high)
+    return mine.reshape(2, 4, mine.shape[1] // 4, WIDTH)
+
+
+def over_y(mine):
+    y = lax.axis_index("dp") // 2
+    own = pick(mine, y, 1).astype(f32)
+    for by in (1, 2, 3):
+        own = own + along_y(pick(mine, (y + by) % 4, 1), by).astype(f32)
+    return own.astype(bf16)
+
+
+def over_z(own, layer, pipe, high):
+    near, far = pick(own, high), pick(own, 1 - high)
     step = 1 if layer == 1 else -1
     total = jnp.where(pipe == layer, near.astype(f32), 0.0)
     total = total + along_z(near, step, only=1 - layer).astype(f32)
@@ -243,80 +259,162 @@
     return total.astype(bf16)
 
 
-def over_y(total):
-    rows = total.shape[0]
+def back_over_y(own):
+    rows = own.shape[0]
     y = lax.axis_index("dp") // 2
-    chunks = total.reshape(4, rows // 4, WIDTH)
-    own = pick(chunks, y).astype(f32)
-    for by in (1, 2, 3):
-        own = own + along_y(pick(chunks, (y + by) % 4), by).astype(f32)
-    own = own.astype(bf16)
-    whole = jnp.zeros((4, rows // 4, WIDTH), bf16)
+    whole = jnp.zeros((4, rows, WIDTH), bf16)
     whole = place(whole, own[None], (y, 0, 0))
     for by in (1, 2, 3):
         whole = place(whole, along_y(own, by)[None], ((y - by) % 4, 0, 0))
-    whole = whole.reshape(rows, WIDTH)
+    whole = whole.reshape(4 * rows, WIDTH)
     core = lax.axis_index("dp") % 2
-    both = jnp.zeros((2, rows, WIDTH), bf16)
+    both = jnp.zeros((2, 4 * rows, WIDTH), bf16)
     both = place(both, whole[None], (core, 0, 0))
     return place(both, other_core(whole)[None], (1 - core, 0, 0)).astype(f32)
 
 
-def everywhere(array):
-    array = array + other_core(array)
-    for along in (along_x, along_y, along_z):
-        array = array + along(array, 1) + along(array, 2) + along(array, 3)
-    return array
+def everywhere(array, pipe):
+    mine, other = pick(array, pipe), pick(array, 1 - pipe)
+    total = mine + along_z(other, 1) + along_z(other, 3) + along_z(mine, 2)
+    total = total + other_core(total)
+    for along in (along_x, along_y):
+        total = total + along(total, 1) + along(total, 2) + along(total, 3)
+    return total
+
+
+def held(value, *others):
+    return lax.optimization_barrier((value,) + others)[0]
+
+
+def lay_out(here, copies, sources, shapes):
+    def kernel(at_ref, *refs):
+        inputs, outputs = refs[: len(sources)], refs[len(sources) : -1]
+        semaphores = refs[-1]
+        started = []
+        for source, start, output, stop in copies(at_ref[0], at_ref[1], at_ref[2]):
+            copy = pltpu.make_async_copy(
+                inputs[source].at[start], outputs[output].at[stop], semaphores.at[len(started)]
+            )
+            copy.start()
+            started.append(copy)
+        for copy in started:
+            copy.wait()
+
+    count = len(copies(0, 0, 0))
+    whole = pl.BlockSpec(memory_space=pl.ANY)
+    return pl.pallas_call(
+        kernel,
+        out_shape=tuple(jax.ShapeDtypeStruct(shape, bf16) for shape in shapes),
+        in_specs=[pl.BlockSpec(memory_space=pltpu.SMEM)] + [whole] * len(sources),
+        out_specs=tuple(pl.BlockSpec(memory_space=pltpu.VMEM) for _ in shapes),
+        scratch_shapes=[pltpu.SemaphoreType.DMA((count,))],
+        compiler_params=pltpu.CompilerParams(vmem_limit_bytes=24 * 1024 * 1024),
+    )(jnp.stack(here).astype(jnp.int32), *sources)
+
+
+def span(start, size, unit=None):
+    if unit is not None and not isinstance(start, int):
+        start = pl.multiple_of(start, unit)
+    return pl.ds(start, size)
+
+
+ORDER = (1, 3, 2)
+
+
+def sources_of(pipe, high):
+    z = high * 2 + pipe
+    return [((z + 4 - by) % 2, (z + 4 - by) % 4 // 2) for by in ORDER]
 
 
 def spread_weights(here, w_qkv, w_out, w_fc, w_proj, smalls):
     pipe, high, core = here
-    z = high * 2 + pipe
-    group_one = jnp.concatenate(
-        [lax.dynamic_slice_in_dim(w_qkv, core * 512, 512, 0), smalls], axis=0
-    )
-    group_two = jnp.concatenate(
+
+    def exchanged(group, after):
+        group = held(group, *after)
+        came = [along_z(group, by) for by in ORDER]
+        return came, other_core(jnp.stack(came))
+
+    group = jnp.concatenate([lax.dynamic_slice_in_dim(w_qkv, core * 512, 512, 0), smalls], axis=0)
+    came, swapped = exchanged(group, ())
+
+    def copies(pipe, high, core):
+        rows = span(0, 512)
+        result = [(0, (span(0, 1024),), 0, (pipe, span(0, 1024), span(high * 384, 384, 128)))]
+        result.append((1, (span(0, 32),), 1, (pipe, high)))
+        for i, (layer, slot) in enumerate(sources_of(pipe, high)):
+            columns = span(slot * 384, 384, 128)
+            result.append((2 + i, (rows,), 0, (layer, span(core * 512, 512, 512), columns)))
+            result.append(
+                (5, (i, rows), 0, (layer, span((1 - core) * 512, 512, 512), columns))
+            )
+            result.append((2 + i, (span(512, 32),), 1, (layer, slot)))
+        return result
+
+    all_qkv, all_small = lay_out(
+        here, copies, [w_qkv, smalls, *came, swapped], [(2, 1024, 768), (2, 2, 32, 384)]
+    )
+
+    half = lax.dynamic_slice_in_dim(w_fc, core * 512, 512, 0)
+    group = jnp.concatenate(
         [
+            jnp.concatenate([half[:256], half[256:]], axis=1),
             lax.dynamic_slice_in_dim(w_out, core * 64, 64, 0),
-            lax.dynamic_slice_in_dim(w_proj, core * 256, 256, 0),
         ],
         axis=0,
     )
-    group_three = lax.dynamic_slice_in_dim(w_fc, core * 512, 512, 0)
-    all_qkv = jnp.zeros((2, 1024, 768), bf16)
-    all_out = jnp.zeros((2, 256, 1024), bf16)
-    all_fc = jnp.zeros((2, 1024, 1024), bf16)
-    all_proj = jnp.zeros((2, 1024, 1024), bf16)
-    all_small = jnp.zeros((2, 2, 32, 384), bf16)
-    all_qkv = place(all_qkv, w_qkv[None], (pipe, 0, high * 384))
-    all_out = place(all_out, w_out[None], (pipe, high * 128, 0))
-    all_fc = place(all_fc, w_fc[None], (pipe, 0, high * 512))
-    all_proj = place(all_proj, w_proj[None], (pipe, high * 512, 0))
-    all_small = place(all_small, smalls[None, None], (pipe, high, 0, 0))
-    order = (1, 3, 2)
-    came = [along_z(group_one, by) for by in order]
-    swapped = other_core(jnp.stack([item[:512] for item in came]))
-    for i, by in enumerate(order):
-        source = (z - by) % 4
-        layer, slot = source % 2, source // 2
-        all_small = place(all_small, came[i][None, None, 512:], (layer, slot, 0, 0))
-        all_qkv = place(all_qkv, came[i][None, :512], (layer, core * 512, slot * 384))
-        all_qkv = place(all_qkv, swapped[i][None], (layer, (1 - core) * 512, slot * 384))
-    came = [along_z(group_two, by) for by in order]
-    swapped = other_core(jnp.stack(came))
-    for i, by in enumerate(order):
-        source = (z - by) % 4
-        layer, slot = source % 2, source // 2
-        for half, item in ((core, came[i]), (1 - core, swapped[i])):
-            all_out = place(all_out, item[None, :64], (layer, slot * 128 + half * 64, 0))
-            all_proj = place(all_proj, item[None, 64:], (layer, slot * 512 + half * 256, 0))
-    came = [along_z(group_three, by) for by in order]
-    swapped = other_core(jnp.stack(came))
-    for i, by in enumerate(order):
-        source = (z - by) % 4
-        layer, slot = source % 2, source // 2
-        for half, item in ((core, came[i]), (1 - core, swapped[i])):
-            all_fc = place(all_fc, item[None], (layer, half * 512, slot * 512))
+    came, swapped = exchanged(group, came)
+
+    def copies(pipe, high, core):
+        columns = span(0, 1024)
+        result = [(0, (span(0, 1024),), 0, (pipe, span(0, 1024), span(high * 512, 512, 512)))]
+        result.append((1, (span(0, 128),), 1, (pipe, span(high * 128, 128, 128))))
+        for i, (layer, slot) in enumerate(sources_of(pipe, high)):
+            for source, lead, number in ((2 + i, (), core), (5, (i,), 1 - core)):
+                for part in range(2):
+                    result.append(
+                        (
+                            source,
+                            (*lead, span(0, 256), span(part * 512, 512)),
+                            0,
+                            (
+                                layer,
+                                span(number * 512 + part * 256, 256, 256),
+                                span(slot * 512, 512, 512),
+                            ),
+                        )
+                    )
+                result.append(
+                    (
+                        source,
+                        (*lead, span(256, 64)),
+                        1,
+                        (layer, span(slot * 128 + number * 64, 64, 64)),
+                    )
+                )
+        return result
+
+    all_fc, all_out = lay_out(
+        here, copies, [w_fc, w_out, *came, swapped], [(2, 1024, 1024), (2, 256, 1024)]
+    )
+
+    group = lax.dynamic_slice_in_dim(w_proj, core * 256, 256, 0)
+    came, swapped = exchanged(group, came)
+
+    def copies(pipe, high, core):
+        result = [(0, (span(0, 512),), 0, (pipe, span(high * 512, 512, 512)))]
+        for i, (layer, slot) in enumerate(sources_of(pipe, high)):
+            for source, lead, number in ((1 + i, (), core), (4, (i,), 1 - core)):
+                result.append(
+                    (
+                        source,
+                        (*lead, span(0, 256)),
+                        0,
+                        (layer, span(slot * 512 + number * 256, 256, 256)),
+                    )
+                )
+        return result
+
+    (all_proj,) = lay_out(here, copies, [w_proj, *came, swapped], [(2, 1024, 1024)])
     return all_qkv, all_out, all_fc, all_proj, all_small
 
 
@@ -356,16 +454,17 @@
 
     smalls = jnp.concatenate(
         [
-            ln1_gain[0],
-            ln1_bias[0],
-            out_bias[0],
-            ln2_gain[0],
-            ln2_bias[0],
-            proj_bias[0],
-            qv_bias[0].reshape(-1),
-            fc_bias[0],
-            jnp.zeros((32 * 384 - 6912,), bf16),
-        ]
+            ln1_gain,
+            ln1_bias,
+            out_bias,
+            ln2_gain,
+            ln2_bias,
+            proj_bias,
+            qv_bias.reshape(1, 256),
+            fc_bias,
+            jnp.zeros((1, 32 * 384 - 6912), bf16),
+        ],
+        axis=1,
     ).reshape(32, 384)
     all_qkv, all_out, all_fc, all_proj, all_small = spread_weights(
         here, w_qkv[0].reshape(WIDTH, 384), w_out[0], w_fc[0], w_proj[0], smalls
@@ -382,20 +481,46 @@
 
     first, saved_first = layer_forward(stream, allowed, vectors[0], weights[0])
     second, saved_second = layer_forward(first.astype(f32), allowed, vectors[1], weights[1])
-    middle_grad, feed_one, attention_one, early_one, late_one = layer_backward(
-        cotangent_rows, allowed, vectors[1], weights[1], saved_second
+    waiting = {}
+
+    def keep(step, value, group=None):
+        if group is not None:
+            waiting[step] = group
+        return value
+
+    middle_grad, early_one, late_one = layer_backward(
+        cotangent_rows, allowed, vectors[1], weights[1], saved_second, keep
     )
     middle_low = middle_grad.astype(bf16)
-    feed_owned = to_owner(feed_one, 1, here)
-    attention_owned = to_owner(attention_one, 1, here)
-    last_grad, feed_zero, attention_zero, early_zero, late_zero = layer_backward(
-        middle_low.astype(f32), allowed, vectors[0], weights[0], saved_first
+    groups_one = (waiting[1], waiting[4])
+    kept = {}
+
+    def reduce_along(step, value, group=None):
+        if step == 0:
+            halved = [over_cores(item, core) for item in groups_one]
+            kept["one"] = jnp.concatenate(halved, axis=2)
+            return held(value, kept["one"])
+        if step == 1:
+            kept["one"] = over_y(kept["one"])
+            kept["feed"] = over_cores(group, core)
+            return held(value, kept["one"])
+        if step == 2:
+            kept["one"] = over_z(kept["one"], 1, pipe, high)
+            return held(value, kept["one"], kept["feed"])
+        if step == 3:
+            kept["feed"] = over_y(kept["feed"])
+            return held(value, kept["feed"])
+        kept["feed"] = over_z(kept["feed"], 0, pipe, high)
+        kept["attention"] = over_cores(group, core)
+        return held(value, kept["feed"], kept["attention"])
+
+    last_grad, early_zero, late_zero = layer_backward(
+        middle_low.astype(f32), allowed, vectors[0], weights[0], saved_first, reduce_along
     )
     last_low = last_grad.astype(bf16)
-    feed_owned = jnp.where(pipe == 1, feed_owned, to_owner(feed_zero, 0, here))
-    attention_owned = jnp.where(pipe == 1, attention_owned, to_owner(attention_zero, 0, here))
-    feed_total = over_y(feed_owned)
-    attention_total = over_y(attention_owned)
+    feed_total = back_over_y(jnp.where(pipe == 1, kept["one"][:128], kept["feed"]))
+    attention_owned = over_z(over_y(kept["attention"]), 0, pipe, high)
+    attention_total = back_over_y(jnp.where(pipe == 1, kept["one"][128:], attention_owned))
 
     def bias_rows(fc_bias_grad):
         return place(jnp.zeros((4, WIDTH), f32), fc_bias_grad[None], (x, 0))
@@ -407,14 +532,14 @@
         wide = place(jnp.zeros((2, WIDTH), f32), pairs, (0, x * 256))
         return jnp.concatenate([gain_grad[None], shift_grad[None], wide])
 
-    early = jnp.stack(
+    small = jnp.stack(
         [
-            jnp.concatenate([jnp.stack(item[:4]), bias_rows(item[4])])
-            for item in (early_zero, early_one)
+            jnp.concatenate([jnp.stack(early[:4]), bias_rows(early[4]), late_rows(late)])
+            for early, late in ((early_zero, late_zero), (early_one, late_one))
         ]
     )
-    early = pick(lax.psum(early, AXES), pipe)
-    late = pick(everywhere(jnp.stack([late_rows(late_zero), late_rows(late_one)])), pipe)
+    small = everywhere(small, pipe)
+    early, late = small[:8], small[8:]
 
     w_fc_grad = feed_total[:, :256].reshape(512, WIDTH).T
     w_proj_grad = feed_total[:, 256:].reshape(512, WIDTH)

time: 746 us -> 546 us (0.73)
  waiting for transfers between devices: 355 us -> 210 us
  local copies, waits for them, and re-layouts: 87.8 us -> 58.6 us
  matrix products: 63.3 us -> 47.1 us
  between operations: 17.7 us -> 3.56 us
    psum x1 -> x0, waiting for transfers between devices: 132 us -> none  [on_device(): early = pick(lax.psum(early, AXES), pipe)]
    dynamic_update_slice x44 -> x12, local copies, waits for them, and re-layouts: 33.6 us -> 1.79 us  [place(): return lax.dynamic_update_slice(buffer, piece, starts)]
    ppermute x111, waiting for transfers between devices: 223 us -> 210 us  [move(): return lax.ppermute(array, axes, sorted(pairs.items()))]
    dot_general x24, matrix products: 44.7 us -> 33.3 us  [dot(): lax.dot_general(left, right, (((left_dim,), (right_dim,)), ((), ())), pre...]
    unnamed x221 -> x247, local copies, waits for them, and re-layouts: 19.3 us -> 22.4 us
  transfers between devices with their start and end apart: 112 -> 111, of which waited for: 41 -> 55; matrix products, arithmetic and copies ran while one was open for 23% -> 20% of each run, Pallas kernels for 0% -> 1%
where the time goes in v2:
time: 546 us; the launch traced here: 538 us
  waiting for transfers between devices  210 us (38%)
  starting transfers between devices  161 us (29%)
  local copies, waits for them, and re-layouts  58.6 us (11%)
  other arithmetic  49.4 us (9%)
  matrix products  47.1 us (9%)
  Pallas kernels  7.44 us (1%)
    ppermute x111, waiting for transfers between devices, move(): return lax.ppermute(array, axes, sorted(pairs.items()))  210 us
    ppermute x111, starting transfers between devices, move(): return lax.ppermute(array, axes, sorted(pairs.items()))  161 us
    dot_general x24, matrix products, dot(): lax.dot_general(left, right, (((left_dim,), (right_dim,)), ((), ())), pre...  33.3 us
    unnamed x247, local copies, waits for them, and re-layouts  22.4 us
  transfers between devices with their start and end apart: 111, of which 55 were waited for; matrix products, arithmetic and copies ran while one was open for 20% of the time, Pallas kernels for 1%

profile of v2, /device:TPU:1, one launch (start us, length us, event | category | flops | bytes accessed | tf_op | source)
XLA Modules:
  0.0 537.5 jit_solution(13797115998101715348)
XLA Ops:
  11.9 4.7 collective-permute-start
  21.1 8.3 %collective-permute-done.3.refs_4_ = bf16[544,384]{1,0:T(8,128)(2,1)} collective-permute-done((bf16[544,384]{1,0:T(8,128)(2,1)}, bf16[544,384]{1,0:T(8,128)(2,1)}, u32[]{:S(2)}, u32[]{:S(2)}) %collective-permute-start.3) | collective-permute-done | bytes 417824 | tf_op jit(solution)/shard_map/ppermute | solution.py:38
  35.4 2.8 collective-permute-start.11
  39.7 13.8 %collective-permute-done.10.refs_2_ = bf16[320,1024]{1,0:T(8,128)(2,1)S(1)} collective-permute-done((bf16[320,1024]{1,0:T(8,128)(2,1)}, bf16[320,1024]{1,0:T(8,128)(2,1)S(1)}, u32[]{:S(2)}, u32[]{:S(2)}) %collective-permute-start.10) | collective-permute-done | bytes 655392 | tf_op jit(solution)/shard_map/ppermute | solution.py:38
  53.5 13.1 %collective-permute-done.11.refs_3_ = bf16[320,1024]{1,0:T(8,128)(2,1)S(1)} collective-permute-done((bf16[320,1024]{1,0:T(8,128)(2,1)}, bf16[320,1024]{1,0:T(8,128)(2,1)S(1)}, u32[]{:S(2)}, u32[]{:S(2)}) %collective-permute-start.11) | collective-permute-done | bytes 655392 | tf_op jit(solution)/shard_map/ppermute | solution.py:38
  84.4 6.2 %collective-permute-done.5 = bf16[96,1024]{1,0:T(8,128)(2,1)} collective-permute-done((bf16[96,1024]{1,0:T(8,128)(2,1)S(1)}, bf16[96,1024]{1,0:T(8,128)(2,1)}, u32[]{:S(2)}, u32[]{:S(2)}) %collective-permute-start.5) | collective-permute-done | bytes 196640 | tf_op jit(solution)/shard_map/ppermute | solution.py:38
  90.7 3.3 fusion.98
  116.5 3.0 collective-permute-start.15
  121.0 3.6 collective-permute-done.16
  124.6 3.9 collective-permute-done.15
  138.7 5.8 %collective-permute-done.19 = bf16[96,1024]{1,0:T(8,128)(2,1)S(1)} collective-permute-done((bf16[96,1024]{1,0:T(8,128)(2,1)S(1)}, bf16[96,1024]{1,0:T(8,128)(2,1)S(1)}, u32[]{:S(2)}, u32[]{:S(2)}) %collective-permute-start.19) | collective-permute-done | bytes 196640 | tf_op jit(solution)/shard_map/ppermute | solution.py:38
  147.2 4.4 collective-permute-start.25
  154.5 5.1 collective-permute-done.25
  160.3 3.5 collective-permute-start.29
  171.2 4.7 collective-permute-done.27
  194.1 9.2 %collective-permute-done.33 = bf16[96,1024]{1,0:T(8,128)(2,1)S(1)} collective-permute-done((bf16[96,1024]{1,0:T(8,128)(2,1)S(1)}, bf16[96,1024]{1,0:T(8,128)(2,1)S(1)}, u32[]{:S(2)}, u32[]{:S(2)}) %collective-permute-start.33) | collective-permute-done | bytes 196640 | tf_op jit(solution)/shard_map/ppermute | solution.py:38
  207.6 3.8 collective-permute-done.36
  213.7 5.4 %collective-permute-done.34 = bf16[96,1024]{1,0:T(8,128)(2,1)S(1)} collective-permute-done((bf16[96,1024]{1,0:T(8,128)(2,1)S(1)}, bf16[96,1024]{1,0:T(8,128)(2,1)S(1)}, u32[]{:S(2)}, u32[]{:S(2)}) %collective-permute-start.34) | collective-permute-done | bytes 196640 | tf_op jit(solution)/shard_map/ppermute | solution.py:38
  229.6 2.8 collective-permute-start.48
  239.4 7.9 %collective-permute-done.48 = bf16[96,1024]{1,0:T(8,128)(2,1)S(1)} collective-permute-done((bf16[96,1024]{1,0:T(8,128)(2,1)}, bf16[96,1024]{1,0:T(8,128)(2,1)S(1)}, u32[]{:S(2)}, u32[]{:S(2)}) %collective-permute-start.48) | collective-permute-done | bytes 196640 | tf_op jit(solution)/shard_map/ppermute | solution.py:38
  252.2 3.4 collective-permute-start.50
  260.7 4.5 collective-permute-done.49
  279.6 3.4 collective-permute-done.55
  283.0 3.2 collective-permute-done.54
  288.6 3.4 collective-permute-start.58
  296.8 7.9 %collective-permute-start.40 = (bf16[96,1024]{1,0:T(8,128)(2,1)S(1)}, bf16[96,1024]{1,0:T(8,128)(2,1)S(1)}, u32[]{:S(2)}, u32[]{:S(2)}) collective-permute-start(bf16[96,1024]{1,0:T(8,128)(2,1)S(1)} %get-tuple-element.99), channel_id=1, source_target_pairs={{0,0},{1,8},{2,2},{3,10},{4,4},{5,12},{6,6},{7,14},{8,1},{9,9},{10... | collective-permute-start | bytes 589832 | tf_op jit(solution)/shard_map/ppermute | solution.py:38
  319.0 4.7 collective-permute-start.62
  329.0 3.6 collective-permute-done.61
  332.8 17.0 %collective-permute-done.66 = bf16[2,192,1024]{2,1,0:T(8,128)(2,1)S(1)} collective-permute-done((bf16[2,192,1024]{2,1,0:T(8,128)(2,1)S(1)}, bf16[2,192,1024]{2,1,0:T(8,128)(2,1)S(1)}, u32[]{:S(2)}, u32[]{:S(2)}) %collective-permute-start.66) | collective-permute-done | bytes 786464 | tf_op jit(solution)/shard_map/ppermute | solution.py:38
  349.7 4.7 collective-permute-done.64
  358.3 3.4 collective-permute-start.69
  370.4 5.5 %collective-permute-start.71 = (bf16[192,1024]{1,0:T(8,128)(2,1)S(1)}, bf16[192,1024]{1,0:T(8,128)(2,1)S(1)}, u32[]{:S(2)}, u32[]{:S(2)}) collective-permute-start(bf16[192,1024]{1,0:T(8,128)(2,1)S(1)} %get-tuple-element.124), channel_id=1, source_target_pairs={{0,72},{8,64},{16,88},{24,80},{32,104},{40,96},{48,120},{56,112},{... | collective-permute-start | bytes 1179656 | tf_op jit(solution)/shard_map/ppermute | solution.py:38
  379.0 2.8 fusion
  381.8 8.1 %collective-permute-done.71 = bf16[192,1024]{1,0:T(8,128)(2,1)S(1)} collective-permute-done((bf16[192,1024]{1,0:T(8,128)(2,1)S(1)}, bf16[192,1024]{1,0:T(8,128)(2,1)S(1)}, u32[]{:S(2)}, u32[]{:S(2)}) %collective-permute-start.71) | collective-permute-done | bytes 393248 | tf_op jit(solution)/shard_map/ppermute | solution.py:38
  399.0 11.0 %collective-permute-done.77 = bf16[2,128,1024]{2,1,0:T(8,128)(2,1)S(1)} collective-permute-done((bf16[2,128,1024]{2,1,0:T(8,128)(2,1)S(1)}, bf16[2,128,1024]{2,1,0:T(8,128)(2,1)S(1)}, u32[]{:S(2)}, u32[]{:S(2)}) %collective-permute-start.77) | collective-permute-done | bytes 524320 | tf_op jit(solution)/shard_map/ppermute | solution.py:38
  411.6 11.5 %collective-permute-done.75 = bf16[2,128,1024]{2,1,0:T(8,128)(2,1)S(1)} collective-permute-done((bf16[2,128,1024]{2,1,0:T(8,128)(2,1)S(1)}, bf16[2,128,1024]{2,1,0:T(8,128)(2,1)S(1)}, u32[]{:S(2)}, u32[]{:S(2)}) %collective-permute-start.75) | collective-permute-done | bytes 524320 | tf_op jit(solution)/shard_map/ppermute | solution.py:38
  423.6 4.2 collective-permute-start.83
  447.0 5.7 %collective-permute-done.107 = bf16[128,1024]{1,0:T(8,128)(2,1)S(1)} collective-permute-done((bf16[128,1024]{1,0:T(8,128)(2,1)S(1)}, bf16[128,1024]{1,0:T(8,128)(2,1)S(1)}, u32[]{:S(2)}, u32[]{:S(2)}) %collective-permute-start.107) | collective-permute-done | bytes 262176 | tf_op jit(solution)/shard_map/ppermute | solution.py:38
  453.3 3.6 collective-permute-done.109
  461.0 2.8 concatenate.156
  464.7 3.8 collective-permute-start.88
  481.1 3.8 collective-permute-start.86
  490.1 3.6 collective-permute-done.85
  499.6 3.7 collective-permute-start.94
  508.1 4.0 collective-permute-done.102
  519.9 3.4 collective-permute-done.104
  524.1 4.7 collective-permute-start.106
  531.3 2.9 copy.55
  (646 shorter events, 274.4 us)
Async XLA Ops:
  5.3 15.7 %collective-permute-start.1 = (bf16[544,384]{1,0:T(8,128)(2,1)}, bf16[544,384]{1,0:T(8,128)(2,1)}, u32[]{:S(2)}, u32[]{:S(2)}) collective-permute-start(bf16[544,384]{1,0:T(8,128)(2,1)} %pad_maximum_fusion.18), channel_id=1, source_target_pairs={{0,64},{8,72},{16,80},{24,88},{32,96},{40,104},{48,112},{56,120},{... | collective-permute-start | bytes 1253384 | tf_op jit(solution)/shard_map/ppermute | solution.py:38
  7.8 13.3 %collective-permute-start.2 = (bf16[544,384]{1,0:T(8,128)(2,1)}, bf16[544,384]{1,0:T(8,128)(2,1)}, u32[]{:S(2)}, u32[]{:S(2)}) collective-permute-start(bf16[544,384]{1,0:T(8,128)(2,1)} %pad_maximum_fusion.18), channel_id=1, source_target_pairs={{0,72},{8,64},{16,88},{24,80},{32,104},{40,96},{48,120},{56,112},{... | collective-permute-start | bytes 1253384 | tf_op jit(solution)/shard_map/ppermute | solution.py:38
  9.9 19.5 %collective-permute-start.3 = (bf16[544,384]{1,0:T(8,128)(2,1)}, bf16[544,384]{1,0:T(8,128)(2,1)}, u32[]{:S(2)}, u32[]{:S(2)}) collective-permute-start(bf16[544,384]{1,0:T(8,128)(2,1)} %pad_maximum_fusion.18), channel_id=1, source_target_pairs={{0,8},{8,0},{16,24},{24,16},{32,40},{40,32},{48,56},{56,48},{64,72... | collective-permute-start | bytes 1253384 | tf_op jit(solution)/shard_map/ppermute | solution.py:38
  11.9 27.4 %collective-permute-start = (bf16[96,1024]{1,0:T(8,128)(2,1)}, bf16[96,1024]{1,0:T(8,128)(2,1)S(1)}, u32[]{:S(2)}, u32[]{:S(2)}) collective-permute-start(bf16[96,1024]{1,0:T(8,128)(2,1)} %dynamic-slice_bitcast_fusion.14), channel_id=1, source_target_pairs={{0,0},{1,8},{2,2},{3,10},{4,4},{5,12},{6,6},{7,14},{8,1},{9,9},{10... | collective-permute-start | bytes 589832 | tf_op jit(solution)/shard_map/ppermute | solution.py:38
  16.7 17.3 %collective-permute-start.9 = (s32[8,96]{1,0:T(8,128)S(1)}, s32[8,96]{1,0:T(8,128)S(1)}, u32[]{:S(2)}, u32[]{:S(2)}) collective-permute-start(s32[8,96]{1,0:T(8,128)S(1)} %reshape.652), channel_id=1, source_target_pairs={{0,1},{1,0},{2,3},{3,2},{4,5},{5,4},{6,7},{7,6},{8,9},{9,8},{10,11... | collective-permute-start | bytes 9224 | tf_op jit(solution)/shard_map/ppermute | solution.py:38
  31.9 39.3 %collective-permute-start.4 = (bf16[3,544,384]{2,1,0:T(8,128)(2,1)}, bf16[3,544,384]{2,1,0:T(8,128)(2,1)}, u32[]{:S(2)}, u32[]{:S(2)}) collective-permute-start(bf16[3,544,384]{2,1,0:T(8,128)(2,1)} %pad_maximum_fusion.3), channel_id=1, source_target_pairs={{0,1},{1,0},{2,3},{3,2},{4,5},{5,4},{6,7},{7,6},{8,9},{9,8},{10,11... | collective-permute-start | bytes 3760136 | tf_op jit(solution)/shard_map/ppermute | solution.py:38
  34.8 18.7 %collective-permute-start.10 = (bf16[320,1024]{1,0:T(8,128)(2,1)}, bf16[320,1024]{1,0:T(8,128)(2,1)S(1)}, u32[]{:S(2)}, u32[]{:S(2)}) collective-permute-start(bf16[320,1024]{1,0:T(8,128)(2,1)} %pad_maximum_fusion.15), channel_id=1, source_target_pairs={{0,64},{8,72},{16,80},{24,88},{32,96},{40,104},{48,112},{56,120},{... | collective-permute-start | bytes 1966088 | tf_op jit(solution)/shard_map/ppermute | solution.py:38
  35.4 31.2 %collective-permute-start.11 = (bf16[320,1024]{1,0:T(8,128)(2,1)}, bf16[320,1024]{1,0:T(8,128)(2,1)S(1)}, u32[]{:S(2)}, u32[]{:S(2)}) collective-permute-start(bf16[320,1024]{1,0:T(8,128)(2,1)} %pad_maximum_fusion.15), channel_id=1, source_target_pairs={{0,72},{8,64},{16,88},{24,80},{32,104},{40,96},{48,120},{56,112},{... | collective-permute-start | bytes 1966088 | tf_op jit(solution)/shard_map/ppermute | solution.py:38
  38.2 30.3 %collective-permute-start.12 = (bf16[320,1024]{1,0:T(8,128)(2,1)}, bf16[320,1024]{1,0:T(8,128)(2,1)S(1)}, u32[]{:S(2)}, u32[]{:S(2)}) collective-permute-start(bf16[320,1024]{1,0:T(8,128)(2,1)} %pad_maximum_fusion.15), channel_id=1, source_target_pairs={{0,8},{8,0},{16,24},{24,16},{32,40},{40,32},{48,56},{56,48},{64,72... | collective-permute-start | bytes 1966088 | tf_op jit(solution)/shard_map/ppermute | solution.py:38
  68.5 30.3 %collective-permute-start.20 = (bf16[256,1024]{1,0:T(8,128)(2,1)}, bf16[256,1024]{1,0:T(8,128)(2,1)}, u32[]{:S(2)}, u32[]{:S(2)}) collective-permute-start(bf16[256,1024]{1,0:T(8,128)(2,1)} %dynamic-slice_bitcast_fusion.3), channel_id=1, source_target_pairs={{0,64},{8,72},{16,80},{24,88},{32,96},{40,104},{48,112},{56,120},{... | collective-permute-start | bytes 1572872 | tf_op jit(solution)/shard_map/ppermute | solution.py:38
  69.0 32.1 %collective-permute-start.21 = (bf16[256,1024]{1,0:T(8,128)(2,1)}, bf16[256,1024]{1,0:T(8,128)(2,1)}, u32[]{:S(2)}, u32[]{:S(2)}) collective-permute-start(bf16[256,1024]{1,0:T(8,128)(2,1)} %dynamic-slice_bitcast_fusion.3), channel_id=1, source_target_pairs={{0,72},{8,64},{16,88},{24,80},{32,104},{40,96},{48,120},{56,112},{... | collective-permute-start | bytes 1572872 | tf_op jit(solution)/shard_map/ppermute | solution.py:38
  82.6 18.5 %collective-permute-start.22 = (bf16[256,1024]{1,0:T(8,128)(2,1)}, bf16[256,1024]{1,0:T(8,128)(2,1)S(1)}, u32[]{:S(2)}, u32[]{:S(2)}) collective-permute-start(bf16[256,1024]{1,0:T(8,128)(2,1)} %dynamic-slice_bitcast_fusion.3), channel_id=1, source_target_pairs={{0,8},{8,0},{16,24},{24,16},{32,40},{40,32},{48,56},{56,48},{64,72... | collective-permute-start | bytes 1572872 | tf_op jit(solution)/shard_map/ppermute | solution.py:38
  98.7 20.8 %collective-permute-start.42 = (bf16[96,1024]{1,0:T(8,128)(2,1)}, bf16[96,1024]{1,0:T(8,128)(2,1)}, u32[]{:S(2)}, u32[]{:S(2)}) collective-permute-start(bf16[96,1024]{1,0:T(8,128)(2,1)} %dynamic-slice_bitcast_fusion.13), channel_id=1, source_target_pairs={{0,0},{1,8},{2,2},{3,10},{4,4},{5,12},{6,6},{7,14},{8,1},{9,9},{10... | collective-permute-start | bytes 589832 | tf_op jit(solution)/shard_map/ppermute | solution.py:38
  103.9 29.8 %collective-permute-start.23 = (bf16[3,256,1024]{2,1,0:T(8,128)(2,1)}, bf16[3,256,1024]{2,1,0:T(8,128)(2,1)}, u32[]{:S(2)}, u32[]{:S(2)}) collective-permute-start(bf16[3,256,1024]{2,1,0:T(8,128)(2,1)} %pad_maximum_fusion.2), channel_id=1, source_target_pairs={{0,1},{1,0},{2,3},{3,2},{4,5},{5,4},{6,7},{7,6},{8,9},{9,8},{10,11... | collective-permute-start | bytes 4718600 | tf_op jit(solution)/shard_map/ppermute | solution.py:38
  119.6 45.9 %collective-permute-start.43 = (bf16[96,1024]{1,0:T(8,128)(2,1)}, bf16[96,1024]{1,0:T(8,128)(2,1)S(1)}, u32[]{:S(2)}, u32[]{:S(2)}) collective-permute-start(bf16[96,1024]{1,0:T(8,128)(2,1)} %collective-permute-done.42), channel_id=1, source_target_pairs={{0,16},{8,24},{16,32},{24,40},{32,48},{40,56},{48,0},{56,8},{1,17}... | collective-permute-start | bytes 589832 | tf_op jit(solution)/shard_map/ppermute | solution.py:38
  129.6 14.9 %collective-permute-start.19 = (bf16[96,1024]{1,0:T(8,128)(2,1)S(1)}, bf16[96,1024]{1,0:T(8,128)(2,1)S(1)}, u32[]{:S(2)}, u32[]{:S(2)}) collective-permute-start(bf16[96,1024]{1,0:T(8,128)(2,1)S(1)} %add_convert_fusion.5), channel_id=1, source_target_pairs={{0,48},{8,56},{16,0},{24,8},{32,16},{40,24},{48,32},{56,40},{1,49}... | collective-permute-start | bytes 589832 | tf_op jit(solution)/shard_map/ppermute | solution.py:38
  132.3 12.5 %collective-permute-start.17 = (bf16[96,1024]{1,0:T(8,128)(2,1)S(1)}, bf16[96,1024]{1,0:T(8,128)(2,1)S(1)}, u32[]{:S(2)}, u32[]{:S(2)}) collective-permute-start(bf16[96,1024]{1,0:T(8,128)(2,1)S(1)} %add_convert_fusion.5), channel_id=1, source_target_pairs={{0,16},{8,24},{16,32},{24,40},{32,48},{40,56},{48,0},{56,8},{1,17}... | collective-permute-start | bytes 589832 | tf_op jit(solution)/shard_map/ppermute | solution.py:38
  133.7 47.3 %collective-permute-start.44 = (bf16[96,1024]{1,0:T(8,128)(2,1)}, bf16[96,1024]{1,0:T(8,128)(2,1)}, u32[]{:S(2)}, u32[]{:S(2)}) collective-permute-start(bf16[96,1024]{1,0:T(8,128)(2,1)} %collective-permute-done.42), channel_id=1, source_target_pairs={{0,32},{8,40},{16,48},{24,56},{32,0},{40,8},{48,16},{56,24},{1,33}... | collective-permute-start | bytes 589832 | tf_op jit(solution)/shard_map/ppermute | solution.py:38
  147.2 12.4 %collective-permute-start.25 = (bf16[96,1024]{1,0:T(8,128)(2,1)S(1)}, bf16[96,1024]{1,0:T(8,128)(2,1)S(1)}, u32[]{:S(2)}, u32[]{:S(2)}) collective-permute-start(bf16[96,1024]{1,0:T(8,128)(2,1)S(1)} %get-tuple-element.144), channel_id=1, source_target_pairs={{0,32},{8,40},{16,48},{24,56},{32,0},{40,8},{48,16},{56,24},{1,33}... | collective-permute-start | bytes 589832 | tf_op jit(solution)/shard_map/ppermute | solution.py:38
  165.5 17.2 %collective-permute-start.45 = (bf16[96,1024]{1,0:T(8,128)(2,1)}, bf16[96,1024]{1,0:T(8,128)(2,1)}, u32[]{:S(2)}, u32[]{:S(2)}) collective-permute-start(bf16[96,1024]{1,0:T(8,128)(2,1)} %collective-permute-done.42), channel_id=1, source_target_pairs={{0,48},{8,56},{16,0},{24,8},{32,16},{40,24},{48,32},{56,40},{1,49}... | collective-permute-start | bytes 589832 | tf_op jit(solution)/shard_map/ppermute | solution.py:38
  227.1 25.1 %collective-permute-start.39 = (bf16[96,1024]{1,0:T(8,128)(2,1)S(1)}, bf16[96,1024]{1,0:T(8,128)(2,1)}, u32[]{:S(2)}, u32[]{:S(2)}) collective-permute-start(bf16[96,1024]{1,0:T(8,128)(2,1)S(1)} %get-tuple-element.135), channel_id=1, source_target_pairs={{0,16},{8,24},{16,32},{24,40},{32,48},{40,56},{48,0},{56,8},{1,17}... | collective-permute-start | bytes 589832 | tf_op jit(solution)/shard_map/ppermute | solution.py:38
  227.2 28.4 %collective-permute-start.38 = (bf16[96,1024]{1,0:T(8,128)(2,1)S(1)}, bf16[96,1024]{1,0:T(8,128)(2,1)}, u32[]{:S(2)}, u32[]{:S(2)}) collective-permute-start(bf16[96,1024]{1,0:T(8,128)(2,1)S(1)} %get-tuple-element.136), channel_id=1, source_target_pairs={{0,32},{8,40},{16,48},{24,56},{32,0},{40,8},{48,16},{56,24},{1,33}... | collective-permute-start | bytes 589832 | tf_op jit(solution)/shard_map/ppermute | solution.py:38
  229.6 17.7 %collective-permute-start.48 = (bf16[96,1024]{1,0:T(8,128)(2,1)}, bf16[96,1024]{1,0:T(8,128)(2,1)S(1)}, u32[]{:S(2)}, u32[]{:S(2)}) collective-permute-start(bf16[96,1024]{1,0:T(8,128)(2,1)} %get-tuple-element.132), channel_id=1, source_target_pairs={{0,16},{8,24},{16,32},{24,40},{32,48},{40,56},{48,0},{56,8},{1,17}... | collective-permute-start | bytes 589832 | tf_op jit(solution)/shard_map/ppermute | solution.py:38
  232.4 14.9 %collective-permute-start.47 = (bf16[96,1024]{1,0:T(8,128)(2,1)}, bf16[96,1024]{1,0:T(8,128)(2,1)}, u32[]{:S(2)}, u32[]{:S(2)}) collective-permute-start(bf16[96,1024]{1,0:T(8,128)(2,1)} %get-tuple-element.133), channel_id=1, source_target_pairs={{0,32},{8,40},{16,48},{24,56},{32,0},{40,8},{48,16},{56,24},{1,33}... | collective-permute-start | bytes 589832 | tf_op jit(solution)/shard_map/ppermute | solution.py:38
  233.0 15.5 %collective-permute-start.46 = (bf16[96,1024]{1,0:T(8,128)(2,1)}, bf16[96,1024]{1,0:T(8,128)(2,1)}, u32[]{:S(2)}, u32[]{:S(2)}) collective-permute-start(bf16[96,1024]{1,0:T(8,128)(2,1)} %get-tuple-element.131), channel_id=1, source_target_pairs={{0,48},{8,56},{16,0},{24,8},{32,16},{40,24},{48,32},{56,40},{1,49}... | collective-permute-start | bytes 589832 | tf_op jit(solution)/shard_map/ppermute | solution.py:38
  247.3 63.3 %collective-permute-start.59 = (bf16[2,512,1024]{2,1,0:T(8,128)(2,1)S(1)}, bf16[2,512,1024]{2,1,0:T(8,128)(2,1)S(1)}, u32[]{:S(2)}, u32[]{:S(2)}) collective-permute-start(bf16[2,512,1024]{2,1,0:T(8,128)(2,1)S(1)} %fusion.19), channel_id=1, source_target_pairs={{0,1},{1,0},{2,3},{3,2},{4,5},{5,4},{6,7},{7,6},{8,9},{9,8},{10,11... | collective-permute-start | bytes 6291464 | tf_op jit(solution)/shard_map/ppermute | solution.py:38
  270.9 46.0 %collective-permute-start.41 = (bf16[96,1024]{1,0:T(8,128)(2,1)S(1)}, bf16[96,1024]{1,0:T(8,128)(2,1)S(1)}, u32[]{:S(2)}, u32[]{:S(2)}) collective-permute-start(bf16[96,1024]{1,0:T(8,128)(2,1)S(1)} %broadcast_select_fusion.2), channel_id=1, source_target_pairs={{0,64},{1,72},{2,66},{3,74},{4,68},{5,76},{6,70},{7,78},{8,65},{9,... | collective-permute-start | bytes 589832 | tf_op jit(solution)/shard_map/ppermute | solution.py:38
  292.0 12.7 %collective-permute-start.57 = (bf16[96,1024]{1,0:T(8,128)(2,1)S(1)}, bf16[96,1024]{1,0:T(8,128)(2,1)S(1)}, u32[]{:S(2)}, u32[]{:S(2)}) collective-permute-start(bf16[96,1024]{1,0:T(8,128)(2,1)S(1)} %get-tuple-element.91), channel_id=1, source_target_pairs={{0,32},{8,40},{16,48},{24,56},{32,0},{40,8},{48,16},{56,24},{1,33}... | collective-permute-start | bytes 589832 | tf_op jit(solution)/shard_map/ppermute | solution.py:38
  296.8 22.2 %collective-permute-start.40 = (bf16[96,1024]{1,0:T(8,128)(2,1)S(1)}, bf16[96,1024]{1,0:T(8,128)(2,1)S(1)}, u32[]{:S(2)}, u32[]{:S(2)}) collective-permute-start(bf16[96,1024]{1,0:T(8,128)(2,1)S(1)} %get-tuple-element.99), channel_id=1, source_target_pairs={{0,0},{1,8},{2,2},{3,10},{4,4},{5,12},{6,6},{7,14},{8,1},{9,9},{10... | collective-permute-start | bytes 589832 | tf_op jit(solution)/shard_map/ppermute | solution.py:38
  308.5 16.6 %collective-permute-start.63 = (bf16[96,1024]{1,0:T(8,128)(2,1)S(1)}, bf16[96,1024]{1,0:T(8,128)(2,1)S(1)}, u32[]{:S(2)}, u32[]{:S(2)}) collective-permute-start(bf16[96,1024]{1,0:T(8,128)(2,1)S(1)} %get-tuple-element.126), channel_id=1, source_target_pairs={{0,16},{8,24},{16,32},{24,40},{32,48},{40,56},{48,0},{56,8},{1,17}... | collective-permute-start | bytes 589832 | tf_op jit(solution)/shard_map/ppermute | solution.py:38
  313.8 35.9 %collective-permute-start.66 = (bf16[2,192,1024]{2,1,0:T(8,128)(2,1)S(1)}, bf16[2,192,1024]{2,1,0:T(8,128)(2,1)S(1)}, u32[]{:S(2)}, u32[]{:S(2)}) collective-permute-start(bf16[2,192,1024]{2,1,0:T(8,128)(2,1)S(1)} %get-tuple-element.109), channel_id=1, source_target_pairs={{0,6},{1,7},{2,0},{3,1},{4,2},{5,3},{6,4},{7,5},{8,14},{9,15},{10,... | collective-permute-start | bytes 2359304 | tf_op jit(solution)/shard_map/ppermute | solution.py:38
  316.6 33.1 %collective-permute-start.65 = (bf16[2,192,1024]{2,1,0:T(8,128)(2,1)S(1)}, bf16[2,192,1024]{2,1,0:T(8,128)(2,1)S(1)}, u32[]{:S(2)}, u32[]{:S(2)}) collective-permute-start(bf16[2,192,1024]{2,1,0:T(8,128)(2,1)S(1)} %get-tuple-element.108), channel_id=1, source_target_pairs={{0,4},{1,5},{2,6},{3,7},{4,0},{5,1},{6,2},{7,3},{8,12},{9,13},{10,... | collective-permute-start | bytes 2359304 | tf_op jit(solution)/shard_map/ppermute | solution.py:38
  317.0 37.4 %collective-permute-start.64 = (bf16[2,192,1024]{2,1,0:T(8,128)(2,1)S(1)}, bf16[2,192,1024]{2,1,0:T(8,128)(2,1)S(1)}, u32[]{:S(2)}, u32[]{:S(2)}) collective-permute-start(bf16[2,192,1024]{2,1,0:T(8,128)(2,1)S(1)} %get-tuple-element.107), channel_id=1, source_target_pairs={{0,2},{1,3},{2,4},{3,5},{4,6},{5,7},{6,0},{7,1},{8,10},{9,11},{10,... | collective-permute-start | bytes 2359304 | tf_op jit(solution)/shard_map/ppermute | solution.py:38
  325.1 53.8 %collective-permute-start.73 = (bf16[2,512,1024]{2,1,0:T(8,128)(2,1)}, bf16[2,512,1024]{2,1,0:T(8,128)(2,1)}, u32[]{:S(2)}, u32[]{:S(2)}) collective-permute-start(bf16[2,512,1024]{2,1,0:T(8,128)(2,1)} %fusion.15), channel_id=1, source_target_pairs={{0,1},{1,0},{2,3},{3,2},{4,5},{5,4},{6,7},{7,6},{8,9},{9,8},{10,11... | collective-permute-start | bytes 6291464 | tf_op jit(solution)/shard_map/ppermute | solution.py:38
  361.7 14.3 %collective-permute-start.68 = (bf16[96,1024]{1,0:T(8,128)(2,1)}, bf16[96,1024]{1,0:T(8,128)(2,1)}, u32[]{:S(2)}, u32[]{:S(2)}) collective-permute-start(bf16[96,1024]{1,0:T(8,128)(2,1)} %get-tuple-element.93), channel_id=1, source_target_pairs={{0,32},{8,40},{16,48},{24,56},{32,0},{40,8},{48,16},{56,24},{1,33}... | collective-permute-start | bytes 589832 | tf_op jit(solution)/shard_map/ppermute | solution.py:38
  362.9 14.6 %collective-permute-start.67 = (bf16[96,1024]{1,0:T(8,128)(2,1)}, bf16[96,1024]{1,0:T(8,128)(2,1)}, u32[]{:S(2)}, u32[]{:S(2)}) collective-permute-start(bf16[96,1024]{1,0:T(8,128)(2,1)} %get-tuple-element.93), channel_id=1, source_target_pairs={{0,16},{8,24},{16,32},{24,40},{32,48},{40,56},{48,0},{56,8},{1,17}... | collective-permute-start | bytes 589832 | tf_op jit(solution)/shard_map/ppermute | solution.py:38
  370.4 19.5 %collective-permute-start.71 = (bf16[192,1024]{1,0:T(8,128)(2,1)S(1)}, bf16[192,1024]{1,0:T(8,128)(2,1)S(1)}, u32[]{:S(2)}, u32[]{:S(2)}) collective-permute-start(bf16[192,1024]{1,0:T(8,128)(2,1)S(1)} %get-tuple-element.124), channel_id=1, source_target_pairs={{0,72},{8,64},{16,88},{24,80},{32,104},{40,96},{48,120},{56,112},{... | collective-permute-start | bytes 1179656 | tf_op jit(solution)/shard_map/ppermute | solution.py:38
  376.0 13.9 %collective-permute-start.70 = (bf16[192,1024]{1,0:T(8,128)(2,1)S(1)}, bf16[192,1024]{1,0:T(8,128)(2,1)S(1)}, u32[]{:S(2)}, u32[]{:S(2)}) collective-permute-start(bf16[192,1024]{1,0:T(8,128)(2,1)S(1)} %get-tuple-element.123), channel_id=1, source_target_pairs={{0,64},{8,72},{16,80},{24,88},{32,96},{40,104},{48,112},{56,120},{... | collective-permute-start | bytes 1179656 | tf_op jit(solution)/shard_map/ppermute | solution.py:38
  396.4 13.6 %collective-permute-start.77 = (bf16[2,128,1024]{2,1,0:T(8,128)(2,1)S(1)}, bf16[2,128,1024]{2,1,0:T(8,128)(2,1)S(1)}, u32[]{:S(2)}, u32[]{:S(2)}) collective-permute-start(bf16[2,128,1024]{2,1,0:T(8,128)(2,1)S(1)} %get-tuple-element.113), channel_id=1, source_target_pairs={{0,6},{1,7},{2,0},{3,1},{4,2},{5,3},{6,4},{7,5},{8,14},{9,15},{10,... | collective-permute-start | bytes 1572872 | tf_op jit(solution)/shard_map/ppermute | solution.py:38
  396.4 15.2 %collective-permute-start.76 = (bf16[2,128,1024]{2,1,0:T(8,128)(2,1)S(1)}, bf16[2,128,1024]{2,1,0:T(8,128)(2,1)S(1)}, u32[]{:S(2)}, u32[]{:S(2)}) collective-permute-start(bf16[2,128,1024]{2,1,0:T(8,128)(2,1)S(1)} %get-tuple-element.114), channel_id=1, source_target_pairs={{0,4},{1,5},{2,6},{3,7},{4,0},{5,1},{6,2},{7,3},{8,12},{9,13},{10,... | collective-permute-start | bytes 1572872 | tf_op jit(solution)/shard_map/ppermute | solution.py:38
  396.9 26.3 %collective-permute-start.75 = (bf16[2,128,1024]{2,1,0:T(8,128)(2,1)S(1)}, bf16[2,128,1024]{2,1,0:T(8,128)(2,1)S(1)}, u32[]{:S(2)}, u32[]{:S(2)}) collective-permute-start(bf16[2,128,1024]{2,1,0:T(8,128)(2,1)S(1)} %get-tuple-element.112), channel_id=1, source_target_pairs={{0,2},{1,3},{2,4},{3,5},{4,6},{5,7},{6,0},{7,1},{8,10},{9,11},{10,... | collective-permute-start | bytes 1572872 | tf_op jit(solution)/shard_map/ppermute | solution.py:38
  423.6 15.9 %collective-permute-start.83 = (bf16[128,1024]{1,0:T(8,128)(2,1)S(1)}, bf16[128,1024]{1,0:T(8,128)(2,1)S(1)}, u32[]{:S(2)}, u32[]{:S(2)}) collective-permute-start(bf16[128,1024]{1,0:T(8,128)(2,1)S(1)} %get-tuple-element.157), channel_id=1, source_target_pairs={{0,8},{8,0},{16,24},{24,16},{32,40},{40,32},{48,56},{56,48},{1,9},... | collective-permute-start | bytes 786440 | tf_op jit(solution)/shard_map/ppermute | solution.py:38
  427.7 13.2 %collective-permute-start.82 = (bf16[128,1024]{1,0:T(8,128)(2,1)S(1)}, bf16[128,1024]{1,0:T(8,128)(2,1)S(1)}, u32[]{:S(2)}, u32[]{:S(2)}) collective-permute-start(bf16[128,1024]{1,0:T(8,128)(2,1)S(1)} %get-tuple-element.157), channel_id=1, source_target_pairs={{64,8},{72,0},{80,24},{88,16},{96,40},{104,32},{112,56},{120,48},{... | collective-permute-start | bytes 786440 | tf_op jit(solution)/shard_map/ppermute | solution.py:38
  431.5 12.7 %collective-permute-start.79 = (bf16[96,1024]{1,0:T(8,128)(2,1)}, bf16[96,1024]{1,0:T(8,128)(2,1)}, u32[]{:S(2)}, u32[]{:S(2)}) collective-permute-start(bf16[96,1024]{1,0:T(8,128)(2,1)} %get-tuple-element.122), channel_id=1, source_target_pairs={{0,32},{8,40},{16,48},{24,56},{32,0},{40,8},{48,16},{56,24},{1,33}... | collective-permute-start | bytes 589832 | tf_op jit(solution)/shard_map/ppermute | solution.py:38
  440.9 17.0 %collective-permute-start.84 = (bf16[2,256,1024]{2,1,0:T(8,128)(2,1)}, bf16[2,256,1024]{2,1,0:T(8,128)(2,1)S(1)}, u32[]{:S(2)}, u32[]{:S(2)}) collective-permute-start(bf16[2,256,1024]{2,1,0:T(8,128)(2,1)} %fusion.106), channel_id=1, source_target_pairs={{0,1},{1,0},{2,3},{3,2},{4,5},{5,4},{6,7},{7,6},{8,9},{9,8},{10,11... | collective-permute-start | bytes 3145736 | tf_op jit(solution)/shard_map/ppermute | solution.py:38
  486.9 12.7 %collective-permute-start.99 = (bf16[2,64,1024]{2,1,0:T(8,128)(2,1)S(1)}, bf16[2,64,1024]{2,1,0:T(8,128)(2,1)S(1)}, u32[]{:S(2)}, u32[]{:S(2)}) collective-permute-start(bf16[2,64,1024]{2,1,0:T(8,128)(2,1)S(1)} %get-tuple-element.116), channel_id=1, source_target_pairs={{0,6},{1,7},{2,0},{3,1},{4,2},{5,3},{6,4},{7,5},{8,14},{9,15},{10,... | collective-permute-start | bytes 786440 | tf_op jit(solution)/shard_map/ppermute | solution.py:38
  489.3 14.0 %collective-permute-start.97 = (bf16[2,64,1024]{2,1,0:T(8,128)(2,1)S(1)}, bf16[2,64,1024]{2,1,0:T(8,128)(2,1)S(1)}, u32[]{:S(2)}, u32[]{:S(2)}) collective-permute-start(bf16[2,64,1024]{2,1,0:T(8,128)(2,1)S(1)} %get-tuple-element.115), channel_id=1, source_target_pairs={{0,2},{1,3},{2,4},{3,5},{4,6},{5,7},{6,0},{7,1},{8,10},{9,11},{10,... | collective-permute-start | bytes 786440 | tf_op jit(solution)/shard_map/ppermute | solution.py:38
  490.0 38.7 %collective-permute-start.110 = (bf16[512,1024]{1,0:T(8,128)(2,1)S(1)}, bf16[512,1024]{1,0:T(8,128)(2,1)S(1)}, u32[]{:S(2)}, u32[]{:S(2)}) collective-permute-start(bf16[512,1024]{1,0:T(8,128)(2,1)S(1)} %bitcast.421), channel_id=1, source_target_pairs={{0,1},{1,0},{2,3},{3,2},{4,5},{5,4},{6,7},{7,6},{8,9},{9,8},{10,11... | collective-permute-start | bytes 3145736 | tf_op jit(solution)/shard_map/ppermute | solution.py:38
  (177 other events, 1773.3 us)

commit v3 on v2

--- a/solution.py
+++ b/solution.py
@@ -145,12 +145,12 @@
     return tuple(view[:, :, part].reshape(4 * BLOCK, 4, HEAD_DIM) for part in range(3))
 
 
-def layer_forward(stream, allowed, vectors, weights):
+def layer_forward(stream, allowed, vectors, w_qkv, w_out, w_fc_after, w_proj_after):
     gain_one, shift_one, out_bias, gain_two, shift_two, proj_bias, qkv_bias, fc_bias = vectors
-    w_qkv, w_out, w_fc, w_proj = weights
     normed_one, standard_one, inverse_one = norm_forward(stream, gain_one, shift_one)
     rows_one = gather_rows(normed_one)
     projected = (dot(rows_one, w_qkv, 1, 0) + qkv_bias).astype(bf16)
+    w_fc = w_fc_after(projected)
     query, key, value = split_heads(projected)
     both = jnp.stack([key, value]).reshape(2, 4 * BLOCK, 256)
     keys, values = (
@@ -159,7 +159,8 @@
     )
     context, log_total = attend_forward(query, keys, values, allowed)
     context = context.reshape(4 * BLOCK, 256)
-    middle = stream + scatter_rows(dot(context, w_out, 1, 0)) + out_bias
+    w_proj = w_proj_after(context)
+    middle = stream + scatter_rows(dot(context, w_out, 1, 1)) + out_bias
     normed_two, standard_two, inverse_two = norm_forward(middle, gain_two, shift_two)
     rows_two = gather_rows(normed_two)
     gelu_input = dot(rows_two, w_fc, 1, 0) + fc_bias
@@ -170,7 +171,7 @@
         (query, keys, values, log_total, context),
         (standard_two, inverse_two, rows_two, gelu_input, hidden),
     )
-    return result.astype(bf16), saved
+    return result.astype(bf16), (w_qkv, w_out, w_fc, w_proj), saved
 
 
 def halves(grad, rows):
@@ -205,7 +206,7 @@
     grad_attention = middle_grad.astype(bf16)
     out_bias_grad = jnp.sum(grad_attention.astype(f32), axis=0)
     attention_rows = hook(2, gather_rows(grad_attention))
-    context_grad = dot(attention_rows, w_out, 1, 1).astype(bf16)
+    context_grad = dot(attention_rows, w_out, 1, 0).astype(bf16)
     w_out_grad = dot(context, attention_rows, 0, 0)
     query_grad, key_grad, value_grad = attend_backward(
         query,
@@ -270,7 +271,8 @@
     core = lax.axis_index("dp") % 2
     both = jnp.zeros((2, 4 * rows, WIDTH), bf16)
     both = place(both, whole[None], (core, 0, 0))
-    return place(both, other_core(whole)[None], (1 - core, 0, 0)).astype(f32)
+    both = place(both, other_core(whole)[None], (1 - core, 0, 0))
+    return both.reshape(2, 4, rows, WIDTH)
 
 
 def everywhere(array, pipe):
@@ -326,96 +328,81 @@
     return [((z + 4 - by) % 2, (z + 4 - by) % 4 // 2) for by in ORDER]
 
 
-def spread_weights(here, w_qkv, w_out, w_fc, w_proj, smalls):
-    pipe, high, core = here
-
-    def exchanged(group, after):
-        group = held(group, *after)
-        came = [along_z(group, by) for by in ORDER]
-        return came, other_core(jnp.stack(came))
-
-    group = jnp.concatenate([lax.dynamic_slice_in_dim(w_qkv, core * 512, 512, 0), smalls], axis=0)
-    came, swapped = exchanged(group, ())
-
-    def copies(pipe, high, core):
-        rows = span(0, 512)
-        result = [(0, (span(0, 1024),), 0, (pipe, span(0, 1024), span(high * 384, 384, 128)))]
-        result.append((1, (span(0, 32),), 1, (pipe, high)))
-        for i, (layer, slot) in enumerate(sources_of(pipe, high)):
-            columns = span(slot * 384, 384, 128)
-            result.append((2 + i, (rows,), 0, (layer, span(core * 512, 512, 512), columns)))
-            result.append(
-                (5, (i, rows), 0, (layer, span((1 - core) * 512, 512, 512), columns))
-            )
-            result.append((2 + i, (span(512, 32),), 1, (layer, slot)))
-        return result
-
-    all_qkv, all_small = lay_out(
-        here, copies, [w_qkv, smalls, *came, swapped], [(2, 1024, 768), (2, 2, 32, 384)]
-    )
-
-    half = lax.dynamic_slice_in_dim(w_fc, core * 512, 512, 0)
+def exchanged(group, after):
+    group = held(group, *after)
+    return [along_z(group, by) for by in ORDER]
+
+
+def spread_first(here, w_qkv, w_out, smalls):
+    core = here[2]
+    turned_out = w_out.T
     group = jnp.concatenate(
         [
-            jnp.concatenate([half[:256], half[256:]], axis=1),
-            lax.dynamic_slice_in_dim(w_out, core * 64, 64, 0),
+            lax.dynamic_slice_in_dim(w_qkv, core * 512, 512, 0),
+            lax.dynamic_slice_in_dim(turned_out, core * 512, 512, 0),
         ],
-        axis=0,
-    )
-    came, swapped = exchanged(group, came)
+        axis=1,
+    )
+    came = exchanged(jnp.concatenate([group, smalls], axis=0), ())
+    swapped = [other_core(item) for item in came]
 
     def copies(pipe, high, core):
-        columns = span(0, 1024)
-        result = [(0, (span(0, 1024),), 0, (pipe, span(0, 1024), span(high * 512, 512, 512)))]
-        result.append((1, (span(0, 128),), 1, (pipe, span(high * 128, 128, 128))))
+        rows = span(0, 1024)
+        result = [(0, (rows,), 0, (pipe, rows, span(high * 384, 384, 128)))]
+        result.append((1, (rows,), 1, (pipe, rows, span(high * 128, 128, 128))))
+        result.append((2, (span(0, 16),), 2, (pipe, high)))
+        rows = span(0, 512)
         for i, (layer, slot) in enumerate(sources_of(pipe, high)):
-            for source, lead, number in ((2 + i, (), core), (5, (i,), 1 - core)):
-                for part in range(2):
-                    result.append(
-                        (
-                            source,
-                            (*lead, span(0, 256), span(part * 512, 512)),
-                            0,
-                            (
-                                layer,
-                                span(number * 512 + part * 256, 256, 256),
-                                span(slot * 512, 512, 512),
-                            ),
-                        )
-                    )
+            for source, half in ((3 + i, core), (6 + i, 1 - core)):
+                goal = span(half * 512, 512, 512)
                 result.append(
-                    (
-                        source,
-                        (*lead, span(256, 64)),
-                        1,
-                        (layer, span(slot * 128 + number * 64, 64, 64)),
-                    )
+                    (source, (rows, span(0, 384)), 0, (layer, goal, span(slot * 384, 384, 128)))
                 )
+                result.append(
+                    (source, (rows, span(384, 128)), 1, (layer, goal, span(slot * 128, 128, 128)))
+                )
+            result.append((3 + i, (span(512, 16),), 2, (layer, slot)))
         return result
 
-    all_fc, all_out = lay_out(
-        here, copies, [w_fc, w_out, *came, swapped], [(2, 1024, 1024), (2, 256, 1024)]
-    )
-
-    group = lax.dynamic_slice_in_dim(w_proj, core * 256, 256, 0)
-    came, swapped = exchanged(group, came)
+    arrays = lay_out(
+        here,
+        copies,
+        [w_qkv, turned_out, smalls, *came, *swapped],
+        [(2, 1024, 768), (2, 1024, 256), (2, 2, 16, 512)],
+    )
+    return arrays, swapped
+
+
+def spread_fc(here, w_fc, came, after):
+    came = list(lax.optimization_barrier((*came, after)))[:3]
+    swapped = [other_core(item) for item in came]
+
+    def copies(pipe, high, core):
+        rows = span(0, 1024)
+        result = [(0, (rows,), 0, (pipe, rows, span(high * 512, 512, 512)))]
+        for i, (layer, slot) in enumerate(sources_of(pipe, high)):
+            for source, half in ((1 + i, core), (4 + i, 1 - core)):
+                goal = (layer, span(half * 512, 512, 512), span(slot * 512, 512, 512))
+                result.append((source, (span(0, 512),), 0, goal))
+        return result
+
+    (array,) = lay_out(here, copies, [w_fc, *came, *swapped], [(2, 1024, 1024)])
+    return array
+
+
+def spread_proj(here, w_proj, came):
+    swapped = [other_core(item) for item in came]
 
     def copies(pipe, high, core):
         result = [(0, (span(0, 512),), 0, (pipe, span(high * 512, 512, 512)))]
         for i, (layer, slot) in enumerate(sources_of(pipe, high)):
-            for source, lead, number in ((1 + i, (), core), (4, (i,), 1 - core)):
-                result.append(
-                    (
-                        source,
-                        (*lead, span(0, 256)),
-                        0,
-                        (layer, span(slot * 512 + number * 256, 256, 256)),
-                    )
-                )
+            for source, half in ((1 + i, core), (4 + i, 1 - core)):
+                goal = (layer, span(slot * 512 + half * 256, 256, 256))
+                result.append((source, (span(0, 256),), 0, goal))
         return result
 
-    (all_proj,) = lay_out(here, copies, [w_proj, *came, swapped], [(2, 1024, 1024)])
-    return all_qkv, all_out, all_fc, all_proj, all_small
+    (array,) = lay_out(here, copies, [w_proj, *came, *swapped], [(2, 1024, 1024)])
+    return array
 
 
 def on_device(
@@ -462,16 +449,29 @@
             proj_bias,
             qv_bias.reshape(1, 256),
             fc_bias,
-            jnp.zeros((1, 32 * 384 - 6912), bf16),
+            jnp.zeros((1, 16 * 512 - 6912), bf16),
         ],
         axis=1,
-    ).reshape(32, 384)
-    all_qkv, all_out, all_fc, all_proj, all_small = spread_weights(
-        here, w_qkv[0].reshape(WIDTH, 384), w_out[0], w_fc[0], w_proj[0], smalls
-    )
-    weights, vectors = [], []
+    ).reshape(16, 512)
+    (all_qkv, all_out, all_small), swapped = spread_first(
+        here, w_qkv[0].reshape(WIDTH, 384), w_out[0], smalls
+    )
+    half_fc = lax.dynamic_slice_in_dim(w_fc[0], core * 512, 512, 0)
+    came_fc = exchanged(half_fc, swapped)
+    laid = {}
+
+    def fc_after(projected):
+        laid["fc"] = spread_fc(here, w_fc[0], came_fc, projected)
+        return laid["fc"][0]
+
+    def proj_after(context):
+        half = lax.dynamic_slice_in_dim(w_proj[0], core * 256, 256, 0)
+        came = exchanged(half, (context, *came_fc))
+        laid["proj"] = spread_proj(here, w_proj[0], came)
+        return laid["proj"][0]
+
+    vectors = []
     for layer in range(2):
-        weights.append((all_qkv[layer], all_out[layer], all_fc[layer], all_proj[layer]))
         flat = all_small[layer].reshape(2, -1).astype(f32)
         norms = tuple(flat[0, i * WIDTH : (i + 1) * WIDTH] for i in range(6))
         pairs = flat[:, 6144:6400].reshape(2, 2, 128)
@@ -479,8 +479,18 @@
         qkv_bias = jnp.stack([pairs[:, 0], none, pairs[:, 1]], axis=1).reshape(-1)
         vectors.append(norms + (qkv_bias, flat[:, 6400:6912].reshape(-1)))
 
-    first, saved_first = layer_forward(stream, allowed, vectors[0], weights[0])
-    second, saved_second = layer_forward(first.astype(f32), allowed, vectors[1], weights[1])
+    first, weights_first, saved_first = layer_forward(
+        stream, allowed, vectors[0], all_qkv[0], all_out[0], fc_after, proj_after
+    )
+    second, weights_second, saved_second = layer_forward(
+        first.astype(f32),
+        allowed,
+        vectors[1],
+        all_qkv[1],
+        all_out[1],
+        lambda after: laid["fc"][1],
+        lambda after: laid["proj"][1],
+    )
     waiting = {}
 
     def keep(step, value, group=None):
@@ -489,7 +499,7 @@
         return value
 
     middle_grad, early_one, late_one = layer_backward(
-        cotangent_rows, allowed, vectors[1], weights[1], saved_second, keep
+        cotangent_rows, allowed, vectors[1], weights_second, saved_second, keep
     )
     middle_low = middle_grad.astype(bf16)
     groups_one = (waiting[1], waiting[4])
@@ -508,19 +518,18 @@
             kept["one"] = over_z(kept["one"], 1, pipe, high)
             return held(value, kept["one"], kept["feed"])
         if step == 3:
-            kept["feed"] = over_y(kept["feed"])
-            return held(value, kept["feed"])
-        kept["feed"] = over_z(kept["feed"], 0, pipe, high)
+            return value
+        kept["feed"] = over_y(kept["feed"])
         kept["attention"] = over_cores(group, core)
         return held(value, kept["feed"], kept["attention"])
 
     last_grad, early_zero, late_zero = layer_backward(
-        middle_low.astype(f32), allowed, vectors[0], weights[0], saved_first, reduce_along
+        middle_low.astype(f32), allowed, vectors[0], weights_first, saved_first, reduce_along
     )
     last_low = last_grad.astype(bf16)
-    feed_total = back_over_y(jnp.where(pipe == 1, kept["one"][:128], kept["feed"]))
-    attention_owned = over_z(over_y(kept["attention"]), 0, pipe, high)
-    attention_total = back_over_y(jnp.where(pipe == 1, kept["one"][128:], attention_owned))
+    zero = jnp.concatenate([kept["feed"], over_y(kept["attention"])], axis=1)
+    zero = over_z(zero, 0, pipe, high)
+    total = back_over_y(jnp.where(pipe == 1, kept["one"], zero))
 
     def bias_rows(fc_bias_grad):
         return place(jnp.zeros((4, WIDTH), f32), fc_bias_grad[None], (x, 0))
@@ -541,10 +550,12 @@
     small = everywhere(small, pipe)
     early, late = small[:8], small[8:]
 
-    w_fc_grad = feed_total[:, :256].reshape(512, WIDTH).T
-    w_proj_grad = feed_total[:, 256:].reshape(512, WIDTH)
-    w_qkv_grad = attention_total[:, :192].reshape(384, WIDTH).T.reshape(WIDTH, 3, 128)
-    w_out_grad = attention_total[:, 192:].reshape(128, WIDTH)
+    feed_total = total[:, :, :128].reshape(2, 512, WIDTH)
+    attention_total = total[:, :, 128:].reshape(2, 256, WIDTH)
+    w_fc_grad = feed_total[:, :256].reshape(512, WIDTH).T.astype(f32)
+    w_proj_grad = feed_total[:, 256:].reshape(512, WIDTH).astype(f32)
+    w_qkv_grad = attention_total[:, :192].reshape(384, WIDTH).T.reshape(WIDTH, 3, 128).astype(f32)
+    w_out_grad = attention_total[:, 192:].reshape(128, WIDTH).astype(f32)
     fc_bias_grad = lax.dynamic_slice(early[4:], (x, high * 512), (1, 512))[0]
     qv_bias_grad = lax.dynamic_slice(late[2:], (0, tensor * 128), (2, 128))
 

time: 546 us -> 523 us (0.958)
  local copies, waits for them, and re-layouts: 58.6 us -> 39.3 us
  waiting for transfers between devices: 210 us -> 225 us
  other arithmetic: 49.4 us -> 39.3 us
    ppermute x111 -> x110, waiting for transfers between devices: 210 us -> 225 us  [move(): return lax.ppermute(array, axes, sorted(pairs.items()))]
    another operation x8 -> x4, other arithmetic: 5.77 us -> 0.3 us  [the longest x3 5.38 us: exchanged(): return (came, other_core(jnp.stack(came)))]
    unnamed x247 -> x208, local copies, waits for them, and re-layouts: 22.4 us -> 24.7 us
    ppermute x111 -> x110, starting transfers between devices: 161 us -> 160 us  [move(): return lax.ppermute(array, axes, sorted(pairs.items()))]
  transfers between devices with their start and end apart: 111 -> 110, of which waited for: 55 -> 44; matrix products, arithmetic and copies ran while one was open for 20% -> 14% of each run, Pallas kernels for 1% -> 1%
where the time goes in v3:
time: 523 us; the launch traced here: 516 us
  waiting for transfers between devices  225 us (43%)
  starting transfers between devices  160 us (31%)
  matrix products  43 us (8%)
  local copies, waits for them, and re-layouts  39.3 us (8%)
  other arithmetic  39.3 us (8%)
  Pallas kernels  5.49 us (1%)
    ppermute x110, waiting for transfers between devices, move(): return lax.ppermute(array, axes, sorted(pairs.items()))  225 us
    ppermute x110, starting transfers between devices, move(): return lax.ppermute(array, axes, sorted(pairs.items()))  160 us
    dot_general x24, matrix products, dot(): lax.dot_general(left, right, (((left_dim,), (right_dim,)), ((), ())), pre...  29.2 us
    unnamed x208, local copies, waits for them, and re-layouts  24.7 us
  transfers between devices with their start and end apart: 110, of which 44 were waited for; matrix products, arithmetic and copies ran while one was open for 14% of the time, Pallas kernels for 1%

profile of v3, /device:TPU:1, one launch (start us, length us, event | category | flops | bytes accessed | tf_op | source)
XLA Modules:
  0.0 515.6 jit_solution(12563392824724943367)
XLA Ops:
  10.7 4.7 collective-permute-start
  18.1 18.2 %collective-permute-done = bf16[96,1024]{1,0:T(8,128)(2,1)S(1)} collective-permute-done((bf16[96,1024]{1,0:T(8,128)(2,1)}, bf16[96,1024]{1,0:T(8,128)(2,1)S(1)}, u32[]{:S(2)}, u32[]{:S(2)}) %collective-permute-start) | collective-permute-done | bytes 196640 | tf_op jit(solution)/shard_map/ppermute | solution.py:38
  51.5 6.9 %collective-permute-done.9 = bf16[96,1024]{1,0:T(8,128)(2,1)S(1)} collective-permute-done((bf16[96,1024]{1,0:T(8,128)(2,1)S(1)}, bf16[96,1024]{1,0:T(8,128)(2,1)S(1)}, u32[]{:S(2)}, u32[]{:S(2)}) %collective-permute-start.9) | collective-permute-done | bytes 196640 | tf_op jit(solution)/shard_map/ppermute | solution.py:38
  58.4 4.3 collective-permute-done.7
  79.4 3.9 collective-permute-done.18.refs_1_
  83.8 10.2 %collective-permute-done.20.refs_3_ = bf16[512,512]{1,0:T(8,128)(2,1)} collective-permute-done((bf16[512,512]{1,0:T(8,128)(2,1)}, bf16[512,512]{1,0:T(8,128)(2,1)}, u32[]{:S(2)}, u32[]{:S(2)}) %collective-permute-start.20) | collective-permute-done | bytes 524320 | tf_op jit(solution)/shard_map/ppermute | solution.py:38
  98.0 6.6 %collective-permute-start.22 = (bf16[512,512]{1,0:T(8,128)(2,1)}, bf16[512,512]{1,0:T(8,128)(2,1)S(1)}, u32[]{:S(2)}, u32[]{:S(2)}) collective-permute-start(bf16[512,512]{1,0:T(8,128)(2,1)} %collective-permute-done.19.refs_2_), channel_id=1, source_target_pairs={{0,1},{1,0},{2,3},{3,2},{4,5},{5,4},{6,7},{7,6},{8,9},{9,8},{10,11... | collective-permute-start | bytes 1572872 | tf_op jit(solution)/shard_map/ppermute | solution.py:38
  104.7 2.7 collective-permute-start.25
  110.0 20.2 %collective-permute-done.24.refs_1_ = bf16[256,1024]{1,0:T(8,128)(2,1)S(1)} collective-permute-done((bf16[256,1024]{1,0:T(8,128)(2,1)S(1)}, bf16[256,1024]{1,0:T(8,128)(2,1)S(1)}, u32[]{:S(2)}, u32[]{:S(2)}) %collective-permute-start.24) | collective-permute-done | bytes 524320 | tf_op jit(solution)/shard_map/ppermute | solution.py:38
  146.0 8.4 %collective-permute-done.32 = bf16[96,1024]{1,0:T(8,128)(2,1)S(1)} collective-permute-done((bf16[96,1024]{1,0:T(8,128)(2,1)S(1)}, bf16[96,1024]{1,0:T(8,128)(2,1)S(1)}, u32[]{:S(2)}, u32[]{:S(2)}) %collective-permute-start.32) | collective-permute-done | bytes 196640 | tf_op jit(solution)/shard_map/ppermute | solution.py:38
  155.4 2.7 collective-permute-start.35
  165.2 4.8 collective-permute-done.33
  175.8 3.5 collective-permute-start.51
  180.2 3.3 collective-permute-done.51
  189.2 4.6 collective-permute-start.38
  197.1 5.1 collective-permute-done.38
  202.8 3.2 collective-permute-start.42
  206.8 7.3 %collective-permute-done.42 = bf16[96,1024]{1,0:T(8,128)(2,1)S(1)} collective-permute-done((bf16[96,1024]{1,0:T(8,128)(2,1)S(1)}, bf16[96,1024]{1,0:T(8,128)(2,1)S(1)}, u32[]{:S(2)}, u32[]{:S(2)}) %collective-permute-start.42) | collective-permute-done | bytes 196640 | tf_op jit(solution)/shard_map/ppermute | solution.py:38
  214.0 4.4 collective-permute-done.40
  226.8 2.9 collective-permute-start.54
  233.6 11.8 %collective-permute-done.54 = bf16[96,1024]{1,0:T(8,128)(2,1)S(1)} collective-permute-done((bf16[96,1024]{1,0:T(8,128)(2,1)S(1)}, bf16[96,1024]{1,0:T(8,128)(2,1)S(1)}, u32[]{:S(2)}, u32[]{:S(2)}) %collective-permute-start.54) | collective-permute-done | bytes 196640 | tf_op jit(solution)/shard_map/ppermute | solution.py:38
  247.1 3.5 collective-permute-start.56
  251.3 3.7 collective-permute-done.57
  255.7 4.5 collective-permute-done.55
  276.1 2.8 collective-permute-done.61
  278.9 5.6 %collective-permute-done.60 = bf16[96,1024]{1,0:T(8,128)(2,1)S(1)} collective-permute-done((bf16[96,1024]{1,0:T(8,128)(2,1)S(1)}, bf16[96,1024]{1,0:T(8,128)(2,1)S(1)}, u32[]{:S(2)}, u32[]{:S(2)}) %collective-permute-start.60) | collective-permute-done | bytes 196640 | tf_op jit(solution)/shard_map/ppermute | solution.py:38
  291.5 8.7 %collective-permute-start.46 = (bf16[96,1024]{1,0:T(8,128)(2,1)S(1)}, bf16[96,1024]{1,0:T(8,128)(2,1)S(1)}, u32[]{:S(2)}, u32[]{:S(2)}) collective-permute-start(bf16[96,1024]{1,0:T(8,128)(2,1)S(1)} %get-tuple-element.100), channel_id=1, source_target_pairs={{0,0},{1,8},{2,2},{3,10},{4,4},{5,12},{6,6},{7,14},{8,1},{9,9},{10... | collective-permute-start | bytes 589832 | tf_op jit(solution)/shard_map/ppermute | solution.py:38
  306.3 4.6 collective-permute-start.68
  313.9 2.7 collective-permute-start.72
  329.3 4.6 collective-permute-done.72
  336.3 18.5 %collective-permute-done.70 = bf16[2,192,1024]{2,1,0:T(8,128)(2,1)} collective-permute-done((bf16[2,192,1024]{2,1,0:T(8,128)(2,1)}, bf16[2,192,1024]{2,1,0:T(8,128)(2,1)}, u32[]{:S(2)}, u32[]{:S(2)}) %collective-permute-start.70) | collective-permute-done | bytes 786464 | tf_op jit(solution)/shard_map/ppermute | solution.py:38
  361.5 3.6 collective-permute-done.75
  368.6 3.1 collective-permute-done.73
  371.8 2.8 fusion
  374.6 5.1 collective-permute-done.77
  397.7 2.8 collective-permute-start.82
  402.2 5.2 %collective-permute-done.86 = bf16[2,128,1024]{2,1,0:T(8,128)(2,1)S(1)} collective-permute-done((bf16[2,128,1024]{2,1,0:T(8,128)(2,1)S(1)}, bf16[2,128,1024]{2,1,0:T(8,128)(2,1)S(1)}, u32[]{:S(2)}, u32[]{:S(2)}) %collective-permute-start.86) | collective-permute-done | bytes 524320 | tf_op jit(solution)/shard_map/ppermute | solution.py:38
  407.4 2.7 collective-permute-start.81
  410.1 11.0 %collective-permute-start.102 = (bf16[2,64,1024]{2,1,0:T(8,128)(2,1)S(1)}, bf16[2,64,1024]{2,1,0:T(8,128)(2,1)S(1)}, u32[]{:S(2)}, u32[]{:S(2)}) collective-permute-start(bf16[2,64,1024]{2,1,0:T(8,128)(2,1)S(1)} %get-tuple-element.117), channel_id=1, source_target_pairs={{0,6},{1,7},{2,0},{3,1},{4,2},{5,3},{6,4},{7,5},{8,14},{9,15},{10,... | collective-permute-start | bytes 786440 | tf_op jit(solution)/shard_map/ppermute | solution.py:38
  422.2 9.3 %collective-permute-done.102 = bf16[2,64,1024]{2,1,0:T(8,128)(2,1)S(1)} collective-permute-done((bf16[2,64,1024]{2,1,0:T(8,128)(2,1)S(1)}, bf16[2,64,1024]{2,1,0:T(8,128)(2,1)S(1)}, u32[]{:S(2)}, u32[]{:S(2)}) %collective-permute-start.102) | collective-permute-done | bytes 262176 | tf_op jit(solution)/shard_map/ppermute | solution.py:38
  431.5 4.5 collective-permute-done.100
  436.2 5.4 %collective-permute-start.105 = (bf16[192,1024]{1,0:T(8,128)(2,1)S(1)}, bf16[192,1024]{1,0:T(8,128)(2,1)S(1)}, u32[]{:S(2)}, u32[]{:S(2)}) collective-permute-start(bf16[192,1024]{1,0:T(8,128)(2,1)S(1)} %get-tuple-element.120), channel_id=1, source_target_pairs={{0,8},{8,0},{16,24},{24,16},{32,40},{40,32},{48,56},{56,48},{1,9},... | collective-permute-start | bytes 1179656 | tf_op jit(solution)/shard_map/ppermute | solution.py:38
  445.7 3.4 collective-permute-start.91
  450.4 2.6 collective-permute-start.92
  453.1 7.9 %collective-permute-done.104 = bf16[192,1024]{1,0:T(8,128)(2,1)S(1)} collective-permute-done((bf16[192,1024]{1,0:T(8,128)(2,1)S(1)}, bf16[192,1024]{1,0:T(8,128)(2,1)S(1)}, u32[]{:S(2)}, u32[]{:S(2)}) %collective-permute-start.104) | collective-permute-done | bytes 393248 | tf_op jit(solution)/shard_map/ppermute | solution.py:38
  465.4 15.9 %collective-permute-done.106 = bf16[192,1024]{1,0:T(8,128)(2,1)S(1)} collective-permute-done((bf16[192,1024]{1,0:T(8,128)(2,1)S(1)}, bf16[192,1024]{1,0:T(8,128)(2,1)S(1)}, u32[]{:S(2)}, u32[]{:S(2)}) %collective-permute-start.106) | collective-permute-done | bytes 393248 | tf_op jit(solution)/shard_map/ppermute | solution.py:38
  488.5 5.6 %collective-permute-start.88 = (bf16[96,1024]{1,0:T(8,128)(2,1)S(1)}, bf16[96,1024]{1,0:T(8,128)(2,1)S(1)}, u32[]{:S(2)}, u32[]{:S(2)}) collective-permute-start(bf16[96,1024]{1,0:T(8,128)(2,1)S(1)} %get-tuple-element.96), channel_id=1, source_target_pairs={{0,0},{1,8},{2,2},{3,10},{4,4},{5,12},{6,6},{7,14},{8,1},{9,9},{10... | collective-permute-start | bytes 589832 | tf_op jit(solution)/shard_map/ppermute | solution.py:38
  507.5 3.0 copy.63
  (596 shorter events, 219.3 us)
Async XLA Ops:
  4.1 32.3 %collective-permute-start.1 = (bf16[528,512]{1,0:T(8,128)(2,1)}, bf16[528,512]{1,0:T(8,128)(2,1)S(1)}, u32[]{:S(2)}, u32[]{:S(2)}) collective-permute-start(bf16[528,512]{1,0:T(8,128)(2,1)} %pad_maximum_fusion.14), channel_id=1, source_target_pairs={{0,64},{8,72},{16,80},{24,88},{32,96},{40,104},{48,112},{56,120},{... | collective-permute-start | bytes 1622024 | tf_op jit(solution)/shard_map/ppermute | solution.py:38
  6.5 30.8 %collective-permute-start.2 = (bf16[528,512]{1,0:T(8,128)(2,1)}, bf16[528,512]{1,0:T(8,128)(2,1)S(1)}, u32[]{:S(2)}, u32[]{:S(2)}) collective-permute-start(bf16[528,512]{1,0:T(8,128)(2,1)} %pad_maximum_fusion.14), channel_id=1, source_target_pairs={{0,72},{8,64},{16,88},{24,80},{32,104},{40,96},{48,120},{56,112},{... | collective-permute-start | bytes 1622024 | tf_op jit(solution)/shard_map/ppermute | solution.py:38
  8.7 29.9 %collective-permute-start.3 = (bf16[528,512]{1,0:T(8,128)(2,1)}, bf16[528,512]{1,0:T(8,128)(2,1)}, u32[]{:S(2)}, u32[]{:S(2)}) collective-permute-start(bf16[528,512]{1,0:T(8,128)(2,1)} %pad_maximum_fusion.14), channel_id=1, source_target_pairs={{0,8},{8,0},{16,24},{24,16},{32,40},{40,32},{48,56},{56,48},{64,72... | collective-permute-start | bytes 1622024 | tf_op jit(solution)/shard_map/ppermute | solution.py:38
  10.7 25.6 %collective-permute-start = (bf16[96,1024]{1,0:T(8,128)(2,1)}, bf16[96,1024]{1,0:T(8,128)(2,1)S(1)}, u32[]{:S(2)}, u32[]{:S(2)}) collective-permute-start(bf16[96,1024]{1,0:T(8,128)(2,1)} %dynamic-slice_bitcast_fusion.11), channel_id=1, source_target_pairs={{0,0},{1,8},{2,2},{3,10},{4,4},{5,12},{6,6},{7,14},{8,1},{9,9},{10... | collective-permute-start | bytes 589832 | tf_op jit(solution)/shard_map/ppermute | solution.py:38
  15.5 51.4 %collective-permute-start.11 = (s32[8,96]{1,0:T(8,128)S(1)}, s32[8,96]{1,0:T(8,128)S(1)}, u32[]{:S(2)}, u32[]{:S(2)}) collective-permute-start(s32[8,96]{1,0:T(8,128)S(1)} %reshape.698), channel_id=1, source_target_pairs={{0,1},{1,0},{2,3},{3,2},{4,5},{5,4},{6,7},{7,6},{8,9},{9,8},{10,11... | collective-permute-start | bytes 9224 | tf_op jit(solution)/shard_map/ppermute | solution.py:38
  67.9 15.4 %collective-permute-start.18 = (bf16[512,512]{1,0:T(8,128)(2,1)}, bf16[512,512]{1,0:T(8,128)(2,1)}, u32[]{:S(2)}, u32[]{:S(2)}) collective-permute-start(bf16[512,512]{1,0:T(8,128)(2,1)} %dynamic-slice_bitcast_fusion.4), channel_id=1, source_target_pairs={{0,64},{8,72},{16,80},{24,88},{32,96},{40,104},{48,112},{56,120},{... | collective-permute-start | bytes 1572872 | tf_op jit(solution)/shard_map/ppermute | solution.py:38
  68.8 14.9 %collective-permute-start.19 = (bf16[512,512]{1,0:T(8,128)(2,1)}, bf16[512,512]{1,0:T(8,128)(2,1)}, u32[]{:S(2)}, u32[]{:S(2)}) collective-permute-start(bf16[512,512]{1,0:T(8,128)(2,1)} %dynamic-slice_bitcast_fusion.4), channel_id=1, source_target_pairs={{0,72},{8,64},{16,88},{24,80},{32,104},{40,96},{48,120},{56,112},{... | collective-permute-start | bytes 1572872 | tf_op jit(solution)/shard_map/ppermute | solution.py:38
  70.7 23.3 %collective-permute-start.20 = (bf16[512,512]{1,0:T(8,128)(2,1)}, bf16[512,512]{1,0:T(8,128)(2,1)}, u32[]{:S(2)}, u32[]{:S(2)}) collective-permute-start(bf16[512,512]{1,0:T(8,128)(2,1)} %dynamic-slice_bitcast_fusion.4), channel_id=1, source_target_pairs={{0,8},{8,0},{16,24},{24,16},{32,40},{40,32},{48,56},{56,48},{64,72... | collective-permute-start | bytes 1572872 | tf_op jit(solution)/shard_map/ppermute | solution.py:38
  77.7 18.1 %collective-permute-start.14 = (bf16[96,1024]{1,0:T(8,128)(2,1)S(1)}, bf16[96,1024]{1,0:T(8,128)(2,1)S(1)}, u32[]{:S(2)}, u32[]{:S(2)}) collective-permute-start(bf16[96,1024]{1,0:T(8,128)(2,1)S(1)} %get-tuple-element.147), channel_id=1, source_target_pairs={{0,16},{8,24},{16,32},{24,40},{32,48},{40,56},{48,0},{56,8},{1,17}... | collective-permute-start | bytes 589832 | tf_op jit(solution)/shard_map/ppermute | solution.py:38
  77.8 18.0 %collective-permute-start.13 = (bf16[96,1024]{1,0:T(8,128)(2,1)S(1)}, bf16[96,1024]{1,0:T(8,128)(2,1)S(1)}, u32[]{:S(2)}, u32[]{:S(2)}) collective-permute-start(bf16[96,1024]{1,0:T(8,128)(2,1)S(1)} %get-tuple-element.148), channel_id=1, source_target_pairs={{0,32},{8,40},{16,48},{24,56},{32,0},{40,8},{48,16},{56,24},{1,33}... | collective-permute-start | bytes 589832 | tf_op jit(solution)/shard_map/ppermute | solution.py:38
  104.7 25.5 %collective-permute-start.24 = (bf16[256,1024]{1,0:T(8,128)(2,1)S(1)}, bf16[256,1024]{1,0:T(8,128)(2,1)S(1)}, u32[]{:S(2)}, u32[]{:S(2)}) collective-permute-start(bf16[256,1024]{1,0:T(8,128)(2,1)S(1)} %dynamic-slice_bitcast_fusion.3), channel_id=1, source_target_pairs={{0,64},{8,72},{16,80},{24,88},{32,96},{40,104},{48,112},{56,120},{... | collective-permute-start | bytes 1572872 | tf_op jit(solution)/shard_map/ppermute | solution.py:38
  104.7 26.8 %collective-permute-start.25 = (bf16[256,1024]{1,0:T(8,128)(2,1)S(1)}, bf16[256,1024]{1,0:T(8,128)(2,1)S(1)}, u32[]{:S(2)}, u32[]{:S(2)}) collective-permute-start(bf16[256,1024]{1,0:T(8,128)(2,1)S(1)} %dynamic-slice_bitcast_fusion.3), channel_id=1, source_target_pairs={{0,72},{8,64},{16,88},{24,80},{32,104},{40,96},{48,120},{56,112},{... | collective-permute-start | bytes 1572872 | tf_op jit(solution)/shard_map/ppermute | solution.py:38
  107.4 24.1 %collective-permute-start.26 = (bf16[256,1024]{1,0:T(8,128)(2,1)S(1)}, bf16[256,1024]{1,0:T(8,128)(2,1)S(1)}, u32[]{:S(2)}, u32[]{:S(2)}) collective-permute-start(bf16[256,1024]{1,0:T(8,128)(2,1)S(1)} %dynamic-slice_bitcast_fusion.3), channel_id=1, source_target_pairs={{0,8},{8,0},{16,24},{24,16},{32,40},{40,32},{48,56},{56,48},{64,72... | collective-permute-start | bytes 1572872 | tf_op jit(solution)/shard_map/ppermute | solution.py:38
  109.0 26.0 %collective-permute-start.16 = (bf16[96,1024]{1,0:T(8,128)(2,1)}, bf16[96,1024]{1,0:T(8,128)(2,1)S(1)}, u32[]{:S(2)}, u32[]{:S(2)}) collective-permute-start(bf16[96,1024]{1,0:T(8,128)(2,1)} %add_convert_fusion.5), channel_id=1, source_target_pairs={{0,32},{8,40},{16,48},{24,56},{32,0},{40,8},{48,16},{56,24},{1,33}... | collective-permute-start | bytes 589832 | tf_op jit(solution)/shard_map/ppermute | solution.py:38
  109.0 28.0 %collective-permute-start.15 = (bf16[96,1024]{1,0:T(8,128)(2,1)}, bf16[96,1024]{1,0:T(8,128)(2,1)S(1)}, u32[]{:S(2)}, u32[]{:S(2)}) collective-permute-start(bf16[96,1024]{1,0:T(8,128)(2,1)} %add_convert_fusion.5), channel_id=1, source_target_pairs={{0,16},{8,24},{16,32},{24,40},{32,48},{40,56},{48,0},{56,8},{1,17}... | collective-permute-start | bytes 589832 | tf_op jit(solution)/shard_map/ppermute | solution.py:38
  135.0 23.7 %collective-permute-start.48 = (bf16[96,1024]{1,0:T(8,128)(2,1)}, bf16[96,1024]{1,0:T(8,128)(2,1)S(1)}, u32[]{:S(2)}, u32[]{:S(2)}) collective-permute-start(bf16[96,1024]{1,0:T(8,128)(2,1)} %dynamic-slice_bitcast_fusion.10), channel_id=1, source_target_pairs={{0,0},{1,8},{2,2},{3,10},{4,4},{5,12},{6,6},{7,14},{8,1},{9,9},{10... | collective-permute-start | bytes 589832 | tf_op jit(solution)/shard_map/ppermute | solution.py:38
  158.7 20.5 %collective-permute-start.49 = (bf16[96,1024]{1,0:T(8,128)(2,1)S(1)}, bf16[96,1024]{1,0:T(8,128)(2,1)}, u32[]{:S(2)}, u32[]{:S(2)}) collective-permute-start(bf16[96,1024]{1,0:T(8,128)(2,1)S(1)} %collective-permute-done.48), channel_id=1, source_target_pairs={{0,16},{8,24},{16,32},{24,40},{32,48},{40,56},{48,0},{56,8},{1,17}... | collective-permute-start | bytes 589832 | tf_op jit(solution)/shard_map/ppermute | solution.py:38
  160.7 19.5 %collective-permute-start.50 = (bf16[96,1024]{1,0:T(8,128)(2,1)S(1)}, bf16[96,1024]{1,0:T(8,128)(2,1)S(1)}, u32[]{:S(2)}, u32[]{:S(2)}) collective-permute-start(bf16[96,1024]{1,0:T(8,128)(2,1)S(1)} %collective-permute-done.48), channel_id=1, source_target_pairs={{0,32},{8,40},{16,48},{24,56},{32,0},{40,8},{48,16},{56,24},{1,33}... | collective-permute-start | bytes 589832 | tf_op jit(solution)/shard_map/ppermute | solution.py:38
  225.2 21.9 %collective-permute-start.45 = (bf16[96,1024]{1,0:T(8,128)(2,1)S(1)}, bf16[96,1024]{1,0:T(8,128)(2,1)S(1)}, u32[]{:S(2)}, u32[]{:S(2)}) collective-permute-start(bf16[96,1024]{1,0:T(8,128)(2,1)S(1)} %get-tuple-element.136), channel_id=1, source_target_pairs={{0,16},{8,24},{16,32},{24,40},{32,48},{40,56},{48,0},{56,8},{1,17}... | collective-permute-start | bytes 589832 | tf_op jit(solution)/shard_map/ppermute | solution.py:38
  225.3 25.4 %collective-permute-start.44 = (bf16[96,1024]{1,0:T(8,128)(2,1)S(1)}, bf16[96,1024]{1,0:T(8,128)(2,1)S(1)}, u32[]{:S(2)}, u32[]{:S(2)}) collective-permute-start(bf16[96,1024]{1,0:T(8,128)(2,1)S(1)} %get-tuple-element.137), channel_id=1, source_target_pairs={{0,32},{8,40},{16,48},{24,56},{32,0},{40,8},{48,16},{56,24},{1,33}... | collective-permute-start | bytes 589832 | tf_op jit(solution)/shard_map/ppermute | solution.py:38
  226.8 18.6 %collective-permute-start.54 = (bf16[96,1024]{1,0:T(8,128)(2,1)S(1)}, bf16[96,1024]{1,0:T(8,128)(2,1)S(1)}, u32[]{:S(2)}, u32[]{:S(2)}) collective-permute-start(bf16[96,1024]{1,0:T(8,128)(2,1)S(1)} %get-tuple-element.133), channel_id=1, source_target_pairs={{0,16},{8,24},{16,32},{24,40},{32,48},{40,56},{48,0},{56,8},{1,17}... | collective-permute-start | bytes 589832 | tf_op jit(solution)/shard_map/ppermute | solution.py:38
  229.6 15.8 %collective-permute-start.53 = (bf16[96,1024]{1,0:T(8,128)(2,1)S(1)}, bf16[96,1024]{1,0:T(8,128)(2,1)S(1)}, u32[]{:S(2)}, u32[]{:S(2)}) collective-permute-start(bf16[96,1024]{1,0:T(8,128)(2,1)S(1)} %get-tuple-element.134), channel_id=1, source_target_pairs={{0,32},{8,40},{16,48},{24,56},{32,0},{40,8},{48,16},{56,24},{1,33}... | collective-permute-start | bytes 589832 | tf_op jit(solution)/shard_map/ppermute | solution.py:38
  230.3 16.2 %collective-permute-start.52 = (bf16[96,1024]{1,0:T(8,128)(2,1)S(1)}, bf16[96,1024]{1,0:T(8,128)(2,1)S(1)}, u32[]{:S(2)}, u32[]{:S(2)}) collective-permute-start(bf16[96,1024]{1,0:T(8,128)(2,1)S(1)} %get-tuple-element.132), channel_id=1, source_target_pairs={{0,48},{8,56},{16,0},{24,8},{32,16},{40,24},{48,32},{56,40},{1,49}... | collective-permute-start | bytes 589832 | tf_op jit(solution)/shard_map/ppermute | solution.py:38
  245.4 66.0 %collective-permute-start.65 = (bf16[2,512,1024]{2,1,0:T(8,128)(2,1)S(1)}, bf16[2,512,1024]{2,1,0:T(8,128)(2,1)S(1)}, u32[]{:S(2)}, u32[]{:S(2)}) collective-permute-start(bf16[2,512,1024]{2,1,0:T(8,128)(2,1)S(1)} %fusion.19), channel_id=1, source_target_pairs={{0,1},{1,0},{2,3},{3,2},{4,5},{5,4},{6,7},{7,6},{8,9},{9,8},{10,11... | collective-permute-start | bytes 6291464 | tf_op jit(solution)/shard_map/ppermute | solution.py:38
  265.9 50.8 %collective-permute-start.47 = (bf16[96,1024]{1,0:T(8,128)(2,1)S(1)}, bf16[96,1024]{1,0:T(8,128)(2,1)S(1)}, u32[]{:S(2)}, u32[]{:S(2)}) collective-permute-start(bf16[96,1024]{1,0:T(8,128)(2,1)S(1)} %broadcast_select_fusion.2), channel_id=1, source_target_pairs={{0,64},{1,72},{2,66},{3,74},{4,68},{5,76},{6,70},{7,78},{8,65},{9,... | collective-permute-start | bytes 589832 | tf_op jit(solution)/shard_map/ppermute | solution.py:38
  291.5 25.6 %collective-permute-start.46 = (bf16[96,1024]{1,0:T(8,128)(2,1)S(1)}, bf16[96,1024]{1,0:T(8,128)(2,1)S(1)}, u32[]{:S(2)}, u32[]{:S(2)}) collective-permute-start(bf16[96,1024]{1,0:T(8,128)(2,1)S(1)} %get-tuple-element.100), channel_id=1, source_target_pairs={{0,0},{1,8},{2,2},{3,10},{4,4},{5,12},{6,6},{7,14},{8,1},{9,9},{10... | collective-permute-start | bytes 589832 | tf_op jit(solution)/shard_map/ppermute | solution.py:38
  304.7 17.4 %collective-permute-start.69 = (bf16[96,1024]{1,0:T(8,128)(2,1)S(1)}, bf16[96,1024]{1,0:T(8,128)(2,1)S(1)}, u32[]{:S(2)}, u32[]{:S(2)}) collective-permute-start(bf16[96,1024]{1,0:T(8,128)(2,1)S(1)} %get-tuple-element.127), channel_id=1, source_target_pairs={{0,16},{8,24},{16,32},{24,40},{32,48},{40,56},{48,0},{56,8},{1,17}... | collective-permute-start | bytes 589832 | tf_op jit(solution)/shard_map/ppermute | solution.py:38
  306.3 16.5 %collective-permute-start.68 = (bf16[96,1024]{1,0:T(8,128)(2,1)S(1)}, bf16[96,1024]{1,0:T(8,128)(2,1)}, u32[]{:S(2)}, u32[]{:S(2)}) collective-permute-start(bf16[96,1024]{1,0:T(8,128)(2,1)S(1)} %get-tuple-element.128), channel_id=1, source_target_pairs={{0,32},{8,40},{16,48},{24,56},{32,0},{40,8},{48,16},{56,24},{1,33}... | collective-permute-start | bytes 589832 | tf_op jit(solution)/shard_map/ppermute | solution.py:38
  313.9 19.9 %collective-permute-start.72 = (bf16[2,192,1024]{2,1,0:T(8,128)(2,1)}, bf16[2,192,1024]{2,1,0:T(8,128)(2,1)}, u32[]{:S(2)}, u32[]{:S(2)}) collective-permute-start(bf16[2,192,1024]{2,1,0:T(8,128)(2,1)} %get-tuple-element.110), channel_id=1, source_target_pairs={{0,6},{1,7},{2,0},{3,1},{4,2},{5,3},{6,4},{7,5},{8,14},{9,15},{10,... | collective-permute-start | bytes 2359304 | tf_op jit(solution)/shard_map/ppermute | solution.py:38
  316.7 19.6 %collective-permute-start.71 = (bf16[2,192,1024]{2,1,0:T(8,128)(2,1)}, bf16[2,192,1024]{2,1,0:T(8,128)(2,1)}, u32[]{:S(2)}, u32[]{:S(2)}) collective-permute-start(bf16[2,192,1024]{2,1,0:T(8,128)(2,1)} %get-tuple-element.109), channel_id=1, source_target_pairs={{0,4},{1,5},{2,6},{3,7},{4,0},{5,1},{6,2},{7,3},{8,12},{9,13},{10,... | collective-permute-start | bytes 2359304 | tf_op jit(solution)/shard_map/ppermute | solution.py:38
  317.0 37.8 %collective-permute-start.70 = (bf16[2,192,1024]{2,1,0:T(8,128)(2,1)}, bf16[2,192,1024]{2,1,0:T(8,128)(2,1)}, u32[]{:S(2)}, u32[]{:S(2)}) collective-permute-start(bf16[2,192,1024]{2,1,0:T(8,128)(2,1)} %get-tuple-element.108), channel_id=1, source_target_pairs={{0,2},{1,3},{2,4},{3,5},{4,6},{5,7},{6,0},{7,1},{8,10},{9,11},{10,... | collective-permute-start | bytes 2359304 | tf_op jit(solution)/shard_map/ppermute | solution.py:38
  322.8 49.0 %collective-permute-start.79 = (bf16[2,512,1024]{2,1,0:T(8,128)(2,1)}, bf16[2,512,1024]{2,1,0:T(8,128)(2,1)}, u32[]{:S(2)}, u32[]{:S(2)}) collective-permute-start(bf16[2,512,1024]{2,1,0:T(8,128)(2,1)} %fusion.15), channel_id=1, source_target_pairs={{0,1},{1,0},{2,3},{3,2},{4,5},{5,4},{6,7},{7,6},{8,9},{9,8},{10,11... | collective-permute-start | bytes 6291464 | tf_op jit(solution)/shard_map/ppermute | solution.py:38
  365.1 14.6 %collective-permute-start.77 = (bf16[192,1024]{1,0:T(8,128)(2,1)S(1)}, bf16[192,1024]{1,0:T(8,128)(2,1)S(1)}, u32[]{:S(2)}, u32[]{:S(2)}) collective-permute-start(bf16[192,1024]{1,0:T(8,128)(2,1)S(1)} %get-tuple-element.125), channel_id=1, source_target_pairs={{0,72},{8,64},{16,88},{24,80},{32,104},{40,96},{48,120},{56,112},{... | collective-permute-start | bytes 1179656 | tf_op jit(solution)/shard_map/ppermute | solution.py:38
  393.9 16.2 %collective-permute-start.85 = (bf16[2,128,1024]{2,1,0:T(8,128)(2,1)S(1)}, bf16[2,128,1024]{2,1,0:T(8,128)(2,1)S(1)}, u32[]{:S(2)}, u32[]{:S(2)}) collective-permute-start(bf16[2,128,1024]{2,1,0:T(8,128)(2,1)S(1)} %get-tuple-element.115), channel_id=1, source_target_pairs={{0,4},{1,5},{2,6},{3,7},{4,0},{5,1},{6,2},{7,3},{8,12},{9,13},{10,... | collective-permute-start | bytes 1572872 | tf_op jit(solution)/shard_map/ppermute | solution.py:38
  394.3 26.7 %collective-permute-start.84 = (bf16[2,128,1024]{2,1,0:T(8,128)(2,1)S(1)}, bf16[2,128,1024]{2,1,0:T(8,128)(2,1)S(1)}, u32[]{:S(2)}, u32[]{:S(2)}) collective-permute-start(bf16[2,128,1024]{2,1,0:T(8,128)(2,1)S(1)} %get-tuple-element.113), channel_id=1, source_target_pairs={{0,2},{1,3},{2,4},{3,5},{4,6},{5,7},{6,0},{7,1},{8,10},{9,11},{10,... | collective-permute-start | bytes 1572872 | tf_op jit(solution)/shard_map/ppermute | solution.py:38
  396.5 24.6 %collective-permute-start.83 = (bf16[96,1024]{1,0:T(8,128)(2,1)S(1)}, bf16[96,1024]{1,0:T(8,128)(2,1)S(1)}, u32[]{:S(2)}, u32[]{:S(2)}) collective-permute-start(bf16[96,1024]{1,0:T(8,128)(2,1)S(1)} %get-tuple-element.122), channel_id=1, source_target_pairs={{0,16},{8,24},{16,32},{24,40},{32,48},{40,56},{48,0},{56,8},{1,17}... | collective-permute-start | bytes 589832 | tf_op jit(solution)/shard_map/ppermute | solution.py:38
  397.7 24.3 %collective-permute-start.82 = (bf16[96,1024]{1,0:T(8,128)(2,1)S(1)}, bf16[96,1024]{1,0:T(8,128)(2,1)S(1)}, u32[]{:S(2)}, u32[]{:S(2)}) collective-permute-start(bf16[96,1024]{1,0:T(8,128)(2,1)S(1)} %get-tuple-element.123), channel_id=1, source_target_pairs={{0,32},{8,40},{16,48},{24,56},{32,0},{40,8},{48,16},{56,24},{1,33}... | collective-permute-start | bytes 589832 | tf_op jit(solution)/shard_map/ppermute | solution.py:38
  407.4 14.6 %collective-permute-start.81 = (bf16[96,1024]{1,0:T(8,128)(2,1)S(1)}, bf16[96,1024]{1,0:T(8,128)(2,1)S(1)}, u32[]{:S(2)}, u32[]{:S(2)}) collective-permute-start(bf16[96,1024]{1,0:T(8,128)(2,1)S(1)} %get-tuple-element.121), channel_id=1, source_target_pairs={{0,48},{8,56},{16,0},{24,8},{32,16},{40,24},{48,32},{56,40},{1,49}... | collective-permute-start | bytes 589832 | tf_op jit(solution)/shard_map/ppermute | solution.py:38
  410.1 21.4 %collective-permute-start.102 = (bf16[2,64,1024]{2,1,0:T(8,128)(2,1)S(1)}, bf16[2,64,1024]{2,1,0:T(8,128)(2,1)S(1)}, u32[]{:S(2)}, u32[]{:S(2)}) collective-permute-start(bf16[2,64,1024]{2,1,0:T(8,128)(2,1)S(1)} %get-tuple-element.117), channel_id=1, source_target_pairs={{0,6},{1,7},{2,0},{3,1},{4,2},{5,3},{6,4},{7,5},{8,14},{9,15},{10,... | collective-permute-start | bytes 786440 | tf_op jit(solution)/shard_map/ppermute | solution.py:38
  421.1 14.9 %collective-permute-start.100 = (bf16[2,64,1024]{2,1,0:T(8,128)(2,1)S(1)}, bf16[2,64,1024]{2,1,0:T(8,128)(2,1)S(1)}, u32[]{:S(2)}, u32[]{:S(2)}) collective-permute-start(bf16[2,64,1024]{2,1,0:T(8,128)(2,1)S(1)} %get-tuple-element.116), channel_id=1, source_target_pairs={{0,2},{1,3},{2,4},{3,5},{4,6},{5,7},{6,0},{7,1},{8,10},{9,11},{10,... | collective-permute-start | bytes 786440 | tf_op jit(solution)/shard_map/ppermute | solution.py:38
  441.6 19.4 %collective-permute-start.104 = (bf16[192,1024]{1,0:T(8,128)(2,1)S(1)}, bf16[192,1024]{1,0:T(8,128)(2,1)S(1)}, u32[]{:S(2)}, u32[]{:S(2)}) collective-permute-start(bf16[192,1024]{1,0:T(8,128)(2,1)S(1)} %get-tuple-element.120), channel_id=1, source_target_pairs={{64,8},{72,0},{80,24},{88,16},{96,40},{104,32},{112,56},{120,48},{... | collective-permute-start | bytes 1179656 | tf_op jit(solution)/shard_map/ppermute | solution.py:38
  442.9 18.1 %collective-permute-start.103 = (bf16[192,1024]{1,0:T(8,128)(2,1)S(1)}, bf16[192,1024]{1,0:T(8,128)(2,1)S(1)}, u32[]{:S(2)}, u32[]{:S(2)}) collective-permute-start(bf16[192,1024]{1,0:T(8,128)(2,1)S(1)} %get-tuple-element.119), channel_id=1, source_target_pairs={{64,0},{72,8},{80,16},{88,24},{96,32},{104,40},{112,48},{120,56},{... | collective-permute-start | bytes 1179656 | tf_op jit(solution)/shard_map/ppermute | solution.py:38
  445.7 16.5 %collective-permute-start.91 = (f32[12,1024]{1,0:T(8,128)S(1)}, f32[12,1024]{1,0:T(8,128)S(1)}, u32[]{:S(2)}, u32[]{:S(2)}) collective-permute-start(f32[12,1024]{1,0:T(8,128)S(1)} %get-tuple-element.162), channel_id=1, source_target_pairs={{0,72},{8,64},{16,88},{24,80},{32,104},{40,96},{48,120},{56,112},{... | collective-permute-start | bytes 147464 | tf_op jit(solution)/shard_map/ppermute | solution.py:38
  461.6 19.8 %collective-permute-start.106 = (bf16[192,1024]{1,0:T(8,128)(2,1)S(1)}, bf16[192,1024]{1,0:T(8,128)(2,1)S(1)}, u32[]{:S(2)}, u32[]{:S(2)}) collective-permute-start(bf16[192,1024]{1,0:T(8,128)(2,1)S(1)} %get-tuple-element.83), channel_id=1, source_target_pairs={{0,2},{1,3},{2,4},{3,5},{4,6},{5,7},{6,0},{7,1},{8,10},{9,11},{10,... | collective-permute-start | bytes 1179656 | tf_op jit(solution)/shard_map/ppermute | solution.py:38
  461.7 19.7 %collective-permute-start.107 = (bf16[192,1024]{1,0:T(8,128)(2,1)S(1)}, bf16[192,1024]{1,0:T(8,128)(2,1)S(1)}, u32[]{:S(2)}, u32[]{:S(2)}) collective-permute-start(bf16[192,1024]{1,0:T(8,128)(2,1)S(1)} %get-tuple-element.83), channel_id=1, source_target_pairs={{0,4},{1,5},{2,6},{3,7},{4,0},{5,1},{6,2},{7,3},{8,12},{9,13},{10,... | collective-permute-start | bytes 1179656 | tf_op jit(solution)/shard_map/ppermute | solution.py:38
  462.4 21.4 %collective-permute-start.93 = (f32[12,1024]{1,0:T(8,128)S(1)}, f32[12,1024]{1,0:T(8,128)S(1)}, u32[]{:S(2)}, u32[]{:S(2)}) collective-permute-start(f32[12,1024]{1,0:T(8,128)S(1)} %add_add_fusion.2), channel_id=1, source_target_pairs={{0,1},{1,0},{2,3},{3,2},{4,5},{5,4},{6,7},{7,6},{8,9},{9,8},{10,11... | collective-permute-start | bytes 147464 | tf_op jit(solution)/shard_map/ppermute | solution.py:38
  463.4 18.5 %collective-permute-start.108 = (bf16[192,1024]{1,0:T(8,128)(2,1)S(1)}, bf16[192,1024]{1,0:T(8,128)(2,1)S(1)}, u32[]{:S(2)}, u32[]{:S(2)}) collective-permute-start(bf16[192,1024]{1,0:T(8,128)(2,1)S(1)} %get-tuple-element.83), channel_id=1, source_target_pairs={{0,6},{1,7},{2,0},{3,1},{4,2},{5,3},{6,4},{7,5},{8,14},{9,15},{10,... | collective-permute-start | bytes 1179656 | tf_op jit(solution)/shard_map/ppermute | solution.py:38
  482.0 23.6 %collective-permute-start.109 = (bf16[768,1024]{1,0:T(8,128)(2,1)S(1)}, bf16[768,1024]{1,0:T(8,128)(2,1)S(1)}, u32[]{:S(2)}, u32[]{:S(2)}) collective-permute-start(bf16[768,1024]{1,0:T(8,128)(2,1)S(1)} %bitcast.399), channel_id=1, source_target_pairs={{0,1},{1,0},{2,3},{3,2},{4,5},{5,4},{6,7},{7,6},{8,9},{9,8},{10,11... | collective-permute-start | bytes 4718600 | tf_op jit(solution)/shard_map/ppermute | solution.py:38
  (156 other events, 1550.3 us)

commit v4 on v3

--- a/solution.py
+++ b/solution.py
@@ -145,24 +145,24 @@
     return tuple(view[:, :, part].reshape(4 * BLOCK, 4, HEAD_DIM) for part in range(3))
 
 
-def layer_forward(stream, allowed, vectors, w_qkv, w_out, w_fc_after, w_proj_after):
+def layer_forward(stream, allowed, vectors, w_qkv, w_out, hook):
     gain_one, shift_one, out_bias, gain_two, shift_two, proj_bias, qkv_bias, fc_bias = vectors
     normed_one, standard_one, inverse_one = norm_forward(stream, gain_one, shift_one)
     rows_one = gather_rows(normed_one)
     projected = (dot(rows_one, w_qkv, 1, 0) + qkv_bias).astype(bf16)
-    w_fc = w_fc_after(projected)
     query, key, value = split_heads(projected)
     both = jnp.stack([key, value]).reshape(2, 4 * BLOCK, 256)
+    arrived = hook(0, other_core(both))
     keys, values = (
         part.reshape(8 * BLOCK, 4, HEAD_DIM)
-        for part in jnp.concatenate([both, other_core(both)], axis=1)
+        for part in jnp.concatenate([both, arrived], axis=1)
     )
     context, log_total = attend_forward(query, keys, values, allowed)
     context = context.reshape(4 * BLOCK, 256)
-    w_proj = w_proj_after(context)
-    middle = stream + scatter_rows(dot(context, w_out, 1, 1)) + out_bias
+    context = hook(1, context)
+    middle = stream + hook(2, scatter_rows(dot(context, w_out, 1, 1))) + out_bias
     normed_two, standard_two, inverse_two = norm_forward(middle, gain_two, shift_two)
-    rows_two = gather_rows(normed_two)
+    rows_two, w_fc, w_proj = hook(3, gather_rows(normed_two))
     gelu_input = dot(rows_two, w_fc, 1, 0) + fc_bias
     hidden = jax.nn.gelu(gelu_input, approximate=True).astype(bf16)
     result = middle + scatter_rows(dot(hidden, w_proj, 1, 0)) + proj_bias
@@ -242,12 +242,18 @@
     return mine.reshape(2, 4, mine.shape[1] // 4, WIDTH)
 
 
-def over_y(mine):
+def near_y(mine):
     y = lax.axis_index("dp") // 2
     own = pick(mine, y, 1).astype(f32)
-    for by in (1, 2, 3):
+    for by in (1, 3):
         own = own + along_y(pick(mine, (y + by) % 4, 1), by).astype(f32)
-    return own.astype(bf16)
+    return own
+
+
+def far_y(mine, own):
+    y = lax.axis_index("dp") // 2
+    sent = held(pick(mine, (y + 2) % 4, 1), own)
+    return (own + along_y(sent, 2).astype(f32)).astype(bf16)
 
 
 def over_z(own, layer, pipe, high):
@@ -328,11 +334,6 @@
     return [((z + 4 - by) % 2, (z + 4 - by) % 4 // 2) for by in ORDER]
 
 
-def exchanged(group, after):
-    group = held(group, *after)
-    return [along_z(group, by) for by in ORDER]
-
-
 def spread_first(here, w_qkv, w_out, smalls):
     core = here[2]
     turned_out = w_out.T
@@ -343,7 +344,8 @@
         ],
         axis=1,
     )
-    came = exchanged(jnp.concatenate([group, smalls], axis=0), ())
+    group = jnp.concatenate([group, smalls], axis=0)
+    came = [along_z(group, by) for by in ORDER]
     swapped = [other_core(item) for item in came]
 
     def copies(pipe, high, core):
@@ -373,35 +375,34 @@
     return arrays, swapped
 
 
-def spread_fc(here, w_fc, came, after):
-    came = list(lax.optimization_barrier((*came, after)))[:3]
-    swapped = [other_core(item) for item in came]
+def lay_fc(here, w_fc, came):
+    swapped = other_core(jnp.stack(came))
 
     def copies(pipe, high, core):
         rows = span(0, 1024)
         result = [(0, (rows,), 0, (pipe, rows, span(high * 512, 512, 512)))]
         for i, (layer, slot) in enumerate(sources_of(pipe, high)):
-            for source, half in ((1 + i, core), (4 + i, 1 - core)):
+            for source, lead, half in ((1 + i, (), core), (4, (i,), 1 - core)):
                 goal = (layer, span(half * 512, 512, 512), span(slot * 512, 512, 512))
-                result.append((source, (span(0, 512),), 0, goal))
+                result.append((source, (*lead, span(0, 512)), 0, goal))
         return result
 
-    (array,) = lay_out(here, copies, [w_fc, *came, *swapped], [(2, 1024, 1024)])
+    (array,) = lay_out(here, copies, [w_fc, *came, swapped], [(2, 1024, 1024)])
     return array
 
 
-def spread_proj(here, w_proj, came):
-    swapped = [other_core(item) for item in came]
+def lay_proj(here, w_proj, came):
+    swapped = other_core(jnp.stack(came))
 
     def copies(pipe, high, core):
         result = [(0, (span(0, 512),), 0, (pipe, span(high * 512, 512, 512)))]
         for i, (layer, slot) in enumerate(sources_of(pipe, high)):
-            for source, half in ((1 + i, core), (4 + i, 1 - core)):
+            for source, lead, half in ((1 + i, (), core), (4, (i,), 1 - core)):
                 goal = (layer, span(slot * 512 + half * 256, 256, 256))
-                result.append((source, (span(0, 256),), 0, goal))
+                result.append((source, (*lead, span(0, 256)), 0, goal))
         return result
 
-    (array,) = lay_out(here, copies, [w_proj, *came, *swapped], [(2, 1024, 1024)])
+    (array,) = lay_out(here, copies, [w_proj, *came, swapped], [(2, 1024, 1024)])
     return array
 
 
@@ -457,18 +458,28 @@
         here, w_qkv[0].reshape(WIDTH, 384), w_out[0], smalls
     )
     half_fc = lax.dynamic_slice_in_dim(w_fc[0], core * 512, 512, 0)
-    came_fc = exchanged(half_fc, swapped)
-    laid = {}
-
-    def fc_after(projected):
-        laid["fc"] = spread_fc(here, w_fc[0], came_fc, projected)
-        return laid["fc"][0]
-
-    def proj_after(context):
-        half = lax.dynamic_slice_in_dim(w_proj[0], core * 256, 256, 0)
-        came = exchanged(half, (context, *came_fc))
-        laid["proj"] = spread_proj(here, w_proj[0], came)
-        return laid["proj"][0]
+    half_proj = lax.dynamic_slice_in_dim(w_proj[0], core * 256, 256, 0)
+    coming, laid = {}, {}
+
+    def first_hook(step, value):
+        if step == 0:
+            sent = held(half_fc, *swapped)
+            coming["fc"] = [along_z(sent, by) for by in ORDER[:2]]
+            return held(value, *coming["fc"])
+        if step == 1:
+            coming["fc"].append(along_z(held(half_fc, *coming["fc"]), ORDER[2]))
+            return held(value, *coming["fc"])
+        if step == 2:
+            laid["fc"] = lay_fc(here, w_fc[0], coming["fc"])
+            sent = held(half_proj, *coming["fc"])
+            coming["proj"] = [along_z(sent, by) for by in ORDER[:2]]
+            return held(value, *coming["proj"])
+        coming["proj"].append(along_z(held(half_proj, *coming["proj"]), ORDER[2]))
+        laid["proj"] = lay_proj(here, w_proj[0], coming["proj"])
+        return held(value, coming["proj"][2]), laid["fc"][0], laid["proj"][0]
+
+    def second_hook(step, value):
+        return value if step < 3 else (value, laid["fc"][1], laid["proj"][1])
 
     vectors = []
     for layer in range(2):
@@ -480,7 +491,7 @@
         vectors.append(norms + (qkv_bias, flat[:, 6400:6912].reshape(-1)))
 
     first, weights_first, saved_first = layer_forward(
-        stream, allowed, vectors[0], all_qkv[0], all_out[0], fc_after, proj_after
+        stream, allowed, vectors[0], all_qkv[0], all_out[0], first_hook
     )
     second, weights_second, saved_second = layer_forward(
         first.astype(f32),
@@ -488,8 +499,7 @@
         vectors[1],
         all_qkv[1],
         all_out[1],
-        lambda after: laid["fc"][1],
-        lambda after: laid["proj"][1],
+        second_hook,
     )
     waiting = {}
 
@@ -511,25 +521,28 @@
             kept["one"] = jnp.concatenate(halved, axis=2)
             return held(value, kept["one"])
         if step == 1:
-            kept["one"] = over_y(kept["one"])
-            kept["feed"] = over_cores(group, core)
-            return held(value, kept["one"])
+            kept["near"] = near_y(kept["one"])
+            kept["feed"] = group
+            return value
         if step == 2:
-            kept["one"] = over_z(kept["one"], 1, pipe, high)
+            return held(value, kept["near"])
+        if step == 3:
+            kept["one"] = far_y(kept["one"], kept["near"])
+            kept["feed"] = over_cores(kept["feed"], core)
             return held(value, kept["one"], kept["feed"])
-        if step == 3:
-            return value
-        kept["feed"] = over_y(kept["feed"])
+        kept["near"] = near_y(kept["feed"])
         kept["attention"] = over_cores(group, core)
-        return held(value, kept["feed"], kept["attention"])
+        return held(value, kept["near"], kept["attention"])
 
     last_grad, early_zero, late_zero = layer_backward(
         middle_low.astype(f32), allowed, vectors[0], weights_first, saved_first, reduce_along
     )
     last_low = last_grad.astype(bf16)
-    zero = jnp.concatenate([kept["feed"], over_y(kept["attention"])], axis=1)
-    zero = over_z(zero, 0, pipe, high)
-    total = back_over_y(jnp.where(pipe == 1, kept["one"], zero))
+    one = over_z(kept["one"], 1, pipe, high)
+    feed = far_y(kept["feed"], kept["near"])
+    attention = far_y(kept["attention"], near_y(kept["attention"]))
+    zero = over_z(jnp.concatenate([feed, attention], axis=1), 0, pipe, high)
+    total = back_over_y(jnp.where(pipe == 1, one, zero))
 
     def bias_rows(fc_bias_grad):
         return place(jnp.zeros((4, WIDTH), f32), fc_bias_grad[None], (x, 0))

time: 523 us -> 517 us (0.989)
  the two profiles are of different devices: /device:TPU:1 before, /device:TPU:0 now
where the time goes in v4:
time: 517 us; the launch traced here: 507 us
  waiting for transfers between devices  169 us (33%)
  starting transfers between devices  159 us (31%)
  local copies, waits for them, and re-layouts  59.2 us (11%)
  other arithmetic  59.1 us (11%)
  matrix products  51.5 us (10%)
  Pallas kernels  6.43 us (1%)
    ppermute x106, waiting for transfers between devices, move(): return lax.ppermute(array, axes, sorted(pairs.items()))  169 us
    ppermute x106, starting transfers between devices, move(): return lax.ppermute(array, axes, sorted(pairs.items()))  159 us
    dot_general x24, matrix products, dot(): lax.dot_general(left, right, (((left_dim,), (right_dim,)), ((), ())), pre...  37.6 us
    unnamed x252, local copies, waits for them, and re-layouts  27.4 us
  transfers between devices with their start and end apart: 106, of which 50 were waited for; matrix products, arithmetic and copies ran while one was open for 24% of the time, Pallas kernels for 1%

profile of v4, /device:TPU:0, one launch (start us, length us, event | category | flops | bytes accessed | tf_op | source)
XLA Modules:
  0.0 507.2 jit_solution(16951871701937873608)
XLA Ops:
  20.8 14.8 %collective-permute-start.4 = (bf16[528,512]{1,0:T(8,128)(2,1)}, bf16[528,512]{1,0:T(8,128)(2,1)S(1)}, u32[]{:S(2)}, u32[]{:S(2)}) collective-permute-start(bf16[528,512]{1,0:T(8,128)(2,1)} %collective-permute-done.1.refs_3_), channel_id=1, source_target_pairs={{0,1},{1,0},{2,3},{3,2},{4,5},{5,4},{6,7},{7,6},{8,9},{9,8},{10,11... | collective-permute-start | bytes 1622024 | tf_op jit(solution)/shard_map/ppermute | solution.py:38
  44.8 2.8 collective-permute-start.9
  51.3 5.3 %collective-permute-done.9 = bf16[96,1024]{1,0:T(8,128)(2,1)S(1)} collective-permute-done((bf16[96,1024]{1,0:T(8,128)(2,1)S(1)}, bf16[96,1024]{1,0:T(8,128)(2,1)S(1)}, u32[]{:S(2)}, u32[]{:S(2)}) %collective-permute-start.9) | collective-permute-done | bytes 196640 | tf_op jit(solution)/shard_map/ppermute | solution.py:38
  60.4 3.2 fusion.80
  74.9 11.3 %collective-permute-done.14.refs_3_ = bf16[512,512]{1,0:T(8,128)(2,1)S(1)} collective-permute-done((bf16[512,512]{1,0:T(8,128)(2,1)}, bf16[512,512]{1,0:T(8,128)(2,1)S(1)}, u32[]{:S(2)}, u32[]{:S(2)}) %collective-permute-start.14) | collective-permute-done | bytes 524320 | tf_op jit(solution)/shard_map/ppermute | solution.py:38
  93.4 3.4 collective-permute-start.16
  96.9 4.4 collective-permute-done.18.refs_1_
  103.6 3.0 collective-permute-start.44
  110.4 5.4 %collective-permute-done.23.refs_3_ = bf16[256,1024]{1,0:T(8,128)(2,1)} collective-permute-done((bf16[256,1024]{1,0:T(8,128)(2,1)}, bf16[256,1024]{1,0:T(8,128)(2,1)}, u32[]{:S(2)}, u32[]{:S(2)}) %collective-permute-start.23) | collective-permute-done | bytes 524320 | tf_op jit(solution)/shard_map/ppermute | solution.py:38
  120.3 5.4 %collective-permute-done.22 = bf16[96,1024]{1,0:T(8,128)(2,1)S(1)} collective-permute-done((bf16[96,1024]{1,0:T(8,128)(2,1)S(1)}, bf16[96,1024]{1,0:T(8,128)(2,1)S(1)}, u32[]{:S(2)}, u32[]{:S(2)}) %collective-permute-start.22) | collective-permute-done | bytes 196640 | tf_op jit(solution)/shard_map/ppermute | solution.py:38
  145.5 6.2 %collective-permute-done.28 = bf16[96,1024]{1,0:T(8,128)(2,1)S(1)} collective-permute-done((bf16[96,1024]{1,0:T(8,128)(2,1)S(1)}, bf16[96,1024]{1,0:T(8,128)(2,1)S(1)}, u32[]{:S(2)}, u32[]{:S(2)}) %collective-permute-start.28) | collective-permute-done | bytes 196640 | tf_op jit(solution)/shard_map/ppermute | solution.py:38
  157.6 2.9 collective-permute-start.47
  165.1 2.9 collective-permute-done.29
  186.3 9.5 %collective-permute-done.35 = bf16[96,1024]{1,0:T(8,128)(2,1)S(1)} collective-permute-done((bf16[96,1024]{1,0:T(8,128)(2,1)S(1)}, bf16[96,1024]{1,0:T(8,128)(2,1)S(1)}, u32[]{:S(2)}, u32[]{:S(2)}) %collective-permute-start.35) | collective-permute-done | bytes 196640 | tf_op jit(solution)/shard_map/ppermute | solution.py:38
  200.3 7.4 %collective-permute-done.38 = bf16[96,1024]{1,0:T(8,128)(2,1)S(1)} collective-permute-done((bf16[96,1024]{1,0:T(8,128)(2,1)S(1)}, bf16[96,1024]{1,0:T(8,128)(2,1)S(1)}, u32[]{:S(2)}, u32[]{:S(2)}) %collective-permute-start.38) | collective-permute-done | bytes 196640 | tf_op jit(solution)/shard_map/ppermute | solution.py:38
  216.3 2.8 convolution_convert_fusion.2
  219.3 2.7 collective-permute-start.40
  231.0 3.3 fusion.19
  234.3 5.3 %collective-permute-done.50 = bf16[96,1024]{1,0:T(8,128)(2,1)S(1)} collective-permute-done((bf16[96,1024]{1,0:T(8,128)(2,1)}, bf16[96,1024]{1,0:T(8,128)(2,1)S(1)}, u32[]{:S(2)}, u32[]{:S(2)}) %collective-permute-start.50) | collective-permute-done | bytes 196640 | tf_op jit(solution)/shard_map/ppermute | solution.py:38
  243.5 3.9 collective-permute-start.52
  253.1 3.8 collective-permute-done.51
  267.8 4.7 collective-permute-start.57
  272.5 2.9 collective-permute-start.55
  278.9 3.1 collective-permute-done.56
  284.2 2.8 collective-permute-start.60
  290.9 2.8 concatenate.156
  293.6 2.7 collective-permute-done.59
  296.4 3.0 collective-permute-done.58
  300.5 4.3 convert_reduce_fusion.1
  310.3 2.8 convolution_convert_fusion
  313.0 5.0 collective-permute-done.65
  326.2 3.0 collective-permute-start.70
  364.2 15.1 %collective-permute-done.72 = bf16[2,192,1024]{2,1,0:T(8,128)(2,1)S(1)} collective-permute-done((bf16[2,192,1024]{2,1,0:T(8,128)(2,1)S(1)}, bf16[2,192,1024]{2,1,0:T(8,128)(2,1)S(1)}, u32[]{:S(2)}, u32[]{:S(2)}) %collective-permute-start.72) | collective-permute-done | bytes 786464 | tf_op jit(solution)/shard_map/ppermute | solution.py:38
  389.5 3.5 collective-permute-start.75
  402.2 8.1 %collective-permute-start.93 = (bf16[192,1024]{1,0:T(8,128)(2,1)}, bf16[192,1024]{1,0:T(8,128)(2,1)S(1)}, u32[]{:S(2)}, u32[]{:S(2)}) collective-permute-start(bf16[192,1024]{1,0:T(8,128)(2,1)} %get-tuple-element.131), channel_id=1, source_target_pairs={{0,72},{8,64},{16,88},{24,80},{32,104},{40,96},{48,120},{56,112},{... | collective-permute-start | bytes 1179656 | tf_op jit(solution)/shard_map/ppermute | solution.py:38
  411.6 2.9 collective-permute-done.97
  414.4 4.2 collective-permute-start.92
  421.2 6.0 %collective-permute-done.98 = bf16[2,64,1024]{2,1,0:T(8,128)(2,1)S(1)} collective-permute-done((bf16[2,64,1024]{2,1,0:T(8,128)(2,1)S(1)}, bf16[2,64,1024]{2,1,0:T(8,128)(2,1)S(1)}, u32[]{:S(2)}, u32[]{:S(2)}) %collective-permute-start.98) | collective-permute-done | bytes 262176 | tf_op jit(solution)/shard_map/ppermute | solution.py:38
  428.1 3.6 collective-permute-start.101
  434.9 5.4 %collective-permute-start.83 = (f32[12,1024]{1,0:T(8,128)S(1)}, f32[12,1024]{1,0:T(8,128)S(1)}, u32[]{:S(2)}, u32[]{:S(2)}) collective-permute-start(f32[12,1024]{1,0:T(8,128)S(1)} %get-tuple-element.173), channel_id=1, source_target_pairs={{0,72},{8,64},{16,88},{24,80},{32,104},{40,96},{48,120},{56,112},{... | collective-permute-start | bytes 147464 | tf_op jit(solution)/shard_map/ppermute | solution.py:38
  442.9 7.6 %collective-permute-done.100 = bf16[192,1024]{1,0:T(8,128)(2,1)} collective-permute-done((bf16[192,1024]{1,0:T(8,128)(2,1)}, bf16[192,1024]{1,0:T(8,128)(2,1)}, u32[]{:S(2)}, u32[]{:S(2)}) %collective-permute-start.100) | collective-permute-done | bytes 393248 | tf_op jit(solution)/shard_map/ppermute | solution.py:38
  452.5 3.6 collective-permute-start.102
  459.2 7.4 %collective-permute-done.102 = bf16[192,1024]{1,0:T(8,128)(2,1)S(1)} collective-permute-done((bf16[192,1024]{1,0:T(8,128)(2,1)S(1)}, bf16[192,1024]{1,0:T(8,128)(2,1)S(1)}, u32[]{:S(2)}, u32[]{:S(2)}) %collective-permute-start.102) | collective-permute-done | bytes 393248 | tf_op jit(solution)/shard_map/ppermute | solution.py:38
  466.6 9.6 %collective-permute-done.103 = bf16[192,1024]{1,0:T(8,128)(2,1)S(1)} collective-permute-done((bf16[192,1024]{1,0:T(8,128)(2,1)S(1)}, bf16[192,1024]{1,0:T(8,128)(2,1)S(1)}, u32[]{:S(2)}, u32[]{:S(2)}) %collective-permute-start.103) | collective-permute-done | bytes 393248 | tf_op jit(solution)/shard_map/ppermute | solution.py:38
  477.2 3.2 collective-permute-start.87
  482.9 3.0 collective-permute-done.86
  490.7 3.2 collective-permute-done.90
  499.1 3.0 copy.63
  (640 shorter events, 267.2 us)
Async XLA Ops:
  4.1 16.7 %collective-permute-start.1 = (bf16[528,512]{1,0:T(8,128)(2,1)}, bf16[528,512]{1,0:T(8,128)(2,1)}, u32[]{:S(2)}, u32[]{:S(2)}) collective-permute-start(bf16[528,512]{1,0:T(8,128)(2,1)} %pad_maximum_fusion.16), channel_id=1, source_target_pairs={{0,64},{8,72},{16,80},{24,88},{32,96},{40,104},{48,112},{56,120},{... | collective-permute-start | bytes 1622024 | tf_op jit(solution)/shard_map/ppermute | solution.py:38
  6.1 29.5 %collective-permute-start.2 = (bf16[528,512]{1,0:T(8,128)(2,1)}, bf16[528,512]{1,0:T(8,128)(2,1)}, u32[]{:S(2)}, u32[]{:S(2)}) collective-permute-start(bf16[528,512]{1,0:T(8,128)(2,1)} %pad_maximum_fusion.16), channel_id=1, source_target_pairs={{0,72},{8,64},{16,88},{24,80},{32,104},{40,96},{48,120},{56,112},{... | collective-permute-start | bytes 1622024 | tf_op jit(solution)/shard_map/ppermute | solution.py:38
  8.2 27.5 %collective-permute-start.3 = (bf16[528,512]{1,0:T(8,128)(2,1)}, bf16[528,512]{1,0:T(8,128)(2,1)}, u32[]{:S(2)}, u32[]{:S(2)}) collective-permute-start(bf16[528,512]{1,0:T(8,128)(2,1)} %pad_maximum_fusion.16), channel_id=1, source_target_pairs={{0,8},{8,0},{16,24},{24,16},{32,40},{40,32},{48,56},{56,48},{64,72... | collective-permute-start | bytes 1622024 | tf_op jit(solution)/shard_map/ppermute | solution.py:38
  12.4 56.6 %collective-permute-start.13 = (s32[8,96]{1,0:T(8,128)S(1)}, s32[8,96]{1,0:T(8,128)S(1)}, u32[]{:S(2)}, u32[]{:S(2)}) collective-permute-start(s32[8,96]{1,0:T(8,128)S(1)} %reshape.698), channel_id=1, source_target_pairs={{0,1},{1,0},{2,3},{3,2},{4,5},{5,4},{6,7},{7,6},{8,9},{9,8},{10,11... | collective-permute-start | bytes 9224 | tf_op jit(solution)/shard_map/ppermute | solution.py:38
  20.8 16.6 %collective-permute-start.4 = (bf16[528,512]{1,0:T(8,128)(2,1)}, bf16[528,512]{1,0:T(8,128)(2,1)S(1)}, u32[]{:S(2)}, u32[]{:S(2)}) collective-permute-start(bf16[528,512]{1,0:T(8,128)(2,1)} %collective-permute-done.1.refs_3_), channel_id=1, source_target_pairs={{0,1},{1,0},{2,3},{3,2},{4,5},{5,4},{6,7},{7,6},{8,9},{9,8},{10,11... | collective-permute-start | bytes 1622024 | tf_op jit(solution)/shard_map/ppermute | solution.py:38
  50.1 20.0 %collective-permute-start.11 = (bf16[512,512]{1,0:T(8,128)(2,1)}, bf16[512,512]{1,0:T(8,128)(2,1)S(1)}, u32[]{:S(2)}, u32[]{:S(2)}) collective-permute-start(bf16[512,512]{1,0:T(8,128)(2,1)} %dynamic-slice_bitcast_fusion.4), channel_id=1, source_target_pairs={{0,64},{8,72},{16,80},{24,88},{32,96},{40,104},{48,112},{56,120},{... | collective-permute-start | bytes 1572872 | tf_op jit(solution)/shard_map/ppermute | solution.py:38
  56.6 13.5 %collective-permute-start.12 = (bf16[512,512]{1,0:T(8,128)(2,1)}, bf16[512,512]{1,0:T(8,128)(2,1)}, u32[]{:S(2)}, u32[]{:S(2)}) collective-permute-start(bf16[512,512]{1,0:T(8,128)(2,1)} %dynamic-slice_bitcast_fusion.4), channel_id=1, source_target_pairs={{0,72},{8,64},{16,88},{24,80},{32,104},{40,96},{48,120},{56,112},{... | collective-permute-start | bytes 1572872 | tf_op jit(solution)/shard_map/ppermute | solution.py:38
  70.1 16.1 %collective-permute-start.14 = (bf16[512,512]{1,0:T(8,128)(2,1)}, bf16[512,512]{1,0:T(8,128)(2,1)S(1)}, u32[]{:S(2)}, u32[]{:S(2)}) collective-permute-start(bf16[512,512]{1,0:T(8,128)(2,1)} %dynamic-slice_bitcast_fusion.4), channel_id=1, source_target_pairs={{0,8},{8,0},{16,24},{24,16},{32,40},{40,32},{48,56},{56,48},{64,72... | collective-permute-start | bytes 1572872 | tf_op jit(solution)/shard_map/ppermute | solution.py:38
  86.2 15.1 %collective-permute-start.18 = (bf16[256,1024]{1,0:T(8,128)(2,1)}, bf16[256,1024]{1,0:T(8,128)(2,1)}, u32[]{:S(2)}, u32[]{:S(2)}) collective-permute-start(bf16[256,1024]{1,0:T(8,128)(2,1)} %dynamic-slice_bitcast_fusion.3), channel_id=1, source_target_pairs={{0,64},{8,72},{16,80},{24,88},{32,96},{40,104},{48,112},{56,120},{... | collective-permute-start | bytes 1572872 | tf_op jit(solution)/shard_map/ppermute | solution.py:38
  87.4 13.9 %collective-permute-start.19 = (bf16[256,1024]{1,0:T(8,128)(2,1)}, bf16[256,1024]{1,0:T(8,128)(2,1)}, u32[]{:S(2)}, u32[]{:S(2)}) collective-permute-start(bf16[256,1024]{1,0:T(8,128)(2,1)} %dynamic-slice_bitcast_fusion.3), channel_id=1, source_target_pairs={{0,72},{8,64},{16,88},{24,80},{32,104},{40,96},{48,120},{56,112},{... | collective-permute-start | bytes 1572872 | tf_op jit(solution)/shard_map/ppermute | solution.py:38
  93.4 14.4 %collective-permute-start.17 = (bf16[96,1024]{1,0:T(8,128)(2,1)}, bf16[96,1024]{1,0:T(8,128)(2,1)}, u32[]{:S(2)}, u32[]{:S(2)}) collective-permute-start(bf16[96,1024]{1,0:T(8,128)(2,1)} %get-tuple-element.158), channel_id=1, source_target_pairs={{0,16},{8,24},{16,32},{24,40},{32,48},{40,56},{48,0},{56,8},{1,17}... | collective-permute-start | bytes 589832 | tf_op jit(solution)/shard_map/ppermute | solution.py:38
  93.4 15.6 %collective-permute-start.16 = (bf16[96,1024]{1,0:T(8,128)(2,1)}, bf16[96,1024]{1,0:T(8,128)(2,1)}, u32[]{:S(2)}, u32[]{:S(2)}) collective-permute-start(bf16[96,1024]{1,0:T(8,128)(2,1)} %get-tuple-element.159), channel_id=1, source_target_pairs={{0,32},{8,40},{16,48},{24,56},{32,0},{40,8},{48,16},{56,24},{1,33}... | collective-permute-start | bytes 589832 | tf_op jit(solution)/shard_map/ppermute | solution.py:38
  101.3 14.5 %collective-permute-start.23 = (bf16[256,1024]{1,0:T(8,128)(2,1)}, bf16[256,1024]{1,0:T(8,128)(2,1)}, u32[]{:S(2)}, u32[]{:S(2)}) collective-permute-start(bf16[256,1024]{1,0:T(8,128)(2,1)} %dynamic-slice_bitcast_fusion.3), channel_id=1, source_target_pairs={{0,8},{8,0},{16,24},{24,16},{32,40},{40,32},{48,56},{56,48},{64,72... | collective-permute-start | bytes 1572872 | tf_op jit(solution)/shard_map/ppermute | solution.py:38
  103.6 15.9 %collective-permute-start.44 = (bf16[96,1024]{1,0:T(8,128)(2,1)}, bf16[96,1024]{1,0:T(8,128)(2,1)}, u32[]{:S(2)}, u32[]{:S(2)}) collective-permute-start(bf16[96,1024]{1,0:T(8,128)(2,1)} %dynamic-slice_bitcast_fusion.10), channel_id=1, source_target_pairs={{0,0},{1,8},{2,2},{3,10},{4,4},{5,12},{6,6},{7,14},{8,1},{9,9},{10... | collective-permute-start | bytes 589832 | tf_op jit(solution)/shard_map/ppermute | solution.py:38
  107.8 23.5 %collective-permute-start.24 = (bf16[3,512,512]{2,1,0:T(8,128)(2,1)S(1)}, bf16[3,512,512]{2,1,0:T(8,128)(2,1)S(1)}, u32[]{:S(2)}, u32[]{:S(2)}) collective-permute-start(bf16[3,512,512]{2,1,0:T(8,128)(2,1)S(1)} %pad_maximum_fusion.1), channel_id=1, source_target_pairs={{0,1},{1,0},{2,3},{3,2},{4,5},{5,4},{6,7},{7,6},{8,9},{9,8},{10,11... | collective-permute-start | bytes 4718600 | tf_op jit(solution)/shard_map/ppermute | solution.py:38
  117.3 18.0 %collective-permute-start.25 = (bf16[3,256,1024]{2,1,0:T(8,128)(2,1)S(1)}, bf16[3,256,1024]{2,1,0:T(8,128)(2,1)S(1)}, u32[]{:S(2)}, u32[]{:S(2)}) collective-permute-start(bf16[3,256,1024]{2,1,0:T(8,128)(2,1)S(1)} %pad_maximum_fusion.2), channel_id=1, source_target_pairs={{0,1},{1,0},{2,3},{3,2},{4,5},{5,4},{6,7},{7,6},{8,9},{9,8},{10,11... | collective-permute-start | bytes 4718600 | tf_op jit(solution)/shard_map/ppermute | solution.py:38
  125.8 31.8 %collective-permute-start.45 = (bf16[96,1024]{1,0:T(8,128)(2,1)}, bf16[96,1024]{1,0:T(8,128)(2,1)S(1)}, u32[]{:S(2)}, u32[]{:S(2)}) collective-permute-start(bf16[96,1024]{1,0:T(8,128)(2,1)} %collective-permute-done.44), channel_id=1, source_target_pairs={{0,16},{8,24},{16,32},{24,40},{32,48},{40,56},{48,0},{56,8},{1,17}... | collective-permute-start | bytes 589832 | tf_op jit(solution)/shard_map/ppermute | solution.py:38
  127.4 45.2 %collective-permute-start.46 = (bf16[96,1024]{1,0:T(8,128)(2,1)}, bf16[96,1024]{1,0:T(8,128)(2,1)}, u32[]{:S(2)}, u32[]{:S(2)}) collective-permute-start(bf16[96,1024]{1,0:T(8,128)(2,1)} %collective-permute-done.44), channel_id=1, source_target_pairs={{0,32},{8,40},{16,48},{24,56},{32,0},{40,8},{48,16},{56,24},{1,33}... | collective-permute-start | bytes 589832 | tf_op jit(solution)/shard_map/ppermute | solution.py:38
  157.6 16.6 %collective-permute-start.47 = (bf16[96,1024]{1,0:T(8,128)(2,1)}, bf16[96,1024]{1,0:T(8,128)(2,1)}, u32[]{:S(2)}, u32[]{:S(2)}) collective-permute-start(bf16[96,1024]{1,0:T(8,128)(2,1)} %collective-permute-done.44), channel_id=1, source_target_pairs={{0,48},{8,56},{16,0},{24,8},{32,16},{40,24},{48,32},{56,40},{1,49}... | collective-permute-start | bytes 589832 | tf_op jit(solution)/shard_map/ppermute | solution.py:38
  219.2 24.3 %collective-permute-start.41 = (bf16[96,1024]{1,0:T(8,128)(2,1)S(1)}, bf16[96,1024]{1,0:T(8,128)(2,1)}, u32[]{:S(2)}, u32[]{:S(2)}) collective-permute-start(bf16[96,1024]{1,0:T(8,128)(2,1)S(1)} %get-tuple-element.147), channel_id=1, source_target_pairs={{0,16},{8,24},{16,32},{24,40},{32,48},{40,56},{48,0},{56,8},{1,17}... | collective-permute-start | bytes 589832 | tf_op jit(solution)/shard_map/ppermute | solution.py:38
  219.3 28.1 %collective-permute-start.40 = (bf16[96,1024]{1,0:T(8,128)(2,1)S(1)}, bf16[96,1024]{1,0:T(8,128)(2,1)}, u32[]{:S(2)}, u32[]{:S(2)}) collective-permute-start(bf16[96,1024]{1,0:T(8,128)(2,1)S(1)} %get-tuple-element.148), channel_id=1, source_target_pairs={{0,32},{8,40},{16,48},{24,56},{32,0},{40,8},{48,16},{56,24},{1,33}... | collective-permute-start | bytes 589832 | tf_op jit(solution)/shard_map/ppermute | solution.py:38
  223.9 15.7 %collective-permute-start.50 = (bf16[96,1024]{1,0:T(8,128)(2,1)}, bf16[96,1024]{1,0:T(8,128)(2,1)S(1)}, u32[]{:S(2)}, u32[]{:S(2)}) collective-permute-start(bf16[96,1024]{1,0:T(8,128)(2,1)} %get-tuple-element.144), channel_id=1, source_target_pairs={{0,16},{8,24},{16,32},{24,40},{32,48},{40,56},{48,0},{56,8},{1,17}... | collective-permute-start | bytes 589832 | tf_op jit(solution)/shard_map/ppermute | solution.py:38
  225.7 13.9 %collective-permute-start.49 = (bf16[96,1024]{1,0:T(8,128)(2,1)}, bf16[96,1024]{1,0:T(8,128)(2,1)}, u32[]{:S(2)}, u32[]{:S(2)}) collective-permute-start(bf16[96,1024]{1,0:T(8,128)(2,1)} %get-tuple-element.145), channel_id=1, source_target_pairs={{0,32},{8,40},{16,48},{24,56},{32,0},{40,8},{48,16},{56,24},{1,33}... | collective-permute-start | bytes 589832 | tf_op jit(solution)/shard_map/ppermute | solution.py:38
  239.6 81.8 %collective-permute-start.61 = (bf16[2,512,1024]{2,1,0:T(8,128)(2,1)}, bf16[2,512,1024]{2,1,0:T(8,128)(2,1)}, u32[]{:S(2)}, u32[]{:S(2)}) collective-permute-start(bf16[2,512,1024]{2,1,0:T(8,128)(2,1)} %fusion.19), channel_id=1, source_target_pairs={{0,1},{1,0},{2,3},{3,2},{4,5},{5,4},{6,7},{7,6},{8,9},{9,8},{10,11... | collective-permute-start | bytes 6291464 | tf_op jit(solution)/shard_map/ppermute | solution.py:38
  248.8 14.6 %collective-permute-start.43 = (bf16[96,1024]{1,0:T(8,128)(2,1)S(1)}, bf16[96,1024]{1,0:T(8,128)(2,1)S(1)}, u32[]{:S(2)}, u32[]{:S(2)}) collective-permute-start(bf16[96,1024]{1,0:T(8,128)(2,1)S(1)} %broadcast_select_fusion.2), channel_id=1, source_target_pairs={{0,64},{1,72},{2,66},{3,74},{4,68},{5,76},{6,70},{7,78},{8,65},{9,... | collective-permute-start | bytes 589832 | tf_op jit(solution)/shard_map/ppermute | solution.py:38
  278.7 40.9 %collective-permute-start.62 = (bf16[2,256,1024]{2,1,0:T(8,128)(2,1)}, bf16[2,256,1024]{2,1,0:T(8,128)(2,1)}, u32[]{:S(2)}, u32[]{:S(2)}) collective-permute-start(bf16[2,256,1024]{2,1,0:T(8,128)(2,1)} %fusion.92), channel_id=1, source_target_pairs={{0,1},{1,0},{2,3},{3,2},{4,5},{5,4},{6,7},{7,6},{8,9},{9,8},{10,11... | collective-permute-start | bytes 3145736 | tf_op jit(solution)/shard_map/ppermute | solution.py:38
  326.2 20.5 %collective-permute-start.70 = (bf16[2,192,1024]{2,1,0:T(8,128)(2,1)}, bf16[2,192,1024]{2,1,0:T(8,128)(2,1)}, u32[]{:S(2)}, u32[]{:S(2)}) collective-permute-start(bf16[2,192,1024]{2,1,0:T(8,128)(2,1)} %get-tuple-element.121), channel_id=1, source_target_pairs={{0,6},{1,7},{2,0},{3,1},{4,2},{5,3},{6,4},{7,5},{8,14},{9,15},{10,... | collective-permute-start | bytes 2359304 | tf_op jit(solution)/shard_map/ppermute | solution.py:38
  329.2 19.6 %collective-permute-start.69 = (bf16[2,192,1024]{2,1,0:T(8,128)(2,1)}, bf16[2,192,1024]{2,1,0:T(8,128)(2,1)}, u32[]{:S(2)}, u32[]{:S(2)}) collective-permute-start(bf16[2,192,1024]{2,1,0:T(8,128)(2,1)} %get-tuple-element.120), channel_id=1, source_target_pairs={{0,2},{1,3},{2,4},{3,5},{4,6},{5,7},{6,0},{7,1},{8,10},{9,11},{10,... | collective-permute-start | bytes 2359304 | tf_op jit(solution)/shard_map/ppermute | solution.py:38
  342.0 16.6 %collective-permute-start.73 = (bf16[2,512,1024]{2,1,0:T(8,128)(2,1)S(1)}, bf16[2,512,1024]{2,1,0:T(8,128)(2,1)S(1)}, u32[]{:S(2)}, u32[]{:S(2)}) collective-permute-start(bf16[2,512,1024]{2,1,0:T(8,128)(2,1)S(1)} %fusion.15), channel_id=1, source_target_pairs={{0,1},{1,0},{2,3},{3,2},{4,5},{5,4},{6,7},{7,6},{8,9},{9,8},{10,11... | collective-permute-start | bytes 6291464 | tf_op jit(solution)/shard_map/ppermute | solution.py:38
  357.3 22.0 %collective-permute-start.72 = (bf16[2,192,1024]{2,1,0:T(8,128)(2,1)S(1)}, bf16[2,192,1024]{2,1,0:T(8,128)(2,1)S(1)}, u32[]{:S(2)}, u32[]{:S(2)}) collective-permute-start(bf16[2,192,1024]{2,1,0:T(8,128)(2,1)S(1)} %copy-done.48), channel_id=1, source_target_pairs={{0,4},{1,5},{2,6},{3,7},{4,0},{5,1},{6,2},{7,3},{8,12},{9,13},{10,... | collective-permute-start | bytes 2359304 | tf_op jit(solution)/shard_map/ppermute | solution.py:38
  361.9 33.3 %collective-permute-start.78 = (bf16[2,128,1024]{2,1,0:T(8,128)(2,1)}, bf16[2,128,1024]{2,1,0:T(8,128)(2,1)}, u32[]{:S(2)}, u32[]{:S(2)}) collective-permute-start(bf16[2,128,1024]{2,1,0:T(8,128)(2,1)} %get-tuple-element.125), channel_id=1, source_target_pairs={{0,6},{1,7},{2,0},{3,1},{4,2},{5,3},{6,4},{7,5},{8,14},{9,15},{10,... | collective-permute-start | bytes 1572872 | tf_op jit(solution)/shard_map/ppermute | solution.py:38
  363.6 31.7 %collective-permute-start.77 = (bf16[2,128,1024]{2,1,0:T(8,128)(2,1)}, bf16[2,128,1024]{2,1,0:T(8,128)(2,1)}, u32[]{:S(2)}, u32[]{:S(2)}) collective-permute-start(bf16[2,128,1024]{2,1,0:T(8,128)(2,1)} %get-tuple-element.126), channel_id=1, source_target_pairs={{0,2},{1,3},{2,4},{3,5},{4,6},{5,7},{6,0},{7,1},{8,10},{9,11},{10,... | collective-permute-start | bytes 1572872 | tf_op jit(solution)/shard_map/ppermute | solution.py:38
  396.9 24.0 %collective-permute-start.95 = (bf16[2,128,1024]{2,1,0:T(8,128)(2,1)S(1)}, bf16[2,128,1024]{2,1,0:T(8,128)(2,1)S(1)}, u32[]{:S(2)}, u32[]{:S(2)}) collective-permute-start(bf16[2,128,1024]{2,1,0:T(8,128)(2,1)S(1)} %copy-done.57), channel_id=1, source_target_pairs={{0,4},{1,5},{2,6},{3,7},{4,0},{5,1},{6,2},{7,3},{8,12},{9,13},{10,... | collective-permute-start | bytes 1572872 | tf_op jit(solution)/shard_map/ppermute | solution.py:38
  399.0 15.4 %collective-permute-start.97 = (bf16[2,64,1024]{2,1,0:T(8,128)(2,1)S(1)}, bf16[2,64,1024]{2,1,0:T(8,128)(2,1)S(1)}, u32[]{:S(2)}, u32[]{:S(2)}) collective-permute-start(bf16[2,64,1024]{2,1,0:T(8,128)(2,1)S(1)} %get-tuple-element.128), channel_id=1, source_target_pairs={{0,6},{1,7},{2,0},{3,1},{4,2},{5,3},{6,4},{7,5},{8,14},{9,15},{10,... | collective-permute-start | bytes 786440 | tf_op jit(solution)/shard_map/ppermute | solution.py:38
  400.8 17.9 %collective-permute-start.96 = (bf16[2,64,1024]{2,1,0:T(8,128)(2,1)S(1)}, bf16[2,64,1024]{2,1,0:T(8,128)(2,1)S(1)}, u32[]{:S(2)}, u32[]{:S(2)}) collective-permute-start(bf16[2,64,1024]{2,1,0:T(8,128)(2,1)S(1)} %get-tuple-element.129), channel_id=1, source_target_pairs={{0,2},{1,3},{2,4},{3,5},{4,6},{5,7},{6,0},{7,1},{8,10},{9,11},{10,... | collective-permute-start | bytes 786440 | tf_op jit(solution)/shard_map/ppermute | solution.py:38
  401.5 31.6 %collective-permute-start.94 = (bf16[192,1024]{1,0:T(8,128)(2,1)}, bf16[192,1024]{1,0:T(8,128)(2,1)S(1)}, u32[]{:S(2)}, u32[]{:S(2)}) collective-permute-start(bf16[192,1024]{1,0:T(8,128)(2,1)} %get-tuple-element.131), channel_id=1, source_target_pairs={{64,72},{72,64},{80,88},{88,80},{96,104},{104,96},{112,120},{120,1... | collective-permute-start | bytes 1179656 | tf_op jit(solution)/shard_map/ppermute | solution.py:38
  402.2 32.6 %collective-permute-start.93 = (bf16[192,1024]{1,0:T(8,128)(2,1)}, bf16[192,1024]{1,0:T(8,128)(2,1)S(1)}, u32[]{:S(2)}, u32[]{:S(2)}) collective-permute-start(bf16[192,1024]{1,0:T(8,128)(2,1)} %get-tuple-element.131), channel_id=1, source_target_pairs={{0,72},{8,64},{16,88},{24,80},{32,104},{40,96},{48,120},{56,112},{... | collective-permute-start | bytes 1179656 | tf_op jit(solution)/shard_map/ppermute | solution.py:38
  414.4 25.8 %collective-permute-start.92 = (bf16[192,1024]{1,0:T(8,128)(2,1)S(1)}, bf16[192,1024]{1,0:T(8,128)(2,1)S(1)}, u32[]{:S(2)}, u32[]{:S(2)}) collective-permute-start(bf16[192,1024]{1,0:T(8,128)(2,1)S(1)} %get-tuple-element.130), channel_id=1, source_target_pairs={{0,64},{8,72},{16,80},{24,88},{32,96},{40,104},{48,112},{56,120},{... | collective-permute-start | bytes 1179656 | tf_op jit(solution)/shard_map/ppermute | solution.py:38
  431.8 18.8 %collective-permute-start.100 = (bf16[192,1024]{1,0:T(8,128)(2,1)}, bf16[192,1024]{1,0:T(8,128)(2,1)}, u32[]{:S(2)}, u32[]{:S(2)}) collective-permute-start(bf16[192,1024]{1,0:T(8,128)(2,1)} %get-tuple-element.133), channel_id=1, source_target_pairs={{64,8},{72,0},{80,24},{88,16},{96,40},{104,32},{112,56},{120,48},{... | collective-permute-start | bytes 1179656 | tf_op jit(solution)/shard_map/ppermute | solution.py:38
  433.1 17.4 %collective-permute-start.99 = (bf16[192,1024]{1,0:T(8,128)(2,1)S(1)}, bf16[192,1024]{1,0:T(8,128)(2,1)}, u32[]{:S(2)}, u32[]{:S(2)}) collective-permute-start(bf16[192,1024]{1,0:T(8,128)(2,1)S(1)} %get-tuple-element.132), channel_id=1, source_target_pairs={{64,0},{72,8},{80,16},{88,24},{96,32},{104,40},{112,48},{120,56},{... | collective-permute-start | bytes 1179656 | tf_op jit(solution)/shard_map/ppermute | solution.py:38
  434.9 24.0 %collective-permute-start.83 = (f32[12,1024]{1,0:T(8,128)S(1)}, f32[12,1024]{1,0:T(8,128)S(1)}, u32[]{:S(2)}, u32[]{:S(2)}) collective-permute-start(f32[12,1024]{1,0:T(8,128)S(1)} %get-tuple-element.173), channel_id=1, source_target_pairs={{0,72},{8,64},{16,88},{24,80},{32,104},{40,96},{48,120},{56,112},{... | collective-permute-start | bytes 147464 | tf_op jit(solution)/shard_map/ppermute | solution.py:38
  440.3 18.6 %collective-permute-start.82 = (f32[12,1024]{1,0:T(8,128)S(1)}, f32[12,1024]{1,0:T(8,128)S(1)}, u32[]{:S(2)}, u32[]{:S(2)}) collective-permute-start(f32[12,1024]{1,0:T(8,128)S(1)} %get-tuple-element.173), channel_id=1, source_target_pairs={{0,64},{8,72},{16,80},{24,88},{32,96},{40,104},{48,112},{56,120},{... | collective-permute-start | bytes 147464 | tf_op jit(solution)/shard_map/ppermute | solution.py:38
  441.3 17.6 %collective-permute-start.84 = (f32[12,1024]{1,0:T(8,128)S(1)}, f32[12,1024]{1,0:T(8,128)S(1)}, u32[]{:S(2)}, u32[]{:S(2)}) collective-permute-start(f32[12,1024]{1,0:T(8,128)S(1)} %get-tuple-element.174), channel_id=1, source_target_pairs={{0,8},{8,0},{16,24},{24,16},{32,40},{40,32},{48,56},{56,48},{64,72... | collective-permute-start | bytes 147464 | tf_op jit(solution)/shard_map/ppermute | solution.py:38
  452.5 14.1 %collective-permute-start.102 = (bf16[192,1024]{1,0:T(8,128)(2,1)S(1)}, bf16[192,1024]{1,0:T(8,128)(2,1)S(1)}, u32[]{:S(2)}, u32[]{:S(2)}) collective-permute-start(bf16[192,1024]{1,0:T(8,128)(2,1)S(1)} %get-tuple-element.95), channel_id=1, source_target_pairs={{0,2},{1,3},{2,4},{3,5},{4,6},{5,7},{6,0},{7,1},{8,10},{9,11},{10,... | collective-permute-start | bytes 1179656 | tf_op jit(solution)/shard_map/ppermute | solution.py:38
  456.2 20.0 %collective-permute-start.103 = (bf16[192,1024]{1,0:T(8,128)(2,1)S(1)}, bf16[192,1024]{1,0:T(8,128)(2,1)S(1)}, u32[]{:S(2)}, u32[]{:S(2)}) collective-permute-start(bf16[192,1024]{1,0:T(8,128)(2,1)S(1)} %get-tuple-element.95), channel_id=1, source_target_pairs={{0,4},{1,5},{2,6},{3,7},{4,0},{5,1},{6,2},{7,3},{8,12},{9,13},{10,... | collective-permute-start | bytes 1179656 | tf_op jit(solution)/shard_map/ppermute | solution.py:38
  458.9 17.8 %collective-permute-start.85 = (f32[12,1024]{1,0:T(8,128)S(1)}, f32[12,1024]{1,0:T(8,128)S(1)}, u32[]{:S(2)}, u32[]{:S(2)}) collective-permute-start(f32[12,1024]{1,0:T(8,128)S(1)} %add_add_fusion.2), channel_id=1, source_target_pairs={{0,1},{1,0},{2,3},{3,2},{4,5},{5,4},{6,7},{7,6},{8,9},{9,8},{10,11... | collective-permute-start | bytes 147464 | tf_op jit(solution)/shard_map/ppermute | solution.py:38
  459.0 17.3 %collective-permute-start.104 = (bf16[192,1024]{1,0:T(8,128)(2,1)S(1)}, bf16[192,1024]{1,0:T(8,128)(2,1)S(1)}, u32[]{:S(2)}, u32[]{:S(2)}) collective-permute-start(bf16[192,1024]{1,0:T(8,128)(2,1)S(1)} %get-tuple-element.95), channel_id=1, source_target_pairs={{0,6},{1,7},{2,0},{3,1},{4,2},{5,3},{6,4},{7,5},{8,14},{9,15},{10,... | collective-permute-start | bytes 1179656 | tf_op jit(solution)/shard_map/ppermute | solution.py:38
  476.3 20.8 %collective-permute-start.105 = (bf16[768,1024]{1,0:T(8,128)(2,1)S(1)}, bf16[768,1024]{1,0:T(8,128)(2,1)S(1)}, u32[]{:S(2)}, u32[]{:S(2)}) collective-permute-start(bf16[768,1024]{1,0:T(8,128)(2,1)S(1)} %bitcast.410), channel_id=1, source_target_pairs={{0,1},{1,0},{2,3},{3,2},{4,5},{5,4},{6,7},{7,6},{8,9},{9,8},{10,11... | collective-permute-start | bytes 4718600 | tf_op jit(solution)/shard_map/ppermute | solution.py:38
  (174 other events, 1541.4 us)

commit v5 on v4

--- a/solution.py
+++ b/solution.py
@@ -145,10 +145,10 @@
     return tuple(view[:, :, part].reshape(4 * BLOCK, 4, HEAD_DIM) for part in range(3))
 
 
-def layer_forward(stream, allowed, vectors, w_qkv, w_out, hook):
-    gain_one, shift_one, out_bias, gain_two, shift_two, proj_bias, qkv_bias, fc_bias = vectors
+def layer_forward(stream, allowed, vectors, hook):
+    gain_one, shift_one, out_bias, gain_two, shift_two, proj_bias = vectors
     normed_one, standard_one, inverse_one = norm_forward(stream, gain_one, shift_one)
-    rows_one = gather_rows(normed_one)
+    rows_one, w_qkv, w_out, qkv_bias, fc_bias = hook(-1, gather_rows(normed_one))
     projected = (dot(rows_one, w_qkv, 1, 0) + qkv_bias).astype(bf16)
     query, key, value = split_heads(projected)
     both = jnp.stack([key, value]).reshape(2, 4 * BLOCK, 256)
@@ -179,7 +179,7 @@
 
 
 def layer_backward(incoming, allowed, vectors, weights, saved, hook):
-    gain_one, shift_one, out_bias, gain_two, shift_two, proj_bias, qkv_bias, fc_bias = vectors
+    gain_one, shift_one, out_bias, gain_two, shift_two, proj_bias = vectors
     w_qkv, w_out, w_fc, w_proj = weights
     (
         (standard_one, inverse_one, rows_one),
@@ -252,17 +252,18 @@
 
 def far_y(mine, own):
     y = lax.axis_index("dp") // 2
-    sent = held(pick(mine, (y + 2) % 4, 1), own)
+    sent, own = tied(pick(mine, (y + 2) % 4, 1), own)
     return (own + along_y(sent, 2).astype(f32)).astype(bf16)
 
 
-def over_z(own, layer, pipe, high):
-    near, far = pick(own, high), pick(own, 1 - high)
-    step = 1 if layer == 1 else -1
-    total = jnp.where(pipe == layer, near.astype(f32), 0.0)
-    total = total + along_z(near, step, only=1 - layer).astype(f32)
-    total = total + along_z(far, -step, only=1 - layer).astype(f32)
-    total = total + along_z(far, 2, only=layer).astype(f32)
+def over_z(zero, one, pipe, high):
+    zero_near, zero_far = pick(zero, high), pick(zero, 1 - high)
+    one_near, one_far = pick(one, high), pick(one, 1 - high)
+    even = pipe == 0
+    total = jnp.where(even, zero_near, one_near).astype(f32)
+    total = total + along_z(jnp.where(even, one_near, zero_far), 1).astype(f32)
+    total = total + along_z(jnp.where(even, one_far, zero_near), -1).astype(f32)
+    total = total + along_z(jnp.where(even, zero_far, one_far), 2).astype(f32)
     return total.astype(bf16)
 
 
@@ -290,8 +291,8 @@
     return total
 
 
-def held(value, *others):
-    return lax.optimization_barrier((value,) + others)[0]
+def tied(*arrays):
+    return lax.optimization_barrier(arrays)
 
 
 def lay_out(here, copies, sources, shapes):
@@ -334,9 +335,7 @@
     return [((z + 4 - by) % 2, (z + 4 - by) % 4 // 2) for by in ORDER]
 
 
-def spread_first(here, w_qkv, w_out, smalls):
-    core = here[2]
-    turned_out = w_out.T
+def send_first(core, w_qkv, turned_out, smalls):
     group = jnp.concatenate(
         [
             lax.dynamic_slice_in_dim(w_qkv, core * 512, 512, 0),
@@ -345,8 +344,16 @@
         axis=1,
     )
     group = jnp.concatenate([group, smalls], axis=0)
-    came = [along_z(group, by) for by in ORDER]
-    swapped = [other_core(item) for item in came]
+    came = [along_z(group, by) for by in ORDER[:2]]
+    group, *came = tied(group, *came)
+    return came + [along_z(group, ORDER[2])]
+
+
+def lay_first(here, w_qkv, turned_out, smalls, came, after):
+    swapped = [other_core(item) for item in came[:2]]
+    last, after = tied(came[2], after)
+    came = came[:2] + [last]
+    swapped.append(other_core(last))
 
     def copies(pipe, high, core):
         rows = span(0, 1024)
@@ -372,7 +379,7 @@
         [w_qkv, turned_out, smalls, *came, *swapped],
         [(2, 1024, 768), (2, 1024, 256), (2, 2, 16, 512)],
     )
-    return arrays, swapped
+    return arrays, after
 
 
 def lay_fc(here, w_fc, came):
@@ -454,51 +461,62 @@
         ],
         axis=1,
     ).reshape(16, 512)
-    (all_qkv, all_out, all_small), swapped = spread_first(
-        here, w_qkv[0].reshape(WIDTH, 384), w_out[0], smalls
-    )
+    before = along_z(smalls, 1)
+    flat_w_qkv, turned_out = w_qkv[0].reshape(WIDTH, 384), w_out[0].T
+    came_first = send_first(core, flat_w_qkv, turned_out, smalls)
     half_fc = lax.dynamic_slice_in_dim(w_fc[0], core * 512, 512, 0)
     half_proj = lax.dynamic_slice_in_dim(w_proj[0], core * 256, 256, 0)
     coming, laid = {}, {}
 
-    def first_hook(step, value):
-        if step == 0:
-            sent = held(half_fc, *swapped)
-            coming["fc"] = [along_z(sent, by) for by in ORDER[:2]]
-            return held(value, *coming["fc"])
-        if step == 1:
-            coming["fc"].append(along_z(held(half_fc, *coming["fc"]), ORDER[2]))
-            return held(value, *coming["fc"])
-        if step == 2:
-            laid["fc"] = lay_fc(here, w_fc[0], coming["fc"])
-            sent = held(half_proj, *coming["fc"])
-            coming["proj"] = [along_z(sent, by) for by in ORDER[:2]]
-            return held(value, *coming["proj"])
-        coming["proj"].append(along_z(held(half_proj, *coming["proj"]), ORDER[2]))
-        laid["proj"] = lay_proj(here, w_proj[0], coming["proj"])
-        return held(value, coming["proj"][2]), laid["fc"][0], laid["proj"][0]
-
-    def second_hook(step, value):
-        return value if step < 3 else (value, laid["fc"][1], laid["proj"][1])
-
-    vectors = []
-    for layer in range(2):
+    def biases(all_small, layer):
         flat = all_small[layer].reshape(2, -1).astype(f32)
-        norms = tuple(flat[0, i * WIDTH : (i + 1) * WIDTH] for i in range(6))
         pairs = flat[:, 6144:6400].reshape(2, 2, 128)
         none = jnp.zeros((2, 128), f32)
         qkv_bias = jnp.stack([pairs[:, 0], none, pairs[:, 1]], axis=1).reshape(-1)
-        vectors.append(norms + (qkv_bias, flat[:, 6400:6912].reshape(-1)))
+        return qkv_bias, flat[:, 6400:6912].reshape(-1)
+
+    def first_hook(step, value):
+        if step == -1:
+            laid["first"], value = lay_first(
+                here, flat_w_qkv, turned_out, smalls, came_first, value
+            )
+            return second_hook(step, value, 0)
+        if step == 0:
+            sent, *laid["first"] = tied(half_fc, *laid["first"])
+            value, *coming["fc"] = tied(value, *[along_z(sent, by) for by in ORDER[:2]])
+            return value
+        if step == 1:
+            sent, *came = tied(half_fc, *coming["fc"])
+            value, *coming["fc"] = tied(value, *came, along_z(sent, ORDER[2]))
+            return value
+        if step == 2:
+            sent, *coming["fc"] = tied(half_proj, *coming["fc"])
+            laid["fc"] = lay_fc(here, w_fc[0], coming["fc"])
+            value, *coming["proj"] = tied(value, *[along_z(sent, by) for by in ORDER[:2]])
+            return value
+        sent, *came = tied(half_proj, *coming["proj"])
+        value, last = tied(value, along_z(sent, ORDER[2]))
+        laid["proj"] = lay_proj(here, w_proj[0], came + [last])
+        return value, laid["fc"][0], laid["proj"][0]
+
+    def second_hook(step, value, layer=1):
+        if step == -1:
+            all_qkv, all_out, all_small = laid["first"]
+            return (value, all_qkv[layer], all_out[layer]) + biases(all_small, layer)
+        return value if step < 3 else (value, laid["fc"][1], laid["proj"][1])
+
+    vectors = []
+    for layer in range(2):
+        flat = jnp.where(pipe == layer, smalls, before).astype(f32).reshape(-1)
+        vectors.append(tuple(flat[i * WIDTH : (i + 1) * WIDTH] for i in range(6)))
 
     first, weights_first, saved_first = layer_forward(
-        stream, allowed, vectors[0], all_qkv[0], all_out[0], first_hook
+        stream, allowed, vectors[0], first_hook
     )
     second, weights_second, saved_second = layer_forward(
         first.astype(f32),
         allowed,
         vectors[1],
-        all_qkv[1],
-        all_out[1],
         second_hook,
     )
     waiting = {}
@@ -518,31 +536,33 @@
     def reduce_along(step, value, group=None):
         if step == 0:
             halved = [over_cores(item, core) for item in groups_one]
-            kept["one"] = jnp.concatenate(halved, axis=2)
-            return held(value, kept["one"])
+            value, kept["one"] = tied(value, jnp.concatenate(halved, axis=2))
+            return value
         if step == 1:
             kept["near"] = near_y(kept["one"])
             kept["feed"] = group
             return value
         if step == 2:
-            return held(value, kept["near"])
+            value, kept["near"] = tied(value, kept["near"])
+            return value
         if step == 3:
             kept["one"] = far_y(kept["one"], kept["near"])
-            kept["feed"] = over_cores(kept["feed"], core)
-            return held(value, kept["one"], kept["feed"])
-        kept["near"] = near_y(kept["feed"])
-        kept["attention"] = over_cores(group, core)
-        return held(value, kept["near"], kept["attention"])
+            value, kept["feed"] = tied(value, over_cores(kept["feed"], core))
+            return value
+        near, attention = near_y(kept["feed"]), over_cores(group, core)
+        value, *rest = tied(value, kept["one"], near, attention)
+        kept["one"], kept["near"], kept["attention"] = rest
+        return value
 
     last_grad, early_zero, late_zero = layer_backward(
         middle_low.astype(f32), allowed, vectors[0], weights_first, saved_first, reduce_along
     )
     last_low = last_grad.astype(bf16)
-    one = over_z(kept["one"], 1, pipe, high)
-    feed = far_y(kept["feed"], kept["near"])
-    attention = far_y(kept["attention"], near_y(kept["attention"]))
-    zero = over_z(jnp.concatenate([feed, attention], axis=1), 0, pipe, high)
-    total = back_over_y(jnp.where(pipe == 1, one, zero))
+    y = dp // 2
+    near = jnp.concatenate([kept["near"], near_y(kept["attention"])], axis=1)
+    far = [pick(kept[name], (y + 2) % 4, 1) for name in ("feed", "attention")]
+    zero = near + along_y(jnp.concatenate(far, axis=1), 2).astype(f32)
+    total = back_over_y(over_z(zero.astype(bf16), kept["one"], pipe, high))
 
     def bias_rows(fc_bias_grad):
         return place(jnp.zeros((4, WIDTH), f32), fc_bias_grad[None], (x, 0))

time: 517 us -> 480 us (0.928)
  the two profiles are of different devices: /device:TPU:0 before, /device:TPU:1 now
where the time goes in v5:
time: 480 us; the launch traced here: 472 us
  waiting for transfers between devices  166 us (35%)
  starting transfers between devices  152 us (32%)
  local copies, waits for them, and re-layouts  53.8 us (11%)
  other arithmetic  47.3 us (10%)
  matrix products  44.3 us (9%)
    ppermute x103, waiting for transfers between devices, move(): return lax.ppermute(array, axes, sorted(pairs.items()))  166 us
    ppermute x103, starting transfers between devices, move(): return lax.ppermute(array, axes, sorted(pairs.items()))  152 us
    unnamed x243, local copies, waits for them, and re-layouts  31.3 us
    dot_general x24, matrix products, dot(): lax.dot_general(left, right, (((left_dim,), (right_dim,)), ((), ())), pre...  30.3 us
  transfers between devices with their start and end apart: 103, of which 45 were waited for; matrix products, arithmetic and copies ran while one was open for 19% of the time, Pallas kernels for 1%

profile of v5, /device:TPU:1, one launch (start us, length us, event | category | flops | bytes accessed | tf_op | source)
XLA Modules:
  0.0 471.6 jit_solution(8860837319007552694)
XLA Ops:
  6.4 2.5 collective-permute-start.4
  15.0 5.4 %collective-permute-start = (bf16[96,1024]{1,0:T(8,128)(2,1)S(1)}, bf16[96,1024]{1,0:T(8,128)(2,1)S(1)}, u32[]{:S(2)}, u32[]{:S(2)}) collective-permute-start(bf16[96,1024]{1,0:T(8,128)(2,1)S(1)} %dynamic-slice_bitcast_fusion.12), channel_id=1, source_target_pairs={{0,0},{1,8},{2,2},{3,10},{4,4},{5,12},{6,6},{7,14},{8,1},{9,9},{10... | collective-permute-start | bytes 589832 | tf_op jit(solution)/shard_map/ppermute | solution.py:38
  21.5 9.0 %collective-permute-done = bf16[96,1024]{1,0:T(8,128)(2,1)S(1)} collective-permute-done((bf16[96,1024]{1,0:T(8,128)(2,1)S(1)}, bf16[96,1024]{1,0:T(8,128)(2,1)S(1)}, u32[]{:S(2)}, u32[]{:S(2)}) %collective-permute-start) | collective-permute-done | bytes 196640 | tf_op jit(solution)/shard_map/ppermute | solution.py:38
  38.1 4.5 collective-permute-done.6
  44.8 3.2 collective-permute-start.8
  60.6 3.2 fusion.81
  80.6 6.0 %collective-permute-done.15.refs_3_ = bf16[512,512]{1,0:T(8,128)(2,1)S(1)} collective-permute-done((bf16[512,512]{1,0:T(8,128)(2,1)}, bf16[512,512]{1,0:T(8,128)(2,1)S(1)}, u32[]{:S(2)}, u32[]{:S(2)}) %collective-permute-start.15) | collective-permute-done | bytes 524320 | tf_op jit(solution)/shard_map/ppermute | solution.py:38
  86.6 2.7 collective-permute-start.20
  93.1 3.2 collective-permute-done.16
  97.9 5.0 %collective-permute-done.18 = bf16[96,1024]{1,0:T(8,128)(2,1)S(1)} collective-permute-done((bf16[96,1024]{1,0:T(8,128)(2,1)S(1)}, bf16[96,1024]{1,0:T(8,128)(2,1)S(1)}, u32[]{:S(2)}, u32[]{:S(2)}) %collective-permute-start.18) | collective-permute-done | bytes 196640 | tf_op jit(solution)/shard_map/ppermute | solution.py:38
  107.3 3.4 collective-permute-start.25
  110.7 4.9 %collective-permute-done.21 = bf16[96,1024]{1,0:T(8,128)(2,1)S(1)} collective-permute-done((bf16[96,1024]{1,0:T(8,128)(2,1)S(1)}, bf16[96,1024]{1,0:T(8,128)(2,1)S(1)}, u32[]{:S(2)}, u32[]{:S(2)}) %collective-permute-start.21) | collective-permute-done | bytes 196640 | tf_op jit(solution)/shard_map/ppermute | solution.py:38
  116.7 2.9 collective-permute-start.26
  128.7 4.4 collective-permute-start.45
  134.5 4.8 %collective-permute-done.29 = bf16[96,1024]{1,0:T(8,128)(2,1)S(1)} collective-permute-done((bf16[96,1024]{1,0:T(8,128)(2,1)S(1)}, bf16[96,1024]{1,0:T(8,128)(2,1)S(1)}, u32[]{:S(2)}, u32[]{:S(2)}) %collective-permute-start.29) | collective-permute-done | bytes 196640 | tf_op jit(solution)/shard_map/ppermute | solution.py:38
  152.9 2.8 fusion.78
  157.2 2.9 collective-permute-start.33
  163.8 2.9 collective-permute-done.48
  172.3 3.0 collective-permute-start.34
  176.7 6.2 %collective-permute-done.34 = bf16[96,1024]{1,0:T(8,128)(2,1)S(1)} collective-permute-done((bf16[96,1024]{1,0:T(8,128)(2,1)S(1)}, bf16[96,1024]{1,0:T(8,128)(2,1)S(1)}, u32[]{:S(2)}, u32[]{:S(2)}) %collective-permute-start.34) | collective-permute-done | bytes 196640 | tf_op jit(solution)/shard_map/ppermute | solution.py:38
  182.9 4.3 collective-permute-done.36
  190.8 8.6 %collective-permute-done.37 = bf16[96,1024]{1,0:T(8,128)(2,1)S(1)} collective-permute-done((bf16[96,1024]{1,0:T(8,128)(2,1)S(1)}, bf16[96,1024]{1,0:T(8,128)(2,1)S(1)}, u32[]{:S(2)}, u32[]{:S(2)}) %collective-permute-start.37) | collective-permute-done | bytes 196640 | tf_op jit(solution)/shard_map/ppermute | solution.py:38
  218.1 5.5 %collective-permute-done.49 = bf16[96,1024]{1,0:T(8,128)(2,1)S(1)} collective-permute-done((bf16[96,1024]{1,0:T(8,128)(2,1)S(1)}, bf16[96,1024]{1,0:T(8,128)(2,1)S(1)}, u32[]{:S(2)}, u32[]{:S(2)}) %collective-permute-start.49) | collective-permute-done | bytes 196640 | tf_op jit(solution)/shard_map/ppermute | solution.py:38
  223.6 4.2 collective-permute-start.42
  230.6 3.5 collective-permute-start.54
  238.1 3.9 collective-permute-done.52
  260.8 6.2 %collective-permute-start.43 = (bf16[96,1024]{1,0:T(8,128)(2,1)S(1)}, bf16[96,1024]{1,0:T(8,128)(2,1)S(1)}, u32[]{:S(2)}, u32[]{:S(2)}) collective-permute-start(bf16[96,1024]{1,0:T(8,128)(2,1)S(1)} %get-tuple-element.167), channel_id=1, source_target_pairs={{0,0},{1,8},{2,2},{3,10},{4,4},{5,12},{6,6},{7,14},{8,1},{9,9},{10... | collective-permute-start | bytes 589832 | tf_op jit(solution)/shard_map/ppermute | solution.py:38
  277.7 3.1 collective-permute-done.60
  283.8 2.6 fusion.1
  295.8 3.6 collective-permute-start.64
  301.5 5.6 %collective-permute-done.64 = bf16[96,1024]{1,0:T(8,128)(2,1)S(1)} collective-permute-done((bf16[96,1024]{1,0:T(8,128)(2,1)S(1)}, bf16[96,1024]{1,0:T(8,128)(2,1)S(1)}, u32[]{:S(2)}, u32[]{:S(2)}) %collective-permute-start.64) | collective-permute-done | bytes 196640 | tf_op jit(solution)/shard_map/ppermute | solution.py:38
  307.1 4.8 %collective-permute-done.66 = bf16[96,1024]{1,0:T(8,128)(2,1)S(1)} collective-permute-done((bf16[96,1024]{1,0:T(8,128)(2,1)S(1)}, bf16[96,1024]{1,0:T(8,128)(2,1)S(1)}, u32[]{:S(2)}, u32[]{:S(2)}) %collective-permute-start.66) | collective-permute-done | bytes 196640 | tf_op jit(solution)/shard_map/ppermute | solution.py:38
  318.5 7.6 %collective-permute-done.67 = bf16[96,1024]{1,0:T(8,128)(2,1)S(1)} collective-permute-done((bf16[96,1024]{1,0:T(8,128)(2,1)S(1)}, bf16[96,1024]{1,0:T(8,128)(2,1)S(1)}, u32[]{:S(2)}, u32[]{:S(2)}) %collective-permute-start.67) | collective-permute-done | bytes 196640 | tf_op jit(solution)/shard_map/ppermute | solution.py:38
  347.6 7.4 %collective-permute-done.77 = bf16[2,192,1024]{2,1,0:T(8,128)(2,1)S(1)} collective-permute-done((bf16[2,192,1024]{2,1,0:T(8,128)(2,1)S(1)}, bf16[2,192,1024]{2,1,0:T(8,128)(2,1)S(1)}, u32[]{:S(2)}, u32[]{:S(2)}) %collective-permute-start.77) | collective-permute-done | bytes 786464 | tf_op jit(solution)/shard_map/ppermute | solution.py:38
  357.2 3.9 collective-permute-done.75
  361.1 5.0 %collective-permute-done.76 = bf16[96,1024]{1,0:T(8,128)(2,1)S(1)} collective-permute-done((bf16[96,1024]{1,0:T(8,128)(2,1)S(1)}, bf16[96,1024]{1,0:T(8,128)(2,1)S(1)}, u32[]{:S(2)}, u32[]{:S(2)}) %collective-permute-start.76) | collective-permute-done | bytes 196640 | tf_op jit(solution)/shard_map/ppermute | solution.py:38
  374.6 2.5 collective-permute-start.94
  377.2 19.2 %collective-permute-done.93 = bf16[2,64,1024]{2,1,0:T(8,128)(2,1)S(1)} collective-permute-done((bf16[2,64,1024]{2,1,0:T(8,128)(2,1)}, bf16[2,64,1024]{2,1,0:T(8,128)(2,1)S(1)}, u32[]{:S(2)}, u32[]{:S(2)}) %collective-permute-start.93) | collective-permute-done | bytes 262176 | tf_op jit(solution)/shard_map/ppermute | solution.py:38
  399.1 2.7 collective-permute-start.97
  403.0 2.7 collective-permute-start.84
  405.7 5.4 %collective-permute-done.96 = bf16[192,1024]{1,0:T(8,128)(2,1)S(1)} collective-permute-done((bf16[192,1024]{1,0:T(8,128)(2,1)}, bf16[192,1024]{1,0:T(8,128)(2,1)S(1)}, u32[]{:S(2)}, u32[]{:S(2)}) %collective-permute-start.96) | collective-permute-done | bytes 393248 | tf_op jit(solution)/shard_map/ppermute | solution.py:38
  411.8 7.0 %collective-permute-done.98 = bf16[192,1024]{1,0:T(8,128)(2,1)} collective-permute-done((bf16[192,1024]{1,0:T(8,128)(2,1)}, bf16[192,1024]{1,0:T(8,128)(2,1)}, u32[]{:S(2)}, u32[]{:S(2)}) %collective-permute-start.98) | collective-permute-done | bytes 393248 | tf_op jit(solution)/shard_map/ppermute | solution.py:38
  420.5 2.9 collective-permute-start.100
  423.4 4.6 collective-permute-start.86
  429.4 7.3 %collective-permute-done.100 = bf16[192,1024]{1,0:T(8,128)(2,1)S(1)} collective-permute-done((bf16[192,1024]{1,0:T(8,128)(2,1)S(1)}, bf16[192,1024]{1,0:T(8,128)(2,1)S(1)}, u32[]{:S(2)}, u32[]{:S(2)}) %collective-permute-start.100) | collective-permute-done | bytes 393248 | tf_op jit(solution)/shard_map/ppermute | solution.py:38
  436.8 4.3 collective-permute-done.101
  443.2 2.8 collective-permute-start.88
  448.3 4.8 %collective-permute-start.81 = (bf16[96,1024]{1,0:T(8,128)(2,1)S(1)}, bf16[96,1024]{1,0:T(8,128)(2,1)S(1)}, u32[]{:S(2)}, u32[]{:S(2)}) collective-permute-start(bf16[96,1024]{1,0:T(8,128)(2,1)S(1)} %get-tuple-element.162), channel_id=1, source_target_pairs={{0,0},{1,8},{2,2},{3,10},{4,4},{5,12},{6,6},{7,14},{8,1},{9,9},{10... | collective-permute-start | bytes 589832 | tf_op jit(solution)/shard_map/ppermute | solution.py:38
  (626 shorter events, 239.4 us)
Async XLA Ops:
  6.4 14.4 %collective-permute-start.4 = (bf16[16,512]{1,0:T(8,128)(2,1)S(1)}, bf16[16,512]{1,0:T(8,128)(2,1)S(1)}, u32[]{:S(2)}, u32[]{:S(2)}) collective-permute-start(bf16[16,512]{1,0:T(8,128)(2,1)S(1)} %reshape.743.refs_2_), channel_id=1, source_target_pairs={{0,64},{8,72},{16,80},{24,88},{32,96},{40,104},{48,112},{56,120},{... | collective-permute-start | bytes 49160 | tf_op jit(solution)/shard_map/ppermute | solution.py:38
  12.3 18.6 %collective-permute-start.1 = (bf16[528,512]{1,0:T(8,128)(2,1)}, bf16[528,512]{1,0:T(8,128)(2,1)}, u32[]{:S(2)}, u32[]{:S(2)}) collective-permute-start(bf16[528,512]{1,0:T(8,128)(2,1)} %pad_maximum_fusion.17), channel_id=1, source_target_pairs={{0,64},{8,72},{16,80},{24,88},{32,96},{40,104},{48,112},{56,120},{... | collective-permute-start | bytes 1622024 | tf_op jit(solution)/shard_map/ppermute | solution.py:38
  13.9 16.9 %collective-permute-start.2 = (bf16[528,512]{1,0:T(8,128)(2,1)}, bf16[528,512]{1,0:T(8,128)(2,1)}, u32[]{:S(2)}, u32[]{:S(2)}) collective-permute-start(bf16[528,512]{1,0:T(8,128)(2,1)} %pad_maximum_fusion.17), channel_id=1, source_target_pairs={{0,72},{8,64},{16,88},{24,80},{32,104},{40,96},{48,120},{56,112},{... | collective-permute-start | bytes 1622024 | tf_op jit(solution)/shard_map/ppermute | solution.py:38
  15.0 15.5 %collective-permute-start = (bf16[96,1024]{1,0:T(8,128)(2,1)S(1)}, bf16[96,1024]{1,0:T(8,128)(2,1)S(1)}, u32[]{:S(2)}, u32[]{:S(2)}) collective-permute-start(bf16[96,1024]{1,0:T(8,128)(2,1)S(1)} %dynamic-slice_bitcast_fusion.12), channel_id=1, source_target_pairs={{0,0},{1,8},{2,2},{3,10},{4,4},{5,12},{6,6},{7,14},{8,1},{9,9},{10... | collective-permute-start | bytes 589832 | tf_op jit(solution)/shard_map/ppermute | solution.py:38
  20.5 49.4 %collective-permute-start.14 = (s32[8,96]{1,0:T(8,128)S(1)}, s32[8,96]{1,0:T(8,128)S(1)}, u32[]{:S(2)}, u32[]{:S(2)}) collective-permute-start(s32[8,96]{1,0:T(8,128)S(1)} %reshape.746), channel_id=1, source_target_pairs={{0,1},{1,0},{2,3},{3,2},{4,5},{5,4},{6,7},{7,6},{8,9},{9,8},{10,11... | collective-permute-start | bytes 9224 | tf_op jit(solution)/shard_map/ppermute | solution.py:38
  30.8 17.2 %collective-permute-start.3 = (bf16[528,512]{1,0:T(8,128)(2,1)}, bf16[528,512]{1,0:T(8,128)(2,1)}, u32[]{:S(2)}, u32[]{:S(2)}) collective-permute-start(bf16[528,512]{1,0:T(8,128)(2,1)} %pad_maximum_fusion.17), channel_id=1, source_target_pairs={{0,8},{8,0},{16,24},{24,16},{32,40},{40,32},{48,56},{56,48},{64,72... | collective-permute-start | bytes 1622024 | tf_op jit(solution)/shard_map/ppermute | solution.py:38
  56.3 15.5 %collective-permute-start.12 = (bf16[512,512]{1,0:T(8,128)(2,1)}, bf16[512,512]{1,0:T(8,128)(2,1)S(1)}, u32[]{:S(2)}, u32[]{:S(2)}) collective-permute-start(bf16[512,512]{1,0:T(8,128)(2,1)} %dynamic-slice_bitcast_fusion.7), channel_id=1, source_target_pairs={{0,64},{8,72},{16,80},{24,88},{32,96},{40,104},{48,112},{56,120},{... | collective-permute-start | bytes 1572872 | tf_op jit(solution)/shard_map/ppermute | solution.py:38
  57.3 14.6 %collective-permute-start.13 = (bf16[512,512]{1,0:T(8,128)(2,1)}, bf16[512,512]{1,0:T(8,128)(2,1)S(1)}, u32[]{:S(2)}, u32[]{:S(2)}) collective-permute-start(bf16[512,512]{1,0:T(8,128)(2,1)} %dynamic-slice_bitcast_fusion.7), channel_id=1, source_target_pairs={{0,72},{8,64},{16,88},{24,80},{32,104},{40,96},{48,120},{56,112},{... | collective-permute-start | bytes 1572872 | tf_op jit(solution)/shard_map/ppermute | solution.py:38
  71.8 14.7 %collective-permute-start.15 = (bf16[512,512]{1,0:T(8,128)(2,1)}, bf16[512,512]{1,0:T(8,128)(2,1)S(1)}, u32[]{:S(2)}, u32[]{:S(2)}) collective-permute-start(bf16[512,512]{1,0:T(8,128)(2,1)} %dynamic-slice_bitcast_fusion.7), channel_id=1, source_target_pairs={{0,8},{8,0},{16,24},{24,16},{32,40},{40,32},{48,56},{56,48},{64,72... | collective-permute-start | bytes 1572872 | tf_op jit(solution)/shard_map/ppermute | solution.py:38
  86.6 16.5 %collective-permute-start.19 = (bf16[256,1024]{1,0:T(8,128)(2,1)S(1)}, bf16[256,1024]{1,0:T(8,128)(2,1)S(1)}, u32[]{:S(2)}, u32[]{:S(2)}) collective-permute-start(bf16[256,1024]{1,0:T(8,128)(2,1)S(1)} %copy-done.56), channel_id=1, source_target_pairs={{0,64},{8,72},{16,80},{24,88},{32,96},{40,104},{48,112},{56,120},{... | collective-permute-start | bytes 1572872 | tf_op jit(solution)/shard_map/ppermute | solution.py:38
  86.6 16.5 %collective-permute-start.20 = (bf16[256,1024]{1,0:T(8,128)(2,1)S(1)}, bf16[256,1024]{1,0:T(8,128)(2,1)S(1)}, u32[]{:S(2)}, u32[]{:S(2)}) collective-permute-start(bf16[256,1024]{1,0:T(8,128)(2,1)S(1)} %copy-done.56), channel_id=1, source_target_pairs={{0,72},{8,64},{16,88},{24,80},{32,104},{40,96},{48,120},{56,112},{... | collective-permute-start | bytes 1572872 | tf_op jit(solution)/shard_map/ppermute | solution.py:38
  103.5 13.1 %collective-permute-start.24 = (bf16[256,1024]{1,0:T(8,128)(2,1)S(1)}, bf16[256,1024]{1,0:T(8,128)(2,1)S(1)}, u32[]{:S(2)}, u32[]{:S(2)}) collective-permute-start(bf16[256,1024]{1,0:T(8,128)(2,1)S(1)} %copy-done.56), channel_id=1, source_target_pairs={{0,8},{8,0},{16,24},{24,16},{32,40},{40,32},{48,56},{56,48},{64,72... | collective-permute-start | bytes 1572872 | tf_op jit(solution)/shard_map/ppermute | solution.py:38
  107.3 12.4 %collective-permute-start.25 = (bf16[3,512,512]{2,1,0:T(8,128)(2,1)S(1)}, bf16[3,512,512]{2,1,0:T(8,128)(2,1)S(1)}, u32[]{:S(2)}, u32[]{:S(2)}) collective-permute-start(bf16[3,512,512]{2,1,0:T(8,128)(2,1)S(1)} %pad_maximum_fusion.1), channel_id=1, source_target_pairs={{0,1},{1,0},{2,3},{3,2},{4,5},{5,4},{6,7},{7,6},{8,9},{9,8},{10,11... | collective-permute-start | bytes 4718600 | tf_op jit(solution)/shard_map/ppermute | solution.py:38
  127.2 12.1 %collective-permute-start.29 = (bf16[96,1024]{1,0:T(8,128)(2,1)S(1)}, bf16[96,1024]{1,0:T(8,128)(2,1)S(1)}, u32[]{:S(2)}, u32[]{:S(2)}) collective-permute-start(bf16[96,1024]{1,0:T(8,128)(2,1)S(1)} %get-tuple-element.210), channel_id=1, source_target_pairs={{0,16},{8,24},{16,32},{24,40},{32,48},{40,56},{48,0},{56,8},{1,17}... | collective-permute-start | bytes 589832 | tf_op jit(solution)/shard_map/ppermute | solution.py:38
  128.7 18.1 %collective-permute-start.45 = (bf16[96,1024]{1,0:T(8,128)(2,1)}, bf16[96,1024]{1,0:T(8,128)(2,1)S(1)}, u32[]{:S(2)}, u32[]{:S(2)}) collective-permute-start(bf16[96,1024]{1,0:T(8,128)(2,1)} %dynamic-slice_bitcast_fusion.11), channel_id=1, source_target_pairs={{0,0},{1,8},{2,2},{3,10},{4,4},{5,12},{6,6},{7,14},{8,1},{9,9},{10... | collective-permute-start | bytes 589832 | tf_op jit(solution)/shard_map/ppermute | solution.py:38
  146.8 15.1 %collective-permute-start.46 = (bf16[96,1024]{1,0:T(8,128)(2,1)S(1)}, bf16[96,1024]{1,0:T(8,128)(2,1)}, u32[]{:S(2)}, u32[]{:S(2)}) collective-permute-start(bf16[96,1024]{1,0:T(8,128)(2,1)S(1)} %collective-permute-done.45), channel_id=1, source_target_pairs={{0,16},{8,24},{16,32},{24,40},{32,48},{40,56},{48,0},{56,8},{1,17}... | collective-permute-start | bytes 589832 | tf_op jit(solution)/shard_map/ppermute | solution.py:38
  147.4 15.5 %collective-permute-start.47 = (bf16[96,1024]{1,0:T(8,128)(2,1)S(1)}, bf16[96,1024]{1,0:T(8,128)(2,1)}, u32[]{:S(2)}, u32[]{:S(2)}) collective-permute-start(bf16[96,1024]{1,0:T(8,128)(2,1)S(1)} %collective-permute-done.45), channel_id=1, source_target_pairs={{0,32},{8,40},{16,48},{24,56},{32,0},{40,8},{48,16},{56,24},{1,33}... | collective-permute-start | bytes 589832 | tf_op jit(solution)/shard_map/ppermute | solution.py:38
  211.2 72.6 %collective-permute-start.62 = (bf16[2,512,1024]{2,1,0:T(8,128)(2,1)}, bf16[2,512,1024]{2,1,0:T(8,128)(2,1)}, u32[]{:S(2)}, u32[]{:S(2)}) collective-permute-start(bf16[2,512,1024]{2,1,0:T(8,128)(2,1)} %fusion.19), channel_id=1, source_target_pairs={{0,1},{1,0},{2,3},{3,2},{4,5},{5,4},{6,7},{7,6},{8,9},{9,8},{10,11... | collective-permute-start | bytes 6291464 | tf_op jit(solution)/shard_map/ppermute | solution.py:38
  215.3 12.5 %collective-permute-start.51 = (bf16[96,1024]{1,0:T(8,128)(2,1)S(1)}, bf16[96,1024]{1,0:T(8,128)(2,1)S(1)}, u32[]{:S(2)}, u32[]{:S(2)}) collective-permute-start(bf16[96,1024]{1,0:T(8,128)(2,1)S(1)} %get-tuple-element.199), channel_id=1, source_target_pairs={{0,16},{8,24},{16,32},{24,40},{32,48},{40,56},{48,0},{56,8},{1,17}... | collective-permute-start | bytes 589832 | tf_op jit(solution)/shard_map/ppermute | solution.py:38
  216.0 13.5 %collective-permute-start.40 = (bf16[96,1024]{1,0:T(8,128)(2,1)S(1)}, bf16[96,1024]{1,0:T(8,128)(2,1)S(1)}, u32[]{:S(2)}, u32[]{:S(2)}) collective-permute-start(bf16[96,1024]{1,0:T(8,128)(2,1)S(1)} %get-tuple-element.201), channel_id=1, source_target_pairs={{0,48},{8,56},{16,0},{24,8},{32,16},{40,24},{48,32},{56,40},{1,49}... | collective-permute-start | bytes 589832 | tf_op jit(solution)/shard_map/ppermute | solution.py:38
  223.6 12.7 %collective-permute-start.42 = (bf16[96,1024]{1,0:T(8,128)(2,1)S(1)}, bf16[96,1024]{1,0:T(8,128)(2,1)S(1)}, u32[]{:S(2)}, u32[]{:S(2)}) collective-permute-start(bf16[96,1024]{1,0:T(8,128)(2,1)S(1)} %get-tuple-element.202), channel_id=1, source_target_pairs={{0,16},{8,24},{16,32},{24,40},{32,48},{40,56},{48,0},{56,8},{1,17}... | collective-permute-start | bytes 589832 | tf_op jit(solution)/shard_map/ppermute | solution.py:38
  229.5 12.5 %collective-permute-start.52 = (bf16[96,1024]{1,0:T(8,128)(2,1)S(1)}, bf16[96,1024]{1,0:T(8,128)(2,1)S(1)}, u32[]{:S(2)}, u32[]{:S(2)}) collective-permute-start(bf16[96,1024]{1,0:T(8,128)(2,1)S(1)} %get-tuple-element.155), channel_id=1, source_target_pairs={{0,16},{8,24},{16,32},{24,40},{32,48},{40,56},{48,0},{56,8},{1,17}... | collective-permute-start | bytes 589832 | tf_op jit(solution)/shard_map/ppermute | solution.py:38
  229.6 13.7 %collective-permute-start.53 = (bf16[96,1024]{1,0:T(8,128)(2,1)S(1)}, bf16[96,1024]{1,0:T(8,128)(2,1)S(1)}, u32[]{:S(2)}, u32[]{:S(2)}) collective-permute-start(bf16[96,1024]{1,0:T(8,128)(2,1)S(1)} %get-tuple-element.155), channel_id=1, source_target_pairs={{0,32},{8,40},{16,48},{24,56},{32,0},{40,8},{48,16},{56,24},{1,33}... | collective-permute-start | bytes 589832 | tf_op jit(solution)/shard_map/ppermute | solution.py:38
  230.6 12.6 %collective-permute-start.54 = (bf16[96,1024]{1,0:T(8,128)(2,1)S(1)}, bf16[96,1024]{1,0:T(8,128)(2,1)S(1)}, u32[]{:S(2)}, u32[]{:S(2)}) collective-permute-start(bf16[96,1024]{1,0:T(8,128)(2,1)S(1)} %get-tuple-element.155), channel_id=1, source_target_pairs={{0,48},{8,56},{16,0},{24,8},{32,16},{40,24},{48,32},{56,40},{1,49}... | collective-permute-start | bytes 589832 | tf_op jit(solution)/shard_map/ppermute | solution.py:38
  236.6 32.5 %collective-permute-start.44 = (bf16[96,1024]{1,0:T(8,128)(2,1)S(1)}, bf16[96,1024]{1,0:T(8,128)(2,1)S(1)}, u32[]{:S(2)}, u32[]{:S(2)}) collective-permute-start(bf16[96,1024]{1,0:T(8,128)(2,1)S(1)} %broadcast_select_fusion.2), channel_id=1, source_target_pairs={{0,64},{1,72},{2,66},{3,74},{4,68},{5,76},{6,70},{7,78},{8,65},{9,... | collective-permute-start | bytes 589832 | tf_op jit(solution)/shard_map/ppermute | solution.py:38
  254.8 12.5 %collective-permute-start.58 = (bf16[96,1024]{1,0:T(8,128)(2,1)S(1)}, bf16[96,1024]{1,0:T(8,128)(2,1)S(1)}, u32[]{:S(2)}, u32[]{:S(2)}) collective-permute-start(bf16[96,1024]{1,0:T(8,128)(2,1)S(1)} %get-tuple-element.196), channel_id=1, source_target_pairs={{0,16},{8,24},{16,32},{24,40},{32,48},{40,56},{48,0},{56,8},{1,17}... | collective-permute-start | bytes 589832 | tf_op jit(solution)/shard_map/ppermute | solution.py:38
  266.9 15.0 %collective-permute-start.63 = (bf16[2,256,1024]{2,1,0:T(8,128)(2,1)}, bf16[2,256,1024]{2,1,0:T(8,128)(2,1)}, u32[]{:S(2)}, u32[]{:S(2)}) collective-permute-start(bf16[2,256,1024]{2,1,0:T(8,128)(2,1)} %fusion.93), channel_id=1, source_target_pairs={{0,1},{1,0},{2,3},{3,2},{4,5},{5,4},{6,7},{7,6},{8,9},{9,8},{10,11... | collective-permute-start | bytes 3145736 | tf_op jit(solution)/shard_map/ppermute | solution.py:38
  291.8 35.5 %collective-permute-start.70 = (bf16[2,192,1024]{2,1,0:T(8,128)(2,1)S(1)}, bf16[2,192,1024]{2,1,0:T(8,128)(2,1)S(1)}, u32[]{:S(2)}, u32[]{:S(2)}) collective-permute-start(bf16[2,192,1024]{2,1,0:T(8,128)(2,1)S(1)} %get-tuple-element.177), channel_id=1, source_target_pairs={{0,2},{1,3},{2,4},{3,5},{4,6},{5,7},{6,0},{7,1},{8,10},{9,11},{10,... | collective-permute-start | bytes 2359304 | tf_op jit(solution)/shard_map/ppermute | solution.py:38
  293.2 34.1 %collective-permute-start.71 = (bf16[2,192,1024]{2,1,0:T(8,128)(2,1)S(1)}, bf16[2,192,1024]{2,1,0:T(8,128)(2,1)S(1)}, u32[]{:S(2)}, u32[]{:S(2)}) collective-permute-start(bf16[2,192,1024]{2,1,0:T(8,128)(2,1)S(1)} %get-tuple-element.176), channel_id=1, source_target_pairs={{0,6},{1,7},{2,0},{3,1},{4,2},{5,3},{6,4},{7,5},{8,14},{9,15},{10,... | collective-permute-start | bytes 2359304 | tf_op jit(solution)/shard_map/ppermute | solution.py:38
  299.8 12.1 %collective-permute-start.66 = (bf16[96,1024]{1,0:T(8,128)(2,1)S(1)}, bf16[96,1024]{1,0:T(8,128)(2,1)S(1)}, u32[]{:S(2)}, u32[]{:S(2)}) collective-permute-start(bf16[96,1024]{1,0:T(8,128)(2,1)S(1)} %get-tuple-element.193), channel_id=1, source_target_pairs={{0,16},{8,24},{16,32},{24,40},{32,48},{40,56},{48,0},{56,8},{1,17}... | collective-permute-start | bytes 589832 | tf_op jit(solution)/shard_map/ppermute | solution.py:38
  314.3 12.9 %collective-permute-start.68 = (bf16[96,1024]{1,0:T(8,128)(2,1)S(1)}, bf16[96,1024]{1,0:T(8,128)(2,1)S(1)}, u32[]{:S(2)}, u32[]{:S(2)}) collective-permute-start(bf16[96,1024]{1,0:T(8,128)(2,1)S(1)} %get-tuple-element.160), channel_id=1, source_target_pairs={{0,32},{8,40},{16,48},{24,56},{32,0},{40,8},{48,16},{56,24},{1,33}... | collective-permute-start | bytes 589832 | tf_op jit(solution)/shard_map/ppermute | solution.py:38
  314.7 12.5 %collective-permute-start.69 = (bf16[96,1024]{1,0:T(8,128)(2,1)S(1)}, bf16[96,1024]{1,0:T(8,128)(2,1)S(1)}, u32[]{:S(2)}, u32[]{:S(2)}) collective-permute-start(bf16[96,1024]{1,0:T(8,128)(2,1)S(1)} %get-tuple-element.160), channel_id=1, source_target_pairs={{0,48},{8,56},{16,0},{24,8},{32,16},{40,24},{48,32},{56,40},{1,49}... | collective-permute-start | bytes 589832 | tf_op jit(solution)/shard_map/ppermute | solution.py:38
  334.7 20.3 %collective-permute-start.77 = (bf16[2,192,1024]{2,1,0:T(8,128)(2,1)S(1)}, bf16[2,192,1024]{2,1,0:T(8,128)(2,1)S(1)}, u32[]{:S(2)}, u32[]{:S(2)}) collective-permute-start(bf16[2,192,1024]{2,1,0:T(8,128)(2,1)S(1)} %get-tuple-element.100), channel_id=1, source_target_pairs={{0,4},{1,5},{2,6},{3,7},{4,0},{5,1},{6,2},{7,3},{8,12},{9,13},{10,... | collective-permute-start | bytes 2359304 | tf_op jit(solution)/shard_map/ppermute | solution.py:38
  340.2 27.1 %collective-permute-start.80 = (bf16[2,256,1024]{2,1,0:T(8,128)(2,1)S(1)}, bf16[2,256,1024]{2,1,0:T(8,128)(2,1)S(1)}, u32[]{:S(2)}, u32[]{:S(2)}) collective-permute-start(bf16[2,256,1024]{2,1,0:T(8,128)(2,1)S(1)} %fusion.89), channel_id=1, source_target_pairs={{0,1},{1,0},{2,3},{3,2},{4,5},{5,4},{6,7},{7,6},{8,9},{9,8},{10,11... | collective-permute-start | bytes 3145736 | tf_op jit(solution)/shard_map/ppermute | solution.py:38
  344.8 22.2 %collective-permute-start.78 = (bf16[2,128,1024]{2,1,0:T(8,128)(2,1)S(1)}, bf16[2,128,1024]{2,1,0:T(8,128)(2,1)S(1)}, u32[]{:S(2)}, u32[]{:S(2)}) collective-permute-start(bf16[2,128,1024]{2,1,0:T(8,128)(2,1)S(1)} %get-tuple-element.182), channel_id=1, source_target_pairs={{0,2},{1,3},{2,4},{3,5},{4,6},{5,7},{6,0},{7,1},{8,10},{9,11},{10,... | collective-permute-start | bytes 1572872 | tf_op jit(solution)/shard_map/ppermute | solution.py:38
  345.3 21.8 %collective-permute-start.79 = (bf16[2,128,1024]{2,1,0:T(8,128)(2,1)S(1)}, bf16[2,128,1024]{2,1,0:T(8,128)(2,1)S(1)}, u32[]{:S(2)}, u32[]{:S(2)}) collective-permute-start(bf16[2,128,1024]{2,1,0:T(8,128)(2,1)S(1)} %get-tuple-element.181), channel_id=1, source_target_pairs={{0,6},{1,7},{2,0},{3,1},{4,2},{5,3},{6,4},{7,5},{8,14},{9,15},{10,... | collective-permute-start | bytes 1572872 | tf_op jit(solution)/shard_map/ppermute | solution.py:38
  369.5 26.9 %collective-permute-start.95 = (bf16[2,192,1024]{2,1,0:T(8,128)(2,1)}, bf16[2,192,1024]{2,1,0:T(8,128)(2,1)}, u32[]{:S(2)}, u32[]{:S(2)}) collective-permute-start(bf16[2,192,1024]{2,1,0:T(8,128)(2,1)} %pad_maximum_fusion.14), channel_id=1, source_target_pairs={{0,4},{1,5},{2,6},{3,7},{4,0},{5,1},{6,2},{7,3},{8,12},{9,13},{10,... | collective-permute-start | bytes 2359304 | tf_op jit(solution)/shard_map/ppermute | solution.py:38
  374.2 22.2 %collective-permute-start.93 = (bf16[2,64,1024]{2,1,0:T(8,128)(2,1)}, bf16[2,64,1024]{2,1,0:T(8,128)(2,1)S(1)}, u32[]{:S(2)}, u32[]{:S(2)}) collective-permute-start(bf16[2,64,1024]{2,1,0:T(8,128)(2,1)} %get-tuple-element.188), channel_id=1, source_target_pairs={{0,2},{1,3},{2,4},{3,5},{4,6},{5,7},{6,0},{7,1},{8,10},{9,11},{10,... | collective-permute-start | bytes 786440 | tf_op jit(solution)/shard_map/ppermute | solution.py:38
  374.6 21.7 %collective-permute-start.94 = (bf16[2,64,1024]{2,1,0:T(8,128)(2,1)S(1)}, bf16[2,64,1024]{2,1,0:T(8,128)(2,1)S(1)}, u32[]{:S(2)}, u32[]{:S(2)}) collective-permute-start(bf16[2,64,1024]{2,1,0:T(8,128)(2,1)S(1)} %get-tuple-element.187), channel_id=1, source_target_pairs={{0,6},{1,7},{2,0},{3,1},{4,2},{5,3},{6,4},{7,5},{8,14},{9,15},{10,... | collective-permute-start | bytes 786440 | tf_op jit(solution)/shard_map/ppermute | solution.py:38
  399.1 12.8 %collective-permute-start.97 = (bf16[192,1024]{1,0:T(8,128)(2,1)}, bf16[192,1024]{1,0:T(8,128)(2,1)S(1)}, u32[]{:S(2)}, u32[]{:S(2)}) collective-permute-start(bf16[192,1024]{1,0:T(8,128)(2,1)} %get-tuple-element.184), channel_id=1, source_target_pairs={{0,72},{8,64},{16,88},{24,80},{32,104},{40,96},{48,120},{56,112},{... | collective-permute-start | bytes 1179656 | tf_op jit(solution)/shard_map/ppermute | solution.py:38
  401.7 17.1 %collective-permute-start.98 = (bf16[192,1024]{1,0:T(8,128)(2,1)}, bf16[192,1024]{1,0:T(8,128)(2,1)}, u32[]{:S(2)}, u32[]{:S(2)}) collective-permute-start(bf16[192,1024]{1,0:T(8,128)(2,1)} %get-tuple-element.185), channel_id=1, source_target_pairs={{0,8},{8,0},{16,24},{24,16},{32,40},{40,32},{48,56},{56,48},{64,72... | collective-permute-start | bytes 1179656 | tf_op jit(solution)/shard_map/ppermute | solution.py:38
  402.9 20.5 %collective-permute-start.83 = (f32[12,1024]{1,0:T(8,128)S(1)}, f32[12,1024]{1,0:T(8,128)S(1)}, u32[]{:S(2)}, u32[]{:S(2)}) collective-permute-start(f32[12,1024]{1,0:T(8,128)S(1)} %get-tuple-element.228), channel_id=1, source_target_pairs={{0,64},{8,72},{16,80},{24,88},{32,96},{40,104},{48,112},{56,120},{... | collective-permute-start | bytes 147464 | tf_op jit(solution)/shard_map/ppermute | solution.py:38
  403.0 20.4 %collective-permute-start.84 = (f32[12,1024]{1,0:T(8,128)S(1)}, f32[12,1024]{1,0:T(8,128)S(1)}, u32[]{:S(2)}, u32[]{:S(2)}) collective-permute-start(f32[12,1024]{1,0:T(8,128)S(1)} %get-tuple-element.228), channel_id=1, source_target_pairs={{0,72},{8,64},{16,88},{24,80},{32,104},{40,96},{48,120},{56,112},{... | collective-permute-start | bytes 147464 | tf_op jit(solution)/shard_map/ppermute | solution.py:38
  411.1 12.3 %collective-permute-start.85 = (f32[12,1024]{1,0:T(8,128)S(1)}, f32[12,1024]{1,0:T(8,128)S(1)}, u32[]{:S(2)}, u32[]{:S(2)}) collective-permute-start(f32[12,1024]{1,0:T(8,128)S(1)} %get-tuple-element.229), channel_id=1, source_target_pairs={{0,8},{8,0},{16,24},{24,16},{32,40},{40,32},{48,56},{56,48},{64,72... | collective-permute-start | bytes 147464 | tf_op jit(solution)/shard_map/ppermute | solution.py:38
  420.5 16.2 %collective-permute-start.100 = (bf16[192,1024]{1,0:T(8,128)(2,1)S(1)}, bf16[192,1024]{1,0:T(8,128)(2,1)S(1)}, u32[]{:S(2)}, u32[]{:S(2)}) collective-permute-start(bf16[192,1024]{1,0:T(8,128)(2,1)S(1)} %get-tuple-element.151), channel_id=1, source_target_pairs={{0,4},{1,5},{2,6},{3,7},{4,0},{5,1},{6,2},{7,3},{8,12},{9,13},{10,... | collective-permute-start | bytes 1179656 | tf_op jit(solution)/shard_map/ppermute | solution.py:38
  423.4 19.6 %collective-permute-start.86 = (f32[12,1024]{1,0:T(8,128)S(1)}, f32[12,1024]{1,0:T(8,128)S(1)}, u32[]{:S(2)}, u32[]{:S(2)}) collective-permute-start(f32[12,1024]{1,0:T(8,128)S(1)} %add_add_fusion.2), channel_id=1, source_target_pairs={{0,1},{1,0},{2,3},{3,2},{4,5},{5,4},{6,7},{7,6},{8,9},{9,8},{10,11... | collective-permute-start | bytes 147464 | tf_op jit(solution)/shard_map/ppermute | solution.py:38
  428.0 13.1 %collective-permute-start.101 = (bf16[192,1024]{1,0:T(8,128)(2,1)S(1)}, bf16[192,1024]{1,0:T(8,128)(2,1)S(1)}, u32[]{:S(2)}, u32[]{:S(2)}) collective-permute-start(bf16[192,1024]{1,0:T(8,128)(2,1)S(1)} %get-tuple-element.151), channel_id=1, source_target_pairs={{0,6},{1,7},{2,0},{3,1},{4,2},{5,3},{6,4},{7,5},{8,14},{9,15},{10,... | collective-permute-start | bytes 1179656 | tf_op jit(solution)/shard_map/ppermute | solution.py:38
  441.1 21.3 %collective-permute-start.102 = (bf16[768,1024]{1,0:T(8,128)(2,1)S(1)}, bf16[768,1024]{1,0:T(8,128)(2,1)S(1)}, u32[]{:S(2)}, u32[]{:S(2)}) collective-permute-start(bf16[768,1024]{1,0:T(8,128)(2,1)S(1)} %bitcast.433), channel_id=1, source_target_pairs={{0,1},{1,0},{2,3},{3,2},{4,5},{5,4},{6,7},{7,6},{8,9},{9,8},{10,11... | collective-permute-start | bytes 4718600 | tf_op jit(solution)/shard_map/ppermute | solution.py:38
  (160 other events, 1248.1 us)

commit v6 on v5

--- a/solution.py
+++ b/solution.py
@@ -539,30 +539,28 @@
             value, kept["one"] = tied(value, jnp.concatenate(halved, axis=2))
             return value
         if step == 1:
-            kept["near"] = near_y(kept["one"])
+            value, kept["near"] = tied(value, near_y(kept["one"]))
             kept["feed"] = group
             return value
         if step == 2:
-            value, kept["near"] = tied(value, kept["near"])
+            value, kept["feed"] = tied(value, over_cores(kept["feed"], core))
             return value
         if step == 3:
-            kept["one"] = far_y(kept["one"], kept["near"])
-            value, kept["feed"] = tied(value, over_cores(kept["feed"], core))
+            value, kept["one"] = tied(value, far_y(kept["one"], kept["near"]))
             return value
-        near, attention = near_y(kept["feed"]), over_cores(group, core)
-        value, *rest = tied(value, kept["one"], near, attention)
-        kept["one"], kept["near"], kept["attention"] = rest
+        feed = far_y(kept["feed"], near_y(kept["feed"]))
+        value, kept["feed"], kept["attention"] = tied(value, feed, over_cores(group, core))
         return value
 
     last_grad, early_zero, late_zero = layer_backward(
         middle_low.astype(f32), allowed, vectors[0], weights_first, saved_first, reduce_along
     )
     last_low = last_grad.astype(bf16)
-    y = dp // 2
-    near = jnp.concatenate([kept["near"], near_y(kept["attention"])], axis=1)
-    far = [pick(kept[name], (y + 2) % 4, 1) for name in ("feed", "attention")]
-    zero = near + along_y(jnp.concatenate(far, axis=1), 2).astype(f32)
-    total = back_over_y(over_z(zero.astype(bf16), kept["one"], pipe, high))
+    attention = near_y(kept["attention"])
+    far = along_y(pick(kept["attention"], (dp // 2 + 2) % 4, 1), 2)
+    attention = (attention + far.astype(f32)).astype(bf16)
+    zero = jnp.concatenate([kept["feed"], attention], axis=1)
+    total = back_over_y(over_z(zero, kept["one"], pipe, high))
 
     def bias_rows(fc_bias_grad):
         return place(jnp.zeros((4, WIDTH), f32), fc_bias_grad[None], (x, 0))

time: 480 us -> 491 us (1.023)
  local copies, waits for them, and re-layouts: 53.8 us -> 62.2 us
  starting transfers between devices: 152 us -> 145 us
  waiting for transfers between devices: 166 us -> 171 us
    ppermute x103 -> x104, starting transfers between devices: 152 us -> 145 us  [move(): return lax.ppermute(array, axes, sorted(pairs.items()))]
    unnamed x243 -> x251, local copies, waits for them, and re-layouts: 31.3 us -> 38.1 us
    ppermute x103 -> x104, waiting for transfers between devices: 166 us -> 171 us  [move(): return lax.ppermute(array, axes, sorted(pairs.items()))]
  transfers between devices with their start and end apart: 103 -> 104, of which waited for: 45 -> 49; matrix products, arithmetic and copies ran while one was open for 19% -> 21% of each run, Pallas kernels for 1% -> 1%
where the time goes in v6:
time: 491 us; the launch traced here: 483 us
  waiting for transfers between devices  171 us (35%)
  starting transfers between devices  145 us (30%)
  local copies, waits for them, and re-layouts  62.2 us (13%)
  other arithmetic  51 us (10%)
  matrix products  46.1 us (9%)
    ppermute x104, waiting for transfers between devices, move(): return lax.ppermute(array, axes, sorted(pairs.items()))  171 us
    ppermute x104, starting transfers between devices, move(): return lax.ppermute(array, axes, sorted(pairs.items()))  145 us
    unnamed x251, local copies, waits for them, and re-layouts  38.1 us
    dot_general x24, matrix products, dot(): lax.dot_general(left, right, (((left_dim,), (right_dim,)), ((), ())), pre...  29.7 us
  transfers between devices with their start and end apart: 104, of which 49 were waited for; matrix products, arithmetic and copies ran while one was open for 21% of the time, Pallas kernels for 1%

profile of v6, /device:TPU:1, one launch (start us, length us, event | category | flops | bytes accessed | tf_op | source)
XLA Modules:
  0.0 482.8 jit_solution(15009705182834447486)
XLA Ops:
  15.0 5.4 %collective-permute-start = (bf16[96,1024]{1,0:T(8,128)(2,1)S(1)}, bf16[96,1024]{1,0:T(8,128)(2,1)S(1)}, u32[]{:S(2)}, u32[]{:S(2)}) collective-permute-start(bf16[96,1024]{1,0:T(8,128)(2,1)S(1)} %dynamic-slice_bitcast_fusion.12), channel_id=1, source_target_pairs={{0,0},{1,8},{2,2},{3,10},{4,4},{5,12},{6,6},{7,14},{8,1},{9,9},{10... | collective-permute-start | bytes 589832 | tf_op jit(solution)/shard_map/ppermute | solution.py:38
  21.5 9.0 %collective-permute-done = bf16[96,1024]{1,0:T(8,128)(2,1)S(1)} collective-permute-done((bf16[96,1024]{1,0:T(8,128)(2,1)S(1)}, bf16[96,1024]{1,0:T(8,128)(2,1)S(1)}, u32[]{:S(2)}, u32[]{:S(2)}) %collective-permute-start) | collective-permute-done | bytes 196640 | tf_op jit(solution)/shard_map/ppermute | solution.py:38
  38.1 4.5 collective-permute-done.6
  44.8 3.2 collective-permute-start.8
  61.3 3.2 fusion.80
  80.6 7.3 %collective-permute-done.15.refs_3_ = bf16[512,512]{1,0:T(8,128)(2,1)S(1)} collective-permute-done((bf16[512,512]{1,0:T(8,128)(2,1)}, bf16[512,512]{1,0:T(8,128)(2,1)S(1)}, u32[]{:S(2)}, u32[]{:S(2)}) %collective-permute-start.15) | collective-permute-done | bytes 524320 | tf_op jit(solution)/shard_map/ppermute | solution.py:38
  87.9 2.7 collective-permute-start.20
  99.3 5.7 %collective-permute-done.18 = bf16[96,1024]{1,0:T(8,128)(2,1)S(1)} collective-permute-done((bf16[96,1024]{1,0:T(8,128)(2,1)S(1)}, bf16[96,1024]{1,0:T(8,128)(2,1)S(1)}, u32[]{:S(2)}, u32[]{:S(2)}) %collective-permute-start.18) | collective-permute-done | bytes 196640 | tf_op jit(solution)/shard_map/ppermute | solution.py:38
  111.5 6.0 %collective-permute-done.21 = bf16[96,1024]{1,0:T(8,128)(2,1)S(1)} collective-permute-done((bf16[96,1024]{1,0:T(8,128)(2,1)S(1)}, bf16[96,1024]{1,0:T(8,128)(2,1)S(1)}, u32[]{:S(2)}, u32[]{:S(2)}) %collective-permute-start.21) | collective-permute-done | bytes 196640 | tf_op jit(solution)/shard_map/ppermute | solution.py:38
  122.4 3.6 collective-permute-start.45
  156.9 4.2 collective-permute-done.30
  161.1 3.5 collective-permute-done.31
  164.7 2.8 fusion.77
  183.3 4.5 collective-permute-done.34
  190.3 4.3 collective-permute-done.36
  198.2 5.7 %collective-permute-done.37 = bf16[96,1024]{1,0:T(8,128)(2,1)S(1)} collective-permute-done((bf16[96,1024]{1,0:T(8,128)(2,1)S(1)}, bf16[96,1024]{1,0:T(8,128)(2,1)S(1)}, u32[]{:S(2)}, u32[]{:S(2)}) %collective-permute-start.37) | collective-permute-done | bytes 196640 | tf_op jit(solution)/shard_map/ppermute | solution.py:38
  226.4 5.1 %collective-permute-done.49 = bf16[96,1024]{1,0:T(8,128)(2,1)} collective-permute-done((bf16[96,1024]{1,0:T(8,128)(2,1)}, bf16[96,1024]{1,0:T(8,128)(2,1)}, u32[]{:S(2)}, u32[]{:S(2)}) %collective-permute-start.49) | collective-permute-done | bytes 196640 | tf_op jit(solution)/shard_map/ppermute | solution.py:38
  231.6 4.2 collective-permute-start.42
  247.1 3.9 collective-permute-done.53
  251.5 4.1 multiply_reduce_fusion.1
  271.6 2.6 collective-permute-done.57
  274.3 4.9 %collective-permute-done.58 = bf16[96,1024]{1,0:T(8,128)(2,1)S(1)} collective-permute-done((bf16[96,1024]{1,0:T(8,128)(2,1)S(1)}, bf16[96,1024]{1,0:T(8,128)(2,1)S(1)}, u32[]{:S(2)}, u32[]{:S(2)}) %collective-permute-start.58) | collective-permute-done | bytes 196640 | tf_op jit(solution)/shard_map/ppermute | solution.py:38
  283.6 8.8 %collective-permute-done.59 = bf16[96,1024]{1,0:T(8,128)(2,1)S(1)} collective-permute-done((bf16[96,1024]{1,0:T(8,128)(2,1)S(1)}, bf16[96,1024]{1,0:T(8,128)(2,1)S(1)}, u32[]{:S(2)}, u32[]{:S(2)}) %collective-permute-start.59) | collective-permute-done | bytes 196640 | tf_op jit(solution)/shard_map/ppermute | solution.py:38
  293.0 3.6 collective-permute-start.43
  298.9 2.6 fusion.1
  314.9 3.8 collective-permute-done.64
  318.7 2.8 collective-permute-start.72
  322.3 3.8 collective-permute-done.66
  327.4 2.7 collective-permute-start.74
  332.4 3.2 collective-permute-start.70
  335.8 4.8 collective-permute-done.69
  340.6 3.4 collective-permute-done.70
  345.0 3.3 collective-permute-done.74
  365.7 6.3 %collective-permute-done.78 = bf16[2,128,1024]{2,1,0:T(8,128)(2,1)S(1)} collective-permute-done((bf16[2,128,1024]{2,1,0:T(8,128)(2,1)S(1)}, bf16[2,128,1024]{2,1,0:T(8,128)(2,1)S(1)}, u32[]{:S(2)}, u32[]{:S(2)}) %collective-permute-start.78) | collective-permute-done | bytes 524320 | tf_op jit(solution)/shard_map/ppermute | solution.py:38
  375.3 3.1 collective-permute-start.75
  380.5 5.8 %collective-permute-done.75 = bf16[96,1024]{1,0:T(8,128)(2,1)S(1)} collective-permute-done((bf16[96,1024]{1,0:T(8,128)(2,1)}, bf16[96,1024]{1,0:T(8,128)(2,1)S(1)}, u32[]{:S(2)}, u32[]{:S(2)}) %collective-permute-start.75) | collective-permute-done | bytes 196640 | tf_op jit(solution)/shard_map/ppermute | solution.py:38
  386.3 4.2 collective-permute-done.77
  398.1 5.8 %collective-permute-done.94 = bf16[2,64,1024]{2,1,0:T(8,128)(2,1)S(1)} collective-permute-done((bf16[2,64,1024]{2,1,0:T(8,128)(2,1)S(1)}, bf16[2,64,1024]{2,1,0:T(8,128)(2,1)S(1)}, u32[]{:S(2)}, u32[]{:S(2)}) %collective-permute-start.94) | collective-permute-done | bytes 262176 | tf_op jit(solution)/shard_map/ppermute | solution.py:38
  403.9 4.5 collective-permute-done.96
  410.0 2.7 collective-permute-start.98
  417.0 2.7 collective-permute-done.97
  419.7 8.6 %collective-permute-done.99 = bf16[192,1024]{1,0:T(8,128)(2,1)S(1)} collective-permute-done((bf16[192,1024]{1,0:T(8,128)(2,1)}, bf16[192,1024]{1,0:T(8,128)(2,1)S(1)}, u32[]{:S(2)}, u32[]{:S(2)}) %collective-permute-start.99) | collective-permute-done | bytes 393248 | tf_op jit(solution)/shard_map/ppermute | solution.py:38
  431.5 7.1 %collective-permute-start.87 = (f32[12,1024]{1,0:T(8,128)S(1)}, f32[12,1024]{1,0:T(8,128)S(1)}, u32[]{:S(2)}, u32[]{:S(2)}) collective-permute-start(f32[12,1024]{1,0:T(8,128)S(1)} %add_add_fusion.2), channel_id=1, source_target_pairs={{0,1},{1,0},{2,3},{3,2},{4,5},{5,4},{6,7},{7,6},{8,9},{9,8},{10,11... | collective-permute-start | bytes 147464 | tf_op jit(solution)/shard_map/ppermute | solution.py:38
  440.8 2.7 collective-permute-done.101
  443.5 6.9 %collective-permute-done.102 = bf16[192,1024]{1,0:T(8,128)(2,1)S(1)} collective-permute-done((bf16[192,1024]{1,0:T(8,128)(2,1)S(1)}, bf16[192,1024]{1,0:T(8,128)(2,1)S(1)}, u32[]{:S(2)}, u32[]{:S(2)}) %collective-permute-start.102) | collective-permute-done | bytes 393248 | tf_op jit(solution)/shard_map/ppermute | solution.py:38
  454.9 3.2 collective-permute-start.83
  458.5 5.8 %collective-permute-start.82 = (bf16[96,1024]{1,0:T(8,128)(2,1)S(1)}, bf16[96,1024]{1,0:T(8,128)(2,1)S(1)}, u32[]{:S(2)}, u32[]{:S(2)}) collective-permute-start(bf16[96,1024]{1,0:T(8,128)(2,1)S(1)} %get-tuple-element.168), channel_id=1, source_target_pairs={{0,0},{1,8},{2,2},{3,10},{4,4},{5,12},{6,6},{7,14},{8,1},{9,9},{10... | collective-permute-start | bytes 589832 | tf_op jit(solution)/shard_map/ppermute | solution.py:38
  465.3 2.7 collective-permute-start.92
  (637 shorter events, 263.7 us)
Async XLA Ops:
  6.4 14.4 %collective-permute-start.4 = (bf16[16,512]{1,0:T(8,128)(2,1)S(1)}, bf16[16,512]{1,0:T(8,128)(2,1)S(1)}, u32[]{:S(2)}, u32[]{:S(2)}) collective-permute-start(bf16[16,512]{1,0:T(8,128)(2,1)S(1)} %reshape.743.refs_2_), channel_id=1, source_target_pairs={{0,64},{8,72},{16,80},{24,88},{32,96},{40,104},{48,112},{56,120},{... | collective-permute-start | bytes 49160 | tf_op jit(solution)/shard_map/ppermute | solution.py:38
  12.3 18.6 %collective-permute-start.1 = (bf16[528,512]{1,0:T(8,128)(2,1)}, bf16[528,512]{1,0:T(8,128)(2,1)}, u32[]{:S(2)}, u32[]{:S(2)}) collective-permute-start(bf16[528,512]{1,0:T(8,128)(2,1)} %pad_maximum_fusion.16), channel_id=1, source_target_pairs={{0,64},{8,72},{16,80},{24,88},{32,96},{40,104},{48,112},{56,120},{... | collective-permute-start | bytes 1622024 | tf_op jit(solution)/shard_map/ppermute | solution.py:38
  13.9 16.9 %collective-permute-start.2 = (bf16[528,512]{1,0:T(8,128)(2,1)}, bf16[528,512]{1,0:T(8,128)(2,1)}, u32[]{:S(2)}, u32[]{:S(2)}) collective-permute-start(bf16[528,512]{1,0:T(8,128)(2,1)} %pad_maximum_fusion.16), channel_id=1, source_target_pairs={{0,72},{8,64},{16,88},{24,80},{32,104},{40,96},{48,120},{56,112},{... | collective-permute-start | bytes 1622024 | tf_op jit(solution)/shard_map/ppermute | solution.py:38
  15.0 15.5 %collective-permute-start = (bf16[96,1024]{1,0:T(8,128)(2,1)S(1)}, bf16[96,1024]{1,0:T(8,128)(2,1)S(1)}, u32[]{:S(2)}, u32[]{:S(2)}) collective-permute-start(bf16[96,1024]{1,0:T(8,128)(2,1)S(1)} %dynamic-slice_bitcast_fusion.12), channel_id=1, source_target_pairs={{0,0},{1,8},{2,2},{3,10},{4,4},{5,12},{6,6},{7,14},{8,1},{9,9},{10... | collective-permute-start | bytes 589832 | tf_op jit(solution)/shard_map/ppermute | solution.py:38
  20.5 50.2 %collective-permute-start.14 = (s32[8,96]{1,0:T(8,128)S(1)}, s32[8,96]{1,0:T(8,128)}, u32[]{:S(2)}, u32[]{:S(2)}) collective-permute-start(s32[8,96]{1,0:T(8,128)S(1)} %reshape.746), channel_id=1, source_target_pairs={{0,1},{1,0},{2,3},{3,2},{4,5},{5,4},{6,7},{7,6},{8,9},{9,8},{10,11... | collective-permute-start | bytes 9224 | tf_op jit(solution)/shard_map/ppermute | solution.py:38
  30.8 17.2 %collective-permute-start.3 = (bf16[528,512]{1,0:T(8,128)(2,1)}, bf16[528,512]{1,0:T(8,128)(2,1)}, u32[]{:S(2)}, u32[]{:S(2)}) collective-permute-start(bf16[528,512]{1,0:T(8,128)(2,1)} %pad_maximum_fusion.16), channel_id=1, source_target_pairs={{0,8},{8,0},{16,24},{24,16},{32,40},{40,32},{48,56},{56,48},{64,72... | collective-permute-start | bytes 1622024 | tf_op jit(solution)/shard_map/ppermute | solution.py:38
  56.3 16.0 %collective-permute-start.12 = (bf16[512,512]{1,0:T(8,128)(2,1)}, bf16[512,512]{1,0:T(8,128)(2,1)S(1)}, u32[]{:S(2)}, u32[]{:S(2)}) collective-permute-start(bf16[512,512]{1,0:T(8,128)(2,1)} %dynamic-slice_bitcast_fusion.7), channel_id=1, source_target_pairs={{0,64},{8,72},{16,80},{24,88},{32,96},{40,104},{48,112},{56,120},{... | collective-permute-start | bytes 1572872 | tf_op jit(solution)/shard_map/ppermute | solution.py:38
  57.3 15.1 %collective-permute-start.13 = (bf16[512,512]{1,0:T(8,128)(2,1)}, bf16[512,512]{1,0:T(8,128)(2,1)S(1)}, u32[]{:S(2)}, u32[]{:S(2)}) collective-permute-start(bf16[512,512]{1,0:T(8,128)(2,1)} %dynamic-slice_bitcast_fusion.7), channel_id=1, source_target_pairs={{0,72},{8,64},{16,88},{24,80},{32,104},{40,96},{48,120},{56,112},{... | collective-permute-start | bytes 1572872 | tf_op jit(solution)/shard_map/ppermute | solution.py:38
  72.4 15.5 %collective-permute-start.15 = (bf16[512,512]{1,0:T(8,128)(2,1)}, bf16[512,512]{1,0:T(8,128)(2,1)S(1)}, u32[]{:S(2)}, u32[]{:S(2)}) collective-permute-start(bf16[512,512]{1,0:T(8,128)(2,1)} %dynamic-slice_bitcast_fusion.7), channel_id=1, source_target_pairs={{0,8},{8,0},{16,24},{24,16},{32,40},{40,32},{48,56},{56,48},{64,72... | collective-permute-start | bytes 1572872 | tf_op jit(solution)/shard_map/ppermute | solution.py:38
  87.9 17.2 %collective-permute-start.19 = (bf16[256,1024]{1,0:T(8,128)(2,1)S(1)}, bf16[256,1024]{1,0:T(8,128)(2,1)S(1)}, u32[]{:S(2)}, u32[]{:S(2)}) collective-permute-start(bf16[256,1024]{1,0:T(8,128)(2,1)S(1)} %copy-done.58), channel_id=1, source_target_pairs={{0,64},{8,72},{16,80},{24,88},{32,96},{40,104},{48,112},{56,120},{... | collective-permute-start | bytes 1572872 | tf_op jit(solution)/shard_map/ppermute | solution.py:38
  87.9 17.2 %collective-permute-start.20 = (bf16[256,1024]{1,0:T(8,128)(2,1)S(1)}, bf16[256,1024]{1,0:T(8,128)(2,1)S(1)}, u32[]{:S(2)}, u32[]{:S(2)}) collective-permute-start(bf16[256,1024]{1,0:T(8,128)(2,1)S(1)} %copy-done.58), channel_id=1, source_target_pairs={{0,72},{8,64},{16,88},{24,80},{32,104},{40,96},{48,120},{56,112},{... | collective-permute-start | bytes 1572872 | tf_op jit(solution)/shard_map/ppermute | solution.py:38
  105.5 13.8 %collective-permute-start.24 = (bf16[256,1024]{1,0:T(8,128)(2,1)S(1)}, bf16[256,1024]{1,0:T(8,128)(2,1)S(1)}, u32[]{:S(2)}, u32[]{:S(2)}) collective-permute-start(bf16[256,1024]{1,0:T(8,128)(2,1)S(1)} %copy-done.58), channel_id=1, source_target_pairs={{0,8},{8,0},{16,24},{24,16},{32,40},{40,32},{48,56},{56,48},{64,72... | collective-permute-start | bytes 1572872 | tf_op jit(solution)/shard_map/ppermute | solution.py:38
  109.3 16.7 %collective-permute-start.25 = (bf16[3,512,512]{2,1,0:T(8,128)(2,1)S(1)}, bf16[3,512,512]{2,1,0:T(8,128)(2,1)S(1)}, u32[]{:S(2)}, u32[]{:S(2)}) collective-permute-start(bf16[3,512,512]{2,1,0:T(8,128)(2,1)S(1)} %pad_maximum_fusion.1), channel_id=1, source_target_pairs={{0,1},{1,0},{2,3},{3,2},{4,5},{5,4},{6,7},{7,6},{8,9},{9,8},{10,11... | collective-permute-start | bytes 4718600 | tf_op jit(solution)/shard_map/ppermute | solution.py:38
  122.4 19.8 %collective-permute-start.45 = (bf16[96,1024]{1,0:T(8,128)(2,1)}, bf16[96,1024]{1,0:T(8,128)(2,1)}, u32[]{:S(2)}, u32[]{:S(2)}) collective-permute-start(bf16[96,1024]{1,0:T(8,128)(2,1)} %dynamic-slice_bitcast_fusion.11), channel_id=1, source_target_pairs={{0,0},{1,8},{2,2},{3,10},{4,4},{5,12},{6,6},{7,14},{8,1},{9,9},{10... | collective-permute-start | bytes 589832 | tf_op jit(solution)/shard_map/ppermute | solution.py:38
  133.4 12.2 %collective-permute-start.27 = (bf16[96,1024]{1,0:T(8,128)(2,1)}, bf16[96,1024]{1,0:T(8,128)(2,1)}, u32[]{:S(2)}, u32[]{:S(2)}) collective-permute-start(bf16[96,1024]{1,0:T(8,128)(2,1)} %get-tuple-element.214), channel_id=1, source_target_pairs={{0,48},{8,56},{16,0},{24,8},{32,16},{40,24},{48,32},{56,40},{1,49}... | collective-permute-start | bytes 589832 | tf_op jit(solution)/shard_map/ppermute | solution.py:38
  135.7 12.3 %collective-permute-start.29 = (bf16[96,1024]{1,0:T(8,128)(2,1)}, bf16[96,1024]{1,0:T(8,128)(2,1)}, u32[]{:S(2)}, u32[]{:S(2)}) collective-permute-start(bf16[96,1024]{1,0:T(8,128)(2,1)} %get-tuple-element.215), channel_id=1, source_target_pairs={{0,16},{8,24},{16,32},{24,40},{32,48},{40,56},{48,0},{56,8},{1,17}... | collective-permute-start | bytes 589832 | tf_op jit(solution)/shard_map/ppermute | solution.py:38
  142.2 12.6 %collective-permute-start.46 = (bf16[96,1024]{1,0:T(8,128)(2,1)}, bf16[96,1024]{1,0:T(8,128)(2,1)S(1)}, u32[]{:S(2)}, u32[]{:S(2)}) collective-permute-start(bf16[96,1024]{1,0:T(8,128)(2,1)} %collective-permute-done.45), channel_id=1, source_target_pairs={{0,16},{8,24},{16,32},{24,40},{32,48},{40,56},{48,0},{56,8},{1,17}... | collective-permute-start | bytes 589832 | tf_op jit(solution)/shard_map/ppermute | solution.py:38
  144.2 26.0 %collective-permute-start.47 = (bf16[96,1024]{1,0:T(8,128)(2,1)}, bf16[96,1024]{1,0:T(8,128)(2,1)}, u32[]{:S(2)}, u32[]{:S(2)}) collective-permute-start(bf16[96,1024]{1,0:T(8,128)(2,1)} %collective-permute-done.45), channel_id=1, source_target_pairs={{0,32},{8,40},{16,48},{24,56},{32,0},{40,8},{48,16},{56,24},{1,33}... | collective-permute-start | bytes 589832 | tf_op jit(solution)/shard_map/ppermute | solution.py:38
  151.1 13.6 %collective-permute-start.31 = (bf16[96,1024]{1,0:T(8,128)(2,1)}, bf16[96,1024]{1,0:T(8,128)(2,1)}, u32[]{:S(2)}, u32[]{:S(2)}) collective-permute-start(bf16[96,1024]{1,0:T(8,128)(2,1)} %fusion.131), channel_id=1, source_target_pairs={{0,32},{8,40},{16,48},{24,56},{32,0},{40,8},{48,16},{56,24},{1,33}... | collective-permute-start | bytes 589832 | tf_op jit(solution)/shard_map/ppermute | solution.py:38
  154.8 17.1 %collective-permute-start.48 = (bf16[96,1024]{1,0:T(8,128)(2,1)}, bf16[96,1024]{1,0:T(8,128)(2,1)}, u32[]{:S(2)}, u32[]{:S(2)}) collective-permute-start(bf16[96,1024]{1,0:T(8,128)(2,1)} %collective-permute-done.45), channel_id=1, source_target_pairs={{0,48},{8,56},{16,0},{24,8},{32,16},{40,24},{48,32},{56,40},{1,49}... | collective-permute-start | bytes 589832 | tf_op jit(solution)/shard_map/ppermute | solution.py:38
  218.1 79.0 %collective-permute-start.62 = (bf16[2,512,1024]{2,1,0:T(8,128)(2,1)}, bf16[2,512,1024]{2,1,0:T(8,128)(2,1)}, u32[]{:S(2)}, u32[]{:S(2)}) collective-permute-start(bf16[2,512,1024]{2,1,0:T(8,128)(2,1)} %fusion.19), channel_id=1, source_target_pairs={{0,1},{1,0},{2,3},{3,2},{4,5},{5,4},{6,7},{7,6},{8,9},{9,8},{10,11... | collective-permute-start | bytes 6291464 | tf_op jit(solution)/shard_map/ppermute | solution.py:38
  222.9 12.9 %collective-permute-start.51 = (bf16[96,1024]{1,0:T(8,128)(2,1)}, bf16[96,1024]{1,0:T(8,128)(2,1)}, u32[]{:S(2)}, u32[]{:S(2)}) collective-permute-start(bf16[96,1024]{1,0:T(8,128)(2,1)} %get-tuple-element.204), channel_id=1, source_target_pairs={{0,16},{8,24},{16,32},{24,40},{32,48},{40,56},{48,0},{56,8},{1,17}... | collective-permute-start | bytes 589832 | tf_op jit(solution)/shard_map/ppermute | solution.py:38
  224.2 15.4 %collective-permute-start.40 = (bf16[96,1024]{1,0:T(8,128)(2,1)}, bf16[96,1024]{1,0:T(8,128)(2,1)}, u32[]{:S(2)}, u32[]{:S(2)}) collective-permute-start(bf16[96,1024]{1,0:T(8,128)(2,1)} %get-tuple-element.206), channel_id=1, source_target_pairs={{0,48},{8,56},{16,0},{24,8},{32,16},{40,24},{48,32},{56,40},{1,49}... | collective-permute-start | bytes 589832 | tf_op jit(solution)/shard_map/ppermute | solution.py:38
  231.6 12.6 %collective-permute-start.42 = (bf16[96,1024]{1,0:T(8,128)(2,1)S(1)}, bf16[96,1024]{1,0:T(8,128)(2,1)S(1)}, u32[]{:S(2)}, u32[]{:S(2)}) collective-permute-start(bf16[96,1024]{1,0:T(8,128)(2,1)S(1)} %get-tuple-element.207), channel_id=1, source_target_pairs={{0,16},{8,24},{16,32},{24,40},{32,48},{40,56},{48,0},{56,8},{1,17}... | collective-permute-start | bytes 589832 | tf_op jit(solution)/shard_map/ppermute | solution.py:38
  270.3 26.4 %collective-permute-start.63 = (bf16[2,256,1024]{2,1,0:T(8,128)(2,1)S(1)}, bf16[2,256,1024]{2,1,0:T(8,128)(2,1)S(1)}, u32[]{:S(2)}, u32[]{:S(2)}) collective-permute-start(bf16[2,256,1024]{2,1,0:T(8,128)(2,1)S(1)} %fusion.92), channel_id=1, source_target_pairs={{0,1},{1,0},{2,3},{3,2},{4,5},{5,4},{6,7},{7,6},{8,9},{9,8},{10,11... | collective-permute-start | bytes 3145736 | tf_op jit(solution)/shard_map/ppermute | solution.py:38
  280.9 12.1 %collective-permute-start.60 = (bf16[96,1024]{1,0:T(8,128)(2,1)S(1)}, bf16[96,1024]{1,0:T(8,128)(2,1)S(1)}, u32[]{:S(2)}, u32[]{:S(2)}) collective-permute-start(bf16[96,1024]{1,0:T(8,128)(2,1)S(1)} %get-tuple-element.164), channel_id=1, source_target_pairs={{0,32},{8,40},{16,48},{24,56},{32,0},{40,8},{48,16},{56,24},{1,33}... | collective-permute-start | bytes 589832 | tf_op jit(solution)/shard_map/ppermute | solution.py:38
  281.6 15.0 %collective-permute-start.61 = (bf16[96,1024]{1,0:T(8,128)(2,1)S(1)}, bf16[96,1024]{1,0:T(8,128)(2,1)S(1)}, u32[]{:S(2)}, u32[]{:S(2)}) collective-permute-start(bf16[96,1024]{1,0:T(8,128)(2,1)S(1)} %get-tuple-element.164), channel_id=1, source_target_pairs={{0,48},{8,56},{16,0},{24,8},{32,16},{40,24},{48,32},{56,40},{1,49}... | collective-permute-start | bytes 589832 | tf_op jit(solution)/shard_map/ppermute | solution.py:38
  292.4 21.1 %collective-permute-start.44 = (bf16[96,1024]{1,0:T(8,128)(2,1)S(1)}, bf16[96,1024]{1,0:T(8,128)(2,1)S(1)}, u32[]{:S(2)}, u32[]{:S(2)}) collective-permute-start(bf16[96,1024]{1,0:T(8,128)(2,1)S(1)} %broadcast_select_fusion.2), channel_id=1, source_target_pairs={{0,64},{1,72},{2,66},{3,74},{4,68},{5,76},{6,70},{7,78},{8,65},{9,... | collective-permute-start | bytes 589832 | tf_op jit(solution)/shard_map/ppermute | solution.py:38
  293.0 20.6 %collective-permute-start.43 = (bf16[96,1024]{1,0:T(8,128)(2,1)S(1)}, bf16[96,1024]{1,0:T(8,128)(2,1)S(1)}, u32[]{:S(2)}, u32[]{:S(2)}) collective-permute-start(bf16[96,1024]{1,0:T(8,128)(2,1)S(1)} %get-tuple-element.172), channel_id=1, source_target_pairs={{0,0},{1,8},{2,2},{3,10},{4,4},{5,12},{6,6},{7,14},{8,1},{9,9},{10... | collective-permute-start | bytes 589832 | tf_op jit(solution)/shard_map/ppermute | solution.py:38
  307.8 18.9 %collective-permute-start.67 = (bf16[2,192,1024]{2,1,0:T(8,128)(2,1)S(1)}, bf16[2,192,1024]{2,1,0:T(8,128)(2,1)S(1)}, u32[]{:S(2)}, u32[]{:S(2)}) collective-permute-start(bf16[2,192,1024]{2,1,0:T(8,128)(2,1)S(1)} %get-tuple-element.182), channel_id=1, source_target_pairs={{0,2},{1,3},{2,4},{3,5},{4,6},{5,7},{6,0},{7,1},{8,10},{9,11},{10,... | collective-permute-start | bytes 2359304 | tf_op jit(solution)/shard_map/ppermute | solution.py:38
  309.1 17.9 %collective-permute-start.68 = (bf16[2,192,1024]{2,1,0:T(8,128)(2,1)S(1)}, bf16[2,192,1024]{2,1,0:T(8,128)(2,1)S(1)}, u32[]{:S(2)}, u32[]{:S(2)}) collective-permute-start(bf16[2,192,1024]{2,1,0:T(8,128)(2,1)S(1)} %get-tuple-element.181), channel_id=1, source_target_pairs={{0,6},{1,7},{2,0},{3,1},{4,2},{5,3},{6,4},{7,5},{8,14},{9,15},{10,... | collective-permute-start | bytes 2359304 | tf_op jit(solution)/shard_map/ppermute | solution.py:38
  313.6 12.6 %collective-permute-start.66 = (bf16[96,1024]{1,0:T(8,128)(2,1)S(1)}, bf16[96,1024]{1,0:T(8,128)(2,1)S(1)}, u32[]{:S(2)}, u32[]{:S(2)}) collective-permute-start(bf16[96,1024]{1,0:T(8,128)(2,1)S(1)} %get-tuple-element.198), channel_id=1, source_target_pairs={{0,16},{8,24},{16,32},{24,40},{32,48},{40,56},{48,0},{56,8},{1,17}... | collective-permute-start | bytes 589832 | tf_op jit(solution)/shard_map/ppermute | solution.py:38
  318.7 29.9 %collective-permute-start.72 = (bf16[2,512,1024]{2,1,0:T(8,128)(2,1)S(1)}, bf16[2,512,1024]{2,1,0:T(8,128)(2,1)S(1)}, u32[]{:S(2)}, u32[]{:S(2)}) collective-permute-start(bf16[2,512,1024]{2,1,0:T(8,128)(2,1)S(1)} %fusion.15), channel_id=1, source_target_pairs={{0,1},{1,0},{2,3},{3,2},{4,5},{5,4},{6,7},{7,6},{8,9},{9,8},{10,11... | collective-permute-start | bytes 6291464 | tf_op jit(solution)/shard_map/ppermute | solution.py:38
  327.4 20.9 %collective-permute-start.74 = (bf16[2,192,1024]{2,1,0:T(8,128)(2,1)S(1)}, bf16[2,192,1024]{2,1,0:T(8,128)(2,1)S(1)}, u32[]{:S(2)}, u32[]{:S(2)}) collective-permute-start(bf16[2,192,1024]{2,1,0:T(8,128)(2,1)S(1)} %get-tuple-element.103), channel_id=1, source_target_pairs={{0,4},{1,5},{2,6},{3,7},{4,0},{5,1},{6,2},{7,3},{8,12},{9,13},{10,... | collective-permute-start | bytes 2359304 | tf_op jit(solution)/shard_map/ppermute | solution.py:38
  357.3 14.7 %collective-permute-start.78 = (bf16[2,128,1024]{2,1,0:T(8,128)(2,1)S(1)}, bf16[2,128,1024]{2,1,0:T(8,128)(2,1)S(1)}, u32[]{:S(2)}, u32[]{:S(2)}) collective-permute-start(bf16[2,128,1024]{2,1,0:T(8,128)(2,1)S(1)} %get-tuple-element.185), channel_id=1, source_target_pairs={{0,2},{1,3},{2,4},{3,5},{4,6},{5,7},{6,0},{7,1},{8,10},{9,11},{10,... | collective-permute-start | bytes 1572872 | tf_op jit(solution)/shard_map/ppermute | solution.py:38
  358.0 14.0 %collective-permute-start.79 = (bf16[2,128,1024]{2,1,0:T(8,128)(2,1)S(1)}, bf16[2,128,1024]{2,1,0:T(8,128)(2,1)S(1)}, u32[]{:S(2)}, u32[]{:S(2)}) collective-permute-start(bf16[2,128,1024]{2,1,0:T(8,128)(2,1)S(1)} %get-tuple-element.186), channel_id=1, source_target_pairs={{0,6},{1,7},{2,0},{3,1},{4,2},{5,3},{6,4},{7,5},{8,14},{9,15},{10,... | collective-permute-start | bytes 1572872 | tf_op jit(solution)/shard_map/ppermute | solution.py:38
  364.2 29.0 %collective-permute-start.81 = (bf16[2,256,1024]{2,1,0:T(8,128)(2,1)}, bf16[2,256,1024]{2,1,0:T(8,128)(2,1)}, u32[]{:S(2)}, u32[]{:S(2)}) collective-permute-start(bf16[2,256,1024]{2,1,0:T(8,128)(2,1)} %fusion.88), channel_id=1, source_target_pairs={{0,1},{1,0},{2,3},{3,2},{4,5},{5,4},{6,7},{7,6},{8,9},{9,8},{10,11... | collective-permute-start | bytes 3145736 | tf_op jit(solution)/shard_map/ppermute | solution.py:38
  373.2 18.6 %collective-permute-start.80 = (bf16[2,128,1024]{2,1,0:T(8,128)(2,1)}, bf16[2,128,1024]{2,1,0:T(8,128)(2,1)}, u32[]{:S(2)}, u32[]{:S(2)}) collective-permute-start(bf16[2,128,1024]{2,1,0:T(8,128)(2,1)} %get-tuple-element.107), channel_id=1, source_target_pairs={{0,4},{1,5},{2,6},{3,7},{4,0},{5,1},{6,2},{7,3},{8,12},{9,13},{10,... | collective-permute-start | bytes 1572872 | tf_op jit(solution)/shard_map/ppermute | solution.py:38
  378.4 12.2 %collective-permute-start.77 = (bf16[96,1024]{1,0:T(8,128)(2,1)}, bf16[96,1024]{1,0:T(8,128)(2,1)}, u32[]{:S(2)}, u32[]{:S(2)}) collective-permute-start(bf16[96,1024]{1,0:T(8,128)(2,1)} %get-tuple-element.195), channel_id=1, source_target_pairs={{0,16},{8,24},{16,32},{24,40},{32,48},{40,56},{48,0},{56,8},{1,17}... | collective-permute-start | bytes 589832 | tf_op jit(solution)/shard_map/ppermute | solution.py:38
  412.6 15.7 %collective-permute-start.99 = (bf16[192,1024]{1,0:T(8,128)(2,1)}, bf16[192,1024]{1,0:T(8,128)(2,1)S(1)}, u32[]{:S(2)}, u32[]{:S(2)}) collective-permute-start(bf16[192,1024]{1,0:T(8,128)(2,1)} %get-tuple-element.190), channel_id=1, source_target_pairs={{0,8},{8,0},{16,24},{24,16},{32,40},{40,32},{48,56},{56,48},{64,72... | collective-permute-start | bytes 1179656 | tf_op jit(solution)/shard_map/ppermute | solution.py:38
  413.6 17.9 %collective-permute-start.84 = (f32[12,1024]{1,0:T(8,128)S(1)}, f32[12,1024]{1,0:T(8,128)S(1)}, u32[]{:S(2)}, u32[]{:S(2)}) collective-permute-start(f32[12,1024]{1,0:T(8,128)S(1)} %get-tuple-element.233), channel_id=1, source_target_pairs={{0,64},{8,72},{16,80},{24,88},{32,96},{40,104},{48,112},{56,120},{... | collective-permute-start | bytes 147464 | tf_op jit(solution)/shard_map/ppermute | solution.py:38
  414.2 17.2 %collective-permute-start.85 = (f32[12,1024]{1,0:T(8,128)S(1)}, f32[12,1024]{1,0:T(8,128)S(1)}, u32[]{:S(2)}, u32[]{:S(2)}) collective-permute-start(f32[12,1024]{1,0:T(8,128)S(1)} %get-tuple-element.233), channel_id=1, source_target_pairs={{0,72},{8,64},{16,88},{24,80},{32,104},{40,96},{48,120},{56,112},{... | collective-permute-start | bytes 147464 | tf_op jit(solution)/shard_map/ppermute | solution.py:38
  429.2 14.3 %collective-permute-start.101 = (bf16[192,1024]{1,0:T(8,128)(2,1)S(1)}, bf16[192,1024]{1,0:T(8,128)(2,1)S(1)}, u32[]{:S(2)}, u32[]{:S(2)}) collective-permute-start(bf16[192,1024]{1,0:T(8,128)(2,1)S(1)} %get-tuple-element.157), channel_id=1, source_target_pairs={{0,4},{1,5},{2,6},{3,7},{4,0},{5,1},{6,2},{7,3},{8,12},{9,13},{10,... | collective-permute-start | bytes 1179656 | tf_op jit(solution)/shard_map/ppermute | solution.py:38
  431.5 20.6 %collective-permute-start.87 = (f32[12,1024]{1,0:T(8,128)S(1)}, f32[12,1024]{1,0:T(8,128)S(1)}, u32[]{:S(2)}, u32[]{:S(2)}) collective-permute-start(f32[12,1024]{1,0:T(8,128)S(1)} %add_add_fusion.2), channel_id=1, source_target_pairs={{0,1},{1,0},{2,3},{3,2},{4,5},{5,4},{6,7},{7,6},{8,9},{9,8},{10,11... | collective-permute-start | bytes 147464 | tf_op jit(solution)/shard_map/ppermute | solution.py:38
  450.5 23.1 %collective-permute-start.103 = (bf16[768,1024]{1,0:T(8,128)(2,1)S(1)}, bf16[768,1024]{1,0:T(8,128)(2,1)S(1)}, u32[]{:S(2)}, u32[]{:S(2)}) collective-permute-start(bf16[768,1024]{1,0:T(8,128)(2,1)S(1)} %bitcast.435), channel_id=1, source_target_pairs={{0,1},{1,0},{2,3},{3,2},{4,5},{5,4},{6,7},{7,6},{8,9},{9,8},{10,11... | collective-permute-start | bytes 4718600 | tf_op jit(solution)/shard_map/ppermute | solution.py:38
  452.2 12.1 %collective-permute-start.89 = (f32[12,1024]{1,0:T(8,128)S(1)}, f32[12,1024]{1,0:T(8,128)S(1)}, u32[]{:S(2)}, u32[]{:S(2)}) collective-permute-start(f32[12,1024]{1,0:T(8,128)S(1)} %add.733), channel_id=1, source_target_pairs={{0,32},{8,40},{16,48},{24,56},{32,0},{40,8},{48,16},{56,24},{1,33}... | collective-permute-start | bytes 147464 | tf_op jit(solution)/shard_map/ppermute | solution.py:38
  452.3 12.1 %collective-permute-start.90 = (f32[12,1024]{1,0:T(8,128)S(1)}, f32[12,1024]{1,0:T(8,128)S(1)}, u32[]{:S(2)}, u32[]{:S(2)}) collective-permute-start(f32[12,1024]{1,0:T(8,128)S(1)} %add.733), channel_id=1, source_target_pairs={{0,48},{8,56},{16,0},{24,8},{32,16},{40,24},{48,32},{56,40},{1,49}... | collective-permute-start | bytes 147464 | tf_op jit(solution)/shard_map/ppermute | solution.py:38
  454.9 13.1 %collective-permute-start.83 = (bf16[96,1024]{1,0:T(8,128)(2,1)S(1)}, bf16[96,1024]{1,0:T(8,128)(2,1)S(1)}, u32[]{:S(2)}, u32[]{:S(2)}) collective-permute-start(bf16[96,1024]{1,0:T(8,128)(2,1)S(1)} %broadcast_select_fusion), channel_id=1, source_target_pairs={{0,64},{1,72},{2,66},{3,74},{4,68},{5,76},{6,70},{7,78},{8,65},{9,... | collective-permute-start | bytes 589832 | tf_op jit(solution)/shard_map/ppermute | solution.py:38
  (165 other events, 1266.2 us)

commit v7 on v5

--- a/solution.py
+++ b/solution.py
@@ -274,21 +274,24 @@
     whole = place(whole, own[None], (y, 0, 0))
     for by in (1, 2, 3):
         whole = place(whole, along_y(own, by)[None], ((y - by) % 4, 0, 0))
-    whole = whole.reshape(4 * rows, WIDTH)
+    return whole
+
+
+def both_halves(whole):
     core = lax.axis_index("dp") % 2
-    both = jnp.zeros((2, 4 * rows, WIDTH), bf16)
-    both = place(both, whole[None], (core, 0, 0))
-    both = place(both, other_core(whole)[None], (1 - core, 0, 0))
-    return both.reshape(2, 4, rows, WIDTH)
-
-
-def everywhere(array, pipe):
-    mine, other = pick(array, pipe), pick(array, 1 - pipe)
-    total = mine + along_z(other, 1) + along_z(other, 3) + along_z(mine, 2)
-    total = total + other_core(total)
-    for along in (along_x, along_y):
-        total = total + along(total, 1) + along(total, 2) + along(total, 3)
-    return total
+    both = jnp.zeros((2,) + whole.shape, bf16)
+    both = place(both, whole[None], (core, 0, 0, 0))
+    return place(both, other_core(whole)[None], (1 - core, 0, 0, 0))
+
+
+def over_line(small):
+    small = small + other_core(small)
+    return small + along_x(small, 1) + along_x(small, 2) + along_x(small, 3)
+
+
+def small_over_z(small, pipe):
+    mine, other = pick(small, pipe), pick(small, 1 - pipe)
+    return mine + along_z(other, 1) + along_z(other, 3) + along_z(mine, 2)
 
 
 def tied(*arrays):
@@ -562,8 +565,6 @@
     near = jnp.concatenate([kept["near"], near_y(kept["attention"])], axis=1)
     far = [pick(kept[name], (y + 2) % 4, 1) for name in ("feed", "attention")]
     zero = near + along_y(jnp.concatenate(far, axis=1), 2).astype(f32)
-    total = back_over_y(over_z(zero.astype(bf16), kept["one"], pipe, high))
-
     def bias_rows(fc_bias_grad):
         return place(jnp.zeros((4, WIDTH), f32), fc_bias_grad[None], (x, 0))
 
@@ -580,7 +581,11 @@
             for early, late in ((early_zero, late_zero), (early_one, late_one))
         ]
     )
-    small = everywhere(small, pipe)
+    zero, small = tied(zero.astype(bf16), over_line(small))
+    owned, small = tied(over_z(zero, kept["one"], pipe, high), small_over_z(small, pipe))
+    small = small + along_y(small, 1) + along_y(small, 2) + along_y(small, 3)
+    whole, small = tied(back_over_y(owned), small)
+    total = both_halves(whole)
     early, late = small[:8], small[8:]
 
     feed_total = total[:, :, :128].reshape(2, 512, WIDTH)

time: 480 us -> 516 us (1.075)
  waiting for transfers between devices: 166 us -> 192 us
  starting transfers between devices: 152 us -> 138 us
  local copies, waits for them, and re-layouts: 53.8 us -> 65.1 us
  matrix products: 44.3 us -> 51.6 us
  other arithmetic: 47.3 us -> 53.7 us
    ppermute x103, waiting for transfers between devices: 166 us -> 192 us  [move(): return lax.ppermute(array, axes, sorted(pairs.items()))]
    ppermute x103, starting transfers between devices: 152 us -> 138 us  [move(): return lax.ppermute(array, axes, sorted(pairs.items()))]
    unnamed x243 -> x269, local copies, waits for them, and re-layouts: 31.3 us -> 38.1 us
  transfers between devices with their start and end apart: 103 -> 103, of which waited for: 45 -> 45; matrix products, arithmetic and copies ran while one was open for 19% -> 22% of each run, Pallas kernels for 1% -> 1%
where the time goes in v7:
time: 516 us; the launch traced here: 508 us
  waiting for transfers between devices  192 us (37%)
  starting transfers between devices  138 us (27%)
  local copies, waits for them, and re-layouts  65.1 us (13%)
  other arithmetic  53.7 us (10%)
  matrix products  51.6 us (10%)
    ppermute x103, waiting for transfers between devices, move(): return lax.ppermute(array, axes, sorted(pairs.items()))  192 us
    ppermute x103, starting transfers between devices, move(): return lax.ppermute(array, axes, sorted(pairs.items()))  138 us
    unnamed x269, local copies, waits for them, and re-layouts  38.1 us
    dot_general x24, matrix products, dot(): lax.dot_general(left, right, (((left_dim,), (right_dim,)), ((), ())), pre...  32.7 us
  transfers between devices with their start and end apart: 103, of which 45 were waited for; matrix products, arithmetic and copies ran while one was open for 22% of the time, Pallas kernels for 1%

profile of v7, /device:TPU:1, one launch (start us, length us, event | category | flops | bytes accessed | tf_op | source)
XLA Modules:
  0.0 508.2 jit_solution(16193823568933251907)
XLA Ops:
  15.0 5.4 %collective-permute-start = (bf16[96,1024]{1,0:T(8,128)(2,1)S(1)}, bf16[96,1024]{1,0:T(8,128)(2,1)S(1)}, u32[]{:S(2)}, u32[]{:S(2)}) collective-permute-start(bf16[96,1024]{1,0:T(8,128)(2,1)S(1)} %dynamic-slice_bitcast_fusion.12), channel_id=1, source_target_pairs={{0,0},{1,8},{2,2},{3,10},{4,4},{5,12},{6,6},{7,14},{8,1},{9,9},{10... | collective-permute-start | bytes 589832 | tf_op jit(solution)/shard_map/ppermute | solution.py:38
  21.5 9.0 %collective-permute-done = bf16[96,1024]{1,0:T(8,128)(2,1)S(1)} collective-permute-done((bf16[96,1024]{1,0:T(8,128)(2,1)S(1)}, bf16[96,1024]{1,0:T(8,128)(2,1)S(1)}, u32[]{:S(2)}, u32[]{:S(2)}) %collective-permute-start) | collective-permute-done | bytes 196640 | tf_op jit(solution)/shard_map/ppermute | solution.py:38
  38.1 4.5 collective-permute-done.6
  44.8 3.2 collective-permute-start.8
  61.3 3.2 fusion.81
  80.6 7.3 %collective-permute-done.15.refs_3_ = bf16[512,512]{1,0:T(8,128)(2,1)S(1)} collective-permute-done((bf16[512,512]{1,0:T(8,128)(2,1)}, bf16[512,512]{1,0:T(8,128)(2,1)S(1)}, u32[]{:S(2)}, u32[]{:S(2)}) %collective-permute-start.15) | collective-permute-done | bytes 524320 | tf_op jit(solution)/shard_map/ppermute | solution.py:38
  88.0 2.7 collective-permute-start.20
  99.3 5.7 %collective-permute-done.18 = bf16[96,1024]{1,0:T(8,128)(2,1)S(1)} collective-permute-done((bf16[96,1024]{1,0:T(8,128)(2,1)S(1)}, bf16[96,1024]{1,0:T(8,128)(2,1)S(1)}, u32[]{:S(2)}, u32[]{:S(2)}) %collective-permute-start.18) | collective-permute-done | bytes 196640 | tf_op jit(solution)/shard_map/ppermute | solution.py:38
  111.5 6.1 %collective-permute-done.21 = bf16[96,1024]{1,0:T(8,128)(2,1)S(1)} collective-permute-done((bf16[96,1024]{1,0:T(8,128)(2,1)S(1)}, bf16[96,1024]{1,0:T(8,128)(2,1)S(1)}, u32[]{:S(2)}, u32[]{:S(2)}) %collective-permute-start.21) | collective-permute-done | bytes 196640 | tf_op jit(solution)/shard_map/ppermute | solution.py:38
  122.5 3.6 collective-permute-start.45
  157.0 4.2 collective-permute-done.30
  161.1 3.6 collective-permute-done.31
  164.7 2.8 fusion.78
  183.4 4.5 collective-permute-done.34
  187.8 2.6 collective-permute-done.35
  190.4 4.3 collective-permute-done.36
  198.2 5.7 %collective-permute-done.37 = bf16[96,1024]{1,0:T(8,128)(2,1)S(1)} collective-permute-done((bf16[96,1024]{1,0:T(8,128)(2,1)S(1)}, bf16[96,1024]{1,0:T(8,128)(2,1)S(1)}, u32[]{:S(2)}, u32[]{:S(2)}) %collective-permute-start.37) | collective-permute-done | bytes 196640 | tf_op jit(solution)/shard_map/ppermute | solution.py:38
  216.7 3.4 collective-permute-start.49
  225.2 3.3 collective-permute-done.49
  228.5 3.8 collective-permute-done.51
  238.9 7.5 %collective-permute-done.52 = bf16[96,1024]{1,0:T(8,128)(2,1)S(1)} collective-permute-done((bf16[96,1024]{1,0:T(8,128)(2,1)S(1)}, bf16[96,1024]{1,0:T(8,128)(2,1)S(1)}, u32[]{:S(2)}, u32[]{:S(2)}) %collective-permute-start.52) | collective-permute-done | bytes 196640 | tf_op jit(solution)/shard_map/ppermute | solution.py:38
  247.2 4.1 multiply_reduce_fusion.1
  260.2 2.7 collective-permute-start.56
  270.7 4.1 collective-permute-done.58
  278.8 8.5 %collective-permute-done.59 = bf16[96,1024]{1,0:T(8,128)(2,1)S(1)} collective-permute-done((bf16[96,1024]{1,0:T(8,128)(2,1)S(1)}, bf16[96,1024]{1,0:T(8,128)(2,1)S(1)}, u32[]{:S(2)}, u32[]{:S(2)}) %collective-permute-start.59) | collective-permute-done | bytes 196640 | tf_op jit(solution)/shard_map/ppermute | solution.py:38
  290.1 2.6 fusion.1
  302.6 3.5 collective-permute-start.64
  306.8 2.8 convolution_convert_fusion
  309.5 4.4 collective-permute-done.64
  313.9 4.2 collective-permute-done.66
  323.2 2.6 convolution_convert_fusion.1
  327.6 4.5 collective-permute-done.67
  336.5 4.1 multiply_reduce_fusion
  347.8 17.9 %collective-permute-done.77 = bf16[2,192,1024]{2,1,0:T(8,128)(2,1)S(1)} collective-permute-done((bf16[2,192,1024]{2,1,0:T(8,128)(2,1)S(1)}, bf16[2,192,1024]{2,1,0:T(8,128)(2,1)S(1)}, u32[]{:S(2)}, u32[]{:S(2)}) %collective-permute-start.77) | collective-permute-done | bytes 786464 | tf_op jit(solution)/shard_map/ppermute | solution.py:38
  376.1 2.7 collective-permute-start.79
  380.1 5.8 %collective-permute-done.75 = bf16[96,1024]{1,0:T(8,128)(2,1)S(1)} collective-permute-done((bf16[96,1024]{1,0:T(8,128)(2,1)S(1)}, bf16[96,1024]{1,0:T(8,128)(2,1)S(1)}, u32[]{:S(2)}, u32[]{:S(2)}) %collective-permute-start.75) | collective-permute-done | bytes 196640 | tf_op jit(solution)/shard_map/ppermute | solution.py:38
  386.3 3.0 collective-permute-done.76
  396.9 3.3 collective-permute-start.86
  410.2 2.9 collective-permute-done.88
  413.1 2.9 collective-permute-done.89
  416.0 11.0 %collective-permute-done.83 = bf16[2,64,1024]{2,1,0:T(8,128)(2,1)S(1)} collective-permute-done((bf16[2,64,1024]{2,1,0:T(8,128)(2,1)S(1)}, bf16[2,64,1024]{2,1,0:T(8,128)(2,1)S(1)}, u32[]{:S(2)}, u32[]{:S(2)}) %collective-permute-start.83) | collective-permute-done | bytes 262176 | tf_op jit(solution)/shard_map/ppermute | solution.py:38
  427.6 2.7 collective-permute-start.94
  437.3 6.3 %collective-permute-done.90 = bf16[192,1024]{1,0:T(8,128)(2,1)S(1)} collective-permute-done((bf16[192,1024]{1,0:T(8,128)(2,1)S(1)}, bf16[192,1024]{1,0:T(8,128)(2,1)S(1)}, u32[]{:S(2)}, u32[]{:S(2)}) %collective-permute-start.90) | collective-permute-done | bytes 393248 | tf_op jit(solution)/shard_map/ppermute | solution.py:38
  443.7 7.5 %collective-permute-done.92 = bf16[192,1024]{1,0:T(8,128)(2,1)S(1)} collective-permute-done((bf16[192,1024]{1,0:T(8,128)(2,1)S(1)}, bf16[192,1024]{1,0:T(8,128)(2,1)S(1)}, u32[]{:S(2)}, u32[]{:S(2)}) %collective-permute-start.92) | collective-permute-done | bytes 393248 | tf_op jit(solution)/shard_map/ppermute | solution.py:38
  456.2 7.6 %collective-permute-start.43 = (bf16[96,1024]{1,0:T(8,128)(2,1)}, bf16[96,1024]{1,0:T(8,128)(2,1)}, u32[]{:S(2)}, u32[]{:S(2)}) collective-permute-start(bf16[96,1024]{1,0:T(8,128)(2,1)} %get-tuple-element.177), channel_id=1, source_target_pairs={{0,0},{1,8},{2,2},{3,10},{4,4},{5,12},{6,6},{7,14},{8,1},{9,9},{10... | collective-permute-start | bytes 589832 | tf_op jit(solution)/shard_map/ppermute | solution.py:38
  466.4 10.2 %collective-permute-done.97 = bf16[192,1024]{1,0:T(8,128)(2,1)S(1)} collective-permute-done((bf16[192,1024]{1,0:T(8,128)(2,1)S(1)}, bf16[192,1024]{1,0:T(8,128)(2,1)S(1)}, u32[]{:S(2)}, u32[]{:S(2)}) %collective-permute-start.97) | collective-permute-done | bytes 393248 | tf_op jit(solution)/shard_map/ppermute | solution.py:38
  476.6 6.3 %collective-permute-done.98 = bf16[192,1024]{1,0:T(8,128)(2,1)S(1)} collective-permute-done((bf16[192,1024]{1,0:T(8,128)(2,1)S(1)}, bf16[192,1024]{1,0:T(8,128)(2,1)S(1)}, u32[]{:S(2)}, u32[]{:S(2)}) %collective-permute-start.98) | collective-permute-done | bytes 393248 | tf_op jit(solution)/shard_map/ppermute | solution.py:38
  485.6 4.9 collective-permute-start.81
  (655 shorter events, 265.4 us)
Async XLA Ops:
  6.4 14.4 %collective-permute-start.4 = (bf16[16,512]{1,0:T(8,128)(2,1)S(1)}, bf16[16,512]{1,0:T(8,128)(2,1)S(1)}, u32[]{:S(2)}, u32[]{:S(2)}) collective-permute-start(bf16[16,512]{1,0:T(8,128)(2,1)S(1)} %reshape.737.refs_2_), channel_id=1, source_target_pairs={{0,64},{8,72},{16,80},{24,88},{32,96},{40,104},{48,112},{56,120},{... | collective-permute-start | bytes 49160 | tf_op jit(solution)/shard_map/ppermute | solution.py:38
  12.3 18.6 %collective-permute-start.1 = (bf16[528,512]{1,0:T(8,128)(2,1)}, bf16[528,512]{1,0:T(8,128)(2,1)}, u32[]{:S(2)}, u32[]{:S(2)}) collective-permute-start(bf16[528,512]{1,0:T(8,128)(2,1)} %pad_maximum_fusion.17), channel_id=1, source_target_pairs={{0,64},{8,72},{16,80},{24,88},{32,96},{40,104},{48,112},{56,120},{... | collective-permute-start | bytes 1622024 | tf_op jit(solution)/shard_map/ppermute | solution.py:38
  13.9 16.9 %collective-permute-start.2 = (bf16[528,512]{1,0:T(8,128)(2,1)}, bf16[528,512]{1,0:T(8,128)(2,1)}, u32[]{:S(2)}, u32[]{:S(2)}) collective-permute-start(bf16[528,512]{1,0:T(8,128)(2,1)} %pad_maximum_fusion.17), channel_id=1, source_target_pairs={{0,72},{8,64},{16,88},{24,80},{32,104},{40,96},{48,120},{56,112},{... | collective-permute-start | bytes 1622024 | tf_op jit(solution)/shard_map/ppermute | solution.py:38
  15.0 15.5 %collective-permute-start = (bf16[96,1024]{1,0:T(8,128)(2,1)S(1)}, bf16[96,1024]{1,0:T(8,128)(2,1)S(1)}, u32[]{:S(2)}, u32[]{:S(2)}) collective-permute-start(bf16[96,1024]{1,0:T(8,128)(2,1)S(1)} %dynamic-slice_bitcast_fusion.12), channel_id=1, source_target_pairs={{0,0},{1,8},{2,2},{3,10},{4,4},{5,12},{6,6},{7,14},{8,1},{9,9},{10... | collective-permute-start | bytes 589832 | tf_op jit(solution)/shard_map/ppermute | solution.py:38
  20.5 50.1 %collective-permute-start.14 = (s32[8,96]{1,0:T(8,128)S(1)}, s32[8,96]{1,0:T(8,128)}, u32[]{:S(2)}, u32[]{:S(2)}) collective-permute-start(s32[8,96]{1,0:T(8,128)S(1)} %reshape.740), channel_id=1, source_target_pairs={{0,1},{1,0},{2,3},{3,2},{4,5},{5,4},{6,7},{7,6},{8,9},{9,8},{10,11... | collective-permute-start | bytes 9224 | tf_op jit(solution)/shard_map/ppermute | solution.py:38
  30.8 17.2 %collective-permute-start.3 = (bf16[528,512]{1,0:T(8,128)(2,1)}, bf16[528,512]{1,0:T(8,128)(2,1)}, u32[]{:S(2)}, u32[]{:S(2)}) collective-permute-start(bf16[528,512]{1,0:T(8,128)(2,1)} %pad_maximum_fusion.17), channel_id=1, source_target_pairs={{0,8},{8,0},{16,24},{24,16},{32,40},{40,32},{48,56},{56,48},{64,72... | collective-permute-start | bytes 1622024 | tf_op jit(solution)/shard_map/ppermute | solution.py:38
  56.3 16.1 %collective-permute-start.12 = (bf16[512,512]{1,0:T(8,128)(2,1)}, bf16[512,512]{1,0:T(8,128)(2,1)S(1)}, u32[]{:S(2)}, u32[]{:S(2)}) collective-permute-start(bf16[512,512]{1,0:T(8,128)(2,1)} %dynamic-slice_bitcast_fusion.7), channel_id=1, source_target_pairs={{0,64},{8,72},{16,80},{24,88},{32,96},{40,104},{48,112},{56,120},{... | collective-permute-start | bytes 1572872 | tf_op jit(solution)/shard_map/ppermute | solution.py:38
  57.3 15.1 %collective-permute-start.13 = (bf16[512,512]{1,0:T(8,128)(2,1)}, bf16[512,512]{1,0:T(8,128)(2,1)S(1)}, u32[]{:S(2)}, u32[]{:S(2)}) collective-permute-start(bf16[512,512]{1,0:T(8,128)(2,1)} %dynamic-slice_bitcast_fusion.7), channel_id=1, source_target_pairs={{0,72},{8,64},{16,88},{24,80},{32,104},{40,96},{48,120},{56,112},{... | collective-permute-start | bytes 1572872 | tf_op jit(solution)/shard_map/ppermute | solution.py:38
  72.4 15.6 %collective-permute-start.15 = (bf16[512,512]{1,0:T(8,128)(2,1)}, bf16[512,512]{1,0:T(8,128)(2,1)S(1)}, u32[]{:S(2)}, u32[]{:S(2)}) collective-permute-start(bf16[512,512]{1,0:T(8,128)(2,1)} %dynamic-slice_bitcast_fusion.7), channel_id=1, source_target_pairs={{0,8},{8,0},{16,24},{24,16},{32,40},{40,32},{48,56},{56,48},{64,72... | collective-permute-start | bytes 1572872 | tf_op jit(solution)/shard_map/ppermute | solution.py:38
  88.0 17.2 %collective-permute-start.19 = (bf16[256,1024]{1,0:T(8,128)(2,1)S(1)}, bf16[256,1024]{1,0:T(8,128)(2,1)S(1)}, u32[]{:S(2)}, u32[]{:S(2)}) collective-permute-start(bf16[256,1024]{1,0:T(8,128)(2,1)S(1)} %copy-done.69), channel_id=1, source_target_pairs={{0,64},{8,72},{16,80},{24,88},{32,96},{40,104},{48,112},{56,120},{... | collective-permute-start | bytes 1572872 | tf_op jit(solution)/shard_map/ppermute | solution.py:38
  88.0 17.2 %collective-permute-start.20 = (bf16[256,1024]{1,0:T(8,128)(2,1)S(1)}, bf16[256,1024]{1,0:T(8,128)(2,1)S(1)}, u32[]{:S(2)}, u32[]{:S(2)}) collective-permute-start(bf16[256,1024]{1,0:T(8,128)(2,1)S(1)} %copy-done.69), channel_id=1, source_target_pairs={{0,72},{8,64},{16,88},{24,80},{32,104},{40,96},{48,120},{56,112},{... | collective-permute-start | bytes 1572872 | tf_op jit(solution)/shard_map/ppermute | solution.py:38
  105.6 13.8 %collective-permute-start.24 = (bf16[256,1024]{1,0:T(8,128)(2,1)S(1)}, bf16[256,1024]{1,0:T(8,128)(2,1)S(1)}, u32[]{:S(2)}, u32[]{:S(2)}) collective-permute-start(bf16[256,1024]{1,0:T(8,128)(2,1)S(1)} %copy-done.69), channel_id=1, source_target_pairs={{0,8},{8,0},{16,24},{24,16},{32,40},{40,32},{48,56},{56,48},{64,72... | collective-permute-start | bytes 1572872 | tf_op jit(solution)/shard_map/ppermute | solution.py:38
  109.4 16.7 %collective-permute-start.25 = (bf16[3,512,512]{2,1,0:T(8,128)(2,1)S(1)}, bf16[3,512,512]{2,1,0:T(8,128)(2,1)S(1)}, u32[]{:S(2)}, u32[]{:S(2)}) collective-permute-start(bf16[3,512,512]{2,1,0:T(8,128)(2,1)S(1)} %pad_maximum_fusion.1), channel_id=1, source_target_pairs={{0,1},{1,0},{2,3},{3,2},{4,5},{5,4},{6,7},{7,6},{8,9},{9,8},{10,11... | collective-permute-start | bytes 4718600 | tf_op jit(solution)/shard_map/ppermute | solution.py:38
  122.5 19.7 %collective-permute-start.45 = (bf16[96,1024]{1,0:T(8,128)(2,1)}, bf16[96,1024]{1,0:T(8,128)(2,1)}, u32[]{:S(2)}, u32[]{:S(2)}) collective-permute-start(bf16[96,1024]{1,0:T(8,128)(2,1)} %dynamic-slice_bitcast_fusion.11), channel_id=1, source_target_pairs={{0,0},{1,8},{2,2},{3,10},{4,4},{5,12},{6,6},{7,14},{8,1},{9,9},{10... | collective-permute-start | bytes 589832 | tf_op jit(solution)/shard_map/ppermute | solution.py:38
  133.5 12.1 %collective-permute-start.27 = (bf16[96,1024]{1,0:T(8,128)(2,1)}, bf16[96,1024]{1,0:T(8,128)(2,1)}, u32[]{:S(2)}, u32[]{:S(2)}) collective-permute-start(bf16[96,1024]{1,0:T(8,128)(2,1)} %get-tuple-element.219), channel_id=1, source_target_pairs={{0,48},{8,56},{16,0},{24,8},{32,16},{40,24},{48,32},{56,40},{1,49}... | collective-permute-start | bytes 589832 | tf_op jit(solution)/shard_map/ppermute | solution.py:38
  135.8 12.3 %collective-permute-start.29 = (bf16[96,1024]{1,0:T(8,128)(2,1)}, bf16[96,1024]{1,0:T(8,128)(2,1)}, u32[]{:S(2)}, u32[]{:S(2)}) collective-permute-start(bf16[96,1024]{1,0:T(8,128)(2,1)} %get-tuple-element.220), channel_id=1, source_target_pairs={{0,16},{8,24},{16,32},{24,40},{32,48},{40,56},{48,0},{56,8},{1,17}... | collective-permute-start | bytes 589832 | tf_op jit(solution)/shard_map/ppermute | solution.py:38
  142.2 12.6 %collective-permute-start.46 = (bf16[96,1024]{1,0:T(8,128)(2,1)}, bf16[96,1024]{1,0:T(8,128)(2,1)S(1)}, u32[]{:S(2)}, u32[]{:S(2)}) collective-permute-start(bf16[96,1024]{1,0:T(8,128)(2,1)} %collective-permute-done.45), channel_id=1, source_target_pairs={{0,16},{8,24},{16,32},{24,40},{32,48},{40,56},{48,0},{56,8},{1,17}... | collective-permute-start | bytes 589832 | tf_op jit(solution)/shard_map/ppermute | solution.py:38
  144.3 26.0 %collective-permute-start.47 = (bf16[96,1024]{1,0:T(8,128)(2,1)}, bf16[96,1024]{1,0:T(8,128)(2,1)}, u32[]{:S(2)}, u32[]{:S(2)}) collective-permute-start(bf16[96,1024]{1,0:T(8,128)(2,1)} %collective-permute-done.45), channel_id=1, source_target_pairs={{0,32},{8,40},{16,48},{24,56},{32,0},{40,8},{48,16},{56,24},{1,33}... | collective-permute-start | bytes 589832 | tf_op jit(solution)/shard_map/ppermute | solution.py:38
  151.1 13.6 %collective-permute-start.31 = (bf16[96,1024]{1,0:T(8,128)(2,1)}, bf16[96,1024]{1,0:T(8,128)(2,1)}, u32[]{:S(2)}, u32[]{:S(2)}) collective-permute-start(bf16[96,1024]{1,0:T(8,128)(2,1)} %fusion.130), channel_id=1, source_target_pairs={{0,32},{8,40},{16,48},{24,56},{32,0},{40,8},{48,16},{56,24},{1,33}... | collective-permute-start | bytes 589832 | tf_op jit(solution)/shard_map/ppermute | solution.py:38
  154.8 17.1 %collective-permute-start.48 = (bf16[96,1024]{1,0:T(8,128)(2,1)}, bf16[96,1024]{1,0:T(8,128)(2,1)}, u32[]{:S(2)}, u32[]{:S(2)}) collective-permute-start(bf16[96,1024]{1,0:T(8,128)(2,1)} %collective-permute-done.45), channel_id=1, source_target_pairs={{0,48},{8,56},{16,0},{24,8},{32,16},{40,24},{48,32},{56,40},{1,49}... | collective-permute-start | bytes 589832 | tf_op jit(solution)/shard_map/ppermute | solution.py:38
  182.7 12.0 %collective-permute-start.36 = (bf16[96,1024]{1,0:T(8,128)(2,1)S(1)}, bf16[96,1024]{1,0:T(8,128)(2,1)S(1)}, u32[]{:S(2)}, u32[]{:S(2)}) collective-permute-start(bf16[96,1024]{1,0:T(8,128)(2,1)S(1)} %get-tuple-element.215), channel_id=1, source_target_pairs={{0,16},{8,24},{16,32},{24,40},{32,48},{40,56},{48,0},{56,8},{1,17}... | collective-permute-start | bytes 589832 | tf_op jit(solution)/shard_map/ppermute | solution.py:38
  220.1 12.2 %collective-permute-start.51 = (bf16[96,1024]{1,0:T(8,128)(2,1)}, bf16[96,1024]{1,0:T(8,128)(2,1)}, u32[]{:S(2)}, u32[]{:S(2)}) collective-permute-start(bf16[96,1024]{1,0:T(8,128)(2,1)} %get-tuple-element.209), channel_id=1, source_target_pairs={{0,16},{8,24},{16,32},{24,40},{32,48},{40,56},{48,0},{56,8},{1,17}... | collective-permute-start | bytes 589832 | tf_op jit(solution)/shard_map/ppermute | solution.py:38
  224.0 65.4 %collective-permute-start.62 = (bf16[2,512,1024]{2,1,0:T(8,128)(2,1)}, bf16[2,512,1024]{2,1,0:T(8,128)(2,1)}, u32[]{:S(2)}, u32[]{:S(2)}) collective-permute-start(bf16[2,512,1024]{2,1,0:T(8,128)(2,1)} %fusion.19), channel_id=1, source_target_pairs={{0,1},{1,0},{2,3},{3,2},{4,5},{5,4},{6,7},{7,6},{8,9},{9,8},{10,11... | collective-permute-start | bytes 6291464 | tf_op jit(solution)/shard_map/ppermute | solution.py:38
  267.3 20.2 %collective-permute-start.63 = (bf16[2,256,1024]{2,1,0:T(8,128)(2,1)}, bf16[2,256,1024]{2,1,0:T(8,128)(2,1)}, u32[]{:S(2)}, u32[]{:S(2)}) collective-permute-start(bf16[2,256,1024]{2,1,0:T(8,128)(2,1)} %fusion.93), channel_id=1, source_target_pairs={{0,1},{1,0},{2,3},{3,2},{4,5},{5,4},{6,7},{7,6},{8,9},{9,8},{10,11... | collective-permute-start | bytes 3145736 | tf_op jit(solution)/shard_map/ppermute | solution.py:38
  298.8 34.7 %collective-permute-start.70 = (bf16[2,192,1024]{2,1,0:T(8,128)(2,1)}, bf16[2,192,1024]{2,1,0:T(8,128)(2,1)}, u32[]{:S(2)}, u32[]{:S(2)}) collective-permute-start(bf16[2,192,1024]{2,1,0:T(8,128)(2,1)} %get-tuple-element.187), channel_id=1, source_target_pairs={{0,2},{1,3},{2,4},{3,5},{4,6},{5,7},{6,0},{7,1},{8,10},{9,11},{10,... | collective-permute-start | bytes 2359304 | tf_op jit(solution)/shard_map/ppermute | solution.py:38
  300.1 33.4 %collective-permute-start.71 = (bf16[2,192,1024]{2,1,0:T(8,128)(2,1)}, bf16[2,192,1024]{2,1,0:T(8,128)(2,1)}, u32[]{:S(2)}, u32[]{:S(2)}) collective-permute-start(bf16[2,192,1024]{2,1,0:T(8,128)(2,1)} %get-tuple-element.186), channel_id=1, source_target_pairs={{0,6},{1,7},{2,0},{3,1},{4,2},{5,3},{6,4},{7,5},{8,14},{9,15},{10,... | collective-permute-start | bytes 2359304 | tf_op jit(solution)/shard_map/ppermute | solution.py:38
  306.1 12.0 %collective-permute-start.66 = (bf16[96,1024]{1,0:T(8,128)(2,1)S(1)}, bf16[96,1024]{1,0:T(8,128)(2,1)S(1)}, u32[]{:S(2)}, u32[]{:S(2)}) collective-permute-start(bf16[96,1024]{1,0:T(8,128)(2,1)S(1)} %get-tuple-element.203), channel_id=1, source_target_pairs={{0,16},{8,24},{16,32},{24,40},{32,48},{40,56},{48,0},{56,8},{1,17}... | collective-permute-start | bytes 589832 | tf_op jit(solution)/shard_map/ppermute | solution.py:38
  320.5 12.9 %collective-permute-start.68 = (bf16[96,1024]{1,0:T(8,128)(2,1)S(1)}, bf16[96,1024]{1,0:T(8,128)(2,1)S(1)}, u32[]{:S(2)}, u32[]{:S(2)}) collective-permute-start(bf16[96,1024]{1,0:T(8,128)(2,1)S(1)} %get-tuple-element.165), channel_id=1, source_target_pairs={{0,32},{8,40},{16,48},{24,56},{32,0},{40,8},{48,16},{56,24},{1,33}... | collective-permute-start | bytes 589832 | tf_op jit(solution)/shard_map/ppermute | solution.py:38
  321.2 12.3 %collective-permute-start.69 = (bf16[96,1024]{1,0:T(8,128)(2,1)S(1)}, bf16[96,1024]{1,0:T(8,128)(2,1)S(1)}, u32[]{:S(2)}, u32[]{:S(2)}) collective-permute-start(bf16[96,1024]{1,0:T(8,128)(2,1)S(1)} %get-tuple-element.165), channel_id=1, source_target_pairs={{0,48},{8,56},{16,0},{24,8},{32,16},{40,24},{48,32},{56,40},{1,49}... | collective-permute-start | bytes 589832 | tf_op jit(solution)/shard_map/ppermute | solution.py:38
  332.1 34.9 %collective-permute-start.73 = (bf16[2,512,1024]{2,1,0:T(8,128)(2,1)S(1)}, bf16[2,512,1024]{2,1,0:T(8,128)(2,1)S(1)}, u32[]{:S(2)}, u32[]{:S(2)}) collective-permute-start(bf16[2,512,1024]{2,1,0:T(8,128)(2,1)S(1)} %fusion.15), channel_id=1, source_target_pairs={{0,1},{1,0},{2,3},{3,2},{4,5},{5,4},{6,7},{7,6},{8,9},{9,8},{10,11... | collective-permute-start | bytes 6291464 | tf_op jit(solution)/shard_map/ppermute | solution.py:38
  345.5 20.3 %collective-permute-start.77 = (bf16[2,192,1024]{2,1,0:T(8,128)(2,1)S(1)}, bf16[2,192,1024]{2,1,0:T(8,128)(2,1)S(1)}, u32[]{:S(2)}, u32[]{:S(2)}) collective-permute-start(bf16[2,192,1024]{2,1,0:T(8,128)(2,1)S(1)} %copy-done.65), channel_id=1, source_target_pairs={{0,4},{1,5},{2,6},{3,7},{4,0},{5,1},{6,2},{7,3},{8,12},{9,13},{10,... | collective-permute-start | bytes 2359304 | tf_op jit(solution)/shard_map/ppermute | solution.py:38
  371.3 22.8 %collective-permute-start.80 = (bf16[2,256,1024]{2,1,0:T(8,128)(2,1)}, bf16[2,256,1024]{2,1,0:T(8,128)(2,1)}, u32[]{:S(2)}, u32[]{:S(2)}) collective-permute-start(bf16[2,256,1024]{2,1,0:T(8,128)(2,1)} %fusion.89), channel_id=1, source_target_pairs={{0,1},{1,0},{2,3},{3,2},{4,5},{5,4},{6,7},{7,6},{8,9},{9,8},{10,11... | collective-permute-start | bytes 3145736 | tf_op jit(solution)/shard_map/ppermute | solution.py:38
  376.1 16.3 %collective-permute-start.78 = (bf16[2,128,1024]{2,1,0:T(8,128)(2,1)S(1)}, bf16[2,128,1024]{2,1,0:T(8,128)(2,1)S(1)}, u32[]{:S(2)}, u32[]{:S(2)}) collective-permute-start(bf16[2,128,1024]{2,1,0:T(8,128)(2,1)S(1)} %get-tuple-element.192), channel_id=1, source_target_pairs={{0,2},{1,3},{2,4},{3,5},{4,6},{5,7},{6,0},{7,1},{8,10},{9,11},{10,... | collective-permute-start | bytes 1572872 | tf_op jit(solution)/shard_map/ppermute | solution.py:38
  376.1 16.6 %collective-permute-start.79 = (bf16[2,128,1024]{2,1,0:T(8,128)(2,1)S(1)}, bf16[2,128,1024]{2,1,0:T(8,128)(2,1)S(1)}, u32[]{:S(2)}, u32[]{:S(2)}) collective-permute-start(bf16[2,128,1024]{2,1,0:T(8,128)(2,1)S(1)} %get-tuple-element.191), channel_id=1, source_target_pairs={{0,6},{1,7},{2,0},{3,1},{4,2},{5,3},{6,4},{7,5},{8,14},{9,15},{10,... | collective-permute-start | bytes 1572872 | tf_op jit(solution)/shard_map/ppermute | solution.py:38
  385.9 16.8 %collective-permute-start.40 = (bf16[96,1024]{1,0:T(8,128)(2,1)}, bf16[96,1024]{1,0:T(8,128)(2,1)}, u32[]{:S(2)}, u32[]{:S(2)}) collective-permute-start(bf16[96,1024]{1,0:T(8,128)(2,1)} %get-tuple-element.211), channel_id=1, source_target_pairs={{0,48},{8,56},{16,0},{24,8},{32,16},{40,24},{48,32},{56,40},{1,49}... | collective-permute-start | bytes 589832 | tf_op jit(solution)/shard_map/ppermute | solution.py:38
  389.3 13.4 %collective-permute-start.41 = (bf16[96,1024]{1,0:T(8,128)(2,1)}, bf16[96,1024]{1,0:T(8,128)(2,1)}, u32[]{:S(2)}, u32[]{:S(2)}) collective-permute-start(bf16[96,1024]{1,0:T(8,128)(2,1)} %get-tuple-element.213), channel_id=1, source_target_pairs={{0,32},{8,40},{16,48},{24,56},{32,0},{40,8},{48,16},{56,24},{1,33}... | collective-permute-start | bytes 589832 | tf_op jit(solution)/shard_map/ppermute | solution.py:38
  400.3 26.8 %collective-permute-start.85 = (bf16[2,192,1024]{2,1,0:T(8,128)(2,1)S(1)}, bf16[2,192,1024]{2,1,0:T(8,128)(2,1)S(1)}, u32[]{:S(2)}, u32[]{:S(2)}) collective-permute-start(bf16[2,192,1024]{2,1,0:T(8,128)(2,1)S(1)} %pad_maximum_fusion.14), channel_id=1, source_target_pairs={{0,4},{1,5},{2,6},{3,7},{4,0},{5,1},{6,2},{7,3},{8,12},{9,13},{10,... | collective-permute-start | bytes 2359304 | tf_op jit(solution)/shard_map/ppermute | solution.py:38
  404.8 22.2 %collective-permute-start.83 = (bf16[2,64,1024]{2,1,0:T(8,128)(2,1)S(1)}, bf16[2,64,1024]{2,1,0:T(8,128)(2,1)S(1)}, u32[]{:S(2)}, u32[]{:S(2)}) collective-permute-start(bf16[2,64,1024]{2,1,0:T(8,128)(2,1)S(1)} %get-tuple-element.198), channel_id=1, source_target_pairs={{0,2},{1,3},{2,4},{3,5},{4,6},{5,7},{6,0},{7,1},{8,10},{9,11},{10,... | collective-permute-start | bytes 786440 | tf_op jit(solution)/shard_map/ppermute | solution.py:38
  405.0 22.0 %collective-permute-start.84 = (bf16[2,64,1024]{2,1,0:T(8,128)(2,1)S(1)}, bf16[2,64,1024]{2,1,0:T(8,128)(2,1)S(1)}, u32[]{:S(2)}, u32[]{:S(2)}) collective-permute-start(bf16[2,64,1024]{2,1,0:T(8,128)(2,1)S(1)} %get-tuple-element.197), channel_id=1, source_target_pairs={{0,6},{1,7},{2,0},{3,1},{4,2},{5,3},{6,4},{7,5},{8,14},{9,15},{10,... | collective-permute-start | bytes 786440 | tf_op jit(solution)/shard_map/ppermute | solution.py:38
  430.3 13.4 %collective-permute-start.90 = (bf16[192,1024]{1,0:T(8,128)(2,1)S(1)}, bf16[192,1024]{1,0:T(8,128)(2,1)S(1)}, u32[]{:S(2)}, u32[]{:S(2)}) collective-permute-start(bf16[192,1024]{1,0:T(8,128)(2,1)S(1)} %get-tuple-element.193), channel_id=1, source_target_pairs={{0,64},{8,72},{16,80},{24,88},{32,96},{40,104},{48,112},{56,120},{... | collective-permute-start | bytes 1179656 | tf_op jit(solution)/shard_map/ppermute | solution.py:38
  431.0 12.7 %collective-permute-start.91 = (bf16[192,1024]{1,0:T(8,128)(2,1)S(1)}, bf16[192,1024]{1,0:T(8,128)(2,1)S(1)}, u32[]{:S(2)}, u32[]{:S(2)}) collective-permute-start(bf16[192,1024]{1,0:T(8,128)(2,1)S(1)} %get-tuple-element.194), channel_id=1, source_target_pairs={{0,72},{8,64},{16,88},{24,80},{32,104},{40,96},{48,120},{56,112},{... | collective-permute-start | bytes 1179656 | tf_op jit(solution)/shard_map/ppermute | solution.py:38
  433.1 18.1 %collective-permute-start.92 = (bf16[192,1024]{1,0:T(8,128)(2,1)S(1)}, bf16[192,1024]{1,0:T(8,128)(2,1)S(1)}, u32[]{:S(2)}, u32[]{:S(2)}) collective-permute-start(bf16[192,1024]{1,0:T(8,128)(2,1)S(1)} %get-tuple-element.195), channel_id=1, source_target_pairs={{0,8},{8,0},{16,24},{24,16},{32,40},{40,32},{48,56},{56,48},{64,72... | collective-permute-start | bytes 1179656 | tf_op jit(solution)/shard_map/ppermute | solution.py:38
  434.9 55.7 %collective-permute-start.44 = (bf16[96,1024]{1,0:T(8,128)(2,1)S(1)}, bf16[96,1024]{1,0:T(8,128)(2,1)S(1)}, u32[]{:S(2)}, u32[]{:S(2)}) collective-permute-start(bf16[96,1024]{1,0:T(8,128)(2,1)S(1)} %broadcast_select_fusion.2), channel_id=1, source_target_pairs={{0,64},{1,72},{2,66},{3,74},{4,68},{5,76},{6,70},{7,78},{8,65},{9,... | collective-permute-start | bytes 589832 | tf_op jit(solution)/shard_map/ppermute | solution.py:38
  454.2 11.9 %collective-permute-start.99 = (f32[12,1024]{1,0:T(8,128)S(1)}, f32[12,1024]{1,0:T(8,128)S(1)}, u32[]{:S(2)}, u32[]{:S(2)}) collective-permute-start(f32[12,1024]{1,0:T(8,128)S(1)} %add_add_fusion.2), channel_id=1, source_target_pairs={{0,2},{1,3},{2,4},{3,5},{4,6},{5,7},{6,0},{7,1},{8,10},{9,11},{10,... | collective-permute-start | bytes 147464 | tf_op jit(solution)/shard_map/ppermute | solution.py:38
  456.2 34.4 %collective-permute-start.43 = (bf16[96,1024]{1,0:T(8,128)(2,1)}, bf16[96,1024]{1,0:T(8,128)(2,1)}, u32[]{:S(2)}, u32[]{:S(2)}) collective-permute-start(bf16[96,1024]{1,0:T(8,128)(2,1)} %get-tuple-element.177), channel_id=1, source_target_pairs={{0,0},{1,8},{2,2},{3,10},{4,4},{5,12},{6,6},{7,14},{8,1},{9,9},{10... | collective-permute-start | bytes 589832 | tf_op jit(solution)/shard_map/ppermute | solution.py:38
  463.8 12.8 %collective-permute-start.97 = (bf16[192,1024]{1,0:T(8,128)(2,1)S(1)}, bf16[192,1024]{1,0:T(8,128)(2,1)S(1)}, u32[]{:S(2)}, u32[]{:S(2)}) collective-permute-start(bf16[192,1024]{1,0:T(8,128)(2,1)S(1)} %fusion.107), channel_id=1, source_target_pairs={{0,4},{1,5},{2,6},{3,7},{4,0},{5,1},{6,2},{7,3},{8,12},{9,13},{10,... | collective-permute-start | bytes 1179656 | tf_op jit(solution)/shard_map/ppermute | solution.py:38
  466.2 16.8 %collective-permute-start.98 = (bf16[192,1024]{1,0:T(8,128)(2,1)S(1)}, bf16[192,1024]{1,0:T(8,128)(2,1)S(1)}, u32[]{:S(2)}, u32[]{:S(2)}) collective-permute-start(bf16[192,1024]{1,0:T(8,128)(2,1)S(1)} %fusion.107), channel_id=1, source_target_pairs={{0,6},{1,7},{2,0},{3,1},{4,2},{5,3},{6,4},{7,5},{8,14},{9,15},{10,... | collective-permute-start | bytes 1179656 | tf_op jit(solution)/shard_map/ppermute | solution.py:38
  483.0 14.6 %collective-permute-start.102 = (bf16[4,192,1024]{2,1,0:T(8,128)(2,1)S(1)}, bf16[4,192,1024]{2,1,0:T(8,128)(2,1)}, u32[]{:S(2)}, u32[]{:S(2)}) collective-permute-start(bf16[4,192,1024]{2,1,0:T(8,128)(2,1)S(1)} %bitcast_dynamic-update-slice_fusion.2), channel_id=1, source_target_pairs={{0,1},{1,0},{2,3},{3,2},{4,5},{5,4},{6,7},{7,6},{8,9},{9,8},{10,11... | collective-permute-start | bytes 4718600 | tf_op jit(solution)/shard_map/ppermute | solution.py:38
  (173 other events, 1302.4 us)

commit v8 on v5

--- a/solution.py
+++ b/solution.py
@@ -549,9 +549,9 @@
             kept["one"] = far_y(kept["one"], kept["near"])
             value, kept["feed"] = tied(value, over_cores(kept["feed"], core))
             return value
-        near, attention = near_y(kept["feed"]), over_cores(group, core)
-        value, *rest = tied(value, kept["one"], near, attention)
-        kept["one"], kept["near"], kept["attention"] = rest
+        kept["one"], kept["feed"] = tied(kept["one"], kept["feed"])
+        kept["near"] = near_y(kept["feed"])
+        value, kept["attention"] = tied(value, over_cores(group, core))
         return value
 
     last_grad, early_zero, late_zero = layer_backward(

time: 480 us -> 509 us (1.060)
  waiting for transfers between devices: 166 us -> 186 us
  starting transfers between devices: 152 us -> 135 us
  local copies, waits for them, and re-layouts: 53.8 us -> 66.7 us
  other arithmetic: 47.3 us -> 54.9 us
  matrix products: 44.3 us -> 50 us
    ppermute x103, waiting for transfers between devices: 166 us -> 186 us  [move(): return lax.ppermute(array, axes, sorted(pairs.items()))]
    ppermute x103, starting transfers between devices: 152 us -> 135 us  [move(): return lax.ppermute(array, axes, sorted(pairs.items()))]
    unnamed x243 -> x255, local copies, waits for them, and re-layouts: 31.3 us -> 38 us
  transfers between devices with their start and end apart: 103 -> 103, of which waited for: 45 -> 44; matrix products, arithmetic and copies ran while one was open for 19% -> 23% of each run, Pallas kernels for 1% -> 1%
where the time goes in v8:
time: 509 us; the launch traced here: 501 us
  waiting for transfers between devices  186 us (37%)
  starting transfers between devices  135 us (27%)
  local copies, waits for them, and re-layouts  66.7 us (13%)
  other arithmetic  54.9 us (11%)
  matrix products  50 us (10%)
    ppermute x103, waiting for transfers between devices, move(): return lax.ppermute(array, axes, sorted(pairs.items()))  186 us
    ppermute x103, starting transfers between devices, move(): return lax.ppermute(array, axes, sorted(pairs.items()))  135 us
    unnamed x255, local copies, waits for them, and re-layouts  38 us
    dot_general x24, matrix products, dot(): lax.dot_general(left, right, (((left_dim,), (right_dim,)), ((), ())), pre...  31 us
  transfers between devices with their start and end apart: 103, of which 44 were waited for; matrix products, arithmetic and copies ran while one was open for 23% of the time, Pallas kernels for 1%

profile of v8, /device:TPU:1, one launch (start us, length us, event | category | flops | bytes accessed | tf_op | source)
XLA Modules:
  0.0 500.8 jit_solution(1689219980643030623)
XLA Ops:
  6.4 2.5 collective-permute-start.4
  15.0 5.4 %collective-permute-start = (bf16[96,1024]{1,0:T(8,128)(2,1)S(1)}, bf16[96,1024]{1,0:T(8,128)(2,1)S(1)}, u32[]{:S(2)}, u32[]{:S(2)}) collective-permute-start(bf16[96,1024]{1,0:T(8,128)(2,1)S(1)} %dynamic-slice_bitcast_fusion.12), channel_id=1, source_target_pairs={{0,0},{1,8},{2,2},{3,10},{4,4},{5,12},{6,6},{7,14},{8,1},{9,9},{10... | collective-permute-start | bytes 589832 | tf_op jit(solution)/shard_map/ppermute | solution.py:38
  21.5 9.0 %collective-permute-done = bf16[96,1024]{1,0:T(8,128)(2,1)S(1)} collective-permute-done((bf16[96,1024]{1,0:T(8,128)(2,1)S(1)}, bf16[96,1024]{1,0:T(8,128)(2,1)S(1)}, u32[]{:S(2)}, u32[]{:S(2)}) %collective-permute-start) | collective-permute-done | bytes 196640 | tf_op jit(solution)/shard_map/ppermute | solution.py:38
  33.0 2.5 collective-permute-start.6
  38.1 4.5 collective-permute-done.6
  44.8 3.2 collective-permute-start.8
  57.3 2.5 collective-permute-start.13
  61.3 3.2 fusion.81
  80.6 7.3 %collective-permute-done.15.refs_3_ = bf16[512,512]{1,0:T(8,128)(2,1)S(1)} collective-permute-done((bf16[512,512]{1,0:T(8,128)(2,1)}, bf16[512,512]{1,0:T(8,128)(2,1)S(1)}, u32[]{:S(2)}, u32[]{:S(2)}) %collective-permute-start.15) | collective-permute-done | bytes 524320 | tf_op jit(solution)/shard_map/ppermute | solution.py:38
  88.0 2.7 collective-permute-start.20
  94.4 2.5 collective-permute-done.16
  96.9 2.4 collective-permute-done.17
  99.3 5.7 %collective-permute-done.18 = bf16[96,1024]{1,0:T(8,128)(2,1)S(1)} collective-permute-done((bf16[96,1024]{1,0:T(8,128)(2,1)S(1)}, bf16[96,1024]{1,0:T(8,128)(2,1)S(1)}, u32[]{:S(2)}, u32[]{:S(2)}) %collective-permute-start.18) | collective-permute-done | bytes 196640 | tf_op jit(solution)/shard_map/ppermute | solution.py:38
  111.5 6.1 %collective-permute-done.21 = bf16[96,1024]{1,0:T(8,128)(2,1)S(1)} collective-permute-done((bf16[96,1024]{1,0:T(8,128)(2,1)S(1)}, bf16[96,1024]{1,0:T(8,128)(2,1)S(1)}, u32[]{:S(2)}, u32[]{:S(2)}) %collective-permute-start.21) | collective-permute-done | bytes 196640 | tf_op jit(solution)/shard_map/ppermute | solution.py:38
  122.5 3.6 collective-permute-start.45
  157.0 4.2 collective-permute-done.30
  161.2 3.6 collective-permute-done.31
  164.7 2.8 fusion.78
  183.4 4.5 collective-permute-done.34
  187.8 2.6 collective-permute-done.35
  190.4 4.3 collective-permute-done.36
  198.3 5.7 %collective-permute-done.37 = bf16[96,1024]{1,0:T(8,128)(2,1)S(1)} collective-permute-done((bf16[96,1024]{1,0:T(8,128)(2,1)S(1)}, bf16[96,1024]{1,0:T(8,128)(2,1)S(1)}, u32[]{:S(2)}, u32[]{:S(2)}) %collective-permute-start.37) | collective-permute-done | bytes 196640 | tf_op jit(solution)/shard_map/ppermute | solution.py:38
  226.5 5.2 %collective-permute-done.49 = bf16[96,1024]{1,0:T(8,128)(2,1)} collective-permute-done((bf16[96,1024]{1,0:T(8,128)(2,1)}, bf16[96,1024]{1,0:T(8,128)(2,1)}, u32[]{:S(2)}, u32[]{:S(2)}) %collective-permute-start.49) | collective-permute-done | bytes 196640 | tf_op jit(solution)/shard_map/ppermute | solution.py:38
  231.7 4.2 collective-permute-start.42
  239.6 2.5 collective-permute-start.54
  245.6 3.6 collective-permute-done.52
  249.2 4.7 collective-permute-start.43
  254.4 4.1 multiply_reduce_fusion.1
  275.4 5.0 collective-permute-done.58
  285.6 7.5 %collective-permute-done.59 = bf16[96,1024]{1,0:T(8,128)(2,1)S(1)} collective-permute-done((bf16[96,1024]{1,0:T(8,128)(2,1)S(1)}, bf16[96,1024]{1,0:T(8,128)(2,1)S(1)}, u32[]{:S(2)}, u32[]{:S(2)}) %collective-permute-start.59) | collective-permute-done | bytes 196640 | tf_op jit(solution)/shard_map/ppermute | solution.py:38
  297.1 2.6 fusion.1
  305.7 2.5 convert_reduce_fusion.1
  309.2 2.9 collective-permute-start.64
  314.3 5.7 %collective-permute-done.64 = bf16[96,1024]{1,0:T(8,128)(2,1)S(1)} collective-permute-done((bf16[96,1024]{1,0:T(8,128)(2,1)S(1)}, bf16[96,1024]{1,0:T(8,128)(2,1)S(1)}, u32[]{:S(2)}, u32[]{:S(2)}) %collective-permute-start.64) | collective-permute-done | bytes 196640 | tf_op jit(solution)/shard_map/ppermute | solution.py:38
  320.0 4.1 collective-permute-done.66
  329.2 2.6 convolution_convert_fusion.1
  335.1 3.1 collective-permute-done.67
  343.6 4.1 multiply_reduce_fusion
  355.0 17.6 %collective-permute-done.90 = bf16[2,192,1024]{2,1,0:T(8,128)(2,1)S(1)} collective-permute-done((bf16[2,192,1024]{2,1,0:T(8,128)(2,1)S(1)}, bf16[2,192,1024]{2,1,0:T(8,128)(2,1)S(1)}, u32[]{:S(2)}, u32[]{:S(2)}) %collective-permute-start.90) | collective-permute-done | bytes 786464 | tf_op jit(solution)/shard_map/ppermute | solution.py:38
  389.5 4.8 collective-permute-done.76
  403.2 20.7 %collective-permute-done.93 = bf16[2,64,1024]{2,1,0:T(8,128)(2,1)S(1)} collective-permute-done((bf16[2,64,1024]{2,1,0:T(8,128)(2,1)S(1)}, bf16[2,64,1024]{2,1,0:T(8,128)(2,1)S(1)}, u32[]{:S(2)}, u32[]{:S(2)}) %collective-permute-start.93) | collective-permute-done | bytes 262176 | tf_op jit(solution)/shard_map/ppermute | solution.py:38
  426.3 2.7 collective-permute-start.97
  432.2 14.2 %collective-permute-done.96 = bf16[192,1024]{1,0:T(8,128)(2,1)S(1)} collective-permute-done((bf16[192,1024]{1,0:T(8,128)(2,1)}, bf16[192,1024]{1,0:T(8,128)(2,1)S(1)}, u32[]{:S(2)}, u32[]{:S(2)}) %collective-permute-start.96) | collective-permute-done | bytes 393248 | tf_op jit(solution)/shard_map/ppermute | solution.py:38
  448.7 2.7 collective-permute-start.100
  451.4 3.1 collective-permute-start.83
  458.1 8.6 %collective-permute-done.100 = bf16[192,1024]{1,0:T(8,128)(2,1)S(1)} collective-permute-done((bf16[192,1024]{1,0:T(8,128)(2,1)S(1)}, bf16[192,1024]{1,0:T(8,128)(2,1)S(1)}, u32[]{:S(2)}, u32[]{:S(2)}) %collective-permute-start.100) | collective-permute-done | bytes 393248 | tf_op jit(solution)/shard_map/ppermute | solution.py:38
  476.8 5.6 %collective-permute-start.78 = (bf16[96,1024]{1,0:T(8,128)(2,1)S(1)}, bf16[96,1024]{1,0:T(8,128)(2,1)S(1)}, u32[]{:S(2)}, u32[]{:S(2)}) collective-permute-start(bf16[96,1024]{1,0:T(8,128)(2,1)S(1)} %get-tuple-element.162), channel_id=1, source_target_pairs={{0,0},{1,8},{2,2},{3,10},{4,4},{5,12},{6,6},{7,14},{8,1},{9,9},{10... | collective-permute-start | bytes 589832 | tf_op jit(solution)/shard_map/ppermute | solution.py:38
  483.2 2.8 collective-permute-start.88
  (639 shorter events, 259.7 us)
Async XLA Ops:
  6.4 14.4 %collective-permute-start.4 = (bf16[16,512]{1,0:T(8,128)(2,1)S(1)}, bf16[16,512]{1,0:T(8,128)(2,1)S(1)}, u32[]{:S(2)}, u32[]{:S(2)}) collective-permute-start(bf16[16,512]{1,0:T(8,128)(2,1)S(1)} %reshape.743.refs_2_), channel_id=1, source_target_pairs={{0,64},{8,72},{16,80},{24,88},{32,96},{40,104},{48,112},{56,120},{... | collective-permute-start | bytes 49160 | tf_op jit(solution)/shard_map/ppermute | solution.py:38
  12.3 18.6 %collective-permute-start.1 = (bf16[528,512]{1,0:T(8,128)(2,1)}, bf16[528,512]{1,0:T(8,128)(2,1)}, u32[]{:S(2)}, u32[]{:S(2)}) collective-permute-start(bf16[528,512]{1,0:T(8,128)(2,1)} %pad_maximum_fusion.17), channel_id=1, source_target_pairs={{0,64},{8,72},{16,80},{24,88},{32,96},{40,104},{48,112},{56,120},{... | collective-permute-start | bytes 1622024 | tf_op jit(solution)/shard_map/ppermute | solution.py:38
  13.9 16.9 %collective-permute-start.2 = (bf16[528,512]{1,0:T(8,128)(2,1)}, bf16[528,512]{1,0:T(8,128)(2,1)}, u32[]{:S(2)}, u32[]{:S(2)}) collective-permute-start(bf16[528,512]{1,0:T(8,128)(2,1)} %pad_maximum_fusion.17), channel_id=1, source_target_pairs={{0,72},{8,64},{16,88},{24,80},{32,104},{40,96},{48,120},{56,112},{... | collective-permute-start | bytes 1622024 | tf_op jit(solution)/shard_map/ppermute | solution.py:38
  15.0 15.5 %collective-permute-start = (bf16[96,1024]{1,0:T(8,128)(2,1)S(1)}, bf16[96,1024]{1,0:T(8,128)(2,1)S(1)}, u32[]{:S(2)}, u32[]{:S(2)}) collective-permute-start(bf16[96,1024]{1,0:T(8,128)(2,1)S(1)} %dynamic-slice_bitcast_fusion.12), channel_id=1, source_target_pairs={{0,0},{1,8},{2,2},{3,10},{4,4},{5,12},{6,6},{7,14},{8,1},{9,9},{10... | collective-permute-start | bytes 589832 | tf_op jit(solution)/shard_map/ppermute | solution.py:38
  20.5 50.2 %collective-permute-start.14 = (s32[8,96]{1,0:T(8,128)S(1)}, s32[8,96]{1,0:T(8,128)}, u32[]{:S(2)}, u32[]{:S(2)}) collective-permute-start(s32[8,96]{1,0:T(8,128)S(1)} %reshape.746), channel_id=1, source_target_pairs={{0,1},{1,0},{2,3},{3,2},{4,5},{5,4},{6,7},{7,6},{8,9},{9,8},{10,11... | collective-permute-start | bytes 9224 | tf_op jit(solution)/shard_map/ppermute | solution.py:38
  30.8 17.2 %collective-permute-start.3 = (bf16[528,512]{1,0:T(8,128)(2,1)}, bf16[528,512]{1,0:T(8,128)(2,1)}, u32[]{:S(2)}, u32[]{:S(2)}) collective-permute-start(bf16[528,512]{1,0:T(8,128)(2,1)} %pad_maximum_fusion.17), channel_id=1, source_target_pairs={{0,8},{8,0},{16,24},{24,16},{32,40},{40,32},{48,56},{56,48},{64,72... | collective-permute-start | bytes 1622024 | tf_op jit(solution)/shard_map/ppermute | solution.py:38
  56.3 16.1 %collective-permute-start.12 = (bf16[512,512]{1,0:T(8,128)(2,1)}, bf16[512,512]{1,0:T(8,128)(2,1)S(1)}, u32[]{:S(2)}, u32[]{:S(2)}) collective-permute-start(bf16[512,512]{1,0:T(8,128)(2,1)} %dynamic-slice_bitcast_fusion.7), channel_id=1, source_target_pairs={{0,64},{8,72},{16,80},{24,88},{32,96},{40,104},{48,112},{56,120},{... | collective-permute-start | bytes 1572872 | tf_op jit(solution)/shard_map/ppermute | solution.py:38
  57.3 15.1 %collective-permute-start.13 = (bf16[512,512]{1,0:T(8,128)(2,1)}, bf16[512,512]{1,0:T(8,128)(2,1)S(1)}, u32[]{:S(2)}, u32[]{:S(2)}) collective-permute-start(bf16[512,512]{1,0:T(8,128)(2,1)} %dynamic-slice_bitcast_fusion.7), channel_id=1, source_target_pairs={{0,72},{8,64},{16,88},{24,80},{32,104},{40,96},{48,120},{56,112},{... | collective-permute-start | bytes 1572872 | tf_op jit(solution)/shard_map/ppermute | solution.py:38
  72.4 15.5 %collective-permute-start.15 = (bf16[512,512]{1,0:T(8,128)(2,1)}, bf16[512,512]{1,0:T(8,128)(2,1)S(1)}, u32[]{:S(2)}, u32[]{:S(2)}) collective-permute-start(bf16[512,512]{1,0:T(8,128)(2,1)} %dynamic-slice_bitcast_fusion.7), channel_id=1, source_target_pairs={{0,8},{8,0},{16,24},{24,16},{32,40},{40,32},{48,56},{56,48},{64,72... | collective-permute-start | bytes 1572872 | tf_op jit(solution)/shard_map/ppermute | solution.py:38
  87.9 17.2 %collective-permute-start.19 = (bf16[256,1024]{1,0:T(8,128)(2,1)S(1)}, bf16[256,1024]{1,0:T(8,128)(2,1)S(1)}, u32[]{:S(2)}, u32[]{:S(2)}) collective-permute-start(bf16[256,1024]{1,0:T(8,128)(2,1)S(1)} %copy-done.65), channel_id=1, source_target_pairs={{0,64},{8,72},{16,80},{24,88},{32,96},{40,104},{48,112},{56,120},{... | collective-permute-start | bytes 1572872 | tf_op jit(solution)/shard_map/ppermute | solution.py:38
  88.0 17.2 %collective-permute-start.20 = (bf16[256,1024]{1,0:T(8,128)(2,1)S(1)}, bf16[256,1024]{1,0:T(8,128)(2,1)S(1)}, u32[]{:S(2)}, u32[]{:S(2)}) collective-permute-start(bf16[256,1024]{1,0:T(8,128)(2,1)S(1)} %copy-done.65), channel_id=1, source_target_pairs={{0,72},{8,64},{16,88},{24,80},{32,104},{40,96},{48,120},{56,112},{... | collective-permute-start | bytes 1572872 | tf_op jit(solution)/shard_map/ppermute | solution.py:38
  105.6 13.8 %collective-permute-start.24 = (bf16[256,1024]{1,0:T(8,128)(2,1)S(1)}, bf16[256,1024]{1,0:T(8,128)(2,1)S(1)}, u32[]{:S(2)}, u32[]{:S(2)}) collective-permute-start(bf16[256,1024]{1,0:T(8,128)(2,1)S(1)} %copy-done.65), channel_id=1, source_target_pairs={{0,8},{8,0},{16,24},{24,16},{32,40},{40,32},{48,56},{56,48},{64,72... | collective-permute-start | bytes 1572872 | tf_op jit(solution)/shard_map/ppermute | solution.py:38
  109.4 16.7 %collective-permute-start.25 = (bf16[3,512,512]{2,1,0:T(8,128)(2,1)S(1)}, bf16[3,512,512]{2,1,0:T(8,128)(2,1)S(1)}, u32[]{:S(2)}, u32[]{:S(2)}) collective-permute-start(bf16[3,512,512]{2,1,0:T(8,128)(2,1)S(1)} %pad_maximum_fusion.1), channel_id=1, source_target_pairs={{0,1},{1,0},{2,3},{3,2},{4,5},{5,4},{6,7},{7,6},{8,9},{9,8},{10,11... | collective-permute-start | bytes 4718600 | tf_op jit(solution)/shard_map/ppermute | solution.py:38
  122.5 19.8 %collective-permute-start.45 = (bf16[96,1024]{1,0:T(8,128)(2,1)}, bf16[96,1024]{1,0:T(8,128)(2,1)}, u32[]{:S(2)}, u32[]{:S(2)}) collective-permute-start(bf16[96,1024]{1,0:T(8,128)(2,1)} %dynamic-slice_bitcast_fusion.11), channel_id=1, source_target_pairs={{0,0},{1,8},{2,2},{3,10},{4,4},{5,12},{6,6},{7,14},{8,1},{9,9},{10... | collective-permute-start | bytes 589832 | tf_op jit(solution)/shard_map/ppermute | solution.py:38
  142.2 12.6 %collective-permute-start.46 = (bf16[96,1024]{1,0:T(8,128)(2,1)}, bf16[96,1024]{1,0:T(8,128)(2,1)S(1)}, u32[]{:S(2)}, u32[]{:S(2)}) collective-permute-start(bf16[96,1024]{1,0:T(8,128)(2,1)} %collective-permute-done.45), channel_id=1, source_target_pairs={{0,16},{8,24},{16,32},{24,40},{32,48},{40,56},{48,0},{56,8},{1,17}... | collective-permute-start | bytes 589832 | tf_op jit(solution)/shard_map/ppermute | solution.py:38
  144.3 26.0 %collective-permute-start.47 = (bf16[96,1024]{1,0:T(8,128)(2,1)}, bf16[96,1024]{1,0:T(8,128)(2,1)}, u32[]{:S(2)}, u32[]{:S(2)}) collective-permute-start(bf16[96,1024]{1,0:T(8,128)(2,1)} %collective-permute-done.45), channel_id=1, source_target_pairs={{0,32},{8,40},{16,48},{24,56},{32,0},{40,8},{48,16},{56,24},{1,33}... | collective-permute-start | bytes 589832 | tf_op jit(solution)/shard_map/ppermute | solution.py:38
  151.1 13.6 %collective-permute-start.31 = (bf16[96,1024]{1,0:T(8,128)(2,1)}, bf16[96,1024]{1,0:T(8,128)(2,1)}, u32[]{:S(2)}, u32[]{:S(2)}) collective-permute-start(bf16[96,1024]{1,0:T(8,128)(2,1)} %fusion.130), channel_id=1, source_target_pairs={{0,32},{8,40},{16,48},{24,56},{32,0},{40,8},{48,16},{56,24},{1,33}... | collective-permute-start | bytes 589832 | tf_op jit(solution)/shard_map/ppermute | solution.py:38
  154.9 17.1 %collective-permute-start.48 = (bf16[96,1024]{1,0:T(8,128)(2,1)}, bf16[96,1024]{1,0:T(8,128)(2,1)}, u32[]{:S(2)}, u32[]{:S(2)}) collective-permute-start(bf16[96,1024]{1,0:T(8,128)(2,1)} %collective-permute-done.45), channel_id=1, source_target_pairs={{0,48},{8,56},{16,0},{24,8},{32,16},{40,24},{48,32},{56,40},{1,49}... | collective-permute-start | bytes 589832 | tf_op jit(solution)/shard_map/ppermute | solution.py:38
  218.2 78.2 %collective-permute-start.62 = (bf16[2,512,1024]{2,1,0:T(8,128)(2,1)}, bf16[2,512,1024]{2,1,0:T(8,128)(2,1)}, u32[]{:S(2)}, u32[]{:S(2)}) collective-permute-start(bf16[2,512,1024]{2,1,0:T(8,128)(2,1)} %fusion.19), channel_id=1, source_target_pairs={{0,1},{1,0},{2,3},{3,2},{4,5},{5,4},{6,7},{7,6},{8,9},{9,8},{10,11... | collective-permute-start | bytes 6291464 | tf_op jit(solution)/shard_map/ppermute | solution.py:38
  223.0 12.9 %collective-permute-start.51 = (bf16[96,1024]{1,0:T(8,128)(2,1)}, bf16[96,1024]{1,0:T(8,128)(2,1)}, u32[]{:S(2)}, u32[]{:S(2)}) collective-permute-start(bf16[96,1024]{1,0:T(8,128)(2,1)} %get-tuple-element.199), channel_id=1, source_target_pairs={{0,16},{8,24},{16,32},{24,40},{32,48},{40,56},{48,0},{56,8},{1,17}... | collective-permute-start | bytes 589832 | tf_op jit(solution)/shard_map/ppermute | solution.py:38
  224.3 14.4 %collective-permute-start.40 = (bf16[96,1024]{1,0:T(8,128)(2,1)}, bf16[96,1024]{1,0:T(8,128)(2,1)}, u32[]{:S(2)}, u32[]{:S(2)}) collective-permute-start(bf16[96,1024]{1,0:T(8,128)(2,1)} %get-tuple-element.201), channel_id=1, source_target_pairs={{0,48},{8,56},{16,0},{24,8},{32,16},{40,24},{48,32},{56,40},{1,49}... | collective-permute-start | bytes 589832 | tf_op jit(solution)/shard_map/ppermute | solution.py:38
  231.7 12.6 %collective-permute-start.42 = (bf16[96,1024]{1,0:T(8,128)(2,1)S(1)}, bf16[96,1024]{1,0:T(8,128)(2,1)S(1)}, u32[]{:S(2)}, u32[]{:S(2)}) collective-permute-start(bf16[96,1024]{1,0:T(8,128)(2,1)S(1)} %get-tuple-element.202), channel_id=1, source_target_pairs={{0,16},{8,24},{16,32},{24,40},{32,48},{40,56},{48,0},{56,8},{1,17}... | collective-permute-start | bytes 589832 | tf_op jit(solution)/shard_map/ppermute | solution.py:38
  238.7 15.2 %collective-permute-start.53 = (bf16[96,1024]{1,0:T(8,128)(2,1)S(1)}, bf16[96,1024]{1,0:T(8,128)(2,1)S(1)}, u32[]{:S(2)}, u32[]{:S(2)}) collective-permute-start(bf16[96,1024]{1,0:T(8,128)(2,1)S(1)} %get-tuple-element.155), channel_id=1, source_target_pairs={{0,32},{8,40},{16,48},{24,56},{32,0},{40,8},{48,16},{56,24},{1,33}... | collective-permute-start | bytes 589832 | tf_op jit(solution)/shard_map/ppermute | solution.py:38
  239.6 14.3 %collective-permute-start.54 = (bf16[96,1024]{1,0:T(8,128)(2,1)S(1)}, bf16[96,1024]{1,0:T(8,128)(2,1)S(1)}, u32[]{:S(2)}, u32[]{:S(2)}) collective-permute-start(bf16[96,1024]{1,0:T(8,128)(2,1)S(1)} %get-tuple-element.155), channel_id=1, source_target_pairs={{0,48},{8,56},{16,0},{24,8},{32,16},{40,24},{48,32},{56,40},{1,49}... | collective-permute-start | bytes 589832 | tf_op jit(solution)/shard_map/ppermute | solution.py:38
  245.5 17.4 %collective-permute-start.44 = (bf16[96,1024]{1,0:T(8,128)(2,1)S(1)}, bf16[96,1024]{1,0:T(8,128)(2,1)S(1)}, u32[]{:S(2)}, u32[]{:S(2)}) collective-permute-start(bf16[96,1024]{1,0:T(8,128)(2,1)S(1)} %broadcast_select_fusion.2), channel_id=1, source_target_pairs={{0,64},{1,72},{2,66},{3,74},{4,68},{5,76},{6,70},{7,78},{8,65},{9,... | collective-permute-start | bytes 589832 | tf_op jit(solution)/shard_map/ppermute | solution.py:38
  249.2 13.7 %collective-permute-start.43 = (bf16[96,1024]{1,0:T(8,128)(2,1)S(1)}, bf16[96,1024]{1,0:T(8,128)(2,1)S(1)}, u32[]{:S(2)}, u32[]{:S(2)}) collective-permute-start(bf16[96,1024]{1,0:T(8,128)(2,1)S(1)} %get-tuple-element.167), channel_id=1, source_target_pairs={{0,0},{1,8},{2,2},{3,10},{4,4},{5,12},{6,6},{7,14},{8,1},{9,9},{10... | collective-permute-start | bytes 589832 | tf_op jit(solution)/shard_map/ppermute | solution.py:38
  272.3 22.4 %collective-permute-start.63 = (bf16[2,256,1024]{2,1,0:T(8,128)(2,1)}, bf16[2,256,1024]{2,1,0:T(8,128)(2,1)}, u32[]{:S(2)}, u32[]{:S(2)}) collective-permute-start(bf16[2,256,1024]{2,1,0:T(8,128)(2,1)} %fusion.93), channel_id=1, source_target_pairs={{0,1},{1,0},{2,3},{3,2},{4,5},{5,4},{6,7},{7,6},{8,9},{9,8},{10,11... | collective-permute-start | bytes 3145736 | tf_op jit(solution)/shard_map/ppermute | solution.py:38
  302.8 37.7 %collective-permute-start.70 = (bf16[2,192,1024]{2,1,0:T(8,128)(2,1)}, bf16[2,192,1024]{2,1,0:T(8,128)(2,1)}, u32[]{:S(2)}, u32[]{:S(2)}) collective-permute-start(bf16[2,192,1024]{2,1,0:T(8,128)(2,1)} %get-tuple-element.177), channel_id=1, source_target_pairs={{0,2},{1,3},{2,4},{3,5},{4,6},{5,7},{6,0},{7,1},{8,10},{9,11},{10,... | collective-permute-start | bytes 2359304 | tf_op jit(solution)/shard_map/ppermute | solution.py:38
  304.1 36.4 %collective-permute-start.71 = (bf16[2,192,1024]{2,1,0:T(8,128)(2,1)}, bf16[2,192,1024]{2,1,0:T(8,128)(2,1)}, u32[]{:S(2)}, u32[]{:S(2)}) collective-permute-start(bf16[2,192,1024]{2,1,0:T(8,128)(2,1)} %get-tuple-element.176), channel_id=1, source_target_pairs={{0,6},{1,7},{2,0},{3,1},{4,2},{5,3},{6,4},{7,5},{8,14},{9,15},{10,... | collective-permute-start | bytes 2359304 | tf_op jit(solution)/shard_map/ppermute | solution.py:38
  326.5 13.0 %collective-permute-start.68 = (bf16[96,1024]{1,0:T(8,128)(2,1)}, bf16[96,1024]{1,0:T(8,128)(2,1)S(1)}, u32[]{:S(2)}, u32[]{:S(2)}) collective-permute-start(bf16[96,1024]{1,0:T(8,128)(2,1)} %get-tuple-element.160), channel_id=1, source_target_pairs={{0,32},{8,40},{16,48},{24,56},{32,0},{40,8},{48,16},{56,24},{1,33}... | collective-permute-start | bytes 589832 | tf_op jit(solution)/shard_map/ppermute | solution.py:38
  338.3 35.6 %collective-permute-start.73 = (bf16[2,512,1024]{2,1,0:T(8,128)(2,1)S(1)}, bf16[2,512,1024]{2,1,0:T(8,128)(2,1)S(1)}, u32[]{:S(2)}, u32[]{:S(2)}) collective-permute-start(bf16[2,512,1024]{2,1,0:T(8,128)(2,1)S(1)} %fusion.15), channel_id=1, source_target_pairs={{0,1},{1,0},{2,3},{3,2},{4,5},{5,4},{6,7},{7,6},{8,9},{9,8},{10,11... | collective-permute-start | bytes 6291464 | tf_op jit(solution)/shard_map/ppermute | solution.py:38
  352.6 20.1 %collective-permute-start.90 = (bf16[2,192,1024]{2,1,0:T(8,128)(2,1)S(1)}, bf16[2,192,1024]{2,1,0:T(8,128)(2,1)S(1)}, u32[]{:S(2)}, u32[]{:S(2)}) collective-permute-start(bf16[2,192,1024]{2,1,0:T(8,128)(2,1)S(1)} %copy-done.61), channel_id=1, source_target_pairs={{0,4},{1,5},{2,6},{3,7},{4,0},{5,1},{6,2},{7,3},{8,12},{9,13},{10,... | collective-permute-start | bytes 2359304 | tf_op jit(solution)/shard_map/ppermute | solution.py:38
  377.1 18.4 %collective-permute-start.77 = (bf16[2,256,1024]{2,1,0:T(8,128)(2,1)}, bf16[2,256,1024]{2,1,0:T(8,128)(2,1)}, u32[]{:S(2)}, u32[]{:S(2)}) collective-permute-start(bf16[2,256,1024]{2,1,0:T(8,128)(2,1)} %fusion.89), channel_id=1, source_target_pairs={{0,1},{1,0},{2,3},{3,2},{4,5},{5,4},{6,7},{7,6},{8,9},{9,8},{10,11... | collective-permute-start | bytes 3145736 | tf_op jit(solution)/shard_map/ppermute | solution.py:38
  384.0 17.7 %collective-permute-start.91 = (bf16[2,128,1024]{2,1,0:T(8,128)(2,1)}, bf16[2,128,1024]{2,1,0:T(8,128)(2,1)}, u32[]{:S(2)}, u32[]{:S(2)}) collective-permute-start(bf16[2,128,1024]{2,1,0:T(8,128)(2,1)} %get-tuple-element.182), channel_id=1, source_target_pairs={{0,2},{1,3},{2,4},{3,5},{4,6},{5,7},{6,0},{7,1},{8,10},{9,11},{10,... | collective-permute-start | bytes 1572872 | tf_op jit(solution)/shard_map/ppermute | solution.py:38
  386.0 15.8 %collective-permute-start.92 = (bf16[2,128,1024]{2,1,0:T(8,128)(2,1)}, bf16[2,128,1024]{2,1,0:T(8,128)(2,1)S(1)}, u32[]{:S(2)}, u32[]{:S(2)}) collective-permute-start(bf16[2,128,1024]{2,1,0:T(8,128)(2,1)} %get-tuple-element.181), channel_id=1, source_target_pairs={{0,6},{1,7},{2,0},{3,1},{4,2},{5,3},{6,4},{7,5},{8,14},{9,15},{10,... | collective-permute-start | bytes 1572872 | tf_op jit(solution)/shard_map/ppermute | solution.py:38
  397.3 26.8 %collective-permute-start.95 = (bf16[2,192,1024]{2,1,0:T(8,128)(2,1)S(1)}, bf16[2,192,1024]{2,1,0:T(8,128)(2,1)S(1)}, u32[]{:S(2)}, u32[]{:S(2)}) collective-permute-start(bf16[2,192,1024]{2,1,0:T(8,128)(2,1)S(1)} %pad_maximum_fusion.14), channel_id=1, source_target_pairs={{0,4},{1,5},{2,6},{3,7},{4,0},{5,1},{6,2},{7,3},{8,12},{9,13},{10,... | collective-permute-start | bytes 2359304 | tf_op jit(solution)/shard_map/ppermute | solution.py:38
  399.0 24.9 %collective-permute-start.93 = (bf16[2,64,1024]{2,1,0:T(8,128)(2,1)S(1)}, bf16[2,64,1024]{2,1,0:T(8,128)(2,1)S(1)}, u32[]{:S(2)}, u32[]{:S(2)}) collective-permute-start(bf16[2,64,1024]{2,1,0:T(8,128)(2,1)S(1)} %get-tuple-element.188), channel_id=1, source_target_pairs={{0,2},{1,3},{2,4},{3,5},{4,6},{5,7},{6,0},{7,1},{8,10},{9,11},{10,... | collective-permute-start | bytes 786440 | tf_op jit(solution)/shard_map/ppermute | solution.py:38
  399.6 24.4 %collective-permute-start.94 = (bf16[2,64,1024]{2,1,0:T(8,128)(2,1)S(1)}, bf16[2,64,1024]{2,1,0:T(8,128)(2,1)S(1)}, u32[]{:S(2)}, u32[]{:S(2)}) collective-permute-start(bf16[2,64,1024]{2,1,0:T(8,128)(2,1)S(1)} %get-tuple-element.187), channel_id=1, source_target_pairs={{0,6},{1,7},{2,0},{3,1},{4,2},{5,3},{6,4},{7,5},{8,14},{9,15},{10,... | collective-permute-start | bytes 786440 | tf_op jit(solution)/shard_map/ppermute | solution.py:38
  426.3 20.0 %collective-permute-start.96 = (bf16[192,1024]{1,0:T(8,128)(2,1)}, bf16[192,1024]{1,0:T(8,128)(2,1)S(1)}, u32[]{:S(2)}, u32[]{:S(2)}) collective-permute-start(bf16[192,1024]{1,0:T(8,128)(2,1)} %get-tuple-element.183), channel_id=1, source_target_pairs={{0,64},{8,72},{16,80},{24,88},{32,96},{40,104},{48,112},{56,120},{... | collective-permute-start | bytes 1179656 | tf_op jit(solution)/shard_map/ppermute | solution.py:38
  426.3 20.3 %collective-permute-start.97 = (bf16[192,1024]{1,0:T(8,128)(2,1)}, bf16[192,1024]{1,0:T(8,128)(2,1)S(1)}, u32[]{:S(2)}, u32[]{:S(2)}) collective-permute-start(bf16[192,1024]{1,0:T(8,128)(2,1)} %get-tuple-element.184), channel_id=1, source_target_pairs={{0,72},{8,64},{16,88},{24,80},{32,104},{40,96},{48,120},{56,112},{... | collective-permute-start | bytes 1179656 | tf_op jit(solution)/shard_map/ppermute | solution.py:38
  429.0 17.6 %collective-permute-start.98 = (bf16[192,1024]{1,0:T(8,128)(2,1)}, bf16[192,1024]{1,0:T(8,128)(2,1)}, u32[]{:S(2)}, u32[]{:S(2)}) collective-permute-start(bf16[192,1024]{1,0:T(8,128)(2,1)} %get-tuple-element.185), channel_id=1, source_target_pairs={{0,8},{8,0},{16,24},{24,16},{32,40},{40,32},{48,56},{56,48},{64,72... | collective-permute-start | bytes 1179656 | tf_op jit(solution)/shard_map/ppermute | solution.py:38
  429.5 21.9 %collective-permute-start.80 = (f32[12,1024]{1,0:T(8,128)S(1)}, f32[12,1024]{1,0:T(8,128)S(1)}, u32[]{:S(2)}, u32[]{:S(2)}) collective-permute-start(f32[12,1024]{1,0:T(8,128)S(1)} %get-tuple-element.228), channel_id=1, source_target_pairs={{0,64},{8,72},{16,80},{24,88},{32,96},{40,104},{48,112},{56,120},{... | collective-permute-start | bytes 147464 | tf_op jit(solution)/shard_map/ppermute | solution.py:38
  430.1 21.2 %collective-permute-start.81 = (f32[12,1024]{1,0:T(8,128)S(1)}, f32[12,1024]{1,0:T(8,128)S(1)}, u32[]{:S(2)}, u32[]{:S(2)}) collective-permute-start(f32[12,1024]{1,0:T(8,128)S(1)} %get-tuple-element.228), channel_id=1, source_target_pairs={{0,72},{8,64},{16,88},{24,80},{32,104},{40,96},{48,120},{56,112},{... | collective-permute-start | bytes 147464 | tf_op jit(solution)/shard_map/ppermute | solution.py:38
  448.7 18.1 %collective-permute-start.100 = (bf16[192,1024]{1,0:T(8,128)(2,1)S(1)}, bf16[192,1024]{1,0:T(8,128)(2,1)S(1)}, u32[]{:S(2)}, u32[]{:S(2)}) collective-permute-start(bf16[192,1024]{1,0:T(8,128)(2,1)S(1)} %get-tuple-element.151), channel_id=1, source_target_pairs={{0,4},{1,5},{2,6},{3,7},{4,0},{5,1},{6,2},{7,3},{8,12},{9,13},{10,... | collective-permute-start | bytes 1179656 | tf_op jit(solution)/shard_map/ppermute | solution.py:38
  451.4 19.0 %collective-permute-start.83 = (f32[12,1024]{1,0:T(8,128)S(1)}, f32[12,1024]{1,0:T(8,128)S(1)}, u32[]{:S(2)}, u32[]{:S(2)}) collective-permute-start(f32[12,1024]{1,0:T(8,128)S(1)} %add_add_fusion.2), channel_id=1, source_target_pairs={{0,1},{1,0},{2,3},{3,2},{4,5},{5,4},{6,7},{7,6},{8,9},{9,8},{10,11... | collective-permute-start | bytes 147464 | tf_op jit(solution)/shard_map/ppermute | solution.py:38
  454.5 13.9 %collective-permute-start.101 = (bf16[192,1024]{1,0:T(8,128)(2,1)S(1)}, bf16[192,1024]{1,0:T(8,128)(2,1)S(1)}, u32[]{:S(2)}, u32[]{:S(2)}) collective-permute-start(bf16[192,1024]{1,0:T(8,128)(2,1)S(1)} %get-tuple-element.151), channel_id=1, source_target_pairs={{0,6},{1,7},{2,0},{3,1},{4,2},{5,3},{6,4},{7,5},{8,14},{9,15},{10,... | collective-permute-start | bytes 1179656 | tf_op jit(solution)/shard_map/ppermute | solution.py:38
  468.5 23.2 %collective-permute-start.102 = (bf16[768,1024]{1,0:T(8,128)(2,1)S(1)}, bf16[768,1024]{1,0:T(8,128)(2,1)S(1)}, u32[]{:S(2)}, u32[]{:S(2)}) collective-permute-start(bf16[768,1024]{1,0:T(8,128)(2,1)S(1)} %bitcast.435), channel_id=1, source_target_pairs={{0,1},{1,0},{2,3},{3,2},{4,5},{5,4},{6,7},{7,6},{8,9},{9,8},{10,11... | collective-permute-start | bytes 4718600 | tf_op jit(solution)/shard_map/ppermute | solution.py:38
  473.2 12.8 %collective-permute-start.79 = (bf16[96,1024]{1,0:T(8,128)(2,1)S(1)}, bf16[96,1024]{1,0:T(8,128)(2,1)S(1)}, u32[]{:S(2)}, u32[]{:S(2)}) collective-permute-start(bf16[96,1024]{1,0:T(8,128)(2,1)S(1)} %broadcast_select_fusion), channel_id=1, source_target_pairs={{0,64},{1,72},{2,66},{3,74},{4,68},{5,76},{6,70},{7,78},{8,65},{9,... | collective-permute-start | bytes 589832 | tf_op jit(solution)/shard_map/ppermute | solution.py:38
  (166 other events, 1228.4 us)
